TPU v7x, 512 devices: a whole 4x4x16 slice. The times are simulated.
512 devices in a mesh: leaf: 8 (over z_hi, y), row: 8 (over x, core), col: 8 (over z_lo).
Axes of the slice: x: 4, y: 4, z: 16 (z_hi: 2, z_lo: 8; z = z_hi * 8 + z_lo), core: 2. Of those that a mesh axis runs over, the one named last changes fastest.
Arguments:
- root_inverse: float32 [8192, 8192], P('row', ('leaf', 'col')), as said below
- root_row: int32 [8, 6144], replicated, may hold values from -1 to 8191, as said below
- coupling: float32 [8, 6144, 3072], P('leaf', 'row', 'col')
- pivot_variance: float32 [8, 3072], P('leaf', 'col'), may hold values from 0.5 to 2
Outputs:
- off_diagonal_inverse: float32 [8, 6144, 3072], P('leaf', 'row', 'col')
- pivot_marginal: float32 [8, 3072], P('leaf', 'col')
Inputs may be any that keep to these rules, and one draw needn't show every extreme that they name: `root_row`: in each aligned block of 128 update rows of a child, the entries that are not -1 come first, increase, lie in one aligned block of 128 root rows, and number 128 // 2 to 128; the blocks of one child use distinct root blocks, increasing along the child; block b uses a root block within rows k * 1024 to (k + 1) * 1024 - 1, where k = b // 6. `root_inverse`: Symmetric.
All inputs are finite; a program needn't handle non-finite values.
Results may differ from a plain program's by a relative error of at most 0.0003.
Values sent between devices are 32-bit elements; how exact they have to be, the bound alone decides.
No kernel may reach another device: no remote copies, remote signals or barrier semaphores. Data moves between devices by JAX's collectives and lax.ppermute only.
A program may use at most 128 MiB of HBM per device.

v0:
```python
import jax
import jax.numpy as jnp
from jax import lax
from jax.sharding import PartitionSpec as P


def select_rows(matrix, mapping, offset):
    usable = mapping >= 0
    position = jnp.where(usable, mapping - offset, 0)
    picked = jnp.take(matrix, position, axis=0)
    return jnp.where(usable[..., None], picked, 0.0)


def select_columns(matrix, mapping, offset):
    usable = mapping >= 0
    position = jnp.where(usable, mapping - offset, 0)
    picked = jnp.take(matrix, position, axis=1)
    return jnp.where(usable[None, :], picked, 0.0)


def per_device(root_inverse, root_row, coupling, pivot_variance):
    leaf_count = lax.axis_size("leaf")
    col_count = lax.axis_size("col")
    groups = col_count // leaf_count
    child_index = lax.axis_index("leaf")
    row_index = lax.axis_index("row")
    col_index = lax.axis_index("col")
    range_rows, shard_cols = root_inverse.shape
    tile_rows = coupling.shape[1]
    children = root_row.shape[0]
    slot_mask = (jnp.arange(groups) == col_index // leaf_count).astype(jnp.float32)
    child_rows = lax.dynamic_slice(root_row, (child_index, row_index * tile_rows), (1, tile_rows))[
        0
    ]
    child_cols = lax.dynamic_slice(root_row, (child_index, col_index * tile_rows), (1, tile_rows))[
        0
    ]
    outgoing = jnp.broadcast_to(
        root_inverse[None, None] * slot_mask[None, :, None, None],
        (children, groups, range_rows, shard_cols),
    ).reshape(children * groups, range_rows, shard_cols)
    arrived = lax.all_to_all(
        lax.all_to_all(outgoing, "leaf", split_axis=0, concat_axis=0, tiled=True),
        "col",
        split_axis=0,
        concat_axis=0,
        tiled=True,
    )
    whole_strip = jnp.transpose(arrived, (1, 0, 2)).reshape(range_rows, leaf_count * shard_cols)
    strip = select_rows(whole_strip, child_rows, row_index * range_rows)
    adjoint_tile = select_columns(strip, child_cols, col_index * range_rows)
    factor_tile = coupling[0]
    pivot_cols = factor_tile.shape[1]
    initial = jnp.zeros((tile_rows, pivot_cols), jnp.float32)
    factor_cols = lax.all_gather(factor_tile, "row", axis=0, tiled=True)
    product = initial - jnp.dot(
        lax.all_gather(adjoint_tile, "col", axis=1, tiled=True),
        factor_cols,
        precision=lax.Precision.HIGHEST,
        preferred_element_type=jnp.float32,
    )
    partial_sums = jnp.sum(factor_tile * product, axis=0)
    summed = lax.psum(partial_sums, "row")
    marginal = pivot_variance - summed[None, :]
    return (product[None], marginal)


def solution(mesh):
    placed = (P("row", ("leaf", "col")), P(), P("leaf", "row", "col"), P("leaf", "col"))
    return jax.shard_map(
        per_device,
        mesh=mesh,
        in_specs=placed,
        out_specs=(P("leaf", "row", "col"), P("leaf", "col")),
        check_vma=False,
    )
```

profile of v0, /device:TPU:1, one launch (start us, length us, event | category | flops | bytes accessed | tf_op | source)
XLA Modules:
  0.0 859.0 jit_solution(12131852600011348435)
XLA Ops:
  7.2 1.1 broadcast_multiply_fusion
  8.3 2.2 reshape.120
  10.5 18.3 %all-to-all-start = ((f32[8,1024,128]{2,1,0:T(8,128)}), f32[8,1024,128]{2,1,0:T(8,128)}, u32[]{:S(2)}, u32[]{:S(2)}) async-start(f32[8,1024,128]{2,1,0:T(8,128)} %reshape.120), calls=%async_computation | async-start | bytes 8388608 | tf_op jit(solution)/shard_map/all_to_all | solution.py:43
  28.8 0.0 all-gather.6.cloned.1.call-start
  28.8 0.7 all-gather.6.cloned.1.call-update
  29.5 80.0 %all-to-all-done = f32[8,1024,128]{2,1,0:T(8,128)} async-done(((f32[8,1024,128]{2,1,0:T(8,128)}), f32[8,1024,128]{2,1,0:T(8,128)}, u32[]{:S(2)}, u32[]{:S(2)}) %all-to-all-start) | async-done | bytes 4194336 | tf_op jit(solution)/shard_map/all_to_all | solution.py:43
  109.5 116.2 %all-to-all-start.1 = ((f32[8,1024,128]{2,1,0:T(8,128)}), f32[8,1024,128]{2,1,0:T(8,128)}, u32[]{:S(2)}, u32[]{:S(2)}) async-start(f32[8,1024,128]{2,1,0:T(8,128)} %all-to-all-done), calls=%async_computation.1 | async-start | bytes 8388608 | tf_op jit(solution)/shard_map/all_to_all | solution.py:42
  225.7 0.0 all-gather.4.cloned.1.call-start
  225.8 0.9 compare_reduce_fusion.1
  226.6 0.9 fusion.9
  227.5 0.9 fusion.7
  228.4 181.7 %all-to-all-done.1 = f32[8,1024,128]{2,1,0:T(8,128)} async-done(((f32[8,1024,128]{2,1,0:T(8,128)}), f32[8,1024,128]{2,1,0:T(8,128)}, u32[]{:S(2)}, u32[]{:S(2)}) %all-to-all-start.1) | async-done | bytes 4194336 | tf_op jit(solution)/shard_map/all_to_all | solution.py:42
  410.1 4.7 copy_bitcast_fusion
  414.8 6.1 gather_fusion
  420.9 2.1 select_select_fusion
  423.0 2.4 copy.9
  425.4 3.5 gather_fusion.1
  428.9 0.0 copy-start
  428.9 3.6 select_bitcast_fusion
  432.5 0.0 all-gather.4.cloned.1.call-update
  432.5 0.0 copy-start.1
  432.5 0.0 all-gather.6.cloned.1.call-done
  432.6 372.0 %all-gather.4.cloned.1.call-done = f32[768,6144]{0,1:T(8,128)} async-done(((f32[768,768]{0,1:T(8,128)}), f32[768,6144]{0,1:T(8,128)}) %all-gather.4.cloned.1.call-update) | async-done | bytes 18874384 | tf_op jit(solution)/shard_map/all_gather | solution.py:57
  804.6 0.0 copy-done
  804.6 34.3 %fusion.5 = (f32[384]{0:T(512)S(1)}, f32[768,384]{1,0:T(8,128)}) fusion(f32[1,768,384]{2,1,0:T(8,128)S(1)} %copy-done, f32[768,6144]{0,1:T(8,128)} %all-gather.4.cloned.1.call-done, f32[1,6144,384]{2,1,0:T(8,128)} %all-gather.6.cloned.1.call-done), kind=kOutput, calls=%fused_computation.9 | convolution fusion | flops 21744156672 | bytes 30672384 | tf_op jit(solution)/shard_map/dot_general | solution.py:56
  839.0 12.7 %psum.7 = f32[1,384]{1,0:T(1,128)S(1)} all-reduce(f32[1,384]{1,0:T(1,128)S(1)} %broadcast_in_dim.76), channel_id=1, replica_groups=mesh['leaf'=8,'row'=8,'col'=8] {'row'}, use_global_device_ids=true, to_apply=%region_1.2 | all-reduce | flops 384 | bytes 3072 | tf_op jit(solution)/shard_map/psum | solution.py:63
  851.6 0.0 copy-done.1
  851.6 0.6 sub.53
  (4 shorter events, 0.0 us)
Async XLA Ops:
  10.5 99.0 %all-to-all-start = ((f32[8,1024,128]{2,1,0:T(8,128)}), f32[8,1024,128]{2,1,0:T(8,128)}, u32[]{:S(2)}, u32[]{:S(2)}) async-start(f32[8,1024,128]{2,1,0:T(8,128)} %reshape.120), calls=%async_computation | async-start | bytes 8388608 | tf_op jit(solution)/shard_map/all_to_all | solution.py:43
  28.8 403.8 %all-gather.6.cloned.1.call-start = ((), (), s32[]{:S(2)}) async-start(), calls=%async_computation.3 | async-start | bytes 10616832 | tf_op jit(solution)/shard_map/all_gather | solution.py:55
  109.5 300.6 %all-to-all-start.1 = ((f32[8,1024,128]{2,1,0:T(8,128)}), f32[8,1024,128]{2,1,0:T(8,128)}, u32[]{:S(2)}, u32[]{:S(2)}) async-start(f32[8,1024,128]{2,1,0:T(8,128)} %all-to-all-done), calls=%async_computation.1 | async-start | bytes 8388608 | tf_op jit(solution)/shard_map/all_to_all | solution.py:42
  225.7 578.9 %all-gather.4.cloned.1.call-start = ((), (), s32[]{:S(2)}) async-start(), calls=%async_computation.2 | async-start | bytes 21233664 | tf_op jit(solution)/shard_map/all_gather | solution.py:57
  428.9 375.7 %copy-start = (f32[1,768,384]{2,1,0:T(8,128)S(1)}, f32[1,768,384]{2,1,0:T(8,128)}, u32[]{:S(2)}) copy-start(f32[1,768,384]{2,1,0:T(8,128)} %param.6) | copy-start | bytes 3538948
  432.5 419.1 %copy-start.1 = (f32[1,384]{1,0:T(1,128)S(1)}, f32[1,384]{1,0:T(1,128)}, u32[]{:S(2)}) copy-start(f32[1,384]{1,0:T(1,128)} %param.7) | copy-start | bytes 4612
Sparse Core Ops, SparseCore 0:
  31.7 63.6 all-gather.5
  432.7 371.9 all-gather.3
where the time goes:
time: 861 us; the launch traced here: 859 us
  waiting for transfers between devices  634 us (74%)
  starting transfers between devices  135 us (16%)
  matrix products  34.3 us (4%)
  local copies, waits for them, and re-layouts  19 us (2%)
  between operations  14.1 us (2%)
  blocking collectives  12.7 us (1%)
  other arithmetic  9.91 us (1%)
    all_gather x1, waiting for transfers between devices, per_device(): lax.all_gather(adjoint_tile, 'col', axis=1, tiled=True)  372 us
    all_to_all x1, waiting for transfers between devices, per_device(): lax.all_to_all(lax.all_to_all(outgoing, 'leaf', split_axis=0, concat_axis...  182 us
    all_to_all x1, starting transfers between devices, per_device(): lax.all_to_all(lax.all_to_all(outgoing, 'leaf', split_axis=0, concat_axis...  116 us
    all_to_all x1, waiting for transfers between devices, per_device(): lax.all_to_all(outgoing, 'leaf', split_axis=0, concat_axis=0, tiled=True)  80 us
    dot_general x1, matrix products, per_device(): jnp.dot(lax.all_gather(adjoint_tile, 'col', axis=1, tiled=True), factor_c...  34.3 us
    all_to_all x1, starting transfers between devices, per_device(): lax.all_to_all(outgoing, 'leaf', split_axis=0, concat_axis=0, tiled=True)  18.3 us
  transfers between devices with their start and end apart: 4, of which 3 were waited for; matrix products, arithmetic and copies ran while one was open for 3% of the time, Pallas kernels for 0%

commit v1 on v0

v1 whole, which is shorter than its diff:
```python
import functools

import jax
import jax.numpy as jnp
from jax import lax
from jax.experimental import pallas as pl
from jax.experimental.pallas import tpu as pltpu
from jax.sharding import Mesh, PartitionSpec as P

BLOCK = 128
ORDER = (0, -1, 1, 2)
SPLIT_ROWS = 128


def shift(size, step):
    return [(i, (i + step) % size) for i in range(size)]


def split_into(high_ref, low_ref, value, index):
    high = value.astype(jnp.bfloat16)
    high_ref[index] = high
    low_ref[index] = (value - high.astype(jnp.float32)).astype(jnp.bfloat16)


def product_kernel(table, root_hbm, *rest):
    pieces = rest[:10]
    out_hbm = rest[10]
    (root_f, root_h, root_l, z_f, z_h, z_l, a_h, a_l, out_v, root_sem, z_sem, out_sem) = rest[11:]
    blocks = root_f.shape[0]
    rows = z_f.shape[2]
    half = rows // 2
    per_range = rows // BLOCK
    places = []
    for side in range(2):
        for slot in range(3):
            places.append((side, slot, 0, rows))
        places.append((side, 3, 0, half))
        places.append((side, 3, half, half))
    z_copies = [
        pltpu.make_async_copy(piece, z_f.at[side, slot, pl.ds(start, size)], z_sem.at[i])
        for i, (piece, (side, slot, start, size)) in enumerate(zip(pieces, places))
    ]
    root_copies = [
        pltpu.make_async_copy(root_hbm.at[b], root_f.at[b], root_sem.at[b]) for b in range(blocks)
    ]
    for copy in z_copies:
        copy.start()
    for copy in root_copies:
        copy.start()
    for copy, (side, slot, start, size) in zip(z_copies, places):
        copy.wait()

        def split_z(i, carry, side=side, slot=slot, start=start):
            at = pl.ds(pl.multiple_of(start + i * SPLIT_ROWS, SPLIT_ROWS), SPLIT_ROWS)
            value = z_f[side, slot, at, :]
            high = value.astype(jnp.bfloat16)
            z_h[slot, side, at, :] = high
            z_l[slot, side, at, :] = (value - high.astype(jnp.float32)).astype(jnp.bfloat16)
            return carry

        lax.fori_loop(0, size // SPLIT_ROWS, split_z, 0)
    for b, copy in enumerate(root_copies):
        copy.wait()

        def split_root(i, carry, b=b):
            at = pl.ds(pl.multiple_of(i * 256, 256), 256)
            value = root_f[b, at, :]
            high = value.astype(jnp.bfloat16)
            root_h[b, at, :] = high
            root_l[b, at, :] = (value - high.astype(jnp.float32)).astype(jnp.bfloat16)
            return carry

        lax.fori_loop(0, root_f.shape[1] // 256, split_root, 0)

    def child(t, carry):
        slot = table[t, 0]

        def select(k, inner):
            kb = table[t, 1 + per_range + k]
            for m in range(per_range):
                mb = pl.multiple_of(table[t, 1 + m] * BLOCK, BLOCK)
                at = pl.ds(m * BLOCK, BLOCK)
                a_h[k, at, :] = root_h[kb, pl.ds(mb, BLOCK), :]
                a_l[k, at, :] = root_l[kb, pl.ds(mb, BLOCK), :]
            return inner

        lax.fori_loop(0, 2 * per_range, select, 0)
        zh = z_h[slot].reshape(2 * rows, z_h.shape[3])
        zl = z_l[slot].reshape(2 * rows, z_h.shape[3])

        def part(m, inner):
            at = pl.ds(pl.multiple_of(m * 256, 256), 256)
            ah = jnp.concatenate([a_h[k, at, :] for k in range(2 * per_range)], axis=1)
            al = jnp.concatenate([a_l[k, at, :] for k in range(2 * per_range)], axis=1)
            total = jnp.dot(ah, zl, preferred_element_type=jnp.float32)
            total = total + jnp.dot(al, zh, preferred_element_type=jnp.float32)
            out_v[t, at, :] = total + jnp.dot(ah, zh, preferred_element_type=jnp.float32)
            return inner

        lax.fori_loop(0, rows // 256, part, 0)
        pltpu.make_async_copy(out_v.at[t], out_hbm.at[t], out_sem.at[t]).start()
        return carry

    lax.fori_loop(0, 4, child, 0)
    for t in range(4):
        pltpu.make_async_copy(out_v.at[t], out_hbm.at[t], out_sem.at[t]).wait()


def product(table, root, pieces):
    blocks, range_rows, _ = root.shape
    rows, cols = pieces[0].shape
    any_spec = pl.BlockSpec(memory_space=pl.ANY)
    return pl.pallas_call(
        product_kernel,
        out_shape=jax.ShapeDtypeStruct((4, rows, cols), jnp.float32),
        in_specs=[pl.BlockSpec(memory_space=pltpu.SMEM)] + [any_spec] * (1 + len(pieces)),
        out_specs=any_spec,
        scratch_shapes=[
            pltpu.VMEM((blocks, range_rows, BLOCK), jnp.float32),
            pltpu.VMEM((blocks, range_rows, BLOCK), jnp.bfloat16),
            pltpu.VMEM((blocks, range_rows, BLOCK), jnp.bfloat16),
            pltpu.VMEM((2, 4, rows, cols), jnp.float32),
            pltpu.VMEM((4, 2, rows, cols), jnp.bfloat16),
            pltpu.VMEM((4, 2, rows, cols), jnp.bfloat16),
            pltpu.VMEM((2 * rows // BLOCK, rows, BLOCK), jnp.bfloat16),
            pltpu.VMEM((2 * rows // BLOCK, rows, BLOCK), jnp.bfloat16),
            pltpu.VMEM((4, rows, cols), jnp.float32),
            pltpu.SemaphoreType.DMA((blocks,)),
            pltpu.SemaphoreType.DMA((len(pieces),)),
            pltpu.SemaphoreType.DMA((4,)),
        ],
        compiler_params=pltpu.CompilerParams(vmem_limit_bytes=60 * 1024 * 1024),
        cost_estimate=pl.CostEstimate(
            flops=4 * 3 * 2 * rows * 2 * rows * cols, bytes_accessed=24_000_000, transcendentals=0
        ),
    )(table, root, *pieces)


def per_device(root_inverse, root_row, coupling, pivot_variance):
    zh = lax.axis_index("zh")
    y = lax.axis_index("y")
    x = lax.axis_index("x")
    core = lax.axis_index("core")
    rows, cols = coupling.shape[1:]
    ranges = root_row.shape[1] // rows
    per_range = rows // BLOCK
    own_range = 2 * x + core

    first = root_row[:, ::BLOCK]
    block = (first // BLOCK).reshape(root_row.shape[0], ranges, per_range)
    place = lax.dynamic_slice(root_row, (zh * 4 + y, own_range * rows), (1, rows))
    place = place.reshape(per_range, BLOCK)
    own_block = block[zh * 4 + y, own_range]
    offsets = jnp.arange(BLOCK, dtype=jnp.int32)
    hot = (
        (place - own_block[:, None] * BLOCK)[:, :, None] == offsets[None, None, :]
    ).astype(jnp.float32)
    factor = coupling[0].reshape(per_range, BLOCK, cols)
    spread = jnp.einsum("iuo,iun->ion", hot, factor, precision=lax.Precision.HIGHEST)
    spread = spread.reshape(rows, cols)

    root = lax.all_gather(root_inverse, ("zh", "zl"), axis=0, tiled=False)

    swap = []
    for sy in range(4):
        for sx in range(4):
            for sc in range(2):
                r = 2 * sx + sc
                swap.append(((sy * 4 + sx) * 2 + sc, ((r % 4) * 4 + sy) * 2 + r // 4))
    own = lax.ppermute(spread, ("y", "x", "core"), swap)
    left = lax.ppermute(own, "x", shift(4, 1))
    right = lax.ppermute(own, "x", shift(4, -1))
    half = rows // 2
    far_a = lax.ppermute(left[:half], "x", shift(4, 1))
    far_b = lax.ppermute(right[half:], "x", shift(4, -1))
    mine = [own, left, right, far_a, far_b]
    other = [lax.ppermute(p, "core", [(0, 1), (1, 0)]) for p in mine]

    t = jnp.arange(4)
    child = (y + t) % 4
    slot_of_step = jnp.array([0, 2, 3, 1], jnp.int32)
    slot = slot_of_step[(child - x) % 4]
    row_blocks = block[zh * 4 + child, own_range] % 8
    sides = []
    for side in range(2):
        half_of = core if side == 0 else 1 - core
        column_blocks = block[zh * 4 + child, y + 4 * half_of] % 8
        sides.append(column_blocks + 8 * half_of)
    table = jnp.concatenate([slot[:, None], row_blocks, *sides], axis=1).astype(jnp.int32)

    partial = product(table, root.reshape(-1, *root_inverse.shape), mine + other)

    a = lax.ppermute(partial[2, :half], "y", shift(4, 1))
    b = lax.ppermute(partial[2, half:], "y", shift(4, -1))
    up = jnp.concatenate([partial[1, :half] + a, partial[1, half:]])
    down = jnp.concatenate([partial[3, :half], partial[3, half:] + b])
    summed = partial[0] + lax.ppermute(up, "y", shift(4, 1)) + lax.ppermute(down, "y", shift(4, -1))
    result = -jnp.einsum(
        "iuo,ion->iun", hot, summed.reshape(per_range, BLOCK, cols), precision=lax.Precision.HIGHEST
    )
    sums = jnp.sum(factor * result, axis=(0, 1))
    marginal = pivot_variance - lax.psum(sums, ("x", "core"))[None, :]
    return result.reshape(1, rows, cols), marginal


def solution(mesh):
    split = Mesh(mesh.devices.reshape(2, 4, 4, 2, 8), ("zh", "y", "x", "core", "zl"))
    leaf, row, col = ("zh", "y"), ("x", "core"), "zl"
    return jax.shard_map(
        per_device,
        mesh=split,
        in_specs=(P(row, ("zh", "y", "zl")), P(), P(leaf, row, col), P(leaf, col)),
        out_specs=(P(leaf, row, col), P(leaf, col)),
        check_vma=False,
    )
```

time: 861 us -> 238 us (0.28)
  waiting for transfers between devices: 634 us -> 107 us
  starting transfers between devices: 135 us -> 56.1 us
  matrix products: 34.3 us -> 3.98 us
  Pallas kernels: 0 us -> 27.6 us
  local copies, waits for them, and re-layouts: 19 us -> 10 us
    all_gather x2 -> x1, waiting for transfers between devices: 372 us -> 0.02 us  [per_device(): root = lax.all_gather(root_inverse, ('zh', 'zl'), axis=0, tiled=False)]
    all_to_all x2 -> x0, waiting for transfers between devices: 262 us -> none  [the longest x1 182 us: per_device(): lax.all_to_all(lax.all_to_all(outgoing, 'leaf', split_axis=0, concat_axis...]
    all_to_all x2 -> x0, starting transfers between devices: 134 us -> none  [the longest x1 116 us: per_device(): lax.all_to_all(lax.all_to_all(outgoing, 'leaf', split_axis=0, concat_axis...]
    ppermute x0 -> x14, waiting for transfers between devices: none -> 107 us  [the longest x1 49.4 us: per_device(): own = lax.ppermute(spread, ('y', 'x', 'core'), swap)]
    ppermute x0 -> x14, starting transfers between devices: none -> 56.1 us  [the longest x5 16.3 us: per_device(): other = [lax.ppermute(p, 'core', [(0, 1), (1, 0)]) for p in mine]]
    dot_general x1 -> x2, matrix products: 34.3 us -> 3.98 us  [the longest x1 2.16 us: per_device(): jnp.einsum('iuo,iun->ion', hot, factor, precision=lax.Precision.HIGHEST)]
    pallas_call x0 -> x1, Pallas kernels: none -> 27.6 us  [product(): pl.pallas_call(product_kernel, out_shape=jax.ShapeDtypeStruct((4, rows, c...]
  transfers between devices with their start and end apart: 4 -> 15, of which waited for: 3 -> 6; matrix products, arithmetic and copies ran while one was open for 3% -> 5% of each run, Pallas kernels for 0% -> 0%
where the time goes in v1:
time: 238 us; the launch traced here: 237 us
  waiting for transfers between devices  107 us (45%)
  starting transfers between devices  56.1 us (24%)
  Pallas kernels  27.6 us (12%)
  between operations  14.4 us (6%)
  blocking collectives  13.7 us (6%)
  local copies, waits for them, and re-layouts  10 us (4%)
  matrix products  3.98 us (2%)
  other arithmetic  3.77 us (2%)
    ppermute x1, waiting for transfers between devices, per_device(): own = lax.ppermute(spread, ('y', 'x', 'core'), swap)  49.4 us
    pallas_call x1, Pallas kernels, product(): pl.pallas_call(product_kernel, out_shape=jax.ShapeDtypeStruct((4, rows, c...  27.6 us
    ppermute x1, waiting for transfers between devices, per_device(): lax.ppermute(down, 'y', shift(4, -1))  22.3 us
    ppermute x1, waiting for transfers between devices, per_device(): right = lax.ppermute(own, 'x', shift(4, -1))  16.7 us
    ppermute x5, starting transfers between devices, per_device(): other = [lax.ppermute(p, 'core', [(0, 1), (1, 0)]) for p in mine]  16.3 us
    psum x1, blocking collectives, per_device(): marginal = pivot_variance - lax.psum(sums, ('x', 'core'))[None, :]  13.7 us
    ppermute x1, waiting for transfers between devices, per_device(): a = lax.ppermute(partial[2, :half], 'y', shift(4, 1))  11.8 us
    ppermute x1, starting transfers between devices, per_device(): b = lax.ppermute(partial[2, half:], 'y', shift(4, -1))  6.89 us
  transfers between devices with their start and end apart: 15, of which 6 were waited for; matrix products, arithmetic and copies ran while one was open for 5% of the time, Pallas kernels for 0%

profile of v1, /device:TPU:1, one launch (start us, length us, event | category | flops | bytes accessed | tf_op | source)
XLA Modules:
  0.0 237.0 jit_solution(15756367778222710494)
XLA Ops:
  7.2 0.0 all-gather.3.cloned.1.call-start
  7.2 0.7 all-gather.3.cloned.1.call-update
  7.9 1.0 slice.30
  9.0 0.1 reshape.146
  9.1 0.8 dynamic-slice_reduce_fusion
  9.9 0.1 bitcast_subtract_fusion
  10.0 2.2 fusion.4
  12.2 0.0 copy-done.5
  12.2 0.0 copy-start
  12.2 4.6 %collective-permute-start = (f32[768,384]{1,0:T(8,128)S(1)}, f32[768,384]{1,0:T(8,128)}, u32[]{:S(2)}, u32[]{:S(2)}) collective-permute-start(f32[768,384]{1,0:T(8,128)S(1)} %bitcast.45), channel_id=1, source_target_pairs={{0,0},{8,64},{16,128},{24,192},{32,8},{40,72},{48,136},{56,200},{6... | collective-permute-start | bytes 3538952 | tf_op jit(solution)/shard_map/ppermute | solution.py:170
  16.8 49.4 %collective-permute-done.rest_0_ = f32[768,384]{1,0:T(8,128)} collective-permute-done((f32[768,384]{1,0:T(8,128)S(1)}, f32[768,384]{1,0:T(8,128)}, u32[]{:S(2)}, u32[]{:S(2)}) %collective-permute-start) | collective-permute-done | bytes 1179680 | tf_op jit(solution)/shard_map/ppermute | solution.py:170
  66.1 5.3 %collective-permute-start.2 = (f32[768,384]{1,0:T(8,128)}, f32[768,384]{1,0:T(8,128)S(1)}, u32[]{:S(2)}, u32[]{:S(2)}) collective-permute-start(f32[768,384]{1,0:T(8,128)} %collective-permute-done.rest_0_), channel_id=1, source_target_pairs={{0,48},{16,0},{32,16},{48,32},{1,49},{17,1},{33,17},{49,33},{2,50}... | collective-permute-start | bytes 3538952 | tf_op jit(solution)/shard_map/ppermute | solution.py:172
  71.4 2.9 %collective-permute-start.1 = (f32[768,384]{1,0:T(8,128)}, f32[768,384]{1,0:T(8,128)S(1)}, u32[]{:S(2)}, u32[]{:S(2)}) collective-permute-start(f32[768,384]{1,0:T(8,128)} %collective-permute-done.rest_0_), channel_id=1, source_target_pairs={{0,16},{16,32},{32,48},{48,0},{1,17},{17,33},{33,49},{49,1},{2,18}... | collective-permute-start | bytes 3538952 | tf_op jit(solution)/shard_map/ppermute | solution.py:171
  74.3 16.7 %collective-permute-done.2.rest_2_ = f32[768,384]{1,0:T(8,128)S(1)} collective-permute-done((f32[768,384]{1,0:T(8,128)}, f32[768,384]{1,0:T(8,128)S(1)}, u32[]{:S(2)}, u32[]{:S(2)}) %collective-permute-start.2) | collective-permute-done | bytes 1179680 | tf_op jit(solution)/shard_map/ppermute | solution.py:172
  91.1 6.6 %collective-permute-start.4 = (f32[384,384]{1,0:T(8,128)S(1)}, f32[384,384]{1,0:T(8,128)}, u32[]{:S(2)}, u32[]{:S(2)}) collective-permute-start(f32[384,384]{1,0:T(8,128)S(1)} %slice.49), channel_id=1, source_target_pairs={{0,48},{16,0},{32,16},{48,32},{1,49},{17,1},{33,17},{49,33},{2,50}... | collective-permute-start | bytes 1769480 | tf_op jit(solution)/shard_map/ppermute | solution.py:175
  97.7 0.0 collective-permute-done.1.rest_1_
  97.7 0.0 copy-start.4
  97.8 1.9 collective-permute-start.3
  99.7 7.7 %collective-permute-start.5 = (f32[768,384]{1,0:T(8,128)}, f32[768,384]{1,0:T(8,128)}, u32[]{:S(2)}, u32[]{:S(2)}) collective-permute-start(f32[768,384]{1,0:T(8,128)} %collective-permute-done.rest_0_), channel_id=1, source_target_pairs={{0,8},{8,0},{1,9},{9,1},{2,10},{10,2},{3,11},{11,3},{4,12},{12,4},... | collective-permute-start | bytes 3538952 | tf_op jit(solution)/shard_map/ppermute | solution.py:177
  107.4 0.0 copy-done.3
  107.4 1.9 collective-permute-start.7
  109.3 2.4 %collective-permute-start.6 = (f32[768,384]{1,0:T(8,128)S(1)}, f32[768,384]{1,0:T(8,128)}, u32[]{:S(2)}, u32[]{:S(2)}) collective-permute-start(f32[768,384]{1,0:T(8,128)S(1)} %collective-permute-done.1.rest_1_), channel_id=1, source_target_pairs={{0,8},{8,0},{1,9},{9,1},{2,10},{10,2},{3,11},{11,3},{4,12},{12,4},... | collective-permute-start | bytes 3538952 | tf_op jit(solution)/shard_map/ppermute | solution.py:177
  111.7 1.9 gather_fusion.1
  113.7 1.3 add_select_fusion.3
  114.9 0.0 collective-permute-done.4.rest_4_
  114.9 1.9 collective-permute-start.9
  116.9 0.0 collective-permute-done.3.rest_3_
  116.9 2.4 %collective-permute-start.8 = (f32[384,384]{1,0:T(8,128)}, f32[384,384]{1,0:T(8,128)S(1)}, u32[]{:S(2)}, u32[]{:S(2)}) collective-permute-start(f32[384,384]{1,0:T(8,128)} %collective-permute-done.3.rest_3_), channel_id=1, source_target_pairs={{0,8},{8,0},{1,9},{9,1},{2,10},{10,2},{3,11},{11,3},{4,12},{12,4},... | collective-permute-start | bytes 1769480 | tf_op jit(solution)/shard_map/ppermute | solution.py:177
  119.3 0.0 copy-done
  119.3 0.6 gather_fusion
  120.0 0.1 copy.9
  120.1 1.3 gather_fusion.3
  121.4 1.3 gather_fusion.2
  122.8 1.3 pad_add_fusion.table
  124.1 0.0 collective-permute-done.5.rest_5_
  124.1 0.0 collective-permute-done.9.rest_9_
  124.1 0.0 collective-permute-done.7.rest_7_
  124.1 0.0 collective-permute-done.8.rest_8_
  124.1 0.0 copy-start.7
  124.1 0.0 collective-permute-done.6.rest_6_
  124.1 0.0 all-gather.3.cloned.1.call-done
  124.2 0.0 copy-done.4
  124.2 0.8 copy-done.7
  124.9 27.6 %shard_map.68 = f32[4,768,384]{2,1,0:T(8,128)} custom-call(s32[4,19]{1,0:T(4,128)} %pad_add_fusion.table, f32[16,1024,128]{2,1,0:T(8,128)} %bitcast.48, f32[768,384]{1,0:T(8,128)} %collective-permute-done.rest_0_, f32[768,384]{1,0:T(8,128)} %copy-done.4, f32[768,384]{1,0:T(8,128)} %copy-done.3, f32[384,384]{1,0:T(8,128)} %collective-permute-done.3.rest_3_, ...), custom_call_target="tpu_custom_call" | custom-call | flops 10871635968 | bytes 24000000 | tf_op jit(solution)/shard_map/pallas_call | solution.py:113
  152.5 0.0 copy-start.1
  152.5 1.9 slice_bitcast_fusion.5
  154.4 4.5 %collective-permute-start.10 = (f32[384,384]{1,0:T(8,128)S(1)}, f32[384,384]{1,0:T(8,128)S(1)}, u32[]{:S(2)}, u32[]{:S(2)}) collective-permute-start(f32[384,384]{1,0:T(8,128)S(1)} %get-tuple-element.4), channel_id=1, source_target_pairs={{0,64},{64,128},{128,192},{192,0},{1,65},{65,129},{129,193},{193,1... | collective-permute-start | bytes 1769480 | tf_op jit(solution)/shard_map/ppermute | solution.py:193
  158.9 6.9 %collective-permute-start.12 = (f32[384,384]{1,0:T(8,128)S(1)}, f32[384,384]{1,0:T(8,128)S(1)}, u32[]{:S(2)}, u32[]{:S(2)}) collective-permute-start(f32[384,384]{1,0:T(8,128)S(1)} %get-tuple-element.5), channel_id=1, source_target_pairs={{0,192},{64,0},{128,64},{192,128},{1,193},{65,1},{129,65},{193,129... | collective-permute-start | bytes 1769480 | tf_op jit(solution)/shard_map/ppermute | solution.py:194
  165.8 11.8 %collective-permute-done.10 = f32[384,384]{1,0:T(8,128)S(1)} collective-permute-done((f32[384,384]{1,0:T(8,128)S(1)}, f32[384,384]{1,0:T(8,128)S(1)}, u32[]{:S(2)}, u32[]{:S(2)}) %collective-permute-start.10) | collective-permute-done | bytes 589856 | tf_op jit(solution)/shard_map/ppermute | solution.py:193
  177.6 1.2 collective-permute-done.12
  178.8 0.1 fusion.3
  178.9 0.1 pad_maximum_fusion.1
  179.0 5.1 %collective-permute-start.13 = (f32[768,384]{1,0:T(8,128)S(1)}, f32[768,384]{1,0:T(8,128)S(1)}, u32[]{:S(2)}, u32[]{:S(2)}) collective-permute-start(f32[768,384]{1,0:T(8,128)S(1)} %pad_maximum_fusion.1), channel_id=1, source_target_pairs={{0,192},{64,0},{128,64},{192,128},{1,193},{65,1},{129,65},{193,129... | collective-permute-start | bytes 3538952 | tf_op jit(solution)/shard_map/ppermute | solution.py:197
  184.1 0.1 pad_maximum_fusion
  184.2 0.0 copy-start.2
  184.2 2.1 collective-permute-start.11
  186.2 22.3 %collective-permute-done.13 = f32[768,384]{1,0:T(8,128)S(1)} collective-permute-done((f32[768,384]{1,0:T(8,128)S(1)}, f32[768,384]{1,0:T(8,128)S(1)}, u32[]{:S(2)}, u32[]{:S(2)}) %collective-permute-start.13) | collective-permute-done | bytes 1179680 | tf_op jit(solution)/shard_map/ppermute | solution.py:197
  208.6 5.2 %collective-permute-done.11 = f32[768,384]{1,0:T(8,128)S(1)} collective-permute-done((f32[768,384]{1,0:T(8,128)S(1)}, f32[768,384]{1,0:T(8,128)S(1)}, u32[]{:S(2)}, u32[]{:S(2)}) %collective-permute-start.11) | collective-permute-done | bytes 1179680 | tf_op jit(solution)/shard_map/ppermute | solution.py:197
  213.8 0.2 fusion.1
  214.0 0.0 copy-done.2
  214.0 0.0 copy-start.6
  214.0 1.8 multiply_reduce_fusion
  215.8 13.7 %psum.7 = f32[1,384]{1,0:T(1,128)S(1)} all-reduce(f32[1,384]{1,0:T(1,128)S(1)} %broadcast_in_dim.5), channel_id=1, replica_groups=mesh['zh'=2,'y'=4,'x'=4,'core'=2,'zl'=8] {'x','core'}, use_global_device_ids=true, to_apply=%region_1.2 | all-reduce | flops 384 | bytes 3072 | tf_op jit(solution)/shard_map/psum | solution.py:202
  229.6 0.6 sub.43
  (14 shorter events, 0.2 us)
Async XLA Ops:
  7.2 117.0 %all-gather.3.cloned.1.call-start = ((), (), s32[]{:S(2)}) async-start(), calls=%async_computation | async-start | bytes 8912896 | tf_op jit(solution)/shard_map/all_gather | solution.py:162
  9.0 3.1 %copy-start.5 = (s32[8,8,6]{2,1,0:T(8,128)}, s32[8,8,6]{2,1,0:T(8,128)S(1)}, u32[]{:S(2)}) copy-start(s32[8,8,6]{2,1,0:T(8,128)S(1)} %reshape.146) | copy-start | bytes 4612
  12.2 107.1 %copy-start = (s32[4]{0:T(128)S(1)}, s32[4]{0:T(128)}, u32[]{:S(2)}) copy-start(s32[4]{0:T(128)} %constant.94.clone) | copy-start | bytes 52
  12.2 54.0 %collective-permute-start = (f32[768,384]{1,0:T(8,128)S(1)}, f32[768,384]{1,0:T(8,128)}, u32[]{:S(2)}, u32[]{:S(2)}) collective-permute-start(f32[768,384]{1,0:T(8,128)S(1)} %bitcast.45), channel_id=1, source_target_pairs={{0,0},{8,64},{16,128},{24,192},{32,8},{40,72},{48,136},{56,200},{6... | collective-permute-start | bytes 3538952 | tf_op jit(solution)/shard_map/ppermute | solution.py:170
  66.1 24.9 %collective-permute-start.2 = (f32[768,384]{1,0:T(8,128)}, f32[768,384]{1,0:T(8,128)S(1)}, u32[]{:S(2)}, u32[]{:S(2)}) collective-permute-start(f32[768,384]{1,0:T(8,128)} %collective-permute-done.rest_0_), channel_id=1, source_target_pairs={{0,48},{16,0},{32,16},{48,32},{1,49},{17,1},{33,17},{49,33},{2,50}... | collective-permute-start | bytes 3538952 | tf_op jit(solution)/shard_map/ppermute | solution.py:172
  71.4 26.3 %collective-permute-start.1 = (f32[768,384]{1,0:T(8,128)}, f32[768,384]{1,0:T(8,128)S(1)}, u32[]{:S(2)}, u32[]{:S(2)}) collective-permute-start(f32[768,384]{1,0:T(8,128)} %collective-permute-done.rest_0_), channel_id=1, source_target_pairs={{0,16},{16,32},{32,48},{48,0},{1,17},{17,33},{33,49},{49,1},{2,18}... | collective-permute-start | bytes 3538952 | tf_op jit(solution)/shard_map/ppermute | solution.py:171
  91.0 16.3 %copy-start.3 = (f32[768,384]{1,0:T(8,128)}, f32[768,384]{1,0:T(8,128)S(1)}, u32[]{:S(2)}) copy-start(f32[768,384]{1,0:T(8,128)S(1)} %collective-permute-done.2.rest_2_) | copy-start | bytes 3538948
  91.1 23.9 %collective-permute-start.4 = (f32[384,384]{1,0:T(8,128)S(1)}, f32[384,384]{1,0:T(8,128)}, u32[]{:S(2)}, u32[]{:S(2)}) collective-permute-start(f32[384,384]{1,0:T(8,128)S(1)} %slice.49), channel_id=1, source_target_pairs={{0,48},{16,0},{32,16},{48,32},{1,49},{17,1},{33,17},{49,33},{2,50}... | collective-permute-start | bytes 1769480 | tf_op jit(solution)/shard_map/ppermute | solution.py:175
  97.7 26.5 %copy-start.4 = (f32[768,384]{1,0:T(8,128)}, f32[768,384]{1,0:T(8,128)S(1)}, u32[]{:S(2)}) copy-start(f32[768,384]{1,0:T(8,128)S(1)} %collective-permute-done.1.rest_1_) | copy-start | bytes 3538948
  97.8 19.1 %collective-permute-start.3 = (f32[384,384]{1,0:T(8,128)S(1)}, f32[384,384]{1,0:T(8,128)}, u32[]{:S(2)}, u32[]{:S(2)}) collective-permute-start(f32[384,384]{1,0:T(8,128)S(1)} %slice.48), channel_id=1, source_target_pairs={{0,16},{16,32},{32,48},{48,0},{1,17},{17,33},{33,49},{49,1},{2,18}... | collective-permute-start | bytes 1769480 | tf_op jit(solution)/shard_map/ppermute | solution.py:174
  99.7 24.4 %collective-permute-start.5 = (f32[768,384]{1,0:T(8,128)}, f32[768,384]{1,0:T(8,128)}, u32[]{:S(2)}, u32[]{:S(2)}) collective-permute-start(f32[768,384]{1,0:T(8,128)} %collective-permute-done.rest_0_), channel_id=1, source_target_pairs={{0,8},{8,0},{1,9},{9,1},{2,10},{10,2},{3,11},{11,3},{4,12},{12,4},... | collective-permute-start | bytes 3538952 | tf_op jit(solution)/shard_map/ppermute | solution.py:177
  107.4 16.7 %collective-permute-start.7 = (f32[768,384]{1,0:T(8,128)S(1)}, f32[768,384]{1,0:T(8,128)}, u32[]{:S(2)}, u32[]{:S(2)}) collective-permute-start(f32[768,384]{1,0:T(8,128)S(1)} %collective-permute-done.2.rest_2_), channel_id=1, source_target_pairs={{0,8},{8,0},{1,9},{9,1},{2,10},{10,2},{3,11},{11,3},{4,12},{12,4},... | collective-permute-start | bytes 3538952 | tf_op jit(solution)/shard_map/ppermute | solution.py:177
  109.3 14.8 %collective-permute-start.6 = (f32[768,384]{1,0:T(8,128)S(1)}, f32[768,384]{1,0:T(8,128)}, u32[]{:S(2)}, u32[]{:S(2)}) collective-permute-start(f32[768,384]{1,0:T(8,128)S(1)} %collective-permute-done.1.rest_1_), channel_id=1, source_target_pairs={{0,8},{8,0},{1,9},{9,1},{2,10},{10,2},{3,11},{11,3},{4,12},{12,4},... | collective-permute-start | bytes 3538952 | tf_op jit(solution)/shard_map/ppermute | solution.py:177
  114.9 9.1 %collective-permute-start.9 = (f32[384,384]{1,0:T(8,128)}, f32[384,384]{1,0:T(8,128)}, u32[]{:S(2)}, u32[]{:S(2)}) collective-permute-start(f32[384,384]{1,0:T(8,128)} %collective-permute-done.4.rest_4_), channel_id=1, source_target_pairs={{0,8},{8,0},{1,9},{9,1},{2,10},{10,2},{3,11},{11,3},{4,12},{12,4},... | collective-permute-start | bytes 1769480 | tf_op jit(solution)/shard_map/ppermute | solution.py:177
  116.9 7.2 %collective-permute-start.8 = (f32[384,384]{1,0:T(8,128)}, f32[384,384]{1,0:T(8,128)S(1)}, u32[]{:S(2)}, u32[]{:S(2)}) collective-permute-start(f32[384,384]{1,0:T(8,128)} %collective-permute-done.3.rest_3_), channel_id=1, source_target_pairs={{0,8},{8,0},{1,9},{9,1},{2,10},{10,2},{3,11},{11,3},{4,12},{12,4},... | collective-permute-start | bytes 1769480 | tf_op jit(solution)/shard_map/ppermute | solution.py:177
  124.1 0.8 copy-start.7
  152.5 26.3 %copy-start.1 = (f32[4,768,384]{2,1,0:T(8,128)S(1)}, f32[4,768,384]{2,1,0:T(8,128)}, u32[]{:S(2)}) copy-start(f32[4,768,384]{2,1,0:T(8,128)} %shard_map.68) | copy-start | bytes 14155780
  154.4 23.1 %collective-permute-start.10 = (f32[384,384]{1,0:T(8,128)S(1)}, f32[384,384]{1,0:T(8,128)S(1)}, u32[]{:S(2)}, u32[]{:S(2)}) collective-permute-start(f32[384,384]{1,0:T(8,128)S(1)} %get-tuple-element.4), channel_id=1, source_target_pairs={{0,64},{64,128},{128,192},{192,0},{1,65},{65,129},{129,193},{193,1... | collective-permute-start | bytes 1769480 | tf_op jit(solution)/shard_map/ppermute | solution.py:193
  158.9 19.9 %collective-permute-start.12 = (f32[384,384]{1,0:T(8,128)S(1)}, f32[384,384]{1,0:T(8,128)S(1)}, u32[]{:S(2)}, u32[]{:S(2)}) collective-permute-start(f32[384,384]{1,0:T(8,128)S(1)} %get-tuple-element.5), channel_id=1, source_target_pairs={{0,192},{64,0},{128,64},{192,128},{1,193},{65,1},{129,65},{193,129... | collective-permute-start | bytes 1769480 | tf_op jit(solution)/shard_map/ppermute | solution.py:194
  179.0 29.6 %collective-permute-start.13 = (f32[768,384]{1,0:T(8,128)S(1)}, f32[768,384]{1,0:T(8,128)S(1)}, u32[]{:S(2)}, u32[]{:S(2)}) collective-permute-start(f32[768,384]{1,0:T(8,128)S(1)} %pad_maximum_fusion.1), channel_id=1, source_target_pairs={{0,192},{64,0},{128,64},{192,128},{1,193},{65,1},{129,65},{193,129... | collective-permute-start | bytes 3538952 | tf_op jit(solution)/shard_map/ppermute | solution.py:197
  184.2 29.8 %copy-start.2 = (f32[1,768,384]{2,1,0:T(8,128)S(1)}, f32[1,768,384]{2,1,0:T(8,128)}, u32[]{:S(2)}) copy-start(f32[1,768,384]{2,1,0:T(8,128)} %param.7) | copy-start | bytes 3538948
  184.2 29.6 %collective-permute-start.11 = (f32[768,384]{1,0:T(8,128)S(1)}, f32[768,384]{1,0:T(8,128)S(1)}, u32[]{:S(2)}, u32[]{:S(2)}) collective-permute-start(f32[768,384]{1,0:T(8,128)S(1)} %pad_maximum_fusion), channel_id=1, source_target_pairs={{0,64},{64,128},{128,192},{192,0},{1,65},{65,129},{129,193},{193,1... | collective-permute-start | bytes 3538952 | tf_op jit(solution)/shard_map/ppermute | solution.py:197
  214.0 15.6 %copy-start.6 = (f32[1,384]{1,0:T(1,128)S(1)}, f32[1,384]{1,0:T(1,128)}, u32[]{:S(2)}) copy-start(f32[1,384]{1,0:T(1,128)} %param.8) | copy-start | bytes 4612
Sparse Core Ops, SparseCore 0:
  10.1 111.2 all-gather.2

commit v2 on v0

v2 whole, which is shorter than its diff:
```python
import functools

import jax
import jax.numpy as jnp
from jax import lax
from jax.experimental import pallas as pl
from jax.experimental.pallas import tpu as pltpu
from jax.sharding import Mesh, PartitionSpec as P

BLOCK = 128
PART = 256
SPREAD_X = (
    (3, 1, 0, 0),
    (0, 3, 0, 1),
    (1, 2, 0, 1),
    (2, 0, 1, 1),
    (2, 2, 1, 3),
    (3, 1, 2, 2),
    (3, 0, 2, 3),
    (3, 2, 3, 0),
)


def shift(size, step):
    return [(i, (i + step) % size) for i in range(size)]


def spread_plan():
    pairs, holds, taken = [], {}, {}
    for y in range(4):
        for r in range(8):
            to = (SPREAD_X[r][y], r % 4)
            core = taken.get(to, 0)
            taken[to] = core + 1
            pairs.append(((y * 4 + r // 2) * 2 + r % 2, (to[1] * 4 + to[0]) * 2 + core))
            holds[(to[1], to[0], core)] = (r // 4) * 4 + y
    return pairs, [[[holds[(y, x, c)] for c in range(2)] for x in range(4)] for y in range(4)]


def spread_kernel(place, *rest):
    pieces = rest[:10]
    high_hbm, low_hbm, z_f, z_h, z_l, in_sem, out_sem = rest[10:]
    rows = z_f.shape[1]
    half = rows // 2
    spots = []
    for side in range(2):
        for slot in range(3):
            spots.append((side * 4 + slot, 0, rows))
        spots.append((side * 4 + 3, 0, half))
        spots.append((side * 4 + 3, half, half))
    copies = [
        pltpu.make_async_copy(piece, z_f.at[at, pl.ds(start, size)], in_sem.at[i])
        for i, (piece, (at, start, size)) in enumerate(zip(pieces, spots))
    ]
    for copy in copies:
        copy.start()
    row = lax.broadcasted_iota(jnp.int32, (BLOCK, BLOCK), 0)
    for copy, (at, start, size) in zip(copies, spots):
        copy.wait()

        def one(i, carry, at=at, start=start):
            block = start // BLOCK + i
            here = pl.ds(pl.multiple_of(start + i * BLOCK, BLOCK), BLOCK)
            value = z_f[at, here, :]
            high = value.astype(jnp.bfloat16)
            low = (value - high.astype(jnp.float32)).astype(jnp.bfloat16)
            hot = (place[at, pl.ds(block, 1), :] == row).astype(jnp.float32).astype(jnp.bfloat16)
            z_h[at, here, :] = jnp.dot(hot, high, preferred_element_type=jnp.float32).astype(
                jnp.bfloat16
            )
            z_l[at, here, :] = jnp.dot(hot, low, preferred_element_type=jnp.float32).astype(
                jnp.bfloat16
            )
            return carry

        lax.fori_loop(0, size // BLOCK, one, 0)
    outs = [
        pltpu.make_async_copy(z_h, high_hbm, out_sem.at[0]),
        pltpu.make_async_copy(z_l, low_hbm, out_sem.at[1]),
    ]
    for copy in outs:
        copy.start()
    for copy in outs:
        copy.wait()


def spread(place, pieces):
    rows, cols = pieces[0].shape
    any_spec = pl.BlockSpec(memory_space=pl.ANY)
    shape = (8, rows, cols)
    return pl.pallas_call(
        spread_kernel,
        out_shape=[jax.ShapeDtypeStruct(shape, jnp.bfloat16)] * 2,
        in_specs=[pl.BlockSpec(memory_space=pltpu.VMEM)] + [any_spec] * len(pieces),
        out_specs=[any_spec] * 2,
        scratch_shapes=[
            pltpu.VMEM(shape, jnp.float32),
            pltpu.VMEM(shape, jnp.bfloat16),
            pltpu.VMEM(shape, jnp.bfloat16),
            pltpu.SemaphoreType.DMA((len(pieces),)),
            pltpu.SemaphoreType.DMA((2,)),
        ],
        compiler_params=pltpu.CompilerParams(vmem_limit_bytes=48 * 1024 * 1024),
        cost_estimate=pl.CostEstimate(
            flops=8 * 4 * rows * BLOCK * cols, bytes_accessed=64 * rows * cols, transcendentals=0
        ),
    )(place, *pieces)


def product_kernel(steps, table, root_hbm, high_hbm, low_hbm, out_hbm, *rest):
    a_f, z_h, z_l, out_v, a_sem, z_sem, out_sem = rest
    rows = out_v.shape[1]
    per_range = rows // BLOCK
    parts = rows // PART
    per_part = PART // BLOCK

    def z_copies(i, t):
        found = []
        for side in range(2):
            spot = table[t, 3 * per_range + side]
            at = pl.ds(side * rows, rows)
            found.append(pltpu.make_async_copy(high_hbm.at[spot], z_h.at[i, at], z_sem.at[i, side]))
            found.append(
                pltpu.make_async_copy(low_hbm.at[spot], z_l.at[i, at], z_sem.at[i, 2 + side])
            )
        return found

    def a_start(i, t, part):
        def one(k, carry):
            kb = table[t, per_range + k]
            for m in range(per_part):
                mb = pl.multiple_of(table[t, part * per_part + m] * BLOCK, BLOCK)
                pltpu.make_async_copy(
                    root_hbm.at[kb, pl.ds(mb, BLOCK)],
                    a_f.at[i, part, k, pl.ds(m * BLOCK, BLOCK)],
                    a_sem.at[i, part],
                ).start()
            return carry

        lax.fori_loop(0, 2 * per_range, one, 0)

    for i, t in enumerate(steps):
        for copy in z_copies(i, t):
            copy.start()
        for part in range(parts):
            a_start(i, t, part)
    for i, t in enumerate(steps):
        for copy in z_copies(i, t):
            copy.wait()

        def one(part, carry, i=i):
            pltpu.make_async_copy(a_f.at[i, part], a_f.at[i, part], a_sem.at[i, part]).wait()
            values = [a_f[i, part, k] for k in range(2 * per_range)]
            highs = [v.astype(jnp.bfloat16) for v in values]
            lows = [
                (v - h.astype(jnp.float32)).astype(jnp.bfloat16) for v, h in zip(values, highs)
            ]
            ah = jnp.concatenate(highs, axis=1)
            al = jnp.concatenate(lows, axis=1)
            total = jnp.dot(ah, z_l[i], preferred_element_type=jnp.float32)
            total = total + jnp.dot(al, z_h[i], preferred_element_type=jnp.float32)
            at = pl.ds(pl.multiple_of(part * PART, PART), PART)
            out_v[i, at, :] = total + jnp.dot(ah, z_h[i], preferred_element_type=jnp.float32)
            return carry

        lax.fori_loop(0, parts, one, 0)
        pltpu.make_async_copy(out_v.at[i], out_hbm.at[i], out_sem.at[i]).start()
    for i in range(len(steps)):
        pltpu.make_async_copy(out_v.at[i], out_hbm.at[i], out_sem.at[i]).wait()


def product(steps, table, root, high, low):
    rows, cols = high.shape[1:]
    count = len(steps)
    any_spec = pl.BlockSpec(memory_space=pl.ANY)
    return pl.pallas_call(
        functools.partial(product_kernel, steps),
        out_shape=jax.ShapeDtypeStruct((count, rows, cols), jnp.float32),
        in_specs=[pl.BlockSpec(memory_space=pltpu.SMEM)] + [any_spec] * 3,
        out_specs=any_spec,
        scratch_shapes=[
            pltpu.VMEM((count, rows // PART, 2 * rows // BLOCK, PART, BLOCK), jnp.float32),
            pltpu.VMEM((count, 2 * rows, cols), jnp.bfloat16),
            pltpu.VMEM((count, 2 * rows, cols), jnp.bfloat16),
            pltpu.VMEM((count, rows, cols), jnp.float32),
            pltpu.SemaphoreType.DMA((count, rows // PART)),
            pltpu.SemaphoreType.DMA((count, 4)),
            pltpu.SemaphoreType.DMA((count,)),
        ],
        compiler_params=pltpu.CompilerParams(vmem_limit_bytes=48 * 1024 * 1024),
        cost_estimate=pl.CostEstimate(
            flops=count * 3 * 2 * rows * 2 * rows * cols,
            bytes_accessed=count * (8 * rows * rows + 12 * rows * cols),
            transcendentals=0,
        ),
    )(table, root, high, low)


def per_device(root_inverse, root_row, coupling, pivot_variance):
    zh = lax.axis_index("zh")
    y = lax.axis_index("y")
    x = lax.axis_index("x")
    core = lax.axis_index("core")
    rows, cols = coupling.shape[1:]
    ranges = root_row.shape[1] // rows
    per_range = rows // BLOCK
    half = rows // 2
    own_range = 2 * x + core

    root = lax.all_gather(root_inverse, ("zh", "zl"), axis=0, tiled=False)

    pairs, holds = spread_plan()
    own = lax.ppermute(coupling[0], ("y", "x", "core"), pairs)
    left = lax.ppermute(own, "x", shift(4, 1))
    right = lax.ppermute(own, "x", shift(4, -1))
    far_a = lax.ppermute(left[:half], "x", shift(4, 1))
    far_b = lax.ppermute(right[half:], "x", shift(4, -1))
    mine = [own, left, right, far_a, far_b]
    pieces = mine + [lax.ppermute(p, "core", [(0, 1), (1, 0)]) for p in mine]

    spots = jnp.array(holds, jnp.int32)[
        y, (x + jnp.array([0, -1, 1, 2] * 2)) % 4, jnp.array([0] * 4 + [1] * 4) ^ core
    ]
    by_range = root_row.reshape(root_row.shape[0], ranges, per_range, BLOCK)
    block = by_range[..., 0] // BLOCK
    place = by_range - block[..., None] * BLOCK
    piece_child, piece_range = zh * 4 + spots % 4, y + 4 * (spots // 4)
    high, low = spread(place[piece_child, piece_range], pieces)

    child = (y + jnp.arange(4)) % 4
    row_blocks = block[zh * 4 + child, own_range] % 8
    columns = [block[zh * 4 + child, y + 4 * side] % 8 + 8 * side for side in range(2)]
    found = [
        jnp.argmax(spots[None, :] == child[:, None] + 4 * side, axis=1)[:, None] for side in range(2)
    ]
    table = jnp.concatenate([row_blocks, *columns, *found], axis=1).astype(jnp.int32)

    far = product((2,), table, root, high, low)[0]
    a = lax.ppermute(far[:half], "y", shift(4, 1))
    b = lax.ppermute(far[half:], "y", shift(4, -1))
    near = product((1, 3), table, root, high, low)
    up = lax.ppermute(near[0, half:], "y", shift(4, 1))
    down = lax.ppermute(near[1, :half], "y", shift(4, -1))
    up_far = lax.ppermute(near[0, :half] + a, "y", shift(4, 1))
    down_far = lax.ppermute(near[1, half:] + b, "y", shift(4, -1))
    home = product((0,), table, root, high, low)[0]
    summed = jnp.concatenate([home[:half] + up_far + down, home[half:] + up + down_far])

    own_place = place[zh * 4 + y, own_range]
    hot = (own_place[:, :, None] == jnp.arange(BLOCK, dtype=jnp.int32)).astype(jnp.float32)
    result = -jnp.einsum(
        "iuo,ion->iun", hot, summed.reshape(per_range, BLOCK, cols), precision=lax.Precision.HIGHEST
    )
    sums = jnp.sum(coupling[0] * result.reshape(rows, cols), axis=0, keepdims=True)
    sums = sums + lax.ppermute(sums, "core", [(0, 1), (1, 0)])
    sums = sums + lax.ppermute(sums, "x", [(0, 1), (1, 0), (2, 3), (3, 2)])
    sums = sums + lax.ppermute(sums, "x", [(0, 2), (2, 0), (1, 3), (3, 1)])
    return result.reshape(1, rows, cols), pivot_variance - sums


def solution(mesh):
    split = Mesh(mesh.devices.reshape(2, 4, 4, 2, 8), ("zh", "y", "x", "core", "zl"))
    leaf, row, col = ("zh", "y"), ("x", "core"), "zl"
    return jax.shard_map(
        per_device,
        mesh=split,
        in_specs=(P(row, ("zh", "y", "zl")), P(), P(leaf, row, col), P(leaf, col)),
        out_specs=(P(leaf, row, col), P(leaf, col)),
        check_vma=False,
    )
```

time: 861 us -> 211 us (0.25)
  waiting for transfers between devices: 634 us -> 61.4 us
  starting transfers between devices: 135 us -> 58.6 us
  Pallas kernels: 0 us -> 40.3 us
  matrix products: 34.3 us -> 0.74 us
  blocking collectives: 12.7 us -> 0 us
    all_gather x2 -> x1, waiting for transfers between devices: 372 us -> 2.21 us  [per_device(): root = lax.all_gather(root_inverse, ('zh', 'zl'), axis=0, tiled=False)]
    all_to_all x2 -> x0, waiting for transfers between devices: 262 us -> none  [the longest x1 182 us: per_device(): lax.all_to_all(lax.all_to_all(outgoing, 'leaf', split_axis=0, concat_axis...]
    all_to_all x2 -> x0, starting transfers between devices: 134 us -> none  [the longest x1 116 us: per_device(): lax.all_to_all(lax.all_to_all(outgoing, 'leaf', split_axis=0, concat_axis...]
    ppermute x0 -> x19, starting transfers between devices: none -> 58.6 us  [the longest x5 10.6 us: per_device(): pieces = mine + [lax.ppermute(p, 'core', [(0, 1), (1, 0)]) for p in mine]]
    ppermute x0 -> x19, waiting for transfers between devices: none -> 58.5 us  [the longest x1 26.4 us: per_device(): own = lax.ppermute(coupling[0], ('y', 'x', 'core'), pairs)]
    pallas_call x0 -> x4, Pallas kernels: none -> 40.3 us  [the longest x3 26.1 us: product(): pl.pallas_call(functools.partial(product_kernel, steps), out_shape=jax.Sh...]
    dot_general x1, matrix products: 34.3 us -> 0.74 us  [per_device(): jnp.einsum('iuo,ion->iun', hot, summed.reshape(per_range, BLOCK, cols), p...]
    psum x1 -> x0, blocking collectives: 12.7 us -> none  [per_device(): summed = lax.psum(partial_sums, 'row')]
  transfers between devices with their start and end apart: 4 -> 20, of which waited for: 3 -> 8; matrix products, arithmetic and copies ran while one was open for 3% -> 12% of each run, Pallas kernels for 0% -> 16%
where the time goes in v2:
time: 211 us; the launch traced here: 208 us
  waiting for transfers between devices  61.4 us (29%)
  starting transfers between devices  58.6 us (28%)
  Pallas kernels  40.3 us (19%)
  local copies, waits for them, and re-layouts  23.3 us (11%)
  between operations  14.4 us (7%)
  other arithmetic  9.55 us (5%)
    ppermute x1, waiting for transfers between devices, per_device(): own = lax.ppermute(coupling[0], ('y', 'x', 'core'), pairs)  26.4 us
    pallas_call x3, Pallas kernels, product(): pl.pallas_call(functools.partial(product_kernel, steps), out_shape=jax.Sh...  26.1 us
    ppermute x1, waiting for transfers between devices, per_device(): left = lax.ppermute(own, 'x', shift(4, 1))  19.2 us
    pallas_call x1, Pallas kernels, spread(): pl.pallas_call(spread_kernel, out_shape=[jax.ShapeDtypeStruct(shape, jnp....  14.2 us
    ppermute x5, starting transfers between devices, per_device(): pieces = mine + [lax.ppermute(p, 'core', [(0, 1), (1, 0)]) for p in mine]  10.6 us
    ppermute x1, waiting for transfers between devices, per_device(): up_far = lax.ppermute(near[0, :half] + a, 'y', shift(4, 1))  9.46 us
    unnamed x19, local copies, waits for them, and re-layouts  7.92 us
    ppermute x1, starting transfers between devices, per_device(): sums = sums + lax.ppermute(sums, 'x', [(0, 2), (2, 0), (1, 3), (3, 1)])  4.64 us
  transfers between devices with their start and end apart: 20, of which 8 were waited for; matrix products, arithmetic and copies ran while one was open for 12% of the time, Pallas kernels for 16%

profile of v2, /device:TPU:1, one launch (start us, length us, event | category | flops | bytes accessed | tf_op | source)
XLA Modules:
  0.0 208.3 jit_solution(2758944150588726097)
XLA Ops:
  7.2 0.7 all-gather.3.cloned.1.call-update
  7.9 4.6 %collective-permute-start = (f32[768,384]{1,0:T(8,128)}, f32[768,384]{1,0:T(8,128)S(1)}, u32[]{:S(2)}, u32[]{:S(2)}) collective-permute-start(f32[768,384]{1,0:T(8,128)} %bitcast.90), channel_id=1, source_target_pairs={{0,48},{8,64},{16,144},{24,224},{32,32},{40,112},{48,176},{56,240}... | collective-permute-start | bytes 3538952 | tf_op jit(solution)/shard_map/ppermute | solution.py:213
  12.5 1.0 reshape.180
  13.6 1.1 copy.17
  14.7 26.4 %collective-permute-done.rest_0_ = f32[768,384]{1,0:T(8,128)S(1)} collective-permute-done((f32[768,384]{1,0:T(8,128)}, f32[768,384]{1,0:T(8,128)S(1)}, u32[]{:S(2)}, u32[]{:S(2)}) %collective-permute-start) | collective-permute-done | bytes 1179680 | tf_op jit(solution)/shard_map/ppermute | solution.py:213
  41.1 4.3 %collective-permute-start.1 = (f32[768,384]{1,0:T(8,128)S(1)}, f32[768,384]{1,0:T(8,128)S(1)}, u32[]{:S(2)}, u32[]{:S(2)}) collective-permute-start(f32[768,384]{1,0:T(8,128)S(1)} %collective-permute-done.rest_0_), channel_id=1, source_target_pairs={{0,16},{16,32},{32,48},{48,0},{1,17},{17,33},{33,49},{49,1},{2,18}... | collective-permute-start | bytes 3538952 | tf_op jit(solution)/shard_map/ppermute | solution.py:214
  45.4 2.2 %collective-permute-start.2 = (f32[768,384]{1,0:T(8,128)S(1)}, f32[768,384]{1,0:T(8,128)S(1)}, u32[]{:S(2)}, u32[]{:S(2)}) collective-permute-start(f32[768,384]{1,0:T(8,128)S(1)} %collective-permute-done.rest_0_), channel_id=1, source_target_pairs={{0,48},{16,0},{32,16},{48,32},{1,49},{17,1},{33,17},{49,33},{2,50}... | collective-permute-start | bytes 3538952 | tf_op jit(solution)/shard_map/ppermute | solution.py:215
  47.6 0.7 fusion.23
  48.3 0.7 gather_fusion.3
  49.0 0.8 iota_reduce_fusion.1
  49.8 0.7 iota_reduce_fusion
  50.5 1.4 add_select_fusion
  51.8 19.2 %collective-permute-done.1.rest_1_ = f32[768,384]{1,0:T(8,128)S(1)} collective-permute-done((f32[768,384]{1,0:T(8,128)S(1)}, f32[768,384]{1,0:T(8,128)S(1)}, u32[]{:S(2)}, u32[]{:S(2)}) %collective-permute-start.1) | collective-permute-done | bytes 1179680 | tf_op jit(solution)/shard_map/ppermute | solution.py:214
  71.1 0.9 slice.72
  71.9 1.9 collective-permute-start.3
  73.9 0.9 slice.73
  74.8 4.6 %collective-permute-start.4 = (f32[384,384]{1,0:T(8,128)}, f32[384,384]{1,0:T(8,128)}, u32[]{:S(2)}, u32[]{:S(2)}) collective-permute-start(f32[384,384]{1,0:T(8,128)} %slice.73), channel_id=1, source_target_pairs={{0,48},{16,0},{32,16},{48,32},{1,49},{17,1},{33,17},{49,33},{2,50}... | collective-permute-start | bytes 1769480 | tf_op jit(solution)/shard_map/ppermute | solution.py:217
  79.4 1.9 collective-permute-start.5
  81.3 2.4 %collective-permute-start.6 = (f32[768,384]{1,0:T(8,128)S(1)}, f32[768,384]{1,0:T(8,128)}, u32[]{:S(2)}, u32[]{:S(2)}) collective-permute-start(f32[768,384]{1,0:T(8,128)S(1)} %collective-permute-done.1.rest_1_), channel_id=1, source_target_pairs={{0,8},{8,0},{1,9},{9,1},{2,10},{10,2},{3,11},{11,3},{4,12},{12,4},... | collective-permute-start | bytes 3538952 | tf_op jit(solution)/shard_map/ppermute | solution.py:219
  83.7 1.9 collective-permute-start.7
  85.7 1.9 gather_fusion.2
  87.6 1.3 gather_fusion.1
  88.9 1.3 copy.15
  90.2 1.3 copy.16
  91.5 1.3 gather_fusion
  92.8 0.8 fusion.10
  93.6 1.8 broadcast_subtract_fusion
  95.4 2.1 %gather_fusion.4 = s32[8,6,128]{2,1,0:T(8,128)} fusion(s32[8,8,6,128]{3,2,1,0:T(8,128)} %broadcast_subtract_fusion, s32[8]{0:T(128)S(1)} %fusion.37), kind=kCustom, calls=%fused_computation.4 | custom fusion | bytes 49216 | tf_op jit(solution)/shard_map/gather | solution.py:228
  97.5 2.4 %collective-permute-start.8 = (f32[384,384]{1,0:T(8,128)}, f32[384,384]{1,0:T(8,128)}, u32[]{:S(2)}, u32[]{:S(2)}) collective-permute-start(f32[384,384]{1,0:T(8,128)} %collective-permute-done.3.rest_3_), channel_id=1, source_target_pairs={{0,8},{8,0},{1,9},{9,1},{2,10},{10,2},{3,11},{11,3},{4,12},{12,4},... | collective-permute-start | bytes 1769480 | tf_op jit(solution)/shard_map/ppermute | solution.py:219
  100.0 1.9 collective-permute-start.9
  101.9 0.7 fusion.18
  102.6 0.6 add_select_fusion.3
  103.2 0.8 concatenate.25.table
  104.0 0.2 collective-permute-done.9.rest_9_
  104.2 0.8 copy-done.2
  105.0 14.2 %shard_map.86 = (bf16[8,768,384]{2,1,0:T(8,128)(2,1)}, bf16[8,768,384]{2,1,0:T(8,128)(2,1)}) custom-call(s32[8,6,128]{2,1,0:T(8,128)S(1)} %copy-done.2, f32[768,384]{1,0:T(8,128)S(1)} %collective-permute-done.rest_0_, f32[768,384]{1,0:T(8,128)S(1)} %collective-permute-done.1.rest_1_, f32[768,384]{1,0:T(8,128)S(1)} %collective-permute-done.2.rest_2_, ...), custom_call_target="tpu_custom_call" | custom-call | flops 1207959552 | bytes 18874368 | tf_op jit(solution)/shard_map/pallas_call | solution.py:91
  119.2 2.2 %all-gather.3.cloned.1.call-done = f32[16384,128]{1,0:T(8,128)} async-done(((f32[1024,128]{1,0:T(8,128)}), f32[16384,128]{1,0:T(8,128)}) %all-gather.3.cloned.1.call-update) | async-done | bytes 8388624 | tf_op jit(solution)/shard_map/all_gather | solution.py:210
  121.4 2.3 %copy-done = bf16[8,768,384]{2,1,0:T(8,128)(2,1)S(1)} copy-done((bf16[8,768,384]{2,1,0:T(8,128)(2,1)S(1)}, bf16[8,768,384]{2,1,0:T(8,128)(2,1)}, u32[]{:S(2)}) %copy-start) | copy-done | bytes 4718616
  123.7 6.9 %shard_map.89 = f32[1,768,384]{2,1,0:T(8,128)S(1)} custom-call(s32[4,20]{1,0:T(4,128)S(1)} %concatenate.25.table, f32[16,1024,128]{2,1,0:T(8,128)} %bitcast.84, bf16[8,768,384]{2,1,0:T(8,128)(2,1)S(1)} %copy-done, bf16[8,768,384]{2,1,0:T(8,128)(2,1)} %get-tuple-element.9.low_hbm), custom_call_target="tpu_custom_call" | custom-call | flops 2717908992 | bytes 8257536 | tf_op jit(solution)/shard_map/pallas_call | solution.py:176
  130.7 3.1 %collective-permute-start.10 = (f32[384,384]{1,0:T(8,128)S(1)}, f32[384,384]{1,0:T(8,128)S(1)}, u32[]{:S(2)}, u32[]{:S(2)}) collective-permute-start(f32[384,384]{1,0:T(8,128)S(1)} %get-tuple-element.16), channel_id=1, source_target_pairs={{0,64},{64,128},{128,192},{192,0},{1,65},{65,129},{129,193},{193,1... | collective-permute-start | bytes 1769480 | tf_op jit(solution)/shard_map/ppermute | solution.py:239
  133.8 3.4 %collective-permute-start.14 = (f32[384,384]{1,0:T(8,128)S(1)}, f32[384,384]{1,0:T(8,128)S(1)}, u32[]{:S(2)}, u32[]{:S(2)}) collective-permute-start(f32[384,384]{1,0:T(8,128)S(1)} %get-tuple-element.17), channel_id=1, source_target_pairs={{0,192},{64,0},{128,64},{192,128},{1,193},{65,1},{129,65},{193,129... | collective-permute-start | bytes 1769480 | tf_op jit(solution)/shard_map/ppermute | solution.py:240
  137.2 12.4 %shard_map.88 = f32[2,768,384]{2,1,0:T(8,128)S(1)} custom-call(s32[4,20]{1,0:T(4,128)S(1)} %concatenate.25.table, f32[16,1024,128]{2,1,0:T(8,128)} %bitcast.85, bf16[8,768,384]{2,1,0:T(8,128)(2,1)} %get-tuple-element.8.high_hbm, bf16[8,768,384]{2,1,0:T(8,128)(2,1)} %get-tuple-element.9.low_hbm), custom_call_target="tpu_custom_call" | custom-call | flops 5435817984 | bytes 16515072 | tf_op jit(solution)/shard_map/pallas_call | solution.py:176
  149.6 1.1 slice_bitcast_fusion.4
  150.7 3.1 %collective-permute-start.12 = (f32[384,384]{1,0:T(8,128)}, f32[384,384]{1,0:T(8,128)S(1)}, u32[]{:S(2)}, u32[]{:S(2)}) collective-permute-start(f32[384,384]{1,0:T(8,128)} %get-tuple-element.12), channel_id=1, source_target_pairs={{0,192},{64,0},{128,64},{192,128},{1,193},{65,1},{129,65},{193,129... | collective-permute-start | bytes 1769480 | tf_op jit(solution)/shard_map/ppermute | solution.py:243
  153.8 2.1 %collective-permute-start.13 = (f32[384,384]{1,0:T(8,128)}, f32[384,384]{1,0:T(8,128)S(1)}, u32[]{:S(2)}, u32[]{:S(2)}) collective-permute-start(f32[384,384]{1,0:T(8,128)} %get-tuple-element.13), channel_id=1, source_target_pairs={{0,64},{64,128},{128,192},{192,0},{1,65},{65,129},{129,193},{193,1... | collective-permute-start | bytes 1769480 | tf_op jit(solution)/shard_map/ppermute | solution.py:242
  156.0 1.1 fusion.4
  157.1 1.9 collective-permute-start.11
  159.1 4.6 %collective-permute-start.15 = (f32[384,384]{1,0:T(8,128)}, f32[384,384]{1,0:T(8,128)S(1)}, u32[]{:S(2)}, u32[]{:S(2)}) collective-permute-start(f32[384,384]{1,0:T(8,128)} %get-tuple-element.11), channel_id=1, source_target_pairs={{0,192},{64,0},{128,64},{192,128},{1,193},{65,1},{129,65},{193,129... | collective-permute-start | bytes 1769480 | tf_op jit(solution)/shard_map/ppermute | solution.py:245
  163.6 0.7 dynamic-slice_bitcast_fusion
  164.3 2.3 %copy-done.1 = bf16[8,768,384]{2,1,0:T(8,128)(2,1)S(1)} copy-done((bf16[8,768,384]{2,1,0:T(8,128)(2,1)S(1)}, bf16[8,768,384]{2,1,0:T(8,128)(2,1)}, u32[]{:S(2)}) %copy-start.1) | copy-done | bytes 4718616
  166.7 6.9 %shard_map.87 = f32[1,768,384]{2,1,0:T(8,128)S(1)} custom-call(s32[4,20]{1,0:T(4,128)S(1)} %concatenate.25.table, f32[16,1024,128]{2,1,0:T(8,128)} %bitcast.86, bf16[8,768,384]{2,1,0:T(8,128)(2,1)S(1)} %copy-done.1, bf16[8,768,384]{2,1,0:T(8,128)(2,1)} %get-tuple-element.9.low_hbm), custom_call_target="tpu_custom_call" | custom-call | flops 2717908992 | bytes 8257536 | tf_op jit(solution)/shard_map/pallas_call | solution.py:176
  173.6 9.5 %collective-permute-done.11 = f32[384,384]{1,0:T(8,128)S(1)} collective-permute-done((f32[384,384]{1,0:T(8,128)}, f32[384,384]{1,0:T(8,128)S(1)}, u32[]{:S(2)}, u32[]{:S(2)}) %collective-permute-start.11) | collective-permute-done | bytes 589856 | tf_op jit(solution)/shard_map/ppermute | solution.py:244
  183.0 0.2 fusion.6
  183.3 0.7 convolution_negate_fusion
  184.0 0.5 copy-done.6
  184.5 0.1 fusion
  184.7 0.9 copy-done.4
  185.6 4.4 %collective-permute-start.16 = (f32[1,384]{1,0:T(1,128)S(1)}, f32[1,384]{1,0:T(1,128)S(1)}, u32[]{:S(2)}, u32[]{:S(2)}) collective-permute-start(f32[1,384]{1,0:T(1,128)S(1)} %broadcast_in_dim.17), channel_id=1, source_target_pairs={{0,8},{8,0},{1,9},{9,1},{2,10},{10,2},{3,11},{11,3},{4,12},{12,4},... | collective-permute-start | bytes 4616 | tf_op jit(solution)/shard_map/ppermute | solution.py:255
  190.0 0.8 collective-permute-done.16
  190.8 3.2 %collective-permute-start.17 = (f32[1,384]{1,0:T(1,128)S(1)}, f32[1,384]{1,0:T(1,128)S(1)}, u32[]{:S(2)}, u32[]{:S(2)}) collective-permute-start(f32[1,384]{1,0:T(1,128)S(1)} %reshape_add_fusion), channel_id=1, source_target_pairs={{0,16},{16,0},{32,48},{48,32},{1,17},{17,1},{33,49},{49,33},{2,18}... | collective-permute-start | bytes 4616 | tf_op jit(solution)/shard_map/ppermute | solution.py:256
  193.9 1.1 collective-permute-done.17
  195.1 4.6 %collective-permute-start.18 = (f32[1,384]{1,0:T(1,128)S(1)}, f32[1,384]{1,0:T(1,128)S(1)}, u32[]{:S(2)}, u32[]{:S(2)}) collective-permute-start(f32[1,384]{1,0:T(1,128)S(1)} %add.281), channel_id=1, source_target_pairs={{0,32},{32,0},{16,48},{48,16},{1,33},{33,1},{17,49},{49,17},{2,34}... | collective-permute-start | bytes 4616 | tf_op jit(solution)/shard_map/ppermute | solution.py:257
  199.7 1.2 collective-permute-done.18
  200.9 0.6 add_subtract_fusion
  (36 shorter events, 0.3 us)
Async XLA Ops:
  7.2 40.4 %copy-start.8 = (s32[8]{0:T(128)S(1)}, s32[8]{0:T(128)}, u32[]{:S(2)}) copy-start(s32[8]{0:T(128)} %constant.126.clone) | copy-start | bytes 100
  7.2 41.1 %copy-start.3 = (s32[4,4,2]{2,1,0:T(4,128)S(1)}, s32[4,4,2]{2,1,0:T(4,128)}, u32[]{:S(2)}) copy-start(s32[4,4,2]{2,1,0:T(4,128)} %constant.125.clone) | copy-start | bytes 388
  7.2 114.2 %all-gather.3.cloned.1.call-start = ((), (), s32[]{:S(2)}) async-start(), calls=%async_computation | async-start | bytes 8912896 | tf_op jit(solution)/shard_map/all_gather | solution.py:210
  7.9 33.2 %collective-permute-start = (f32[768,384]{1,0:T(8,128)}, f32[768,384]{1,0:T(8,128)S(1)}, u32[]{:S(2)}, u32[]{:S(2)}) collective-permute-start(f32[768,384]{1,0:T(8,128)} %bitcast.90), channel_id=1, source_target_pairs={{0,48},{8,64},{16,144},{24,224},{32,32},{40,112},{48,176},{56,240}... | collective-permute-start | bytes 3538952 | tf_op jit(solution)/shard_map/ppermute | solution.py:213
  13.6 1.1 copy-start.5
  41.1 30.0 %collective-permute-start.1 = (f32[768,384]{1,0:T(8,128)S(1)}, f32[768,384]{1,0:T(8,128)S(1)}, u32[]{:S(2)}, u32[]{:S(2)}) collective-permute-start(f32[768,384]{1,0:T(8,128)S(1)} %collective-permute-done.rest_0_), channel_id=1, source_target_pairs={{0,16},{16,32},{32,48},{48,0},{1,17},{17,33},{33,49},{49,1},{2,18}... | collective-permute-start | bytes 3538952 | tf_op jit(solution)/shard_map/ppermute | solution.py:214
  45.4 28.5 %collective-permute-start.2 = (f32[768,384]{1,0:T(8,128)S(1)}, f32[768,384]{1,0:T(8,128)S(1)}, u32[]{:S(2)}, u32[]{:S(2)}) collective-permute-start(f32[768,384]{1,0:T(8,128)S(1)} %collective-permute-done.rest_0_), channel_id=1, source_target_pairs={{0,48},{16,0},{32,16},{48,32},{1,49},{17,1},{33,17},{49,33},{2,50}... | collective-permute-start | bytes 3538952 | tf_op jit(solution)/shard_map/ppermute | solution.py:215
  71.9 25.6 %collective-permute-start.3 = (f32[384,384]{1,0:T(8,128)}, f32[384,384]{1,0:T(8,128)}, u32[]{:S(2)}, u32[]{:S(2)}) collective-permute-start(f32[384,384]{1,0:T(8,128)} %slice.72), channel_id=1, source_target_pairs={{0,16},{16,32},{32,48},{48,0},{1,17},{17,33},{33,49},{49,1},{2,18}... | collective-permute-start | bytes 1769480 | tf_op jit(solution)/shard_map/ppermute | solution.py:216
  74.8 25.2 %collective-permute-start.4 = (f32[384,384]{1,0:T(8,128)}, f32[384,384]{1,0:T(8,128)}, u32[]{:S(2)}, u32[]{:S(2)}) collective-permute-start(f32[384,384]{1,0:T(8,128)} %slice.73), channel_id=1, source_target_pairs={{0,48},{16,0},{32,16},{48,32},{1,49},{17,1},{33,17},{49,33},{2,50}... | collective-permute-start | bytes 1769480 | tf_op jit(solution)/shard_map/ppermute | solution.py:217
  79.4 24.6 %collective-permute-start.5 = (f32[768,384]{1,0:T(8,128)S(1)}, f32[768,384]{1,0:T(8,128)}, u32[]{:S(2)}, u32[]{:S(2)}) collective-permute-start(f32[768,384]{1,0:T(8,128)S(1)} %collective-permute-done.rest_0_), channel_id=1, source_target_pairs={{0,8},{8,0},{1,9},{9,1},{2,10},{10,2},{3,11},{11,3},{4,12},{12,4},... | collective-permute-start | bytes 3538952 | tf_op jit(solution)/shard_map/ppermute | solution.py:219
  81.3 22.9 %collective-permute-start.6 = (f32[768,384]{1,0:T(8,128)S(1)}, f32[768,384]{1,0:T(8,128)}, u32[]{:S(2)}, u32[]{:S(2)}) collective-permute-start(f32[768,384]{1,0:T(8,128)S(1)} %collective-permute-done.1.rest_1_), channel_id=1, source_target_pairs={{0,8},{8,0},{1,9},{9,1},{2,10},{10,2},{3,11},{11,3},{4,12},{12,4},... | collective-permute-start | bytes 3538952 | tf_op jit(solution)/shard_map/ppermute | solution.py:219
  83.7 20.5 %collective-permute-start.7 = (f32[768,384]{1,0:T(8,128)S(1)}, f32[768,384]{1,0:T(8,128)}, u32[]{:S(2)}, u32[]{:S(2)}) collective-permute-start(f32[768,384]{1,0:T(8,128)S(1)} %collective-permute-done.2.rest_2_), channel_id=1, source_target_pairs={{0,8},{8,0},{1,9},{9,1},{2,10},{10,2},{3,11},{11,3},{4,12},{12,4},... | collective-permute-start | bytes 3538952 | tf_op jit(solution)/shard_map/ppermute | solution.py:219
  97.5 6.4 %collective-permute-start.8 = (f32[384,384]{1,0:T(8,128)}, f32[384,384]{1,0:T(8,128)}, u32[]{:S(2)}, u32[]{:S(2)}) collective-permute-start(f32[384,384]{1,0:T(8,128)} %collective-permute-done.3.rest_3_), channel_id=1, source_target_pairs={{0,8},{8,0},{1,9},{9,1},{2,10},{10,2},{3,11},{11,3},{4,12},{12,4},... | collective-permute-start | bytes 1769480 | tf_op jit(solution)/shard_map/ppermute | solution.py:219
  100.0 4.2 %collective-permute-start.9 = (f32[384,384]{1,0:T(8,128)}, f32[384,384]{1,0:T(8,128)}, u32[]{:S(2)}, u32[]{:S(2)}) collective-permute-start(f32[384,384]{1,0:T(8,128)} %collective-permute-done.4.rest_4_), channel_id=1, source_target_pairs={{0,8},{8,0},{1,9},{9,1},{2,10},{10,2},{3,11},{11,3},{4,12},{12,4},... | collective-permute-start | bytes 1769480 | tf_op jit(solution)/shard_map/ppermute | solution.py:219
  104.2 0.8 copy-start.2
  121.4 2.3 %copy-start = (bf16[8,768,384]{2,1,0:T(8,128)(2,1)S(1)}, bf16[8,768,384]{2,1,0:T(8,128)(2,1)}, u32[]{:S(2)}) copy-start(bf16[8,768,384]{2,1,0:T(8,128)(2,1)} %get-tuple-element.8.high_hbm) | copy-start | bytes 14155780
  130.7 25.3 %collective-permute-start.10 = (f32[384,384]{1,0:T(8,128)S(1)}, f32[384,384]{1,0:T(8,128)S(1)}, u32[]{:S(2)}, u32[]{:S(2)}) collective-permute-start(f32[384,384]{1,0:T(8,128)S(1)} %get-tuple-element.16), channel_id=1, source_target_pairs={{0,64},{64,128},{128,192},{192,0},{1,65},{65,129},{129,193},{193,1... | collective-permute-start | bytes 1769480 | tf_op jit(solution)/shard_map/ppermute | solution.py:239
  133.8 22.2 %collective-permute-start.14 = (f32[384,384]{1,0:T(8,128)S(1)}, f32[384,384]{1,0:T(8,128)S(1)}, u32[]{:S(2)}, u32[]{:S(2)}) collective-permute-start(f32[384,384]{1,0:T(8,128)S(1)} %get-tuple-element.17), channel_id=1, source_target_pairs={{0,192},{64,0},{128,64},{192,128},{1,193},{65,1},{129,65},{193,129... | collective-permute-start | bytes 1769480 | tf_op jit(solution)/shard_map/ppermute | solution.py:240
  150.7 22.9 %collective-permute-start.12 = (f32[384,384]{1,0:T(8,128)}, f32[384,384]{1,0:T(8,128)S(1)}, u32[]{:S(2)}, u32[]{:S(2)}) collective-permute-start(f32[384,384]{1,0:T(8,128)} %get-tuple-element.12), channel_id=1, source_target_pairs={{0,192},{64,0},{128,64},{192,128},{1,193},{65,1},{129,65},{193,129... | collective-permute-start | bytes 1769480 | tf_op jit(solution)/shard_map/ppermute | solution.py:243
  153.8 19.7 %collective-permute-start.13 = (f32[384,384]{1,0:T(8,128)}, f32[384,384]{1,0:T(8,128)S(1)}, u32[]{:S(2)}, u32[]{:S(2)}) collective-permute-start(f32[384,384]{1,0:T(8,128)} %get-tuple-element.13), channel_id=1, source_target_pairs={{0,64},{64,128},{128,192},{192,0},{1,65},{65,129},{129,193},{193,1... | collective-permute-start | bytes 1769480 | tf_op jit(solution)/shard_map/ppermute | solution.py:242
  157.1 25.9 %collective-permute-start.11 = (f32[384,384]{1,0:T(8,128)}, f32[384,384]{1,0:T(8,128)S(1)}, u32[]{:S(2)}, u32[]{:S(2)}) collective-permute-start(f32[384,384]{1,0:T(8,128)} %get-tuple-element.10), channel_id=1, source_target_pairs={{0,64},{64,128},{128,192},{192,0},{1,65},{65,129},{129,193},{193,1... | collective-permute-start | bytes 1769480 | tf_op jit(solution)/shard_map/ppermute | solution.py:244
  159.1 24.0 %collective-permute-start.15 = (f32[384,384]{1,0:T(8,128)}, f32[384,384]{1,0:T(8,128)S(1)}, u32[]{:S(2)}, u32[]{:S(2)}) collective-permute-start(f32[384,384]{1,0:T(8,128)} %get-tuple-element.11), channel_id=1, source_target_pairs={{0,192},{64,0},{128,64},{192,128},{1,193},{65,1},{129,65},{193,129... | collective-permute-start | bytes 1769480 | tf_op jit(solution)/shard_map/ppermute | solution.py:245
  164.3 2.3 %copy-start.1 = (bf16[8,768,384]{2,1,0:T(8,128)(2,1)S(1)}, bf16[8,768,384]{2,1,0:T(8,128)(2,1)}, u32[]{:S(2)}) copy-start(bf16[8,768,384]{2,1,0:T(8,128)(2,1)} %get-tuple-element.8.high_hbm) | copy-start | bytes 14155780
  183.3 1.3 copy-start.6
  184.5 1.0 copy-start.4
  184.5 16.4 %copy-start.7 = (f32[1,384]{1,0:T(1,128)S(1)}, f32[1,384]{1,0:T(1,128)}, u32[]{:S(2)}) copy-start(f32[1,384]{1,0:T(1,128)} %param.10) | copy-start | bytes 4612
  185.6 5.2 %collective-permute-start.16 = (f32[1,384]{1,0:T(1,128)S(1)}, f32[1,384]{1,0:T(1,128)S(1)}, u32[]{:S(2)}, u32[]{:S(2)}) collective-permute-start(f32[1,384]{1,0:T(1,128)S(1)} %broadcast_in_dim.17), channel_id=1, source_target_pairs={{0,8},{8,0},{1,9},{9,1},{2,10},{10,2},{3,11},{11,3},{4,12},{12,4},... | collective-permute-start | bytes 4616 | tf_op jit(solution)/shard_map/ppermute | solution.py:255
  190.8 4.3 %collective-permute-start.17 = (f32[1,384]{1,0:T(1,128)S(1)}, f32[1,384]{1,0:T(1,128)S(1)}, u32[]{:S(2)}, u32[]{:S(2)}) collective-permute-start(f32[1,384]{1,0:T(1,128)S(1)} %reshape_add_fusion), channel_id=1, source_target_pairs={{0,16},{16,0},{32,48},{48,32},{1,17},{17,1},{33,49},{49,33},{2,18}... | collective-permute-start | bytes 4616 | tf_op jit(solution)/shard_map/ppermute | solution.py:256
  195.1 5.8 %collective-permute-start.18 = (f32[1,384]{1,0:T(1,128)S(1)}, f32[1,384]{1,0:T(1,128)S(1)}, u32[]{:S(2)}, u32[]{:S(2)}) collective-permute-start(f32[1,384]{1,0:T(1,128)S(1)} %add.281), channel_id=1, source_target_pairs={{0,32},{32,0},{16,48},{48,16},{1,33},{33,1},{17,49},{49,17},{2,34}... | collective-permute-start | bytes 4616 | tf_op jit(solution)/shard_map/ppermute | solution.py:257
Sparse Core Ops, SparseCore 0:
  10.1 111.2 all-gather.2

commit v3 on v2

v3 whole, which is shorter than its diff:
```python
import functools

import jax
import jax.numpy as jnp
from jax import lax
from jax.experimental import pallas as pl
from jax.experimental.pallas import tpu as pltpu
from jax.sharding import Mesh, PartitionSpec as P

BLOCK = 128
PART = 256
VMEM_BYTES = 60 * 1024 * 1024
CORES = [(0, 1), (1, 0)]
SPREAD_X = (
    (3, 1, 0, 0),
    (0, 3, 0, 1),
    (1, 2, 0, 1),
    (2, 0, 1, 1),
    (2, 2, 1, 3),
    (3, 1, 2, 2),
    (3, 0, 2, 3),
    (3, 2, 3, 0),
)


def shift(size, step):
    return [(i, (i + step) % size) for i in range(size)]


def opposite(size):
    return [(2 * i + c, (i + 1 - 2 * c) % size * 2 + c) for i in range(size) for c in range(2)]


def spread_plan():
    pairs, holds, taken = [], {}, {}
    for y in range(4):
        for r in range(8):
            to = (SPREAD_X[r][y], r % 4)
            core = taken.get(to, 0)
            taken[to] = core + 1
            pairs.append(((y * 4 + r // 2) * 2 + r % 2, (to[1] * 4 + to[0]) * 2 + core))
            holds[(to[1], to[0], core)] = (r // 4, y)
    return pairs, holds


def piece_plan(holds):
    halves, own, found = [], [], []
    for y in range(4):
        for x in range(4):
            for c in range(2):
                d = 2 * c - 1
                at = [
                    (x, c),
                    (x, 1 - c),
                    (x + d, c),
                    (x + d, 1 - c),
                    (x + 2, c),
                    (x - d, 1 - c),
                    (x - d, c),
                    (x + 2, 1 - c),
                ]
                has = [holds[(y, px % 4, pc)] for px, pc in at]
                mine = [y, (y + d) % 4, (y + 2) % 4, (y - d) % 4]
                halves.append([h * 4 + k for h, k in has])
                own.append(mine)
                found.append(
                    [[has.index((0, k)), has.index((1, k)), 8 + mine.index(k)] for k in range(4)]
                )
    return [jnp.array(v, jnp.int32) for v in (halves, own, found)]


def spread_kernel(start_row, rows_ref, *rest):
    pieces = rest[:12]
    high_hbm, low_hbm, z_f, z_h, z_l, in_sem, out_sem = rest[12:]
    rows = z_f.shape[1]
    copies = [
        pltpu.make_async_copy(piece, z_f.at[i], in_sem.at[i]) for i, piece in enumerate(pieces)
    ]
    outs = []
    for i in range(12):
        outs.append(pltpu.make_async_copy(z_h.at[i], high_hbm.at[i], out_sem.at[2 * i]))
        outs.append(pltpu.make_async_copy(z_l.at[i], low_hbm.at[i], out_sem.at[2 * i + 1]))
    for copy in copies:
        copy.start()
    row = lax.broadcasted_iota(jnp.int32, (BLOCK, BLOCK), 0)
    for at, copy in enumerate(copies):
        copy.wait()

        def one(i, carry, at=at):
            here = pl.ds(pl.multiple_of(i * BLOCK, BLOCK), BLOCK)
            value = z_f[at, here, :]
            high = value.astype(jnp.bfloat16)
            low = (value - high.astype(jnp.float32)).astype(jnp.bfloat16)
            place = rows_ref[pl.ds(start_row[at] + i, 1), :]
            place = jnp.where(place >= 0, place & (BLOCK - 1), -1)
            hot = (place == row).astype(jnp.float32).astype(jnp.bfloat16)
            z_h[at, here, :] = jnp.dot(hot, high, preferred_element_type=jnp.float32).astype(
                jnp.bfloat16
            )
            z_l[at, here, :] = jnp.dot(hot, low, preferred_element_type=jnp.float32).astype(
                jnp.bfloat16
            )
            return carry

        lax.fori_loop(0, rows // BLOCK, one, 0, unroll=2)
        outs[2 * at].start()
        outs[2 * at + 1].start()
    for copy in outs:
        copy.wait()


def spread(start_row, root_row, pieces):
    rows, cols = pieces[0].shape
    any_spec = pl.BlockSpec(memory_space=pl.ANY)
    shape = (len(pieces), rows, cols)
    return pl.pallas_call(
        spread_kernel,
        out_shape=[jax.ShapeDtypeStruct(shape, jnp.bfloat16)] * 2,
        in_specs=[
            pl.BlockSpec(memory_space=pltpu.SMEM),
            pl.BlockSpec(memory_space=pltpu.VMEM),
        ]
        + [any_spec] * len(pieces),
        out_specs=[any_spec] * 2,
        scratch_shapes=[
            pltpu.VMEM(shape, jnp.float32),
            pltpu.VMEM(shape, jnp.bfloat16),
            pltpu.VMEM(shape, jnp.bfloat16),
            pltpu.SemaphoreType.DMA((len(pieces),)),
            pltpu.SemaphoreType.DMA((2 * len(pieces),)),
        ],
        compiler_params=pltpu.CompilerParams(vmem_limit_bytes=VMEM_BYTES),
        cost_estimate=pl.CostEstimate(
            flops=12 * 4 * rows * BLOCK * cols, bytes_accessed=96 * rows * cols, transcendentals=0
        ),
    )(start_row, root_row, *pieces)


def product_kernel(steps, table, root_hbm, high_hbm, low_hbm, out_hbm, sums_hbm, *rest):
    a_f, z_h, z_l, b_h, b_l, out_v, sums_v, a_sem, z_sem, out_sem = rest
    rows = out_v.shape[1]
    per_range = rows // BLOCK
    per_part = PART // BLOCK

    def child(t):
        return (table[0, 3 * per_range + 3] + t) & 3

    def z_copies(i, t):
        c = child(t)
        found = []
        for side in range(2):
            spot = table[c, 3 * per_range + side]
            at = pl.ds(side * rows, rows)
            found.append(pltpu.make_async_copy(high_hbm.at[spot], z_h.at[i, at], z_sem.at[i, side]))
            found.append(
                pltpu.make_async_copy(low_hbm.at[spot], z_l.at[i, at], z_sem.at[i, 2 + side])
            )
        spot = table[c, 3 * per_range + 2]
        found.append(pltpu.make_async_copy(high_hbm.at[spot], b_h.at[i], z_sem.at[i, 4]))
        found.append(pltpu.make_async_copy(low_hbm.at[spot], b_l.at[i], z_sem.at[i, 5]))
        return found

    def a_copy(i, t, m):
        mb = pl.multiple_of(table[child(t), m] * BLOCK, BLOCK)
        return pltpu.make_async_copy(
            root_hbm.at[:, pl.ds(mb, BLOCK)], a_f.at[i, m], a_sem.at[i, m]
        )

    for i, t in enumerate(steps):
        for copy in z_copies(i, t):
            copy.start()
        for m in range(per_range):
            a_copy(i, t, m).start()
    for i, t in enumerate(steps):
        for copy in z_copies(i, t):
            copy.wait()
        c = child(t)

        def one(part, total, i=i, t=t, c=c):
            for m in range(per_part):
                a_copy(i, t, part * per_part + m).wait()
            highs, lows = [], []
            for k in range(2 * per_range):
                kb = table[c, per_range + k]
                value = jnp.concatenate(
                    [a_f[i, part * per_part + m, kb] for m in range(per_part)], axis=0
                )
                high = value.astype(jnp.bfloat16)
                highs.append(high)
                lows.append((value - high.astype(jnp.float32)).astype(jnp.bfloat16))
            high = jnp.concatenate(highs, axis=1)
            both = jnp.concatenate([high, jnp.concatenate(lows, axis=1)], axis=0)
            first = jnp.dot(both, z_h[i], preferred_element_type=jnp.float32)
            second = jnp.dot(high, z_l[i], preferred_element_type=jnp.float32)
            value = first[:PART] + (first[PART:] + second)
            at = pl.ds(pl.multiple_of(part * PART, PART), PART)
            out_v[i, at, :] = value
            factor = b_h[i, at, :].astype(jnp.float32) + b_l[i, at, :].astype(jnp.float32)
            return total + jnp.sum((factor * value).reshape(PART // 8, 8, -1), axis=0)

        sums_v[i] = lax.fori_loop(
            0, rows // PART, one, jnp.zeros(sums_v.shape[1:], jnp.float32)
        )
        pltpu.make_async_copy(out_v.at[i], out_hbm.at[i], out_sem.at[i, 0]).start()
        pltpu.make_async_copy(sums_v.at[i], sums_hbm.at[i], out_sem.at[i, 1]).start()
    for i in range(len(steps)):
        pltpu.make_async_copy(out_v.at[i], out_hbm.at[i], out_sem.at[i, 0]).wait()
        pltpu.make_async_copy(sums_v.at[i], sums_hbm.at[i], out_sem.at[i, 1]).wait()


def product(steps, table, root, high, low):
    rows, cols = high.shape[1:]
    count = len(steps)
    per_range = rows // BLOCK
    any_spec = pl.BlockSpec(memory_space=pl.ANY)
    return pl.pallas_call(
        functools.partial(product_kernel, steps),
        out_shape=[
            jax.ShapeDtypeStruct((count, rows, cols), jnp.float32),
            jax.ShapeDtypeStruct((count, 8, cols), jnp.float32),
        ],
        in_specs=[pl.BlockSpec(memory_space=pltpu.SMEM)] + [any_spec] * 3,
        out_specs=[any_spec] * 2,
        scratch_shapes=[
            pltpu.VMEM((count, per_range, root.shape[0], BLOCK, BLOCK), jnp.float32),
            pltpu.VMEM((count, 2 * rows, cols), jnp.bfloat16),
            pltpu.VMEM((count, 2 * rows, cols), jnp.bfloat16),
            pltpu.VMEM((count, rows, cols), jnp.bfloat16),
            pltpu.VMEM((count, rows, cols), jnp.bfloat16),
            pltpu.VMEM((count, rows, cols), jnp.float32),
            pltpu.VMEM((count, 8, cols), jnp.float32),
            pltpu.SemaphoreType.DMA((count, per_range)),
            pltpu.SemaphoreType.DMA((count, 6)),
            pltpu.SemaphoreType.DMA((count, 2)),
        ],
        compiler_params=pltpu.CompilerParams(vmem_limit_bytes=VMEM_BYTES),
        cost_estimate=pl.CostEstimate(
            flops=count * 3 * 2 * rows * 2 * rows * cols,
            bytes_accessed=count * (12 * rows * rows + 16 * rows * cols),
            transcendentals=0,
        ),
    )(table, root, high, low)


def per_device(root_inverse, root_row, coupling, pivot_variance):
    zh = lax.axis_index("zh")
    y = lax.axis_index("y")
    x = lax.axis_index("x")
    core = lax.axis_index("core")
    rows, cols = coupling.shape[1:]
    ranges = root_row.shape[1] // rows
    per_range = rows // BLOCK
    half = rows // 2
    own_range = 2 * x + core
    device = (y * 4 + x) * 2 + core

    root = lax.all_gather(root_inverse, ("zh", "zl"), axis=0, tiled=False)

    pairs, holds = spread_plan()
    own = lax.ppermute(coupling[0], ("y", "x", "core"), pairs)
    along_x, along_y = opposite(4), opposite(4)
    beside = lax.ppermute(own, "core", CORES)
    near = lax.ppermute(own, ("x", "core"), along_x)
    near_beside = lax.ppermute(beside, ("x", "core"), along_x)
    far = lax.ppermute(near, ("x", "core"), along_x)
    pieces = [own, beside, near, near_beside, far]
    pieces += [lax.ppermute(p, "core", CORES) for p in (near, near_beside, far)]

    y_beside = lax.ppermute(coupling[0], "core", CORES)
    y_near = lax.ppermute(coupling[0], ("y", "core"), along_y)
    y_near_beside = lax.ppermute(y_beside, ("y", "core"), along_y)
    y_far = lax.ppermute(y_near, ("y", "core"), along_y)
    pieces += [coupling[0], y_near, y_far, lax.ppermute(y_near_beside, "core", CORES)]

    halves, own_children, found = piece_plan(holds)
    spots = lax.dynamic_slice(halves, (device, 0), (1, 8))[0]
    own_spots = lax.dynamic_slice(own_children, (device, 0), (1, 4))[0]
    child = zh * 4 + jnp.concatenate([spots & 3, own_spots])
    ranged = jnp.concatenate([y + 4 * (spots >> 2), jnp.full((4,), own_range, jnp.int32)])
    start_row = (child * ranges + ranged) * per_range
    high, low = spread(start_row, root_row.reshape(-1, BLOCK), pieces)

    block = (root_row[:, ::BLOCK] >> 7).reshape(-1, ranges, per_range)

    def blocks_of(r):
        return lax.dynamic_slice(block, (zh * 4, r, 0), (4, 1, per_range))[:, 0] & 7

    table = jnp.concatenate(
        [
            blocks_of(own_range),
            blocks_of(y),
            blocks_of(y + 4) + 8,
            lax.dynamic_slice(found, (device, 0, 0), (1, 4, 3))[0],
            jnp.broadcast_to(y, (4, 1)),
        ],
        axis=1,
    ).astype(jnp.int32)

    far, far_sums = product((2,), table, root, high, low)
    a = lax.ppermute(far[0, :half], "y", shift(4, 1))
    b = lax.ppermute(far[0, half:], "y", shift(4, -1))
    near, near_sums = product((1, 3), table, root, high, low)
    up = lax.ppermute(near[0, half:], "y", shift(4, 1))
    down = lax.ppermute(near[1, :half], "y", shift(4, -1))
    up_far = lax.ppermute(near[0, :half] + a, "y", shift(4, 1))
    down_far = lax.ppermute(near[1, half:] + b, "y", shift(4, -1))
    home, home_sums = product((0,), table, root, high, low)
    summed = jnp.concatenate([home[0, :half] + up_far + down, home[0, half:] + up + down_far])

    own_place = lax.dynamic_slice(root_row, (zh * 4 + y, own_range * rows), (1, rows))[0]
    own_place = jnp.where(own_place >= 0, own_place & (BLOCK - 1), -1).reshape(per_range, BLOCK)
    hot = (own_place[:, :, None] == jnp.arange(BLOCK, dtype=jnp.int32)).astype(jnp.float32)
    result = -jnp.einsum(
        "iuo,ion->iun", hot, summed.reshape(per_range, BLOCK, cols), precision=lax.Precision.HIGHEST
    )

    sums = jnp.concatenate([home_sums, near_sums[:1], far_sums, near_sums[1:]]).sum(axis=1)
    steps = (jnp.arange(4)[:, None] - y) % 4 == jnp.arange(4)[None, :]
    sums = jnp.sum(jnp.where(steps[:, :, None], sums[None], 0.0), axis=1)
    sums = lax.psum(sums, ("y", "x", "core"))
    marginal = pivot_variance + lax.dynamic_slice(sums, (y, 0), (1, cols))
    return result.reshape(1, rows, cols), marginal


def solution(mesh):
    split = Mesh(mesh.devices.reshape(2, 4, 4, 2, 8), ("zh", "y", "x", "core", "zl"))
    leaf, row, col = ("zh", "y"), ("x", "core"), "zl"
    return jax.shard_map(
        per_device,
        mesh=split,
        in_specs=(P(row, ("zh", "y", "zl")), P(), P(leaf, row, col), P(leaf, col)),
        out_specs=(P(leaf, row, col), P(leaf, col)),
        check_vma=False,
    )
```

time: 211 us -> 258 us (1.22)
  blocking collectives: 0 us -> 65.5 us
  waiting for transfers between devices: 61.4 us -> 48.7 us
  local copies, waits for them, and re-layouts: 23.3 us -> 12.4 us
  Pallas kernels: 40.3 us -> 45.9 us
    psum x0 -> x1, blocking collectives: none -> 65.5 us  [per_device(): sums = lax.psum(sums, ('y', 'x', 'core'))]
    ppermute x1, waiting for transfers between devices: 9.46 us -> 0.01 us  [per_device(): up_far = lax.ppermute(near[0, :half] + a, 'y', shift(4, 1))]
    gather x5 -> x0, local copies, waits for them, and re-layouts: 7.35 us -> none  [the longest x2 3.24 us: per_device(): block[zh * 4 + child, y + 4 * side] % 8 + 8 * side]
    unnamed x19 -> x18, local copies, waits for them, and re-layouts: 7.92 us -> 0.61 us
    pallas_call x3, Pallas kernels: 26.1 us -> 32.9 us  [product(): pl.pallas_call(functools.partial(product_kernel, steps), out_shape=[jax.S...]
    ppermute x1, waiting for transfers between devices: 26.4 us -> 22.4 us  [per_device(): own = lax.ppermute(coupling[0], ('y', 'x', 'core'), pairs)]
    squeeze x0 -> x3, local copies, waits for them, and re-layouts: none -> 3.23 us  [the longest x1 1.32 us: per_device(): a = lax.ppermute(far[0, :half], 'y', shift(4, 1))]
    sub x3 -> x0, other arithmetic: 3.14 us -> none  [the longest x2 2.58 us: per_device(): place = by_range - block[..., None] * BLOCK]
  transfers between devices with their start and end apart: 20 -> 20, of which waited for: 8 -> 5; matrix products, arithmetic and copies ran while one was open for 12% -> 7% of each run, Pallas kernels for 16% -> 14%
where the time goes in v3:
time: 258 us; the launch traced here: 256 us
  blocking collectives  65.5 us (25%)
  starting transfers between devices  59.7 us (23%)
  waiting for transfers between devices  48.7 us (19%)
  Pallas kernels  45.9 us (18%)
  between operations  14.5 us (6%)
  local copies, waits for them, and re-layouts  12.4 us (5%)
  other arithmetic  7.83 us (3%)
    psum x1, blocking collectives, per_device(): sums = lax.psum(sums, ('y', 'x', 'core'))  65.5 us
    pallas_call x3, Pallas kernels, product(): pl.pallas_call(functools.partial(product_kernel, steps), out_shape=[jax.S...  32.9 us
    ppermute x1, waiting for transfers between devices, per_device(): own = lax.ppermute(coupling[0], ('y', 'x', 'core'), pairs)  22.4 us
    pallas_call x1, Pallas kernels, spread(): pl.pallas_call(spread_kernel, out_shape=[jax.ShapeDtypeStruct(shape, jnp....  13 us
    ppermute x1, waiting for transfers between devices, per_device(): near_beside = lax.ppermute(beside, ('x', 'core'), along_x)  7.79 us
    ppermute x1, waiting for transfers between devices, per_device(): near = lax.ppermute(own, ('x', 'core'), along_x)  7.64 us
    ppermute x3, starting transfers between devices, per_device(): pieces += [lax.ppermute(p, 'core', CORES) for p in (near, near_beside, far)]  7.19 us
    ppermute x1, starting transfers between devices, per_device(): y_beside = lax.ppermute(coupling[0], 'core', CORES)  6.11 us
  transfers between devices with their start and end apart: 20, of which 5 were waited for; matrix products, arithmetic and copies ran while one was open for 7% of the time, Pallas kernels for 14%

profile of v3, /device:TPU:1, one launch (start us, length us, event | category | flops | bytes accessed | tf_op | source)
XLA Modules:
  0.0 256.3 jit_solution(10283868763833207094)
XLA Ops:
  7.2 0.0 all-gather.3.cloned.1.call-start
  7.2 0.7 all-gather.3.cloned.1.call-update
  7.9 4.6 %collective-permute-start = (f32[768,384]{1,0:T(8,128)}, f32[768,384]{1,0:T(8,128)S(1)}, u32[]{:S(2)}, u32[]{:S(2)}) collective-permute-start(f32[768,384]{1,0:T(8,128)} %bitcast.42), channel_id=1, source_target_pairs={{0,48},{8,64},{16,144},{24,224},{32,32},{40,112},{48,176},{56,240}... | collective-permute-start | bytes 3538952 | tf_op jit(solution)/shard_map/ppermute | solution.py:260
  12.5 6.1 %collective-permute-start.10 = (f32[768,384]{1,0:T(8,128)}, f32[768,384]{1,0:T(8,128)S(1)}, u32[]{:S(2)}, u32[]{:S(2)}) collective-permute-start(f32[768,384]{1,0:T(8,128)} %bitcast.43), channel_id=1, source_target_pairs={{0,8},{8,0},{1,9},{9,1},{2,10},{10,2},{3,11},{11,3},{4,12},{12,4},... | collective-permute-start | bytes 3538952 | tf_op jit(solution)/shard_map/ppermute | solution.py:269
  18.6 22.4 %collective-permute-done.rest_0_ = f32[768,384]{1,0:T(8,128)S(1)} collective-permute-done((f32[768,384]{1,0:T(8,128)}, f32[768,384]{1,0:T(8,128)S(1)}, u32[]{:S(2)}, u32[]{:S(2)}) %collective-permute-start) | collective-permute-done | bytes 1179680 | tf_op jit(solution)/shard_map/ppermute | solution.py:260
  41.1 1.9 collective-permute-start.2
  43.0 1.9 collective-permute-start.1
  44.9 4.8 %collective-permute-start.8 = (f32[768,384]{1,0:T(8,128)}, f32[768,384]{1,0:T(8,128)}, u32[]{:S(2)}, u32[]{:S(2)}) collective-permute-start(f32[768,384]{1,0:T(8,128)} %bitcast.44), channel_id=1, source_target_pairs={{0,64},{8,200},{64,128},{72,8},{128,192},{136,72},{192,0},{200,136... | collective-permute-start | bytes 3538952 | tf_op jit(solution)/shard_map/ppermute | solution.py:270
  49.7 0.0 collective-permute-done.10
  49.8 1.9 collective-permute-start.11
  51.7 7.6 %collective-permute-done.2.rest_2_ = f32[768,384]{1,0:T(8,128)S(1)} collective-permute-done((f32[768,384]{1,0:T(8,128)S(1)}, f32[768,384]{1,0:T(8,128)S(1)}, u32[]{:S(2)}, u32[]{:S(2)}) %collective-permute-start.2) | collective-permute-done | bytes 1179680 | tf_op jit(solution)/shard_map/ppermute | solution.py:263
  59.3 2.2 collective-permute-start.4
  61.6 2.8 %collective-permute-start.3 = (f32[768,384]{1,0:T(8,128)S(1)}, f32[768,384]{1,0:T(8,128)}, u32[]{:S(2)}, u32[]{:S(2)}) collective-permute-start(f32[768,384]{1,0:T(8,128)S(1)} %collective-permute-done.1.rest_1_), channel_id=1, source_target_pairs={{0,16},{8,56},{16,32},{24,8},{32,48},{40,24},{48,0},{56,40},{1,17}... | collective-permute-start | bytes 3538952 | tf_op jit(solution)/shard_map/ppermute | solution.py:264
  64.4 0.0 collective-permute-done.8.rest_9_
  64.4 4.1 %collective-permute-start.9 = (f32[768,384]{1,0:T(8,128)}, f32[768,384]{1,0:T(8,128)}, u32[]{:S(2)}, u32[]{:S(2)}) collective-permute-start(f32[768,384]{1,0:T(8,128)} %collective-permute-done.8.rest_9_), channel_id=1, source_target_pairs={{0,64},{8,200},{64,128},{72,8},{128,192},{136,72},{192,0},{200,136... | collective-permute-start | bytes 3538952 | tf_op jit(solution)/shard_map/ppermute | solution.py:272
  68.5 1.9 collective-permute-start.5
  70.4 5.3 %collective-permute-done.11 = f32[768,384]{1,0:T(8,128)} collective-permute-done((f32[768,384]{1,0:T(8,128)S(1)}, f32[768,384]{1,0:T(8,128)}, u32[]{:S(2)}, u32[]{:S(2)}) %collective-permute-start.11) | collective-permute-done | bytes 1179680 | tf_op jit(solution)/shard_map/ppermute | solution.py:271
  75.7 3.9 %collective-permute-start.12 = (f32[768,384]{1,0:T(8,128)}, f32[768,384]{1,0:T(8,128)}, u32[]{:S(2)}, u32[]{:S(2)}) collective-permute-start(f32[768,384]{1,0:T(8,128)} %collective-permute-done.11), channel_id=1, source_target_pairs={{0,8},{8,0},{1,9},{9,1},{2,10},{10,2},{3,11},{11,3},{4,12},{12,4},... | collective-permute-start | bytes 3538952 | tf_op jit(solution)/shard_map/ppermute | solution.py:273
  79.6 0.0 collective-permute-done.4.rest_4_
  79.6 1.9 collective-permute-start.7
  81.5 7.8 %collective-permute-done.3.rest_3_ = f32[768,384]{1,0:T(8,128)} collective-permute-done((f32[768,384]{1,0:T(8,128)S(1)}, f32[768,384]{1,0:T(8,128)}, u32[]{:S(2)}, u32[]{:S(2)}) %collective-permute-start.3) | collective-permute-done | bytes 1179680 | tf_op jit(solution)/shard_map/ppermute | solution.py:264
  89.3 3.3 %collective-permute-start.6 = (f32[768,384]{1,0:T(8,128)}, f32[768,384]{1,0:T(8,128)}, u32[]{:S(2)}, u32[]{:S(2)}) collective-permute-start(f32[768,384]{1,0:T(8,128)} %collective-permute-done.3.rest_3_), channel_id=1, source_target_pairs={{0,8},{8,0},{1,9},{9,1},{2,10},{10,2},{3,11},{11,3},{4,12},{12,4},... | collective-permute-start | bytes 3538952 | tf_op jit(solution)/shard_map/ppermute | solution.py:267
  92.7 1.7 reshape.92.rows_ref
  94.3 1.0 slice.33
  95.4 0.7 reshape.91
  96.1 1.2 dynamic-slice_bitcast_fusion
  97.3 0.8 and_add_fusion
  98.2 1.3 concatenate.15.table
  99.5 1.4 fusion.3
  100.9 0.7 fusion.5
  101.6 0.7 and_bitcast_fusion
  102.3 0.6 fusion.9.start_row
  102.9 0.6 iota_compare_fusion.2
  103.4 0.0 collective-permute-done.9.rest_10_
  103.4 0.0 collective-permute-done.5.rest_5_
  103.4 0.0 collective-permute-done.7.rest_7_
  103.5 13.0 %shard_map.86 = (bf16[12,768,384]{2,1,0:T(8,128)(2,1)}, bf16[12,768,384]{2,1,0:T(8,128)(2,1)}) custom-call(s32[12]{0:T(128)} %fusion.9.start_row, s32[384,128]{1,0:T(8,128)} %reshape.92.rows_ref, f32[768,384]{1,0:T(8,128)} %copy-done.1, f32[768,384]{1,0:T(8,128)} %copy-done.3, f32[768,384]{1,0:T(8,128)} %copy-done.2, ...), custom_call_target="tpu_custom_call" | custom-call | flops 1811939328 | bytes 28311552 | tf_op jit(solution)/shard_map/pallas_call | solution.py:116
  116.5 4.9 %all-gather.3.cloned.1.call-done = f32[16384,128]{1,0:T(8,128)} async-done(((f32[1024,128]{1,0:T(8,128)}), f32[16384,128]{1,0:T(8,128)}) %all-gather.3.cloned.1.call-update) | async-done | bytes 8388624 | tf_op jit(solution)/shard_map/all_gather | solution.py:257
  121.4 9.5 %shard_map.89 = (f32[1,768,384]{2,1,0:T(8,128)}, f32[1,8,384]{2,1,0:T(8,128)}) custom-call(s32[4,22]{1,0:T(4,128)} %concatenate.15.table, f32[16,1024,128]{2,1,0:T(8,128)} %bitcast.37, bf16[12,768,384]{2,1,0:T(8,128)(2,1)} %get-tuple-element.10.high_hbm, bf16[12,768,384]{2,1,0:T(8,128)(2,1)} %get-tuple-element.11.low_hbm), custom_call_target="tpu_custom_call" | custom-call | flops 2717908992 | bytes 11796480 | tf_op jit(solution)/shard_map/pallas_call | solution.py:216
  130.9 1.3 slice_bitcast_fusion.3
  132.2 3.1 %collective-permute-start.13 = (f32[384,384]{1,0:T(8,128)S(1)}, f32[384,384]{1,0:T(8,128)S(1)}, u32[]{:S(2)}, u32[]{:S(2)}) collective-permute-start(f32[384,384]{1,0:T(8,128)S(1)} %get-tuple-element.24), channel_id=1, source_target_pairs={{0,64},{64,128},{128,192},{192,0},{1,65},{65,129},{129,193},{193,1... | collective-permute-start | bytes 1769480 | tf_op jit(solution)/shard_map/ppermute | solution.py:300
  135.3 3.4 %collective-permute-start.17 = (f32[384,384]{1,0:T(8,128)S(1)}, f32[384,384]{1,0:T(8,128)S(1)}, u32[]{:S(2)}, u32[]{:S(2)}) collective-permute-start(f32[384,384]{1,0:T(8,128)S(1)} %get-tuple-element.25), channel_id=1, source_target_pairs={{0,192},{64,0},{128,64},{192,128},{1,193},{65,1},{129,65},{193,129... | collective-permute-start | bytes 1769480 | tf_op jit(solution)/shard_map/ppermute | solution.py:301
  138.7 13.9 %shard_map.88 = (f32[2,768,384]{2,1,0:T(8,128)}, f32[2,8,384]{2,1,0:T(8,128)}) custom-call(s32[4,22]{1,0:T(4,128)} %concatenate.15.table, f32[16,1024,128]{2,1,0:T(8,128)} %bitcast.38, bf16[12,768,384]{2,1,0:T(8,128)(2,1)} %get-tuple-element.10.high_hbm, bf16[12,768,384]{2,1,0:T(8,128)(2,1)} %get-tuple-element.11.low_hbm), custom_call_target="tpu_custom_call" | custom-call | flops 5435817984 | bytes 23592960 | tf_op jit(solution)/shard_map/pallas_call | solution.py:216
  152.6 2.6 %slice_bitcast_fusion.2 = (f32[384,384]{1,0:T(8,128)}, f32[384,384]{1,0:T(8,128)}) fusion(f32[2,768,384]{2,1,0:T(8,128)} %get-tuple-element.13), kind=kLoop, calls=%fused_computation.10 | loop fusion | bytes 2359296 | tf_op jit(solution)/shard_map/squeeze | solution.py:304
  155.2 3.1 %collective-permute-start.15 = (f32[384,384]{1,0:T(8,128)}, f32[384,384]{1,0:T(8,128)S(1)}, u32[]{:S(2)}, u32[]{:S(2)}) collective-permute-start(f32[384,384]{1,0:T(8,128)} %get-tuple-element.20), channel_id=1, source_target_pairs={{0,192},{64,0},{128,64},{192,128},{1,193},{65,1},{129,65},{193,129... | collective-permute-start | bytes 1769480 | tf_op jit(solution)/shard_map/ppermute | solution.py:304
  158.3 2.1 collective-permute-start.16
  160.5 1.3 fusion.10
  161.8 0.0 collective-permute-done.13
  161.8 0.0 collective-permute-done.17
  161.8 0.1 bitcast_add_fusion.2
  162.0 1.9 collective-permute-start.14
  163.9 4.6 %collective-permute-start.18 = (f32[384,384]{1,0:T(8,128)S(1)}, f32[384,384]{1,0:T(8,128)S(1)}, u32[]{:S(2)}, u32[]{:S(2)}) collective-permute-start(f32[384,384]{1,0:T(8,128)S(1)} %get-tuple-element.19), channel_id=1, source_target_pairs={{0,192},{64,0},{128,64},{192,128},{1,193},{65,1},{129,65},{193,129... | collective-permute-start | bytes 1769480 | tf_op jit(solution)/shard_map/ppermute | solution.py:306
  168.5 9.5 %shard_map.87 = (f32[1,768,384]{2,1,0:T(8,128)}, f32[1,8,384]{2,1,0:T(8,128)}) custom-call(s32[4,22]{1,0:T(4,128)} %concatenate.15.table, f32[16,1024,128]{2,1,0:T(8,128)} %bitcast.39, bf16[12,768,384]{2,1,0:T(8,128)(2,1)} %get-tuple-element.10.high_hbm, bf16[12,768,384]{2,1,0:T(8,128)(2,1)} %get-tuple-element.11.low_hbm), custom_call_target="tpu_custom_call" | custom-call | flops 2717908992 | bytes 11796480 | tf_op jit(solution)/shard_map/pallas_call | solution.py:216
  178.0 0.7 maximum_reduce_fusion
  178.8 0.1 select_reduce_fusion
  178.9 65.5 %psum.7 = f32[4,384]{1,0:T(4,128)S(1)} all-reduce(f32[4,384]{1,0:T(4,128)S(1)} %select_reduce_fusion), channel_id=1, replica_groups=mesh['zh'=2,'y'=4,'x'=4,'core'=2,'zl'=8] {'y','x','core'}, use_global_device_ids=true, to_apply=%region_2.3 | all-reduce | flops 1536 | bytes 12288 | tf_op jit(solution)/shard_map/psum | solution.py:320
  244.3 1.3 fusion.4
  245.6 0.0 collective-permute-done.15
  245.6 0.0 collective-permute-done.16
  245.6 0.0 collective-permute-done.14
  245.6 1.4 fusion.1
  247.0 0.1 pad_maximum_fusion
  247.1 0.6 copy-done.6
  247.7 1.8 convolution_negate_fusion
  (24 shorter events, 0.1 us)
Async XLA Ops:
  7.2 114.2 %all-gather.3.cloned.1.call-start = ((), (), s32[]{:S(2)}) async-start(), calls=%async_computation | async-start | bytes 8912896 | tf_op jit(solution)/shard_map/all_gather | solution.py:257
  7.9 33.2 %collective-permute-start = (f32[768,384]{1,0:T(8,128)}, f32[768,384]{1,0:T(8,128)S(1)}, u32[]{:S(2)}, u32[]{:S(2)}) collective-permute-start(f32[768,384]{1,0:T(8,128)} %bitcast.42), channel_id=1, source_target_pairs={{0,48},{8,64},{16,144},{24,224},{32,32},{40,112},{48,176},{56,240}... | collective-permute-start | bytes 3538952 | tf_op jit(solution)/shard_map/ppermute | solution.py:260
  12.5 37.2 %collective-permute-start.10 = (f32[768,384]{1,0:T(8,128)}, f32[768,384]{1,0:T(8,128)S(1)}, u32[]{:S(2)}, u32[]{:S(2)}) collective-permute-start(f32[768,384]{1,0:T(8,128)} %bitcast.43), channel_id=1, source_target_pairs={{0,8},{8,0},{1,9},{9,1},{2,10},{10,2},{3,11},{11,3},{4,12},{12,4},... | collective-permute-start | bytes 3538952 | tf_op jit(solution)/shard_map/ppermute | solution.py:269
  41.1 62.4 %copy-start.1 = (f32[768,384]{1,0:T(8,128)}, f32[768,384]{1,0:T(8,128)S(1)}, u32[]{:S(2)}) copy-start(f32[768,384]{1,0:T(8,128)S(1)} %collective-permute-done.rest_0_) | copy-start | bytes 3538948
  41.1 18.3 %collective-permute-start.2 = (f32[768,384]{1,0:T(8,128)S(1)}, f32[768,384]{1,0:T(8,128)S(1)}, u32[]{:S(2)}, u32[]{:S(2)}) collective-permute-start(f32[768,384]{1,0:T(8,128)S(1)} %collective-permute-done.rest_0_), channel_id=1, source_target_pairs={{0,16},{8,56},{16,32},{24,8},{32,48},{40,24},{48,0},{56,40},{1,17}... | collective-permute-start | bytes 3538952 | tf_op jit(solution)/shard_map/ppermute | solution.py:263
  43.0 18.6 %collective-permute-start.1 = (f32[768,384]{1,0:T(8,128)S(1)}, f32[768,384]{1,0:T(8,128)S(1)}, u32[]{:S(2)}, u32[]{:S(2)}) collective-permute-start(f32[768,384]{1,0:T(8,128)S(1)} %collective-permute-done.rest_0_), channel_id=1, source_target_pairs={{0,8},{8,0},{1,9},{9,1},{2,10},{10,2},{3,11},{11,3},{4,12},{12,4},... | collective-permute-start | bytes 3538952 | tf_op jit(solution)/shard_map/ppermute | solution.py:262
  44.9 19.5 %collective-permute-start.8 = (f32[768,384]{1,0:T(8,128)}, f32[768,384]{1,0:T(8,128)}, u32[]{:S(2)}, u32[]{:S(2)}) collective-permute-start(f32[768,384]{1,0:T(8,128)} %bitcast.44), channel_id=1, source_target_pairs={{0,64},{8,200},{64,128},{72,8},{128,192},{136,72},{192,0},{200,136... | collective-permute-start | bytes 3538952 | tf_op jit(solution)/shard_map/ppermute | solution.py:270
  49.8 26.0 %collective-permute-start.11 = (f32[768,384]{1,0:T(8,128)S(1)}, f32[768,384]{1,0:T(8,128)}, u32[]{:S(2)}, u32[]{:S(2)}) collective-permute-start(f32[768,384]{1,0:T(8,128)S(1)} %collective-permute-done.10), channel_id=1, source_target_pairs={{0,64},{8,200},{64,128},{72,8},{128,192},{136,72},{192,0},{200,136... | collective-permute-start | bytes 3538952 | tf_op jit(solution)/shard_map/ppermute | solution.py:271
  59.3 44.1 %copy-start.2 = (f32[768,384]{1,0:T(8,128)}, f32[768,384]{1,0:T(8,128)S(1)}, u32[]{:S(2)}) copy-start(f32[768,384]{1,0:T(8,128)S(1)} %collective-permute-done.2.rest_2_) | copy-start | bytes 3538948
  59.3 20.3 %collective-permute-start.4 = (f32[768,384]{1,0:T(8,128)S(1)}, f32[768,384]{1,0:T(8,128)}, u32[]{:S(2)}, u32[]{:S(2)}) collective-permute-start(f32[768,384]{1,0:T(8,128)S(1)} %collective-permute-done.2.rest_2_), channel_id=1, source_target_pairs={{0,16},{8,56},{16,32},{24,8},{32,48},{40,24},{48,0},{56,40},{1,17}... | collective-permute-start | bytes 3538952 | tf_op jit(solution)/shard_map/ppermute | solution.py:265
  61.5 41.9 %copy-start.3 = (f32[768,384]{1,0:T(8,128)}, f32[768,384]{1,0:T(8,128)S(1)}, u32[]{:S(2)}) copy-start(f32[768,384]{1,0:T(8,128)S(1)} %collective-permute-done.1.rest_1_) | copy-start | bytes 3538948
  61.6 27.8 %collective-permute-start.3 = (f32[768,384]{1,0:T(8,128)S(1)}, f32[768,384]{1,0:T(8,128)}, u32[]{:S(2)}, u32[]{:S(2)}) collective-permute-start(f32[768,384]{1,0:T(8,128)S(1)} %collective-permute-done.1.rest_1_), channel_id=1, source_target_pairs={{0,16},{8,56},{16,32},{24,8},{32,48},{40,24},{48,0},{56,40},{1,17}... | collective-permute-start | bytes 3538952 | tf_op jit(solution)/shard_map/ppermute | solution.py:264
  64.4 39.0 %collective-permute-start.9 = (f32[768,384]{1,0:T(8,128)}, f32[768,384]{1,0:T(8,128)}, u32[]{:S(2)}, u32[]{:S(2)}) collective-permute-start(f32[768,384]{1,0:T(8,128)} %collective-permute-done.8.rest_9_), channel_id=1, source_target_pairs={{0,64},{8,200},{64,128},{72,8},{128,192},{136,72},{192,0},{200,136... | collective-permute-start | bytes 3538952 | tf_op jit(solution)/shard_map/ppermute | solution.py:272
  68.5 34.9 %collective-permute-start.5 = (f32[768,384]{1,0:T(8,128)S(1)}, f32[768,384]{1,0:T(8,128)}, u32[]{:S(2)}, u32[]{:S(2)}) collective-permute-start(f32[768,384]{1,0:T(8,128)S(1)} %collective-permute-done.2.rest_2_), channel_id=1, source_target_pairs={{0,8},{8,0},{1,9},{9,1},{2,10},{10,2},{3,11},{11,3},{4,12},{12,4},... | collective-permute-start | bytes 3538952 | tf_op jit(solution)/shard_map/ppermute | solution.py:267
  75.7 27.7 %collective-permute-start.12 = (f32[768,384]{1,0:T(8,128)}, f32[768,384]{1,0:T(8,128)}, u32[]{:S(2)}, u32[]{:S(2)}) collective-permute-start(f32[768,384]{1,0:T(8,128)} %collective-permute-done.11), channel_id=1, source_target_pairs={{0,8},{8,0},{1,9},{9,1},{2,10},{10,2},{3,11},{11,3},{4,12},{12,4},... | collective-permute-start | bytes 3538952 | tf_op jit(solution)/shard_map/ppermute | solution.py:273
  79.6 23.9 %collective-permute-start.7 = (f32[768,384]{1,0:T(8,128)}, f32[768,384]{1,0:T(8,128)}, u32[]{:S(2)}, u32[]{:S(2)}) collective-permute-start(f32[768,384]{1,0:T(8,128)} %collective-permute-done.4.rest_4_), channel_id=1, source_target_pairs={{0,8},{8,0},{1,9},{9,1},{2,10},{10,2},{3,11},{11,3},{4,12},{12,4},... | collective-permute-start | bytes 3538952 | tf_op jit(solution)/shard_map/ppermute | solution.py:267
  89.3 14.1 %collective-permute-start.6 = (f32[768,384]{1,0:T(8,128)}, f32[768,384]{1,0:T(8,128)}, u32[]{:S(2)}, u32[]{:S(2)}) collective-permute-start(f32[768,384]{1,0:T(8,128)} %collective-permute-done.3.rest_3_), channel_id=1, source_target_pairs={{0,8},{8,0},{1,9},{9,1},{2,10},{10,2},{3,11},{11,3},{4,12},{12,4},... | collective-permute-start | bytes 3538952 | tf_op jit(solution)/shard_map/ppermute | solution.py:267
  132.2 29.6 %collective-permute-start.13 = (f32[384,384]{1,0:T(8,128)S(1)}, f32[384,384]{1,0:T(8,128)S(1)}, u32[]{:S(2)}, u32[]{:S(2)}) collective-permute-start(f32[384,384]{1,0:T(8,128)S(1)} %get-tuple-element.24), channel_id=1, source_target_pairs={{0,64},{64,128},{128,192},{192,0},{1,65},{65,129},{129,193},{193,1... | collective-permute-start | bytes 1769480 | tf_op jit(solution)/shard_map/ppermute | solution.py:300
  135.3 26.5 %collective-permute-start.17 = (f32[384,384]{1,0:T(8,128)S(1)}, f32[384,384]{1,0:T(8,128)S(1)}, u32[]{:S(2)}, u32[]{:S(2)}) collective-permute-start(f32[384,384]{1,0:T(8,128)S(1)} %get-tuple-element.25), channel_id=1, source_target_pairs={{0,192},{64,0},{128,64},{192,128},{1,193},{65,1},{129,65},{193,129... | collective-permute-start | bytes 1769480 | tf_op jit(solution)/shard_map/ppermute | solution.py:301
  152.6 9.2 %copy-start = (f32[2,768,384]{2,1,0:T(8,128)S(1)}, f32[2,768,384]{2,1,0:T(8,128)}, u32[]{:S(2)}) copy-start(f32[2,768,384]{2,1,0:T(8,128)} %get-tuple-element.13) | copy-start | bytes 7077892
  155.2 90.4 %collective-permute-start.15 = (f32[384,384]{1,0:T(8,128)}, f32[384,384]{1,0:T(8,128)S(1)}, u32[]{:S(2)}, u32[]{:S(2)}) collective-permute-start(f32[384,384]{1,0:T(8,128)} %get-tuple-element.20), channel_id=1, source_target_pairs={{0,192},{64,0},{128,64},{192,128},{1,193},{65,1},{129,65},{193,129... | collective-permute-start | bytes 1769480 | tf_op jit(solution)/shard_map/ppermute | solution.py:304
  158.3 87.3 %collective-permute-start.16 = (f32[384,384]{1,0:T(8,128)}, f32[384,384]{1,0:T(8,128)S(1)}, u32[]{:S(2)}, u32[]{:S(2)}) collective-permute-start(f32[384,384]{1,0:T(8,128)} %get-tuple-element.21), channel_id=1, source_target_pairs={{0,64},{64,128},{128,192},{192,0},{1,65},{65,129},{129,193},{193,1... | collective-permute-start | bytes 1769480 | tf_op jit(solution)/shard_map/ppermute | solution.py:303
  162.0 83.7 %collective-permute-start.14 = (f32[384,384]{1,0:T(8,128)S(1)}, f32[384,384]{1,0:T(8,128)S(1)}, u32[]{:S(2)}, u32[]{:S(2)}) collective-permute-start(f32[384,384]{1,0:T(8,128)S(1)} %get-tuple-element.18), channel_id=1, source_target_pairs={{0,64},{64,128},{128,192},{192,0},{1,65},{65,129},{129,193},{193,1... | collective-permute-start | bytes 1769480 | tf_op jit(solution)/shard_map/ppermute | solution.py:305
  163.9 14.1 %copy-start.4 = (f32[1,8,384]{2,1,0:T(8,128)S(1)}, f32[1,8,384]{2,1,0:T(8,128)}, u32[]{:S(2)}) copy-start(f32[1,8,384]{2,1,0:T(8,128)} %get-tuple-element.29) | copy-start | bytes 36868
  163.9 14.1 %copy-start.5 = (f32[1,8,384]{2,1,0:T(8,128)S(1)}, f32[1,8,384]{2,1,0:T(8,128)}, u32[]{:S(2)}) copy-start(f32[1,8,384]{2,1,0:T(8,128)} %get-tuple-element.30) | copy-start | bytes 36868
  163.9 14.1 %copy-start.7 = (f32[1,8,384]{2,1,0:T(8,128)S(1)}, f32[1,8,384]{2,1,0:T(8,128)}, u32[]{:S(2)}) copy-start(f32[1,8,384]{2,1,0:T(8,128)} %get-tuple-element.17) | copy-start | bytes 36868
  163.9 14.9 %copy-start.8 = (pred[4,4]{1,0:T(4,128)(4,1)S(1)}, pred[4,4]{1,0:T(4,128)(4,1)}, u32[]{:S(2)}) copy-start(pred[4,4]{1,0:T(4,128)(4,1)} %iota_compare_fusion.2) | copy-start | bytes 52
  163.9 81.7 %collective-permute-start.18 = (f32[384,384]{1,0:T(8,128)S(1)}, f32[384,384]{1,0:T(8,128)S(1)}, u32[]{:S(2)}, u32[]{:S(2)}) collective-permute-start(f32[384,384]{1,0:T(8,128)S(1)} %get-tuple-element.19), channel_id=1, source_target_pairs={{0,192},{64,0},{128,64},{192,128},{1,193},{65,1},{129,65},{193,129... | collective-permute-start | bytes 1769480 | tf_op jit(solution)/shard_map/ppermute | solution.py:306
  247.0 0.7 copy-start.6
Sparse Core Ops, SparseCore 0:
  10.1 111.2 all-gather.2

commit v4 on v3

--- a/solution.py
+++ b/solution.py
@@ -9,7 +9,9 @@
 
 BLOCK = 128
 PART = 256
-VMEM_BYTES = 60 * 1024 * 1024
+SLOTS = 4
+SPREAD_VMEM = 16 * 1024 * 1024
+PRODUCT_VMEM = 42 * 1024 * 1024
 CORES = [(0, 1), (1, 0)]
 SPREAD_X = (
     (3, 1, 0, 0),
@@ -72,47 +74,57 @@
 def spread_kernel(start_row, rows_ref, *rest):
     pieces = rest[:12]
     high_hbm, low_hbm, z_f, z_h, z_l, in_sem, out_sem = rest[12:]
-    rows = z_f.shape[1]
-    copies = [
-        pltpu.make_async_copy(piece, z_f.at[i], in_sem.at[i]) for i, piece in enumerate(pieces)
-    ]
-    outs = []
-    for i in range(12):
-        outs.append(pltpu.make_async_copy(z_h.at[i], high_hbm.at[i], out_sem.at[2 * i]))
-        outs.append(pltpu.make_async_copy(z_l.at[i], low_hbm.at[i], out_sem.at[2 * i + 1]))
-    for copy in copies:
-        copy.start()
+    slots, rows = z_f.shape[:2]
+
+    def fetch(i):
+        return pltpu.make_async_copy(pieces[i], z_f.at[i % slots], in_sem.at[i])
+
+    def store(i):
+        return [
+            pltpu.make_async_copy(z_h.at[i % slots], high_hbm.at[i], out_sem.at[2 * i]),
+            pltpu.make_async_copy(z_l.at[i % slots], low_hbm.at[i], out_sem.at[2 * i + 1]),
+        ]
+
+    for i in range(slots):
+        fetch(i).start()
     row = lax.broadcasted_iota(jnp.int32, (BLOCK, BLOCK), 0)
-    for at, copy in enumerate(copies):
-        copy.wait()
+    for at in range(len(pieces)):
+        fetch(at).wait()
+        if at >= slots:
+            for copy in store(at - slots):
+                copy.wait()
 
         def one(i, carry, at=at):
             here = pl.ds(pl.multiple_of(i * BLOCK, BLOCK), BLOCK)
-            value = z_f[at, here, :]
+            value = z_f[at % slots, here, :]
             high = value.astype(jnp.bfloat16)
             low = (value - high.astype(jnp.float32)).astype(jnp.bfloat16)
             place = rows_ref[pl.ds(start_row[at] + i, 1), :]
             place = jnp.where(place >= 0, place & (BLOCK - 1), -1)
             hot = (place == row).astype(jnp.float32).astype(jnp.bfloat16)
-            z_h[at, here, :] = jnp.dot(hot, high, preferred_element_type=jnp.float32).astype(
-                jnp.bfloat16
-            )
-            z_l[at, here, :] = jnp.dot(hot, low, preferred_element_type=jnp.float32).astype(
-                jnp.bfloat16
-            )
+            z_h[at % slots, here, :] = jnp.dot(
+                hot, high, preferred_element_type=jnp.float32
+            ).astype(jnp.bfloat16)
+            z_l[at % slots, here, :] = jnp.dot(
+                hot, low, preferred_element_type=jnp.float32
+            ).astype(jnp.bfloat16)
             return carry
 
         lax.fori_loop(0, rows // BLOCK, one, 0, unroll=2)
-        outs[2 * at].start()
-        outs[2 * at + 1].start()
-    for copy in outs:
-        copy.wait()
+        for copy in store(at):
+            copy.start()
+        if at + slots < len(pieces):
+            fetch(at + slots).start()
+    for at in range(len(pieces) - slots, len(pieces)):
+        for copy in store(at):
+            copy.wait()
 
 
 def spread(start_row, root_row, pieces):
     rows, cols = pieces[0].shape
     any_spec = pl.BlockSpec(memory_space=pl.ANY)
     shape = (len(pieces), rows, cols)
+    held = (SLOTS, rows, cols)
     return pl.pallas_call(
         spread_kernel,
         out_shape=[jax.ShapeDtypeStruct(shape, jnp.bfloat16)] * 2,
@@ -123,13 +135,13 @@
         + [any_spec] * len(pieces),
         out_specs=[any_spec] * 2,
         scratch_shapes=[
-            pltpu.VMEM(shape, jnp.float32),
-            pltpu.VMEM(shape, jnp.bfloat16),
-            pltpu.VMEM(shape, jnp.bfloat16),
+            pltpu.VMEM(held, jnp.float32),
+            pltpu.VMEM(held, jnp.bfloat16),
+            pltpu.VMEM(held, jnp.bfloat16),
             pltpu.SemaphoreType.DMA((len(pieces),)),
             pltpu.SemaphoreType.DMA((2 * len(pieces),)),
         ],
-        compiler_params=pltpu.CompilerParams(vmem_limit_bytes=VMEM_BYTES),
+        compiler_params=pltpu.CompilerParams(vmem_limit_bytes=SPREAD_VMEM),
         cost_estimate=pl.CostEstimate(
             flops=12 * 4 * rows * BLOCK * cols, bytes_accessed=96 * rows * cols, transcendentals=0
         ),
@@ -141,77 +153,101 @@
     rows = out_v.shape[1]
     per_range = rows // BLOCK
     per_part = PART // BLOCK
+    parts = rows // PART
 
     def child(t):
         return (table[0, 3 * per_range + 3] + t) & 3
 
-    def z_copies(i, t):
-        c = child(t)
+    def factor_copies(source, target, i, t, sem):
         found = []
         for side in range(2):
-            spot = table[c, 3 * per_range + side]
+            spot = table[child(t), 3 * per_range + side]
             at = pl.ds(side * rows, rows)
-            found.append(pltpu.make_async_copy(high_hbm.at[spot], z_h.at[i, at], z_sem.at[i, side]))
             found.append(
-                pltpu.make_async_copy(low_hbm.at[spot], z_l.at[i, at], z_sem.at[i, 2 + side])
+                pltpu.make_async_copy(source.at[spot], target.at[i, at], z_sem.at[i, sem + side])
             )
-        spot = table[c, 3 * per_range + 2]
-        found.append(pltpu.make_async_copy(high_hbm.at[spot], b_h.at[i], z_sem.at[i, 4]))
-        found.append(pltpu.make_async_copy(low_hbm.at[spot], b_l.at[i], z_sem.at[i, 5]))
         return found
 
-    def a_copy(i, t, m):
-        mb = pl.multiple_of(table[child(t), m] * BLOCK, BLOCK)
-        return pltpu.make_async_copy(
-            root_hbm.at[:, pl.ds(mb, BLOCK)], a_f.at[i, m], a_sem.at[i, m]
-        )
+    def high_copies(i, t):
+        return factor_copies(high_hbm, z_h, i, t, 0)
+
+    def low_copies(i, t):
+        return factor_copies(low_hbm, z_l, i, t, 2)
+
+    def own_copies(i, t):
+        spot = table[child(t), 3 * per_range + 2]
+        return [
+            pltpu.make_async_copy(high_hbm.at[spot], b_h.at[i], z_sem.at[i, 4]),
+            pltpu.make_async_copy(low_hbm.at[spot], b_l.at[i], z_sem.at[i, 5]),
+        ]
+
+    def start_root(i, t, part):
+        for m in range(per_part):
+            mb = pl.multiple_of(table[child(t), part * per_part + m] * BLOCK, BLOCK)
+            pltpu.make_async_copy(
+                root_hbm.at[:, pl.ds(mb, BLOCK)],
+                a_f.at[i, part, :, pl.ds(m * BLOCK, BLOCK)],
+                a_sem.at[i, part],
+            ).start()
+
+    def out_copy(i, part):
+        at = pl.ds(part * PART, PART)
+        return pltpu.make_async_copy(out_v.at[i, at], out_hbm.at[i, at], out_sem.at[i, part])
+
+    def sums_copy(i):
+        return pltpu.make_async_copy(sums_v.at[i], sums_hbm.at[i], out_sem.at[i, parts])
 
     for i, t in enumerate(steps):
-        for copy in z_copies(i, t):
+        for copy in high_copies(i, t):
             copy.start()
-        for m in range(per_range):
-            a_copy(i, t, m).start()
+        start_root(i, t, 0)
+        for copy in low_copies(i, t):
+            copy.start()
+        for part in range(1, parts):
+            start_root(i, t, part)
+        for copy in own_copies(i, t):
+            copy.start()
     for i, t in enumerate(steps):
-        for copy in z_copies(i, t):
+        c = child(t)
+        for copy in high_copies(i, t):
             copy.wait()
-        c = child(t)
-
-        def one(part, total, i=i, t=t, c=c):
-            for m in range(per_part):
-                a_copy(i, t, part * per_part + m).wait()
+        for part in range(parts):
+            pltpu.make_async_copy(a_f.at[i, part], a_f.at[i, part], a_sem.at[i, part]).wait()
+            if part == 0:
+                for copy in low_copies(i, t):
+                    copy.wait()
             highs, lows = [], []
             for k in range(2 * per_range):
-                kb = table[c, per_range + k]
-                value = jnp.concatenate(
-                    [a_f[i, part * per_part + m, kb] for m in range(per_part)], axis=0
-                )
+                value = a_f[i, part, table[c, per_range + k]]
                 high = value.astype(jnp.bfloat16)
                 highs.append(high)
                 lows.append((value - high.astype(jnp.float32)).astype(jnp.bfloat16))
             high = jnp.concatenate(highs, axis=1)
-            both = jnp.concatenate([high, jnp.concatenate(lows, axis=1)], axis=0)
-            first = jnp.dot(both, z_h[i], preferred_element_type=jnp.float32)
-            second = jnp.dot(high, z_l[i], preferred_element_type=jnp.float32)
-            value = first[:PART] + (first[PART:] + second)
-            at = pl.ds(pl.multiple_of(part * PART, PART), PART)
-            out_v[i, at, :] = value
+            low = jnp.concatenate(lows, axis=1)
+            total = jnp.dot(high, z_l[i], preferred_element_type=jnp.float32)
+            total = total + jnp.dot(low, z_h[i], preferred_element_type=jnp.float32)
+            total = total + jnp.dot(high, z_h[i], preferred_element_type=jnp.float32)
+            out_v[i, pl.ds(part * PART, PART), :] = total
+            out_copy(i, part).start()
+        for copy in own_copies(i, t):
+            copy.wait()
+
+        def add(p, total, i=i):
+            at = pl.ds(pl.multiple_of(p * 64, 64), 64)
             factor = b_h[i, at, :].astype(jnp.float32) + b_l[i, at, :].astype(jnp.float32)
-            return total + jnp.sum((factor * value).reshape(PART // 8, 8, -1), axis=0)
-
-        sums_v[i] = lax.fori_loop(
-            0, rows // PART, one, jnp.zeros(sums_v.shape[1:], jnp.float32)
-        )
-        pltpu.make_async_copy(out_v.at[i], out_hbm.at[i], out_sem.at[i, 0]).start()
-        pltpu.make_async_copy(sums_v.at[i], sums_hbm.at[i], out_sem.at[i, 1]).start()
+            return total + jnp.sum((factor * out_v[i, at, :]).reshape(8, 8, -1), axis=0)
+
+        sums_v[i] = lax.fori_loop(0, rows // 64, add, jnp.zeros(sums_v.shape[1:], jnp.float32))
+        sums_copy(i).start()
     for i in range(len(steps)):
-        pltpu.make_async_copy(out_v.at[i], out_hbm.at[i], out_sem.at[i, 0]).wait()
-        pltpu.make_async_copy(sums_v.at[i], sums_hbm.at[i], out_sem.at[i, 1]).wait()
+        for part in range(parts):
+            out_copy(i, part).wait()
+        sums_copy(i).wait()
 
 
 def product(steps, table, root, high, low):
     rows, cols = high.shape[1:]
     count = len(steps)
-    per_range = rows // BLOCK
     any_spec = pl.BlockSpec(memory_space=pl.ANY)
     return pl.pallas_call(
         functools.partial(product_kernel, steps),
@@ -222,18 +258,18 @@
         in_specs=[pl.BlockSpec(memory_space=pltpu.SMEM)] + [any_spec] * 3,
         out_specs=[any_spec] * 2,
         scratch_shapes=[
-            pltpu.VMEM((count, per_range, root.shape[0], BLOCK, BLOCK), jnp.float32),
+            pltpu.VMEM((count, rows // PART, root.shape[0], PART, BLOCK), jnp.float32),
             pltpu.VMEM((count, 2 * rows, cols), jnp.bfloat16),
             pltpu.VMEM((count, 2 * rows, cols), jnp.bfloat16),
             pltpu.VMEM((count, rows, cols), jnp.bfloat16),
             pltpu.VMEM((count, rows, cols), jnp.bfloat16),
             pltpu.VMEM((count, rows, cols), jnp.float32),
             pltpu.VMEM((count, 8, cols), jnp.float32),
-            pltpu.SemaphoreType.DMA((count, per_range)),
+            pltpu.SemaphoreType.DMA((count, rows // PART)),
             pltpu.SemaphoreType.DMA((count, 6)),
-            pltpu.SemaphoreType.DMA((count, 2)),
+            pltpu.SemaphoreType.DMA((count, rows // PART + 1)),
         ],
-        compiler_params=pltpu.CompilerParams(vmem_limit_bytes=VMEM_BYTES),
+        compiler_params=pltpu.CompilerParams(vmem_limit_bytes=PRODUCT_VMEM),
         cost_estimate=pl.CostEstimate(
             flops=count * 3 * 2 * rows * 2 * rows * cols,
             bytes_accessed=count * (12 * rows * rows + 16 * rows * cols),
@@ -314,11 +350,13 @@
         "iuo,ion->iun", hot, summed.reshape(per_range, BLOCK, cols), precision=lax.Precision.HIGHEST
     )
 
-    sums = jnp.concatenate([home_sums, near_sums[:1], far_sums, near_sums[1:]]).sum(axis=1)
-    steps = (jnp.arange(4)[:, None] - y) % 4 == jnp.arange(4)[None, :]
-    sums = jnp.sum(jnp.where(steps[:, :, None], sums[None], 0.0), axis=1)
-    sums = lax.psum(sums, ("y", "x", "core"))
-    marginal = pivot_variance + lax.dynamic_slice(sums, (y, 0), (1, cols))
+    sums = (
+        home_sums[0]
+        + lax.ppermute(far_sums[0], "y", shift(4, 2))
+        + lax.ppermute(near_sums[0], "y", shift(4, 1))
+        + lax.ppermute(near_sums[1], "y", shift(4, -1))
+    )
+    marginal = pivot_variance + lax.psum(jnp.sum(sums, axis=0, keepdims=True), ("x", "core"))
     return result.reshape(1, rows, cols), marginal
 
 

time: 258 us -> 234 us (0.907)
  blocking collectives: 65.5 us -> 13.6 us
  waiting for transfers between devices: 48.7 us -> 60.2 us
  starting transfers between devices: 59.7 us -> 69.5 us
  local copies, waits for them, and re-layouts: 12.4 us -> 21.9 us
    psum x1, blocking collectives: 65.5 us -> 13.6 us  [per_device(): lax.psum(jnp.sum(sums, axis=0, keepdims=True), ('x', 'core'))]
    ppermute x0 -> x3, waiting for transfers between devices: none -> 16.3 us  [the longest x1 16.3 us: per_device(): lax.ppermute(near_sums[0], 'y', shift(4, 1))]
    unnamed x18 -> x14, local copies, waits for them, and re-layouts: 0.61 us -> 14 us
    ppermute x0 -> x3, starting transfers between devices: none -> 9.54 us  [the longest x1 5.49 us: per_device(): lax.ppermute(far_sums[0], 'y', shift(4, 2))]
    all_gather x1, waiting for transfers between devices: 4.86 us -> 0.01 us  [per_device(): root = lax.all_gather(root_inverse, ('zh', 'zl'), axis=0, tiled=False)]
  transfers between devices with their start and end apart: 20 -> 23, of which waited for: 5 -> 5; matrix products, arithmetic and copies ran while one was open for 7% -> 5% of each run, Pallas kernels for 14% -> 16%
where the time goes in v4:
time: 234 us; the launch traced here: 233 us
  starting transfers between devices  69.5 us (30%)
  waiting for transfers between devices  60.2 us (26%)
  Pallas kernels  45.7 us (20%)
  local copies, waits for them, and re-layouts  21.9 us (9%)
  between operations  14.4 us (6%)
  blocking collectives  13.6 us (6%)
  other arithmetic  5.63 us (2%)
    pallas_call x3, Pallas kernels, product(): pl.pallas_call(functools.partial(product_kernel, steps), out_shape=[jax.S...  31.6 us
    ppermute x1, waiting for transfers between devices, per_device(): own = lax.ppermute(coupling[0], ('y', 'x', 'core'), pairs)  22.4 us
    ppermute x1, waiting for transfers between devices, per_device(): lax.ppermute(near_sums[0], 'y', shift(4, 1))  16.3 us
    pallas_call x1, Pallas kernels, spread(): pl.pallas_call(spread_kernel, out_shape=[jax.ShapeDtypeStruct(shape, jnp....  14.1 us
    unnamed x14, local copies, waits for them, and re-layouts  14 us
    psum x1, blocking collectives, per_device(): lax.psum(jnp.sum(sums, axis=0, keepdims=True), ('x', 'core'))  13.6 us
    ppermute x1, waiting for transfers between devices, per_device(): near_beside = lax.ppermute(beside, ('x', 'core'), along_x)  7.78 us
    ppermute x1, waiting for transfers between devices, per_device(): near = lax.ppermute(own, ('x', 'core'), along_x)  7.64 us
  transfers between devices with their start and end apart: 23, of which 5 were waited for; matrix products, arithmetic and copies ran while one was open for 5% of the time, Pallas kernels for 16%

profile of v4, /device:TPU:1, one launch (start us, length us, event | category | flops | bytes accessed | tf_op | source)
XLA Modules:
  0.0 232.7 jit_solution(6614376659049068691)
XLA Ops:
  7.2 0.0 all-gather.3.cloned.1.call-start
  7.2 0.7 all-gather.3.cloned.1.call-update
  7.9 4.6 %collective-permute-start = (f32[768,384]{1,0:T(8,128)}, f32[768,384]{1,0:T(8,128)S(1)}, u32[]{:S(2)}, u32[]{:S(2)}) collective-permute-start(f32[768,384]{1,0:T(8,128)} %bitcast.50), channel_id=1, source_target_pairs={{0,48},{8,64},{16,144},{24,224},{32,32},{40,112},{48,176},{56,240}... | collective-permute-start | bytes 3538952 | tf_op jit(solution)/shard_map/ppermute | solution.py:296
  12.5 6.1 %collective-permute-start.10 = (f32[768,384]{1,0:T(8,128)}, f32[768,384]{1,0:T(8,128)S(1)}, u32[]{:S(2)}, u32[]{:S(2)}) collective-permute-start(f32[768,384]{1,0:T(8,128)} %bitcast.51), channel_id=1, source_target_pairs={{0,8},{8,0},{1,9},{9,1},{2,10},{10,2},{3,11},{11,3},{4,12},{12,4},... | collective-permute-start | bytes 3538952 | tf_op jit(solution)/shard_map/ppermute | solution.py:305
  18.6 22.4 %collective-permute-done.rest_0_ = f32[768,384]{1,0:T(8,128)S(1)} collective-permute-done((f32[768,384]{1,0:T(8,128)}, f32[768,384]{1,0:T(8,128)S(1)}, u32[]{:S(2)}, u32[]{:S(2)}) %collective-permute-start) | collective-permute-done | bytes 1179680 | tf_op jit(solution)/shard_map/ppermute | solution.py:296
  41.1 1.9 collective-permute-start.2
  43.0 1.9 collective-permute-start.1
  44.9 4.8 %collective-permute-start.8 = (f32[768,384]{1,0:T(8,128)}, f32[768,384]{1,0:T(8,128)}, u32[]{:S(2)}, u32[]{:S(2)}) collective-permute-start(f32[768,384]{1,0:T(8,128)} %bitcast.52), channel_id=1, source_target_pairs={{0,64},{8,200},{64,128},{72,8},{128,192},{136,72},{192,0},{200,136... | collective-permute-start | bytes 3538952 | tf_op jit(solution)/shard_map/ppermute | solution.py:306
  49.7 0.0 collective-permute-done.10
  49.8 1.9 collective-permute-start.11
  51.7 7.6 %collective-permute-done.2.rest_2_ = f32[768,384]{1,0:T(8,128)S(1)} collective-permute-done((f32[768,384]{1,0:T(8,128)S(1)}, f32[768,384]{1,0:T(8,128)S(1)}, u32[]{:S(2)}, u32[]{:S(2)}) %collective-permute-start.2) | collective-permute-done | bytes 1179680 | tf_op jit(solution)/shard_map/ppermute | solution.py:299
  59.3 2.2 collective-permute-start.4
  61.5 0.0 collective-permute-done.1.rest_1_
  61.5 2.8 %collective-permute-start.3 = (f32[768,384]{1,0:T(8,128)S(1)}, f32[768,384]{1,0:T(8,128)}, u32[]{:S(2)}, u32[]{:S(2)}) collective-permute-start(f32[768,384]{1,0:T(8,128)S(1)} %collective-permute-done.1.rest_1_), channel_id=1, source_target_pairs={{0,16},{8,56},{16,32},{24,8},{32,48},{40,24},{48,0},{56,40},{1,17}... | collective-permute-start | bytes 3538952 | tf_op jit(solution)/shard_map/ppermute | solution.py:300
  64.4 4.1 %collective-permute-start.9 = (f32[768,384]{1,0:T(8,128)}, f32[768,384]{1,0:T(8,128)}, u32[]{:S(2)}, u32[]{:S(2)}) collective-permute-start(f32[768,384]{1,0:T(8,128)} %collective-permute-done.8.rest_9_), channel_id=1, source_target_pairs={{0,64},{8,200},{64,128},{72,8},{128,192},{136,72},{192,0},{200,136... | collective-permute-start | bytes 3538952 | tf_op jit(solution)/shard_map/ppermute | solution.py:308
  68.5 1.9 collective-permute-start.5
  70.4 5.3 %collective-permute-done.11 = f32[768,384]{1,0:T(8,128)} collective-permute-done((f32[768,384]{1,0:T(8,128)S(1)}, f32[768,384]{1,0:T(8,128)}, u32[]{:S(2)}, u32[]{:S(2)}) %collective-permute-start.11) | collective-permute-done | bytes 1179680 | tf_op jit(solution)/shard_map/ppermute | solution.py:307
  75.7 3.9 %collective-permute-start.12 = (f32[768,384]{1,0:T(8,128)}, f32[768,384]{1,0:T(8,128)}, u32[]{:S(2)}, u32[]{:S(2)}) collective-permute-start(f32[768,384]{1,0:T(8,128)} %collective-permute-done.11), channel_id=1, source_target_pairs={{0,8},{8,0},{1,9},{9,1},{2,10},{10,2},{3,11},{11,3},{4,12},{12,4},... | collective-permute-start | bytes 3538952 | tf_op jit(solution)/shard_map/ppermute | solution.py:309
  79.6 1.9 collective-permute-start.7
  81.5 7.8 %collective-permute-done.3.rest_3_ = f32[768,384]{1,0:T(8,128)} collective-permute-done((f32[768,384]{1,0:T(8,128)S(1)}, f32[768,384]{1,0:T(8,128)}, u32[]{:S(2)}, u32[]{:S(2)}) %collective-permute-start.3) | collective-permute-done | bytes 1179680 | tf_op jit(solution)/shard_map/ppermute | solution.py:300
  89.3 3.3 %collective-permute-start.6 = (f32[768,384]{1,0:T(8,128)}, f32[768,384]{1,0:T(8,128)}, u32[]{:S(2)}, u32[]{:S(2)}) collective-permute-start(f32[768,384]{1,0:T(8,128)} %collective-permute-done.3.rest_3_), channel_id=1, source_target_pairs={{0,8},{8,0},{1,9},{9,1},{2,10},{10,2},{3,11},{11,3},{4,12},{12,4},... | collective-permute-start | bytes 3538952 | tf_op jit(solution)/shard_map/ppermute | solution.py:303
  92.7 1.6 reshape.49.rows_ref
  94.3 1.0 slice.33
  95.4 0.7 reshape.48
  96.1 1.3 dynamic-slice_bitcast_fusion
  97.3 0.8 and_add_fusion
  98.2 0.6 broadcast_in_dim.13
  98.8 0.8 concatenate.12.table
  99.6 0.7 fusion.7
  100.3 0.7 and_bitcast_fusion
  101.0 0.1 fusion.10.start_row
  101.0 0.0 collective-permute-done.7.rest_7_
  101.1 0.0 collective-permute-done.6.rest_6_
  101.1 0.0 copy-start.4
  101.1 1.3 copy-done.4
  102.4 0.9 copy-done.5
  103.3 14.1 %shard_map.86 = (bf16[12,768,384]{2,1,0:T(8,128)(2,1)S(1)}, bf16[12,768,384]{2,1,0:T(8,128)(2,1)S(1)}) custom-call(s32[12]{0:T(128)S(1)} %fusion.10.start_row, s32[384,128]{1,0:T(8,128)S(1)} %copy-done.5, f32[768,384]{1,0:T(8,128)S(1)} %collective-permute-done.rest_0_, f32[768,384]{1,0:T(8,128)S(1)} %collective-permute-done.1.rest_1_, ...), custom_call_target="tpu_custom_call" | custom-call | flops 1811939328 | bytes 28311552 | tf_op jit(solution)/shard_map/pallas_call | solution.py:128
  117.4 2.9 %copy-done = bf16[12,768,384]{2,1,0:T(8,128)(2,1)} copy-done((bf16[12,768,384]{2,1,0:T(8,128)(2,1)}, bf16[12,768,384]{2,1,0:T(8,128)(2,1)S(1)}, u32[]{:S(2)}) %copy-start) | copy-done | bytes 7077912
  120.3 2.9 %copy-done.3 = bf16[12,768,384]{2,1,0:T(8,128)(2,1)} copy-done((bf16[12,768,384]{2,1,0:T(8,128)(2,1)}, bf16[12,768,384]{2,1,0:T(8,128)(2,1)S(1)}, u32[]{:S(2)}) %copy-start.3) | copy-done | bytes 7077912
  123.2 3.0 %copy-done.1 = bf16[12,768,384]{2,1,0:T(8,128)(2,1)S(1)} copy-done((bf16[12,768,384]{2,1,0:T(8,128)(2,1)S(1)}, bf16[12,768,384]{2,1,0:T(8,128)(2,1)}, u32[]{:S(2)}) %copy-start.1) | copy-done | bytes 7077912
  126.2 8.8 %shard_map.89 = (f32[1,768,384]{2,1,0:T(8,128)S(1)}, f32[1,8,384]{2,1,0:T(8,128)S(1)}) custom-call(s32[4,22]{1,0:T(4,128)S(1)} %concatenate.12.table, f32[16,1024,128]{2,1,0:T(8,128)} %bitcast.55, bf16[12,768,384]{2,1,0:T(8,128)(2,1)S(1)} %copy-done.1, bf16[12,768,384]{2,1,0:T(8,128)(2,1)} %copy-done.3), custom_call_target="tpu_custom_call" | custom-call | flops 2717908992 | bytes 11796480 | tf_op jit(solution)/shard_map/pallas_call | solution.py:252
  135.0 5.5 %collective-permute-start.19 = (f32[8,384]{1,0:T(8,128)S(1)}, f32[8,384]{1,0:T(8,128)S(1)}, u32[]{:S(2)}, u32[]{:S(2)}) collective-permute-start(f32[8,384]{1,0:T(8,128)S(1)} %bitcast.54), channel_id=1, source_target_pairs={{0,128},{64,192},{128,0},{192,64},{1,129},{65,193},{129,1},{193,65... | collective-permute-start | bytes 36872 | tf_op jit(solution)/shard_map/ppermute | solution.py:355
  140.5 0.1 slice_bitcast_fusion.3
  140.6 2.5 %collective-permute-start.13 = (f32[384,384]{1,0:T(8,128)S(1)}, f32[384,384]{1,0:T(8,128)S(1)}, u32[]{:S(2)}, u32[]{:S(2)}) collective-permute-start(f32[384,384]{1,0:T(8,128)S(1)} %get-tuple-element.24), channel_id=1, source_target_pairs={{0,64},{64,128},{128,192},{192,0},{1,65},{65,129},{129,193},{193,1... | collective-permute-start | bytes 1769480 | tf_op jit(solution)/shard_map/ppermute | solution.py:336
  143.1 4.1 %collective-permute-start.17 = (f32[384,384]{1,0:T(8,128)S(1)}, f32[384,384]{1,0:T(8,128)S(1)}, u32[]{:S(2)}, u32[]{:S(2)}) collective-permute-start(f32[384,384]{1,0:T(8,128)S(1)} %get-tuple-element.25), channel_id=1, source_target_pairs={{0,192},{64,0},{128,64},{192,128},{1,193},{65,1},{129,65},{193,129... | collective-permute-start | bytes 1769480 | tf_op jit(solution)/shard_map/ppermute | solution.py:337
  147.3 14.0 %shard_map.88 = (f32[2,768,384]{2,1,0:T(8,128)S(1)}, f32[2,8,384]{2,1,0:T(8,128)S(1)}) custom-call(s32[4,22]{1,0:T(4,128)S(1)} %concatenate.12.table, f32[16,1024,128]{2,1,0:T(8,128)} %bitcast.56, bf16[12,768,384]{2,1,0:T(8,128)(2,1)S(1)} %copy-done.1, bf16[12,768,384]{2,1,0:T(8,128)(2,1)} %copy-done.3), custom_call_target="tpu_custom_call" | custom-call | flops 5435817984 | bytes 23592960 | tf_op jit(solution)/shard_map/pallas_call | solution.py:252
  161.3 1.1 slice_bitcast_fusion.2
  162.4 1.9 collective-permute-start.15
  164.3 3.4 %collective-permute-start.16 = (f32[384,384]{1,0:T(8,128)}, f32[384,384]{1,0:T(8,128)S(1)}, u32[]{:S(2)}, u32[]{:S(2)}) collective-permute-start(f32[384,384]{1,0:T(8,128)} %get-tuple-element.21), channel_id=1, source_target_pairs={{0,64},{64,128},{128,192},{192,0},{1,65},{65,129},{129,193},{193,1... | collective-permute-start | bytes 1769480 | tf_op jit(solution)/shard_map/ppermute | solution.py:339
  167.7 0.0 collective-permute-done.13
  167.7 1.2 bitcast_add_fusion.2
  168.8 1.9 collective-permute-start.14
  170.8 4.6 %collective-permute-start.18 = (f32[384,384]{1,0:T(8,128)}, f32[384,384]{1,0:T(8,128)}, u32[]{:S(2)}, u32[]{:S(2)}) collective-permute-start(f32[384,384]{1,0:T(8,128)} %get-tuple-element.19), channel_id=1, source_target_pairs={{0,192},{64,0},{128,64},{192,128},{1,193},{65,1},{129,65},{193,129... | collective-permute-start | bytes 1769480 | tf_op jit(solution)/shard_map/ppermute | solution.py:342
  175.4 1.9 collective-permute-start.20
  177.3 0.8 fusion.6
  178.1 16.3 %collective-permute-done.20 = f32[8,384]{1,0:T(8,128)S(1)} collective-permute-done((f32[8,384]{1,0:T(8,128)S(1)}, f32[8,384]{1,0:T(8,128)S(1)}, u32[]{:S(2)}, u32[]{:S(2)}) %collective-permute-start.20) | collective-permute-done | bytes 12320 | tf_op jit(solution)/shard_map/ppermute | solution.py:356
  194.5 2.1 collective-permute-start.21
  196.6 3.0 %copy-done.2 = bf16[12,768,384]{2,1,0:T(8,128)(2,1)S(1)} copy-done((bf16[12,768,384]{2,1,0:T(8,128)(2,1)S(1)}, bf16[12,768,384]{2,1,0:T(8,128)(2,1)}, u32[]{:S(2)}) %copy-start.2) | copy-done | bytes 7077912
  199.6 8.8 %shard_map.87 = (f32[1,768,384]{2,1,0:T(8,128)S(1)}, f32[1,8,384]{2,1,0:T(8,128)S(1)}) custom-call(s32[4,22]{1,0:T(4,128)S(1)} %concatenate.12.table, f32[16,1024,128]{2,1,0:T(8,128)} %bitcast.57, bf16[12,768,384]{2,1,0:T(8,128)(2,1)S(1)} %copy-done.2, bf16[12,768,384]{2,1,0:T(8,128)(2,1)} %copy-done.3), custom_call_target="tpu_custom_call" | custom-call | flops 2717908992 | bytes 11796480 | tf_op jit(solution)/shard_map/pallas_call | solution.py:252
  208.5 13.6 %psum.7 = f32[1,384]{1,0:T(1,128)S(1)} all-reduce(f32[1,384]{1,0:T(1,128)S(1)} %broadcast_in_dim.14), channel_id=1, replica_groups=mesh['zh'=2,'y'=4,'x'=4,'core'=2,'zl'=8] {'x','core'}, use_global_device_ids=true, to_apply=%region_1.2 | all-reduce | flops 384 | bytes 3072 | tf_op jit(solution)/shard_map/psum | solution.py:359
  222.0 0.6 add.129
  222.6 1.3 fusion.1
  224.0 0.1 pad_maximum_fusion
  224.0 1.8 convolution_negate_fusion
  (24 shorter events, 0.1 us)
Async XLA Ops:
  7.2 116.0 %all-gather.3.cloned.1.call-start = ((), (), s32[]{:S(2)}) async-start(), calls=%async_computation | async-start | bytes 8912896 | tf_op jit(solution)/shard_map/all_gather | solution.py:293
  7.9 33.2 %collective-permute-start = (f32[768,384]{1,0:T(8,128)}, f32[768,384]{1,0:T(8,128)S(1)}, u32[]{:S(2)}, u32[]{:S(2)}) collective-permute-start(f32[768,384]{1,0:T(8,128)} %bitcast.50), channel_id=1, source_target_pairs={{0,48},{8,64},{16,144},{24,224},{32,32},{40,112},{48,176},{56,240}... | collective-permute-start | bytes 3538952 | tf_op jit(solution)/shard_map/ppermute | solution.py:296
  12.5 37.2 %collective-permute-start.10 = (f32[768,384]{1,0:T(8,128)}, f32[768,384]{1,0:T(8,128)S(1)}, u32[]{:S(2)}, u32[]{:S(2)}) collective-permute-start(f32[768,384]{1,0:T(8,128)} %bitcast.51), channel_id=1, source_target_pairs={{0,8},{8,0},{1,9},{9,1},{2,10},{10,2},{3,11},{11,3},{4,12},{12,4},... | collective-permute-start | bytes 3538952 | tf_op jit(solution)/shard_map/ppermute | solution.py:305
  41.1 18.3 %collective-permute-start.2 = (f32[768,384]{1,0:T(8,128)S(1)}, f32[768,384]{1,0:T(8,128)S(1)}, u32[]{:S(2)}, u32[]{:S(2)}) collective-permute-start(f32[768,384]{1,0:T(8,128)S(1)} %collective-permute-done.rest_0_), channel_id=1, source_target_pairs={{0,16},{8,56},{16,32},{24,8},{32,48},{40,24},{48,0},{56,40},{1,17}... | collective-permute-start | bytes 3538952 | tf_op jit(solution)/shard_map/ppermute | solution.py:299
  43.0 18.6 %collective-permute-start.1 = (f32[768,384]{1,0:T(8,128)S(1)}, f32[768,384]{1,0:T(8,128)S(1)}, u32[]{:S(2)}, u32[]{:S(2)}) collective-permute-start(f32[768,384]{1,0:T(8,128)S(1)} %collective-permute-done.rest_0_), channel_id=1, source_target_pairs={{0,8},{8,0},{1,9},{9,1},{2,10},{10,2},{3,11},{11,3},{4,12},{12,4},... | collective-permute-start | bytes 3538952 | tf_op jit(solution)/shard_map/ppermute | solution.py:298
  44.9 19.5 %collective-permute-start.8 = (f32[768,384]{1,0:T(8,128)}, f32[768,384]{1,0:T(8,128)}, u32[]{:S(2)}, u32[]{:S(2)}) collective-permute-start(f32[768,384]{1,0:T(8,128)} %bitcast.52), channel_id=1, source_target_pairs={{0,64},{8,200},{64,128},{72,8},{128,192},{136,72},{192,0},{200,136... | collective-permute-start | bytes 3538952 | tf_op jit(solution)/shard_map/ppermute | solution.py:306
  49.8 26.0 %collective-permute-start.11 = (f32[768,384]{1,0:T(8,128)S(1)}, f32[768,384]{1,0:T(8,128)}, u32[]{:S(2)}, u32[]{:S(2)}) collective-permute-start(f32[768,384]{1,0:T(8,128)S(1)} %collective-permute-done.10), channel_id=1, source_target_pairs={{0,64},{8,200},{64,128},{72,8},{128,192},{136,72},{192,0},{200,136... | collective-permute-start | bytes 3538952 | tf_op jit(solution)/shard_map/ppermute | solution.py:307
  59.3 20.3 %collective-permute-start.4 = (f32[768,384]{1,0:T(8,128)S(1)}, f32[768,384]{1,0:T(8,128)}, u32[]{:S(2)}, u32[]{:S(2)}) collective-permute-start(f32[768,384]{1,0:T(8,128)S(1)} %collective-permute-done.2.rest_2_), channel_id=1, source_target_pairs={{0,16},{8,56},{16,32},{24,8},{32,48},{40,24},{48,0},{56,40},{1,17}... | collective-permute-start | bytes 3538952 | tf_op jit(solution)/shard_map/ppermute | solution.py:301
  61.5 27.8 %collective-permute-start.3 = (f32[768,384]{1,0:T(8,128)S(1)}, f32[768,384]{1,0:T(8,128)}, u32[]{:S(2)}, u32[]{:S(2)}) collective-permute-start(f32[768,384]{1,0:T(8,128)S(1)} %collective-permute-done.1.rest_1_), channel_id=1, source_target_pairs={{0,16},{8,56},{16,32},{24,8},{32,48},{40,24},{48,0},{56,40},{1,17}... | collective-permute-start | bytes 3538952 | tf_op jit(solution)/shard_map/ppermute | solution.py:300
  64.4 36.6 %collective-permute-start.9 = (f32[768,384]{1,0:T(8,128)}, f32[768,384]{1,0:T(8,128)}, u32[]{:S(2)}, u32[]{:S(2)}) collective-permute-start(f32[768,384]{1,0:T(8,128)} %collective-permute-done.8.rest_9_), channel_id=1, source_target_pairs={{0,64},{8,200},{64,128},{72,8},{128,192},{136,72},{192,0},{200,136... | collective-permute-start | bytes 3538952 | tf_op jit(solution)/shard_map/ppermute | solution.py:308
  68.5 32.5 %collective-permute-start.5 = (f32[768,384]{1,0:T(8,128)S(1)}, f32[768,384]{1,0:T(8,128)}, u32[]{:S(2)}, u32[]{:S(2)}) collective-permute-start(f32[768,384]{1,0:T(8,128)S(1)} %collective-permute-done.2.rest_2_), channel_id=1, source_target_pairs={{0,8},{8,0},{1,9},{9,1},{2,10},{10,2},{3,11},{11,3},{4,12},{12,4},... | collective-permute-start | bytes 3538952 | tf_op jit(solution)/shard_map/ppermute | solution.py:303
  75.7 25.3 %collective-permute-start.12 = (f32[768,384]{1,0:T(8,128)}, f32[768,384]{1,0:T(8,128)}, u32[]{:S(2)}, u32[]{:S(2)}) collective-permute-start(f32[768,384]{1,0:T(8,128)} %collective-permute-done.11), channel_id=1, source_target_pairs={{0,8},{8,0},{1,9},{9,1},{2,10},{10,2},{3,11},{11,3},{4,12},{12,4},... | collective-permute-start | bytes 3538952 | tf_op jit(solution)/shard_map/ppermute | solution.py:309
  79.6 21.5 %collective-permute-start.7 = (f32[768,384]{1,0:T(8,128)}, f32[768,384]{1,0:T(8,128)}, u32[]{:S(2)}, u32[]{:S(2)}) collective-permute-start(f32[768,384]{1,0:T(8,128)} %collective-permute-done.4.rest_4_), channel_id=1, source_target_pairs={{0,8},{8,0},{1,9},{9,1},{2,10},{10,2},{3,11},{11,3},{4,12},{12,4},... | collective-permute-start | bytes 3538952 | tf_op jit(solution)/shard_map/ppermute | solution.py:303
  89.3 11.8 %collective-permute-start.6 = (f32[768,384]{1,0:T(8,128)}, f32[768,384]{1,0:T(8,128)}, u32[]{:S(2)}, u32[]{:S(2)}) collective-permute-start(f32[768,384]{1,0:T(8,128)} %collective-permute-done.3.rest_3_), channel_id=1, source_target_pairs={{0,8},{8,0},{1,9},{9,1},{2,10},{10,2},{3,11},{11,3},{4,12},{12,4},... | collective-permute-start | bytes 3538952 | tf_op jit(solution)/shard_map/ppermute | solution.py:303
  101.1 1.3 copy-start.4
  102.4 0.9 copy-start.5
  117.4 2.9 %copy-start = (bf16[12,768,384]{2,1,0:T(8,128)(2,1)}, bf16[12,768,384]{2,1,0:T(8,128)(2,1)S(1)}, u32[]{:S(2)}) copy-start(bf16[12,768,384]{2,1,0:T(8,128)(2,1)S(1)} %get-tuple-element.10.high_hbm) | copy-start | bytes 21233668
  120.3 2.9 %copy-start.3 = (bf16[12,768,384]{2,1,0:T(8,128)(2,1)}, bf16[12,768,384]{2,1,0:T(8,128)(2,1)S(1)}, u32[]{:S(2)}) copy-start(bf16[12,768,384]{2,1,0:T(8,128)(2,1)S(1)} %get-tuple-element.11.low_hbm) | copy-start | bytes 21233668
  123.2 3.0 %copy-start.1 = (bf16[12,768,384]{2,1,0:T(8,128)(2,1)S(1)}, bf16[12,768,384]{2,1,0:T(8,128)(2,1)}, u32[]{:S(2)}) copy-start(bf16[12,768,384]{2,1,0:T(8,128)(2,1)} %copy-done) | copy-start | bytes 21233668
  135.0 40.3 %collective-permute-start.19 = (f32[8,384]{1,0:T(8,128)S(1)}, f32[8,384]{1,0:T(8,128)S(1)}, u32[]{:S(2)}, u32[]{:S(2)}) collective-permute-start(f32[8,384]{1,0:T(8,128)S(1)} %bitcast.54), channel_id=1, source_target_pairs={{0,128},{64,192},{128,0},{192,64},{1,129},{65,193},{129,1},{193,65... | collective-permute-start | bytes 36872 | tf_op jit(solution)/shard_map/ppermute | solution.py:355
  140.6 27.1 %collective-permute-start.13 = (f32[384,384]{1,0:T(8,128)S(1)}, f32[384,384]{1,0:T(8,128)S(1)}, u32[]{:S(2)}, u32[]{:S(2)}) collective-permute-start(f32[384,384]{1,0:T(8,128)S(1)} %get-tuple-element.24), channel_id=1, source_target_pairs={{0,64},{64,128},{128,192},{192,0},{1,65},{65,129},{129,193},{193,1... | collective-permute-start | bytes 1769480 | tf_op jit(solution)/shard_map/ppermute | solution.py:336
  143.1 24.5 %collective-permute-start.17 = (f32[384,384]{1,0:T(8,128)S(1)}, f32[384,384]{1,0:T(8,128)S(1)}, u32[]{:S(2)}, u32[]{:S(2)}) collective-permute-start(f32[384,384]{1,0:T(8,128)S(1)} %get-tuple-element.25), channel_id=1, source_target_pairs={{0,192},{64,0},{128,64},{192,128},{1,193},{65,1},{129,65},{193,129... | collective-permute-start | bytes 1769480 | tf_op jit(solution)/shard_map/ppermute | solution.py:337
  162.4 60.2 %collective-permute-start.15 = (f32[384,384]{1,0:T(8,128)}, f32[384,384]{1,0:T(8,128)S(1)}, u32[]{:S(2)}, u32[]{:S(2)}) collective-permute-start(f32[384,384]{1,0:T(8,128)} %get-tuple-element.20), channel_id=1, source_target_pairs={{0,192},{64,0},{128,64},{192,128},{1,193},{65,1},{129,65},{193,129... | collective-permute-start | bytes 1769480 | tf_op jit(solution)/shard_map/ppermute | solution.py:340
  164.3 58.3 %collective-permute-start.16 = (f32[384,384]{1,0:T(8,128)}, f32[384,384]{1,0:T(8,128)S(1)}, u32[]{:S(2)}, u32[]{:S(2)}) collective-permute-start(f32[384,384]{1,0:T(8,128)} %get-tuple-element.21), channel_id=1, source_target_pairs={{0,64},{64,128},{128,192},{192,0},{1,65},{65,129},{129,193},{193,1... | collective-permute-start | bytes 1769480 | tf_op jit(solution)/shard_map/ppermute | solution.py:339
  168.8 53.8 %collective-permute-start.14 = (f32[384,384]{1,0:T(8,128)}, f32[384,384]{1,0:T(8,128)S(1)}, u32[]{:S(2)}, u32[]{:S(2)}) collective-permute-start(f32[384,384]{1,0:T(8,128)} %get-tuple-element.18), channel_id=1, source_target_pairs={{0,64},{64,128},{128,192},{192,0},{1,65},{65,129},{129,193},{193,1... | collective-permute-start | bytes 1769480 | tf_op jit(solution)/shard_map/ppermute | solution.py:341
  170.8 51.8 %collective-permute-start.18 = (f32[384,384]{1,0:T(8,128)}, f32[384,384]{1,0:T(8,128)}, u32[]{:S(2)}, u32[]{:S(2)}) collective-permute-start(f32[384,384]{1,0:T(8,128)} %get-tuple-element.19), channel_id=1, source_target_pairs={{0,192},{64,0},{128,64},{192,128},{1,193},{65,1},{129,65},{193,129... | collective-permute-start | bytes 1769480 | tf_op jit(solution)/shard_map/ppermute | solution.py:342
  175.4 19.1 %collective-permute-start.20 = (f32[8,384]{1,0:T(8,128)S(1)}, f32[8,384]{1,0:T(8,128)S(1)}, u32[]{:S(2)}, u32[]{:S(2)}) collective-permute-start(f32[8,384]{1,0:T(8,128)S(1)} %get-tuple-element.29), channel_id=1, source_target_pairs={{0,64},{64,128},{128,192},{192,0},{1,65},{65,129},{129,193},{193,1... | collective-permute-start | bytes 36872 | tf_op jit(solution)/shard_map/ppermute | solution.py:356
  194.5 14.0 %collective-permute-start.21 = (f32[8,384]{1,0:T(8,128)S(1)}, f32[8,384]{1,0:T(8,128)S(1)}, u32[]{:S(2)}, u32[]{:S(2)}) collective-permute-start(f32[8,384]{1,0:T(8,128)S(1)} %get-tuple-element.30), channel_id=1, source_target_pairs={{0,192},{64,0},{128,64},{192,128},{1,193},{65,1},{129,65},{193,129... | collective-permute-start | bytes 36872 | tf_op jit(solution)/shard_map/ppermute | solution.py:357
  196.6 3.0 %copy-start.2 = (bf16[12,768,384]{2,1,0:T(8,128)(2,1)S(1)}, bf16[12,768,384]{2,1,0:T(8,128)(2,1)}, u32[]{:S(2)}) copy-start(bf16[12,768,384]{2,1,0:T(8,128)(2,1)} %copy-done) | copy-start | bytes 21233668
  199.6 22.4 %copy-start.6 = (f32[1,384]{1,0:T(1,128)S(1)}, f32[1,384]{1,0:T(1,128)}, u32[]{:S(2)}) copy-start(f32[1,384]{1,0:T(1,128)} %param.10) | copy-start | bytes 4612
Sparse Core Ops, SparseCore 0:
  10.1 111.2 all-gather.2

commit v5 on v3

v5 whole, which is shorter than its diff:
```python
import functools

import jax
import jax.numpy as jnp
from jax import lax
from jax.experimental import pallas as pl
from jax.experimental.pallas import tpu as pltpu
from jax.sharding import Mesh, PartitionSpec as P

BLOCK = 128
PART = 256
SLOTS = 4
VMEM_BYTES = 20 * 1024 * 1024
CORES = [(0, 1), (1, 0)]
SPREAD_X = (
    (3, 1, 0, 0),
    (0, 3, 0, 1),
    (1, 2, 0, 1),
    (2, 0, 1, 1),
    (2, 2, 1, 3),
    (3, 1, 2, 2),
    (3, 0, 2, 3),
    (3, 2, 3, 0),
)


def shift(size, step):
    return [(i, (i + step) % size) for i in range(size)]


def opposite(size, way=1):
    return [
        (2 * i + c, (i + way * (1 - 2 * c)) % size * 2 + c) for i in range(size) for c in range(2)
    ]


def spread_plan():
    pairs, holds, taken = [], {}, {}
    for y in range(4):
        for r in range(8):
            to = (SPREAD_X[r][y], r % 4)
            core = taken.get(to, 0)
            taken[to] = core + 1
            pairs.append(((y * 4 + r // 2) * 2 + r % 2, (to[1] * 4 + to[0]) * 2 + core))
            holds[(to[1], to[0], core)] = (r // 4, y)
    return pairs, holds


def piece_plan(holds):
    halves, own, found = [], [], []
    for y in range(4):
        for x in range(4):
            for c in range(2):
                d = 2 * c - 1
                at = [
                    (x, c),
                    (x, 1 - c),
                    (x + d, c),
                    (x + d, 1 - c),
                    (x + 2, c),
                    (x - d, 1 - c),
                    (x - d, c),
                    (x + 2, 1 - c),
                ]
                has = [holds[(y, px % 4, pc)] for px, pc in at]
                mine = [y, (y + d) % 4, (y + 2) % 4, (y - d) % 4]
                halves.append([h * 4 + k for h, k in has])
                own.append(mine)
                found.append(
                    [[has.index((0, k)), has.index((1, k)), 8 + mine.index(k)] for k in range(4)]
                )
    return [jnp.array(v, jnp.int32) for v in (halves, own, found)]


def spread_kernel(start_row, rows_ref, *rest):
    pieces = rest[:12]
    high_ref, low_ref, z_f, in_sem = rest[12:]
    slots, rows = z_f.shape[:2]

    def fetch(i):
        return pltpu.make_async_copy(pieces[i], z_f.at[i % slots], in_sem.at[i])

    for i in range(slots):
        fetch(i).start()
    row = lax.broadcasted_iota(jnp.int32, (BLOCK, BLOCK), 0)
    for at in range(len(pieces)):
        fetch(at).wait()

        def one(i, carry, at=at):
            here = pl.ds(pl.multiple_of(i * BLOCK, BLOCK), BLOCK)
            value = z_f[at % slots, here, :]
            high = value.astype(jnp.bfloat16)
            low = (value - high.astype(jnp.float32)).astype(jnp.bfloat16)
            place = rows_ref[pl.ds(start_row[at] + i, 1), :]
            place = jnp.where(place >= 0, place & (BLOCK - 1), -1)
            hot = (place == row).astype(jnp.float32).astype(jnp.bfloat16)
            high_ref[at, here, :] = jnp.dot(
                hot, high, preferred_element_type=jnp.float32
            ).astype(jnp.bfloat16)
            low_ref[at, here, :] = jnp.dot(
                hot, low, preferred_element_type=jnp.float32
            ).astype(jnp.bfloat16)
            return carry

        lax.fori_loop(0, rows // BLOCK, one, 0, unroll=3)
        if at + slots < len(pieces):
            fetch(at + slots).start()


def spread(start_row, root_row, pieces):
    rows, cols = pieces[0].shape
    any_spec = pl.BlockSpec(memory_space=pl.ANY)
    vmem = pl.BlockSpec(memory_space=pltpu.VMEM)
    shape = (len(pieces), rows, cols)
    return pl.pallas_call(
        spread_kernel,
        out_shape=[pltpu.VMEM(shape, jnp.bfloat16)] * 2,
        in_specs=[pl.BlockSpec(memory_space=pltpu.SMEM), vmem] + [any_spec] * len(pieces),
        out_specs=[vmem] * 2,
        scratch_shapes=[
            pltpu.VMEM((SLOTS, rows, cols), jnp.float32),
            pltpu.SemaphoreType.DMA((len(pieces),)),
        ],
        compiler_params=pltpu.CompilerParams(vmem_limit_bytes=VMEM_BYTES),
        cost_estimate=pl.CostEstimate(
            flops=12 * 4 * rows * BLOCK * cols, bytes_accessed=48 * rows * cols, transcendentals=0
        ),
    )(start_row, root_row, *pieces)


def product_kernel(call, table, root, high_ref, low_ref, out, sums):
    rows = out.shape[0]
    per_range = rows // BLOCK
    per_part = PART // BLOCK
    c = table[call, 3 * per_range + 3]
    spots = [table[c, 3 * per_range + i] for i in range(3)]
    high_z = jnp.concatenate([high_ref[spots[0]], high_ref[spots[1]]], axis=0)
    low_z = jnp.concatenate([low_ref[spots[0]], low_ref[spots[1]]], axis=0)

    def one(part, total):
        at = [
            pl.ds(pl.multiple_of(table[c, part * per_part + m] * BLOCK, BLOCK), BLOCK)
            for m in range(per_part)
        ]
        highs, lows = [], []
        for k in range(2 * per_range):
            kb = table[c, per_range + k]
            value = jnp.concatenate([root[kb, here, :] for here in at], axis=0)
            high = value.astype(jnp.bfloat16)
            highs.append(high)
            lows.append((value - high.astype(jnp.float32)).astype(jnp.bfloat16))
        high = jnp.concatenate(highs, axis=1)
        low = jnp.concatenate(lows, axis=1)
        value = jnp.dot(high, low_z, preferred_element_type=jnp.float32)
        value = value + jnp.dot(low, high_z, preferred_element_type=jnp.float32)
        value = value + jnp.dot(high, high_z, preferred_element_type=jnp.float32)
        here = pl.ds(pl.multiple_of(part * PART, PART), PART)
        out[here, :] = value
        factor = high_ref[spots[2], here, :].astype(jnp.float32) + low_ref[
            spots[2], here, :
        ].astype(jnp.float32)
        return total + jnp.sum((factor * value).reshape(PART // 8, 8, -1), axis=0)

    sums[...] = lax.fori_loop(0, rows // PART, one, jnp.zeros(sums.shape, jnp.float32))


def product(call, table, root, high, low):
    rows, cols = high.shape[1:]
    vmem = pl.BlockSpec(memory_space=pltpu.VMEM)
    return pl.pallas_call(
        functools.partial(product_kernel, call),
        out_shape=[
            jax.ShapeDtypeStruct((rows, cols), jnp.float32),
            jax.ShapeDtypeStruct((8, cols), jnp.float32),
        ],
        in_specs=[pl.BlockSpec(memory_space=pltpu.SMEM)] + [vmem] * 3,
        out_specs=[vmem] * 2,
        compiler_params=pltpu.CompilerParams(vmem_limit_bytes=VMEM_BYTES),
        cost_estimate=pl.CostEstimate(
            flops=3 * 2 * rows * 2 * rows * cols, bytes_accessed=4 * rows * cols, transcendentals=0
        ),
    )(table, root, high, low)


def per_device(root_inverse, root_row, coupling, pivot_variance):
    zh = lax.axis_index("zh")
    y = lax.axis_index("y")
    x = lax.axis_index("x")
    core = lax.axis_index("core")
    rows, cols = coupling.shape[1:]
    ranges = root_row.shape[1] // rows
    per_range = rows // BLOCK
    half = rows // 2
    own_range = 2 * x + core
    device = (y * 4 + x) * 2 + core

    root = lax.all_gather(root_inverse, ("zh", "zl"), axis=0, tiled=False)

    pairs, holds = spread_plan()
    own = lax.ppermute(coupling[0], ("y", "x", "core"), pairs)
    along_x, along_y = opposite(4), opposite(4)
    beside = lax.ppermute(own, "core", CORES)
    near = lax.ppermute(own, ("x", "core"), along_x)
    near_beside = lax.ppermute(beside, ("x", "core"), along_x)
    far = lax.ppermute(near, ("x", "core"), along_x)
    pieces = [own, beside, near, near_beside, far]
    pieces += [lax.ppermute(p, "core", CORES) for p in (near, near_beside, far)]

    y_beside = lax.ppermute(coupling[0], "core", CORES)
    y_near = lax.ppermute(coupling[0], ("y", "core"), along_y)
    y_near_beside = lax.ppermute(y_beside, ("y", "core"), along_y)
    y_far = lax.ppermute(y_near, ("y", "core"), along_y)
    pieces += [coupling[0], y_near, y_far, lax.ppermute(y_near_beside, "core", CORES)]

    halves, own_children, found = piece_plan(holds)
    spots = lax.dynamic_slice(halves, (device, 0), (1, 8))[0]
    own_spots = lax.dynamic_slice(own_children, (device, 0), (1, 4))[0]
    child = zh * 4 + jnp.concatenate([spots & 3, own_spots])
    ranged = jnp.concatenate([y + 4 * (spots >> 2), jnp.full((4,), own_range, jnp.int32)])
    start_row = (child * ranges + ranged) * per_range
    high, low = spread(start_row, root_row.reshape(-1, BLOCK), pieces)

    block = (root_row[:, ::BLOCK] >> 7).reshape(-1, ranges, per_range)

    def blocks_of(r):
        return lax.dynamic_slice(block, (zh * 4, r, 0), (4, 1, per_range))[:, 0] & 7

    order = (y + jnp.stack([2, 3 - 2 * core, 1 + 2 * core, 0])) & 3
    table = jnp.concatenate(
        [
            blocks_of(own_range),
            blocks_of(y),
            blocks_of(y + 4) + 8,
            lax.dynamic_slice(found, (device, 0, 0), (1, 4, 3))[0],
            order[:, None],
        ],
        axis=1,
    ).astype(jnp.int32)

    root = pltpu.with_memory_space_constraint(root.reshape(-1, *root_inverse.shape), pltpu.VMEM)
    high = pltpu.with_memory_space_constraint(high, pltpu.VMEM)
    low = pltpu.with_memory_space_constraint(low, pltpu.VMEM)
    far, far_sums = product(0, table, root, high, low)
    passed = lax.ppermute(far, ("y", "core"), opposite(4))
    first, first_sums = product(1, table, root, high, low)
    back = lax.ppermute(first, ("y", "core"), opposite(4, -1))
    second, second_sums = product(2, table, root, high, low)
    forth = lax.ppermute(second + passed, ("y", "core"), opposite(4))
    home, home_sums = product(3, table, root, high, low)
    summed = home + forth + back

    own_place = lax.dynamic_slice(root_row, (zh * 4 + y, own_range * rows), (1, rows))[0]
    own_place = jnp.where(own_place >= 0, own_place & (BLOCK - 1), -1).reshape(per_range, BLOCK)
    hot = (own_place[:, :, None] == jnp.arange(BLOCK, dtype=jnp.int32)).astype(jnp.float32)
    result = -jnp.einsum(
        "iuo,ion->iun", hot, summed.reshape(per_range, BLOCK, cols), precision=lax.Precision.HIGHEST
    )

    sums = jnp.stack(
        [
            home_sums,
            jnp.where(core == 0, second_sums, first_sums),
            far_sums,
            jnp.where(core == 0, first_sums, second_sums),
        ]
    )
    sums = lax.psum(jnp.sum(sums, axis=1), ("x", "core"))
    marginal = pivot_variance + sums[:1]
    for step in range(1, 4):
        marginal = marginal + lax.ppermute(sums[step : step + 1], "y", shift(4, step))
    return result.reshape(1, rows, cols), marginal


def solution(mesh):
    split = Mesh(mesh.devices.reshape(2, 4, 4, 2, 8), ("zh", "y", "x", "core", "zl"))
    leaf, row, col = ("zh", "y"), ("x", "core"), "zl"
    return jax.shard_map(
        per_device,
        mesh=split,
        in_specs=(P(row, ("zh", "y", "zl")), P(), P(leaf, row, col), P(leaf, col)),
        out_specs=(P(leaf, row, col), P(leaf, col)),
        check_vma=False,
    )
```

time: 258 us -> 216 us (0.84)
  blocking collectives: 65.5 us -> 12.7 us
  local copies, waits for them, and re-layouts: 12.4 us -> 33 us
  Pallas kernels: 45.9 us -> 28.8 us
  starting transfers between devices: 59.7 us -> 64.3 us
  waiting for transfers between devices: 48.7 us -> 52.3 us
    psum x1, blocking collectives: 65.5 us -> 12.7 us  [per_device(): sums = lax.psum(jnp.sum(sums, axis=1), ('x', 'core'))]
    unnamed x18 -> x22, local copies, waits for them, and re-layouts: 0.61 us -> 26.8 us
    pallas_call x4 -> x5, Pallas kernels: 45.9 us -> 28.8 us  [the longest x4 19.7 us: product(): pl.pallas_call(functools.partial(product_kernel, call), out_shape=[jax.Sh...]
    ppermute x6, waiting for transfers between devices: 0.02 us -> 5.45 us  [the longest x1 5.43 us: per_device(): passed = lax.ppermute(far, ('y', 'core'), opposite(4))]
    ppermute x6, starting transfers between devices: 18.3 us -> 22.8 us  [the longest x3 10.9 us: per_device(): marginal = marginal + lax.ppermute(sums[step:step + 1], 'y', shift(4, step))]
    squeeze x2 -> x0, local copies, waits for them, and re-layouts: 3.9 us -> none  [the longest x1 2.57 us: per_device(): down = lax.ppermute(near[1, :half], 'y', shift(4, -1))]
  transfers between devices with their start and end apart: 20 -> 20, of which waited for: 5 -> 6; matrix products, arithmetic and copies ran while one was open for 7% -> 5% of each run, Pallas kernels for 14% -> 11%
where the time goes in v5:
time: 216 us; the launch traced here: 214 us
  starting transfers between devices  64.3 us (30%)
  waiting for transfers between devices  52.3 us (24%)
  local copies, waits for them, and re-layouts  33 us (15%)
  Pallas kernels  28.8 us (13%)
  between operations  14.4 us (7%)
  blocking collectives  12.7 us (6%)
  other arithmetic  6.65 us (3%)
    unnamed x22, local copies, waits for them, and re-layouts  26.8 us
    ppermute x1, waiting for transfers between devices, per_device(): own = lax.ppermute(coupling[0], ('y', 'x', 'core'), pairs)  22.4 us
    pallas_call x4, Pallas kernels, product(): pl.pallas_call(functools.partial(product_kernel, call), out_shape=[jax.Sh...  19.7 us
    psum x1, blocking collectives, per_device(): sums = lax.psum(jnp.sum(sums, axis=1), ('x', 'core'))  12.7 us
    ppermute x3, starting transfers between devices, per_device(): marginal = marginal + lax.ppermute(sums[step:step + 1], 'y', shift(4, step))  10.9 us
    pallas_call x1, Pallas kernels, spread(): pl.pallas_call(spread_kernel, out_shape=[pltpu.VMEM(shape, jnp.bfloat16)]...  9.13 us
    ppermute x1, waiting for transfers between devices, per_device(): near_beside = lax.ppermute(beside, ('x', 'core'), along_x)  7.78 us
    ppermute x1, waiting for transfers between devices, per_device(): near = lax.ppermute(own, ('x', 'core'), along_x)  7.64 us
  transfers between devices with their start and end apart: 20, of which 6 were waited for; matrix products, arithmetic and copies ran while one was open for 5% of the time, Pallas kernels for 11%

profile of v5, /device:TPU:1, one launch (start us, length us, event | category | flops | bytes accessed | tf_op | source)
XLA Modules:
  0.0 214.0 jit_solution(2320186900521565149)
XLA Ops:
  7.2 0.0 all-gather.3.cloned.1.call-start
  7.2 0.7 all-gather.3.cloned.1.call-update
  7.9 4.6 %collective-permute-start = (f32[768,384]{1,0:T(8,128)}, f32[768,384]{1,0:T(8,128)S(1)}, u32[]{:S(2)}, u32[]{:S(2)}) collective-permute-start(f32[768,384]{1,0:T(8,128)} %bitcast.29), channel_id=1, source_target_pairs={{0,48},{8,64},{16,144},{24,224},{32,32},{40,112},{48,176},{56,240}... | collective-permute-start | bytes 3538952 | tf_op jit(solution)/shard_map/ppermute | solution.py:200
  12.5 6.1 %collective-permute-start.10 = (f32[768,384]{1,0:T(8,128)}, f32[768,384]{1,0:T(8,128)S(1)}, u32[]{:S(2)}, u32[]{:S(2)}) collective-permute-start(f32[768,384]{1,0:T(8,128)} %bitcast.30), channel_id=1, source_target_pairs={{0,8},{8,0},{1,9},{9,1},{2,10},{10,2},{3,11},{11,3},{4,12},{12,4},... | collective-permute-start | bytes 3538952 | tf_op jit(solution)/shard_map/ppermute | solution.py:209
  18.6 22.4 %collective-permute-done.rest_0_ = f32[768,384]{1,0:T(8,128)S(1)} collective-permute-done((f32[768,384]{1,0:T(8,128)}, f32[768,384]{1,0:T(8,128)S(1)}, u32[]{:S(2)}, u32[]{:S(2)}) %collective-permute-start) | collective-permute-done | bytes 1179680 | tf_op jit(solution)/shard_map/ppermute | solution.py:200
  41.1 1.9 collective-permute-start.2
  43.0 1.9 collective-permute-start.1
  44.9 4.8 %collective-permute-start.8 = (f32[768,384]{1,0:T(8,128)}, f32[768,384]{1,0:T(8,128)}, u32[]{:S(2)}, u32[]{:S(2)}) collective-permute-start(f32[768,384]{1,0:T(8,128)} %bitcast.31), channel_id=1, source_target_pairs={{0,64},{8,200},{64,128},{72,8},{128,192},{136,72},{192,0},{200,136... | collective-permute-start | bytes 3538952 | tf_op jit(solution)/shard_map/ppermute | solution.py:210
  49.7 0.0 collective-permute-done.10
  49.8 1.9 collective-permute-start.11
  51.7 7.6 %collective-permute-done.2.rest_2_ = f32[768,384]{1,0:T(8,128)S(1)} collective-permute-done((f32[768,384]{1,0:T(8,128)S(1)}, f32[768,384]{1,0:T(8,128)S(1)}, u32[]{:S(2)}, u32[]{:S(2)}) %collective-permute-start.2) | collective-permute-done | bytes 1179680 | tf_op jit(solution)/shard_map/ppermute | solution.py:203
  59.3 2.2 %collective-permute-start.4 = (f32[768,384]{1,0:T(8,128)S(1)}, f32[768,384]{1,0:T(8,128)}, u32[]{:S(2)}, u32[]{:S(2)}) collective-permute-start(f32[768,384]{1,0:T(8,128)S(1)} %collective-permute-done.2.rest_2_), channel_id=1, source_target_pairs={{0,16},{8,56},{16,32},{24,8},{32,48},{40,24},{48,0},{56,40},{1,17}... | collective-permute-start | bytes 3538952 | tf_op jit(solution)/shard_map/ppermute | solution.py:205
  61.5 0.0 collective-permute-done.1.rest_1_
  61.5 2.8 %collective-permute-start.3 = (f32[768,384]{1,0:T(8,128)S(1)}, f32[768,384]{1,0:T(8,128)}, u32[]{:S(2)}, u32[]{:S(2)}) collective-permute-start(f32[768,384]{1,0:T(8,128)S(1)} %collective-permute-done.1.rest_1_), channel_id=1, source_target_pairs={{0,16},{8,56},{16,32},{24,8},{32,48},{40,24},{48,0},{56,40},{1,17}... | collective-permute-start | bytes 3538952 | tf_op jit(solution)/shard_map/ppermute | solution.py:204
  64.4 4.1 %collective-permute-start.9 = (f32[768,384]{1,0:T(8,128)}, f32[768,384]{1,0:T(8,128)}, u32[]{:S(2)}, u32[]{:S(2)}) collective-permute-start(f32[768,384]{1,0:T(8,128)} %collective-permute-done.8.rest_9_), channel_id=1, source_target_pairs={{0,64},{8,200},{64,128},{72,8},{128,192},{136,72},{192,0},{200,136... | collective-permute-start | bytes 3538952 | tf_op jit(solution)/shard_map/ppermute | solution.py:212
  68.5 1.9 collective-permute-start.5
  70.4 5.3 %collective-permute-done.11 = f32[768,384]{1,0:T(8,128)} collective-permute-done((f32[768,384]{1,0:T(8,128)S(1)}, f32[768,384]{1,0:T(8,128)}, u32[]{:S(2)}, u32[]{:S(2)}) %collective-permute-start.11) | collective-permute-done | bytes 1179680 | tf_op jit(solution)/shard_map/ppermute | solution.py:211
  75.7 3.9 %collective-permute-start.12 = (f32[768,384]{1,0:T(8,128)}, f32[768,384]{1,0:T(8,128)}, u32[]{:S(2)}, u32[]{:S(2)}) collective-permute-start(f32[768,384]{1,0:T(8,128)} %collective-permute-done.11), channel_id=1, source_target_pairs={{0,8},{8,0},{1,9},{9,1},{2,10},{10,2},{3,11},{11,3},{4,12},{12,4},... | collective-permute-start | bytes 3538952 | tf_op jit(solution)/shard_map/ppermute | solution.py:213
  79.6 1.9 collective-permute-start.7
  81.5 7.8 %collective-permute-done.3.rest_3_ = f32[768,384]{1,0:T(8,128)} collective-permute-done((f32[768,384]{1,0:T(8,128)S(1)}, f32[768,384]{1,0:T(8,128)}, u32[]{:S(2)}, u32[]{:S(2)}) %collective-permute-start.3) | collective-permute-done | bytes 1179680 | tf_op jit(solution)/shard_map/ppermute | solution.py:204
  89.3 3.3 %collective-permute-start.6 = (f32[768,384]{1,0:T(8,128)}, f32[768,384]{1,0:T(8,128)}, u32[]{:S(2)}, u32[]{:S(2)}) collective-permute-start(f32[768,384]{1,0:T(8,128)} %collective-permute-done.3.rest_3_), channel_id=1, source_target_pairs={{0,8},{8,0},{1,9},{9,1},{2,10},{10,2},{3,11},{11,3},{4,12},{12,4},... | collective-permute-start | bytes 3538952 | tf_op jit(solution)/shard_map/ppermute | solution.py:207
  92.7 1.6 reshape.103.rows_ref
  94.3 1.0 slice.15
  95.4 0.7 reshape.102
  96.1 0.1 pad_add_fusion
  96.1 0.1 copy.12
  96.2 1.3 dynamic-slice_bitcast_fusion
  97.5 0.8 and_add_fusion
  98.3 0.6 add_and_fusion
  98.9 0.8 concatenate.16.table
  99.7 0.7 fusion.5
  100.4 0.7 and_bitcast_fusion
  101.1 0.1 fusion.8.start_row
  101.2 0.0 collective-permute-done.9.rest_10_
  101.2 0.0 copy-start.8
  101.2 1.3 copy-done.8
  102.5 0.9 copy-done.9
  103.4 9.1 %shard_map.86 = (bf16[12,768,384]{2,1,0:T(8,128)(2,1)S(1)}, bf16[12,768,384]{2,1,0:T(8,128)(2,1)S(1)}) custom-call(s32[12]{0:T(128)S(1)} %fusion.8.start_row, s32[384,128]{1,0:T(8,128)S(1)} %copy-done.9, f32[768,384]{1,0:T(8,128)S(1)} %collective-permute-done.rest_0_, f32[768,384]{1,0:T(8,128)S(1)} %collective-permute-done.1.rest_1_, ...), custom_call_target="tpu_custom_call" | custom-call | flops 1811939328 | bytes 14155776 | tf_op jit(solution)/shard_map/pallas_call | solution.py:115
  112.6 2.9 %copy-done.2 = bf16[12,768,384]{2,1,0:T(8,128)(2,1)} copy-done((bf16[12,768,384]{2,1,0:T(8,128)(2,1)}, bf16[12,768,384]{2,1,0:T(8,128)(2,1)S(1)}, u32[]{:S(2)}) %copy-start.2) | copy-done | bytes 7077912
  115.5 2.9 %copy-done.5 = bf16[12,768,384]{2,1,0:T(8,128)(2,1)} copy-done((bf16[12,768,384]{2,1,0:T(8,128)(2,1)}, bf16[12,768,384]{2,1,0:T(8,128)(2,1)S(1)}, u32[]{:S(2)}) %copy-start.5) | copy-done | bytes 7077912
  118.4 3.0 %all-gather.3.cloned.1.call-done = f32[16384,128]{1,0:T(8,128)} async-done(((f32[1024,128]{1,0:T(8,128)}), f32[16384,128]{1,0:T(8,128)}) %all-gather.3.cloned.1.call-update) | async-done | bytes 8388624 | tf_op jit(solution)/shard_map/all_gather | solution.py:197
  121.4 3.4 %copy-done = f32[16384,128]{1,0:T(8,128)S(1)} copy-done((f32[16384,128]{1,0:T(8,128)S(1)}, f32[16384,128]{1,0:T(8,128)}, u32[]{:S(2)}) %copy-start) | copy-done | bytes 8388632
  124.7 3.0 %copy-done.3 = bf16[12,768,384]{2,1,0:T(8,128)(2,1)S(1)} copy-done((bf16[12,768,384]{2,1,0:T(8,128)(2,1)S(1)}, bf16[12,768,384]{2,1,0:T(8,128)(2,1)}, u32[]{:S(2)}) %copy-start.3) | copy-done | bytes 7077912
  127.8 3.0 %copy-done.6 = bf16[12,768,384]{2,1,0:T(8,128)(2,1)S(1)} copy-done((bf16[12,768,384]{2,1,0:T(8,128)(2,1)S(1)}, bf16[12,768,384]{2,1,0:T(8,128)(2,1)}, u32[]{:S(2)}) %copy-start.6) | copy-done | bytes 7077912
  130.8 4.9 %shard_map.89 = (f32[768,384]{1,0:T(8,128)S(1)}, f32[8,384]{1,0:T(8,128)S(1)}) custom-call(s32[4,22]{1,0:T(4,128)S(1)} %concatenate.16.table, f32[16,1024,128]{2,1,0:T(8,128)S(1)} %bitcast.25, bf16[12,768,384]{2,1,0:T(8,128)(2,1)S(1)} %copy-done.3, bf16[12,768,384]{2,1,0:T(8,128)(2,1)S(1)} %copy-done.6), custom_call_target="tpu_custom_call" | custom-call | flops 2717908992 | bytes 1179648 | tf_op jit(solution)/shard_map/pallas_call | solution.py:170
  135.7 4.4 %collective-permute-start.13 = (f32[768,384]{1,0:T(8,128)S(1)}, f32[768,384]{1,0:T(8,128)S(1)}, u32[]{:S(2)}, u32[]{:S(2)}) collective-permute-start(f32[768,384]{1,0:T(8,128)S(1)} %get-tuple-element.16), channel_id=1, source_target_pairs={{0,64},{8,200},{64,128},{72,8},{128,192},{136,72},{192,0},{200,136... | collective-permute-start | bytes 3538952 | tf_op jit(solution)/shard_map/ppermute | solution.py:244
  140.1 4.9 %shard_map.90 = (f32[768,384]{1,0:T(8,128)S(1)}, f32[8,384]{1,0:T(8,128)S(1)}) custom-call(s32[4,22]{1,0:T(4,128)S(1)} %concatenate.16.table, f32[16,1024,128]{2,1,0:T(8,128)S(1)} %bitcast.26, bf16[12,768,384]{2,1,0:T(8,128)(2,1)S(1)} %copy-done.3, bf16[12,768,384]{2,1,0:T(8,128)(2,1)S(1)} %copy-done.6), custom_call_target="tpu_custom_call" | custom-call | flops 2717908992 | bytes 1179648 | tf_op jit(solution)/shard_map/pallas_call | solution.py:170
  145.0 1.9 collective-permute-start.15
  146.9 4.9 %shard_map.88 = (f32[768,384]{1,0:T(8,128)S(1)}, f32[8,384]{1,0:T(8,128)S(1)}) custom-call(s32[4,22]{1,0:T(4,128)S(1)} %concatenate.16.table, f32[16,1024,128]{2,1,0:T(8,128)S(1)} %bitcast.27, bf16[12,768,384]{2,1,0:T(8,128)(2,1)S(1)} %copy-done.3, bf16[12,768,384]{2,1,0:T(8,128)(2,1)S(1)} %copy-done.6), custom_call_target="tpu_custom_call" | custom-call | flops 2717908992 | bytes 1179648 | tf_op jit(solution)/shard_map/pallas_call | solution.py:170
  151.8 5.4 %collective-permute-done.13 = f32[768,384]{1,0:T(8,128)S(1)} collective-permute-done((f32[768,384]{1,0:T(8,128)S(1)}, f32[768,384]{1,0:T(8,128)S(1)}, u32[]{:S(2)}, u32[]{:S(2)}) %collective-permute-start.13) | collective-permute-done | bytes 1179680 | tf_op jit(solution)/shard_map/ppermute | solution.py:244
  157.3 1.1 add.126
  158.4 5.6 %collective-permute-start.14 = (f32[768,384]{1,0:T(8,128)}, f32[768,384]{1,0:T(8,128)}, u32[]{:S(2)}, u32[]{:S(2)}) collective-permute-start(f32[768,384]{1,0:T(8,128)} %add.126), channel_id=1, source_target_pairs={{0,64},{8,200},{64,128},{72,8},{128,192},{136,72},{192,0},{200,136... | collective-permute-start | bytes 3538952 | tf_op jit(solution)/shard_map/ppermute | solution.py:248
  164.0 3.4 %copy-done.1 = f32[16384,128]{1,0:T(8,128)S(1)} copy-done((f32[16384,128]{1,0:T(8,128)S(1)}, f32[16384,128]{1,0:T(8,128)}, u32[]{:S(2)}) %copy-start.1) | copy-done | bytes 8388632
  167.4 3.0 %copy-done.4 = bf16[12,768,384]{2,1,0:T(8,128)(2,1)S(1)} copy-done((bf16[12,768,384]{2,1,0:T(8,128)(2,1)S(1)}, bf16[12,768,384]{2,1,0:T(8,128)(2,1)}, u32[]{:S(2)}) %copy-start.4) | copy-done | bytes 7077912
  170.4 3.0 %copy-done.7 = bf16[12,768,384]{2,1,0:T(8,128)(2,1)S(1)} copy-done((bf16[12,768,384]{2,1,0:T(8,128)(2,1)S(1)}, bf16[12,768,384]{2,1,0:T(8,128)(2,1)}, u32[]{:S(2)}) %copy-start.7) | copy-done | bytes 7077912
  173.4 4.9 %shard_map.87 = (f32[768,384]{1,0:T(8,128)S(1)}, f32[8,384]{1,0:T(8,128)S(1)}) custom-call(s32[4,22]{1,0:T(4,128)S(1)} %concatenate.16.table, f32[16,1024,128]{2,1,0:T(8,128)S(1)} %bitcast.28, bf16[12,768,384]{2,1,0:T(8,128)(2,1)S(1)} %copy-done.4, bf16[12,768,384]{2,1,0:T(8,128)(2,1)S(1)} %copy-done.7), custom_call_target="tpu_custom_call" | custom-call | flops 2717908992 | bytes 1179648 | tf_op jit(solution)/shard_map/pallas_call | solution.py:170
  178.4 12.7 %psum.7 = f32[4,384]{1,0:T(4,128)S(1)} all-reduce(f32[4,384]{1,0:T(4,128)S(1)} %maximum_reduce_fusion), channel_id=1, replica_groups=mesh['zh'=2,'y'=4,'x'=4,'core'=2,'zl'=8] {'x','core'}, use_global_device_ids=true, to_apply=%region_1.2 | all-reduce | flops 1536 | bytes 12288 | tf_op jit(solution)/shard_map/psum | solution.py:267
  191.1 4.1 %collective-permute-start.16 = (f32[1,384]{1,0:T(1,128)S(1)}, f32[1,384]{1,0:T(1,128)S(1)}, u32[]{:S(2)}, u32[]{:S(2)}) collective-permute-start(f32[1,384]{1,0:T(1,128)S(1)} %get-tuple-element.29), channel_id=1, source_target_pairs={{0,64},{64,128},{128,192},{192,0},{1,65},{65,129},{129,193},{193,1... | collective-permute-start | bytes 4616 | tf_op jit(solution)/shard_map/ppermute | solution.py:270
  195.2 2.9 %collective-permute-start.17 = (f32[1,384]{1,0:T(1,128)S(1)}, f32[1,384]{1,0:T(1,128)S(1)}, u32[]{:S(2)}, u32[]{:S(2)}) collective-permute-start(f32[1,384]{1,0:T(1,128)S(1)} %get-tuple-element.31), channel_id=1, source_target_pairs={{0,128},{64,192},{128,0},{192,64},{1,129},{65,193},{129,1},{193,65... | collective-permute-start | bytes 4616 | tf_op jit(solution)/shard_map/ppermute | solution.py:270
  198.1 4.0 %collective-permute-start.18 = (f32[1,384]{1,0:T(1,128)S(1)}, f32[1,384]{1,0:T(1,128)S(1)}, u32[]{:S(2)}, u32[]{:S(2)}) collective-permute-start(f32[1,384]{1,0:T(1,128)S(1)} %get-tuple-element.30), channel_id=1, source_target_pairs={{0,192},{64,0},{128,64},{192,128},{1,193},{65,1},{129,65},{193,129... | collective-permute-start | bytes 4616 | tf_op jit(solution)/shard_map/ppermute | solution.py:270
  202.1 0.8 fusion.1
  203.0 0.6 fusion.4
  203.6 1.8 add_add_fusion
  205.4 1.8 convolution_negate_fusion
  (26 shorter events, 0.1 us)
Async XLA Ops:
  7.2 114.2 %all-gather.3.cloned.1.call-start = ((), (), s32[]{:S(2)}) async-start(), calls=%async_computation | async-start | bytes 8912896 | tf_op jit(solution)/shard_map/all_gather | solution.py:197
  7.9 33.2 %collective-permute-start = (f32[768,384]{1,0:T(8,128)}, f32[768,384]{1,0:T(8,128)S(1)}, u32[]{:S(2)}, u32[]{:S(2)}) collective-permute-start(f32[768,384]{1,0:T(8,128)} %bitcast.29), channel_id=1, source_target_pairs={{0,48},{8,64},{16,144},{24,224},{32,32},{40,112},{48,176},{56,240}... | collective-permute-start | bytes 3538952 | tf_op jit(solution)/shard_map/ppermute | solution.py:200
  12.5 37.2 %collective-permute-start.10 = (f32[768,384]{1,0:T(8,128)}, f32[768,384]{1,0:T(8,128)S(1)}, u32[]{:S(2)}, u32[]{:S(2)}) collective-permute-start(f32[768,384]{1,0:T(8,128)} %bitcast.30), channel_id=1, source_target_pairs={{0,8},{8,0},{1,9},{9,1},{2,10},{10,2},{3,11},{11,3},{4,12},{12,4},... | collective-permute-start | bytes 3538952 | tf_op jit(solution)/shard_map/ppermute | solution.py:209
  41.1 18.3 %collective-permute-start.2 = (f32[768,384]{1,0:T(8,128)S(1)}, f32[768,384]{1,0:T(8,128)S(1)}, u32[]{:S(2)}, u32[]{:S(2)}) collective-permute-start(f32[768,384]{1,0:T(8,128)S(1)} %collective-permute-done.rest_0_), channel_id=1, source_target_pairs={{0,16},{8,56},{16,32},{24,8},{32,48},{40,24},{48,0},{56,40},{1,17}... | collective-permute-start | bytes 3538952 | tf_op jit(solution)/shard_map/ppermute | solution.py:203
  43.0 18.6 %collective-permute-start.1 = (f32[768,384]{1,0:T(8,128)S(1)}, f32[768,384]{1,0:T(8,128)S(1)}, u32[]{:S(2)}, u32[]{:S(2)}) collective-permute-start(f32[768,384]{1,0:T(8,128)S(1)} %collective-permute-done.rest_0_), channel_id=1, source_target_pairs={{0,8},{8,0},{1,9},{9,1},{2,10},{10,2},{3,11},{11,3},{4,12},{12,4},... | collective-permute-start | bytes 3538952 | tf_op jit(solution)/shard_map/ppermute | solution.py:202
  44.9 19.5 %collective-permute-start.8 = (f32[768,384]{1,0:T(8,128)}, f32[768,384]{1,0:T(8,128)}, u32[]{:S(2)}, u32[]{:S(2)}) collective-permute-start(f32[768,384]{1,0:T(8,128)} %bitcast.31), channel_id=1, source_target_pairs={{0,64},{8,200},{64,128},{72,8},{128,192},{136,72},{192,0},{200,136... | collective-permute-start | bytes 3538952 | tf_op jit(solution)/shard_map/ppermute | solution.py:210
  49.8 26.0 %collective-permute-start.11 = (f32[768,384]{1,0:T(8,128)S(1)}, f32[768,384]{1,0:T(8,128)}, u32[]{:S(2)}, u32[]{:S(2)}) collective-permute-start(f32[768,384]{1,0:T(8,128)S(1)} %collective-permute-done.10), channel_id=1, source_target_pairs={{0,64},{8,200},{64,128},{72,8},{128,192},{136,72},{192,0},{200,136... | collective-permute-start | bytes 3538952 | tf_op jit(solution)/shard_map/ppermute | solution.py:211
  59.3 20.3 %collective-permute-start.4 = (f32[768,384]{1,0:T(8,128)S(1)}, f32[768,384]{1,0:T(8,128)}, u32[]{:S(2)}, u32[]{:S(2)}) collective-permute-start(f32[768,384]{1,0:T(8,128)S(1)} %collective-permute-done.2.rest_2_), channel_id=1, source_target_pairs={{0,16},{8,56},{16,32},{24,8},{32,48},{40,24},{48,0},{56,40},{1,17}... | collective-permute-start | bytes 3538952 | tf_op jit(solution)/shard_map/ppermute | solution.py:205
  61.5 27.8 %collective-permute-start.3 = (f32[768,384]{1,0:T(8,128)S(1)}, f32[768,384]{1,0:T(8,128)}, u32[]{:S(2)}, u32[]{:S(2)}) collective-permute-start(f32[768,384]{1,0:T(8,128)S(1)} %collective-permute-done.1.rest_1_), channel_id=1, source_target_pairs={{0,16},{8,56},{16,32},{24,8},{32,48},{40,24},{48,0},{56,40},{1,17}... | collective-permute-start | bytes 3538952 | tf_op jit(solution)/shard_map/ppermute | solution.py:204
  64.4 36.8 %collective-permute-start.9 = (f32[768,384]{1,0:T(8,128)}, f32[768,384]{1,0:T(8,128)}, u32[]{:S(2)}, u32[]{:S(2)}) collective-permute-start(f32[768,384]{1,0:T(8,128)} %collective-permute-done.8.rest_9_), channel_id=1, source_target_pairs={{0,64},{8,200},{64,128},{72,8},{128,192},{136,72},{192,0},{200,136... | collective-permute-start | bytes 3538952 | tf_op jit(solution)/shard_map/ppermute | solution.py:212
  68.5 32.7 %collective-permute-start.5 = (f32[768,384]{1,0:T(8,128)S(1)}, f32[768,384]{1,0:T(8,128)}, u32[]{:S(2)}, u32[]{:S(2)}) collective-permute-start(f32[768,384]{1,0:T(8,128)S(1)} %collective-permute-done.2.rest_2_), channel_id=1, source_target_pairs={{0,8},{8,0},{1,9},{9,1},{2,10},{10,2},{3,11},{11,3},{4,12},{12,4},... | collective-permute-start | bytes 3538952 | tf_op jit(solution)/shard_map/ppermute | solution.py:207
  75.7 25.5 %collective-permute-start.12 = (f32[768,384]{1,0:T(8,128)}, f32[768,384]{1,0:T(8,128)}, u32[]{:S(2)}, u32[]{:S(2)}) collective-permute-start(f32[768,384]{1,0:T(8,128)} %collective-permute-done.11), channel_id=1, source_target_pairs={{0,8},{8,0},{1,9},{9,1},{2,10},{10,2},{3,11},{11,3},{4,12},{12,4},... | collective-permute-start | bytes 3538952 | tf_op jit(solution)/shard_map/ppermute | solution.py:213
  79.6 21.6 %collective-permute-start.7 = (f32[768,384]{1,0:T(8,128)}, f32[768,384]{1,0:T(8,128)}, u32[]{:S(2)}, u32[]{:S(2)}) collective-permute-start(f32[768,384]{1,0:T(8,128)} %collective-permute-done.4.rest_4_), channel_id=1, source_target_pairs={{0,8},{8,0},{1,9},{9,1},{2,10},{10,2},{3,11},{11,3},{4,12},{12,4},... | collective-permute-start | bytes 3538952 | tf_op jit(solution)/shard_map/ppermute | solution.py:207
  89.3 11.9 %collective-permute-start.6 = (f32[768,384]{1,0:T(8,128)}, f32[768,384]{1,0:T(8,128)}, u32[]{:S(2)}, u32[]{:S(2)}) collective-permute-start(f32[768,384]{1,0:T(8,128)} %collective-permute-done.3.rest_3_), channel_id=1, source_target_pairs={{0,8},{8,0},{1,9},{9,1},{2,10},{10,2},{3,11},{11,3},{4,12},{12,4},... | collective-permute-start | bytes 3538952 | tf_op jit(solution)/shard_map/ppermute | solution.py:207
  101.2 1.3 copy-start.8
  102.5 0.9 copy-start.9
  112.6 2.9 %copy-start.2 = (bf16[12,768,384]{2,1,0:T(8,128)(2,1)}, bf16[12,768,384]{2,1,0:T(8,128)(2,1)S(1)}, u32[]{:S(2)}) copy-start(bf16[12,768,384]{2,1,0:T(8,128)(2,1)S(1)} %get-tuple-element.12.high_ref) | copy-start | bytes 21233668
  115.5 2.9 %copy-start.5 = (bf16[12,768,384]{2,1,0:T(8,128)(2,1)}, bf16[12,768,384]{2,1,0:T(8,128)(2,1)S(1)}, u32[]{:S(2)}) copy-start(bf16[12,768,384]{2,1,0:T(8,128)(2,1)S(1)} %get-tuple-element.13.low_ref) | copy-start | bytes 21233668
  121.4 3.4 %copy-start = (f32[16384,128]{1,0:T(8,128)S(1)}, f32[16384,128]{1,0:T(8,128)}, u32[]{:S(2)}) copy-start(f32[16384,128]{1,0:T(8,128)} %all-gather.3.cloned.1.call-done) | copy-start | bytes 25165828
  124.7 3.0 %copy-start.3 = (bf16[12,768,384]{2,1,0:T(8,128)(2,1)S(1)}, bf16[12,768,384]{2,1,0:T(8,128)(2,1)}, u32[]{:S(2)}) copy-start(bf16[12,768,384]{2,1,0:T(8,128)(2,1)} %copy-done.2) | copy-start | bytes 21233668
  127.7 3.0 %copy-start.6 = (bf16[12,768,384]{2,1,0:T(8,128)(2,1)S(1)}, bf16[12,768,384]{2,1,0:T(8,128)(2,1)}, u32[]{:S(2)}) copy-start(bf16[12,768,384]{2,1,0:T(8,128)(2,1)} %copy-done.5) | copy-start | bytes 21233668
  135.7 21.6 %collective-permute-start.13 = (f32[768,384]{1,0:T(8,128)S(1)}, f32[768,384]{1,0:T(8,128)S(1)}, u32[]{:S(2)}, u32[]{:S(2)}) collective-permute-start(f32[768,384]{1,0:T(8,128)S(1)} %get-tuple-element.16), channel_id=1, source_target_pairs={{0,64},{8,200},{64,128},{72,8},{128,192},{136,72},{192,0},{200,136... | collective-permute-start | bytes 3538952 | tf_op jit(solution)/shard_map/ppermute | solution.py:244
  145.0 58.6 %collective-permute-start.15 = (f32[768,384]{1,0:T(8,128)S(1)}, f32[768,384]{1,0:T(8,128)}, u32[]{:S(2)}, u32[]{:S(2)}) collective-permute-start(f32[768,384]{1,0:T(8,128)S(1)} %get-tuple-element.17), channel_id=1, source_target_pairs={{0,192},{8,72},{64,0},{72,136},{128,64},{136,200},{192,128},{200,8... | collective-permute-start | bytes 3538952 | tf_op jit(solution)/shard_map/ppermute | solution.py:246
  158.4 45.2 %collective-permute-start.14 = (f32[768,384]{1,0:T(8,128)}, f32[768,384]{1,0:T(8,128)}, u32[]{:S(2)}, u32[]{:S(2)}) collective-permute-start(f32[768,384]{1,0:T(8,128)} %add.126), channel_id=1, source_target_pairs={{0,64},{8,200},{64,128},{72,8},{128,192},{136,72},{192,0},{200,136... | collective-permute-start | bytes 3538952 | tf_op jit(solution)/shard_map/ppermute | solution.py:248
  164.0 3.4 %copy-start.1 = (f32[16384,128]{1,0:T(8,128)S(1)}, f32[16384,128]{1,0:T(8,128)}, u32[]{:S(2)}) copy-start(f32[16384,128]{1,0:T(8,128)} %all-gather.3.cloned.1.call-done) | copy-start | bytes 25165828
  167.4 3.0 %copy-start.4 = (bf16[12,768,384]{2,1,0:T(8,128)(2,1)S(1)}, bf16[12,768,384]{2,1,0:T(8,128)(2,1)}, u32[]{:S(2)}) copy-start(bf16[12,768,384]{2,1,0:T(8,128)(2,1)} %copy-done.2) | copy-start | bytes 21233668
  170.4 3.0 %copy-start.7 = (bf16[12,768,384]{2,1,0:T(8,128)(2,1)S(1)}, bf16[12,768,384]{2,1,0:T(8,128)(2,1)}, u32[]{:S(2)}) copy-start(bf16[12,768,384]{2,1,0:T(8,128)(2,1)} %copy-done.5) | copy-start | bytes 21233668
  173.4 29.6 %copy-start.10 = (f32[1,384]{1,0:T(1,128)S(1)}, f32[1,384]{1,0:T(1,128)}, u32[]{:S(2)}) copy-start(f32[1,384]{1,0:T(1,128)} %param.10) | copy-start | bytes 4612
  191.1 11.8 %collective-permute-start.16 = (f32[1,384]{1,0:T(1,128)S(1)}, f32[1,384]{1,0:T(1,128)S(1)}, u32[]{:S(2)}, u32[]{:S(2)}) collective-permute-start(f32[1,384]{1,0:T(1,128)S(1)} %get-tuple-element.29), channel_id=1, source_target_pairs={{0,64},{64,128},{128,192},{192,0},{1,65},{65,129},{129,193},{193,1... | collective-permute-start | bytes 4616 | tf_op jit(solution)/shard_map/ppermute | solution.py:270
  195.2 7.7 %collective-permute-start.17 = (f32[1,384]{1,0:T(1,128)S(1)}, f32[1,384]{1,0:T(1,128)S(1)}, u32[]{:S(2)}, u32[]{:S(2)}) collective-permute-start(f32[1,384]{1,0:T(1,128)S(1)} %get-tuple-element.31), channel_id=1, source_target_pairs={{0,128},{64,192},{128,0},{192,64},{1,129},{65,193},{129,1},{193,65... | collective-permute-start | bytes 4616 | tf_op jit(solution)/shard_map/ppermute | solution.py:270
  198.1 4.8 %collective-permute-start.18 = (f32[1,384]{1,0:T(1,128)S(1)}, f32[1,384]{1,0:T(1,128)S(1)}, u32[]{:S(2)}, u32[]{:S(2)}) collective-permute-start(f32[1,384]{1,0:T(1,128)S(1)} %get-tuple-element.30), channel_id=1, source_target_pairs={{0,192},{64,0},{128,64},{192,128},{1,193},{65,1},{129,65},{193,129... | collective-permute-start | bytes 4616 | tf_op jit(solution)/shard_map/ppermute | solution.py:270
Sparse Core Ops, SparseCore 0:
  10.1 111.2 all-gather.2

commit v6 on v5

v6 whole, which is shorter than its diff:
```python
import functools

import jax
import jax.numpy as jnp
from jax import lax
from jax.experimental import pallas as pl
from jax.experimental.pallas import tpu as pltpu
from jax.sharding import Mesh, PartitionSpec as P

BLOCK = 128
PART = 256
SLOTS = 4
VMEM_BYTES = 24 * 1024 * 1024
CORES = [(0, 1), (1, 0)]
SPREAD_X = (
    (3, 1, 0, 0),
    (0, 3, 0, 1),
    (1, 2, 0, 1),
    (2, 0, 1, 1),
    (2, 2, 1, 3),
    (3, 1, 2, 2),
    (3, 0, 2, 3),
    (3, 2, 3, 0),
)


def shift(size, step):
    return [(i, (i + step) % size) for i in range(size)]


def opposite(size, way=1):
    return [
        (2 * i + c, (i + way * (1 - 2 * c)) % size * 2 + c) for i in range(size) for c in range(2)
    ]


def spread_plan():
    pairs, holds, taken = [], {}, {}
    for y in range(4):
        for r in range(8):
            to = (SPREAD_X[r][y], r % 4)
            core = taken.get(to, 0)
            taken[to] = core + 1
            pairs.append(((y * 4 + r // 2) * 2 + r % 2, (to[1] * 4 + to[0]) * 2 + core))
            holds[(to[1], to[0], core)] = (r // 4, y)
    return pairs, holds


def piece_plan(holds):
    halves, found = [], []
    for y in range(4):
        for x in range(4):
            for c in range(2):
                d = 2 * c - 1
                at = [
                    (x, c),
                    (x, 1 - c),
                    (x + d, c),
                    (x + d, 1 - c),
                    (x + 2, c),
                    (x - d, 1 - c),
                    (x - d, c),
                    (x + 2, 1 - c),
                ]
                has = [holds[(y, px % 4, pc)] for px, pc in at]
                halves.append([h * 4 + k for h, k in has])
                found.append([[has.index((0, k)), has.index((1, k))] for k in range(4)])
    return [jnp.array(v, jnp.int32) for v in (halves, found)]


def spread_kernel(start_row, rows_ref, *rest):
    pieces = rest[:8]
    high_hbm, low_hbm, z_f, z_h, z_l, in_sem, out_sem = rest[8:]
    slots, rows = z_f.shape[:2]

    def fetch(i):
        return pltpu.make_async_copy(pieces[i], z_f.at[i % slots], in_sem.at[i])

    def store(i):
        return [
            pltpu.make_async_copy(z_h.at[i % slots], high_hbm.at[i], out_sem.at[2 * i]),
            pltpu.make_async_copy(z_l.at[i % slots], low_hbm.at[i], out_sem.at[2 * i + 1]),
        ]

    for i in range(slots):
        fetch(i).start()
    row = lax.broadcasted_iota(jnp.int32, (BLOCK, BLOCK), 0)
    for at in range(len(pieces)):
        fetch(at).wait()
        if at >= slots:
            for copy in store(at - slots):
                copy.wait()

        def one(i, carry, at=at):
            here = pl.ds(pl.multiple_of(i * BLOCK, BLOCK), BLOCK)
            value = z_f[at % slots, here, :]
            high = value.astype(jnp.bfloat16)
            low = (value - high.astype(jnp.float32)).astype(jnp.bfloat16)
            place = rows_ref[pl.ds(start_row[at] + i, 1), :]
            place = jnp.where(place >= 0, place & (BLOCK - 1), -1)
            hot = (place == row).astype(jnp.float32).astype(jnp.bfloat16)
            z_h[at % slots, here, :] = jnp.dot(
                hot, high, preferred_element_type=jnp.float32
            ).astype(jnp.bfloat16)
            z_l[at % slots, here, :] = jnp.dot(
                hot, low, preferred_element_type=jnp.float32
            ).astype(jnp.bfloat16)
            return carry

        lax.fori_loop(0, rows // BLOCK, one, 0, unroll=3)
        for copy in store(at):
            copy.start()
        if at + slots < len(pieces):
            fetch(at + slots).start()
    for at in range(len(pieces) - slots, len(pieces)):
        for copy in store(at):
            copy.wait()


def spread(start_row, root_row, pieces):
    rows, cols = pieces[0].shape
    any_spec = pl.BlockSpec(memory_space=pl.ANY)
    shape = (len(pieces), rows, cols)
    held = (SLOTS, rows, cols)
    return pl.pallas_call(
        spread_kernel,
        out_shape=[jax.ShapeDtypeStruct(shape, jnp.bfloat16)] * 2,
        in_specs=[
            pl.BlockSpec(memory_space=pltpu.SMEM),
            pl.BlockSpec(memory_space=pltpu.VMEM),
        ]
        + [any_spec] * len(pieces),
        out_specs=[any_spec] * 2,
        scratch_shapes=[
            pltpu.VMEM(held, jnp.float32),
            pltpu.VMEM(held, jnp.bfloat16),
            pltpu.VMEM(held, jnp.bfloat16),
            pltpu.SemaphoreType.DMA((len(pieces),)),
            pltpu.SemaphoreType.DMA((2 * len(pieces),)),
        ],
        compiler_params=pltpu.CompilerParams(vmem_limit_bytes=VMEM_BYTES),
        cost_estimate=pl.CostEstimate(
            flops=8 * 4 * rows * BLOCK * cols, bytes_accessed=64 * rows * cols, transcendentals=0
        ),
    )(start_row, root_row, *pieces)


def product_kernel(call, table, root_hbm, high_hbm, low_hbm, out, a_f, z_h, z_l, a_sem, z_sem):
    rows = out.shape[0]
    per_range = rows // BLOCK
    per_part = PART // BLOCK
    parts = rows // PART
    c = table[call, 3 * per_range + 2]

    def factor_copies(source, target, first):
        return [
            pltpu.make_async_copy(
                source.at[table[c, 3 * per_range + side]],
                target.at[pl.ds(side * rows, rows)],
                z_sem.at[first + side],
            )
            for side in range(2)
        ]

    def start_root(part):
        for m in range(per_part):
            mb = pl.multiple_of(table[c, part * per_part + m] * BLOCK, BLOCK)
            pltpu.make_async_copy(
                root_hbm.at[:, pl.ds(mb, BLOCK)],
                a_f.at[part, :, pl.ds(m * BLOCK, BLOCK)],
                a_sem.at[part],
            ).start()

    highs_in = factor_copies(high_hbm, z_h, 0)
    lows_in = factor_copies(low_hbm, z_l, 2)
    start_root(0)
    for copy in highs_in + lows_in:
        copy.start()
    start_root(1)
    for part in range(parts):
        pltpu.make_async_copy(a_f.at[part], a_f.at[part], a_sem.at[part]).wait()
        if part == 0:
            for copy in highs_in:
                copy.wait()
        if part + 2 < parts:
            start_root(part + 2)
        highs, lows = [], []
        for k in range(2 * per_range):
            value = a_f[part, table[c, per_range + k]]
            high = value.astype(jnp.bfloat16)
            highs.append(high)
            lows.append((value - high.astype(jnp.float32)).astype(jnp.bfloat16))
        high = jnp.concatenate(highs, axis=1)
        low = jnp.concatenate(lows, axis=1)
        value = jnp.dot(high, z_h[...], preferred_element_type=jnp.float32)
        value = value + jnp.dot(low, z_h[...], preferred_element_type=jnp.float32)
        if part == 0:
            for copy in lows_in:
                copy.wait()
        value = value + jnp.dot(high, z_l[...], preferred_element_type=jnp.float32)
        out[part * PART : (part + 1) * PART, :] = value


def product(call, table, root, high, low):
    rows, cols = high.shape[1:]
    any_spec = pl.BlockSpec(memory_space=pl.ANY)
    root, high, low = [pltpu.with_memory_space_constraint(v, pltpu.HBM) for v in (root, high, low)]
    return pl.pallas_call(
        functools.partial(product_kernel, call),
        out_shape=jax.ShapeDtypeStruct((rows, cols), jnp.float32),
        in_specs=[pl.BlockSpec(memory_space=pltpu.SMEM)] + [any_spec] * 3,
        out_specs=pl.BlockSpec(memory_space=pltpu.VMEM),
        scratch_shapes=[
            pltpu.VMEM((rows // PART, root.shape[0], PART, BLOCK), jnp.float32),
            pltpu.VMEM((2 * rows, cols), jnp.bfloat16),
            pltpu.VMEM((2 * rows, cols), jnp.bfloat16),
            pltpu.SemaphoreType.DMA((rows // PART,)),
            pltpu.SemaphoreType.DMA((4,)),
        ],
        compiler_params=pltpu.CompilerParams(vmem_limit_bytes=VMEM_BYTES),
        cost_estimate=pl.CostEstimate(
            flops=3 * 2 * rows * 2 * rows * cols, bytes_accessed=12 * rows * rows, transcendentals=0
        ),
    )(table, root, high, low)


def per_device(root_inverse, root_row, coupling, pivot_variance):
    zh = lax.axis_index("zh")
    y = lax.axis_index("y")
    x = lax.axis_index("x")
    core = lax.axis_index("core")
    rows, cols = coupling.shape[1:]
    ranges = root_row.shape[1] // rows
    per_range = rows // BLOCK
    own_range = 2 * x + core
    device = (y * 4 + x) * 2 + core

    root = lax.all_gather(root_inverse, ("zh", "zl"), axis=0, tiled=False)

    pairs, holds = spread_plan()
    own = lax.ppermute(coupling[0], ("y", "x", "core"), pairs)
    along_x = opposite(4)
    beside = lax.ppermute(own, "core", CORES)
    near = lax.ppermute(own, ("x", "core"), along_x)
    near_beside = lax.ppermute(beside, ("x", "core"), along_x)
    far = lax.ppermute(near, ("x", "core"), along_x)
    pieces = [own, beside, near, near_beside, far]
    pieces += [lax.ppermute(p, "core", CORES) for p in (near, near_beside, far)]

    halves, found = piece_plan(holds)
    spots = lax.dynamic_slice(halves, (device, 0), (1, 8))[0]
    start_row = ((zh * 4 + (spots & 3)) * ranges + y + 4 * (spots >> 2)) * per_range
    high, low = spread(start_row, root_row.reshape(-1, BLOCK), pieces)

    block = (root_row[:, ::BLOCK] >> 7).reshape(-1, ranges, per_range)

    def blocks_of(r):
        return lax.dynamic_slice(block, (zh * 4, r, 0), (4, 1, per_range))[:, 0] & 7

    order = (y + jnp.stack([2, 3 - 2 * core, 1 + 2 * core, 0])) & 3
    table = jnp.concatenate(
        [
            blocks_of(own_range),
            blocks_of(y),
            blocks_of(y + 4) + 8,
            lax.dynamic_slice(found, (device, 0, 0), (1, 4, 2))[0],
            order[:, None],
        ],
        axis=1,
    ).astype(jnp.int32)

    root = root.reshape(-1, *root_inverse.shape)
    far = product(0, table, root, high, low)
    passed = lax.ppermute(far, ("y", "core"), opposite(4))
    first = product(1, table, root, high, low)
    back = lax.ppermute(first, ("y", "core"), opposite(4, -1))
    second = product(2, table, root, high, low)
    forth = lax.ppermute(second + passed, ("y", "core"), opposite(4))
    home = product(3, table, root, high, low)
    summed = home + forth + back

    own_place = lax.dynamic_slice(root_row, (zh * 4 + y, own_range * rows), (1, rows))[0]
    own_place = jnp.where(own_place >= 0, own_place & (BLOCK - 1), -1).reshape(per_range, BLOCK)
    hot = (own_place[:, :, None] == jnp.arange(BLOCK, dtype=jnp.int32)).astype(jnp.float32)
    result = -jnp.einsum(
        "iuo,ion->iun", hot, summed.reshape(per_range, BLOCK, cols), precision=lax.Precision.HIGHEST
    )

    result = result.reshape(1, rows, cols)
    sums = jnp.sum(coupling * result, axis=1)
    sums = lax.all_to_all(
        jnp.broadcast_to(sums, (8, cols)), ("x", "core"), split_axis=0, concat_axis=0, tiled=True
    )
    return result, pivot_variance - jnp.sum(sums, axis=0, keepdims=True)


def solution(mesh):
    split = Mesh(mesh.devices.reshape(2, 4, 4, 2, 8), ("zh", "y", "x", "core", "zl"))
    leaf, row, col = ("zh", "y"), ("x", "core"), "zl"
    return jax.shard_map(
        per_device,
        mesh=split,
        in_specs=(P(row, ("zh", "y", "zl")), P(), P(leaf, row, col), P(leaf, col)),
        out_specs=(P(leaf, row, col), P(leaf, col)),
        check_vma=False,
    )
```

time: 216 us -> 194 us (0.90)
  starting transfers between devices: 64.3 us -> 33.5 us
  waiting for transfers between devices: 52.3 us -> 80.3 us
  local copies, waits for them, and re-layouts: 33 us -> 11.6 us
  Pallas kernels: 28.8 us -> 35.8 us
    ppermute x8 -> x0, starting transfers between devices: 31.8 us -> none  [the longest x3 10.9 us: per_device(): marginal = marginal + lax.ppermute(sums[step:step + 1], 'y', shift(4, step))]
    unnamed x22 -> x12, local copies, waits for them, and re-layouts: 26.8 us -> 6.02 us
    psum x1 -> x0, blocking collectives: 12.7 us -> none  [per_device(): sums = lax.psum(jnp.sum(sums, axis=1), ('x', 'core'))]
    all_to_all x0 -> x1, blocking collectives: none -> 11.2 us  [per_device(): lax.all_to_all(jnp.broadcast_to(sums, (8, cols)), ('x', 'core'), split_ax...]
    ppermute x1, waiting for transfers between devices: 0.01 us -> 10.4 us  [per_device(): far = lax.ppermute(near, ('x', 'core'), along_x)]
    ppermute x1, waiting for transfers between devices: 0.01 us -> 7.27 us  [per_device(): forth = lax.ppermute(second + passed, ('y', 'core'), opposite(4))]
    pallas_call x5, Pallas kernels: 28.8 us -> 35.8 us  [the longest x4 27.4 us: product(): pl.pallas_call(functools.partial(product_kernel, call), out_shape=jax.Sha...]
    ppermute x1, waiting for transfers between devices: 7.64 us -> 14.4 us  [per_device(): near = lax.ppermute(own, ('x', 'core'), along_x)]
  transfers between devices with their start and end apart: 20 -> 12, of which waited for: 6 -> 7; matrix products, arithmetic and copies ran while one was open for 5% -> 5% of each run, Pallas kernels for 11% -> 15%
where the time goes in v6:
time: 194 us; the launch traced here: 193 us
  waiting for transfers between devices  80.3 us (41%)
  Pallas kernels  35.8 us (18%)
  starting transfers between devices  33.5 us (17%)
  between operations  14.3 us (7%)
  local copies, waits for them, and re-layouts  11.6 us (6%)
  blocking collectives  11.2 us (6%)
  other arithmetic  5.46 us (3%)
    ppermute x1, waiting for transfers between devices, per_device(): own = lax.ppermute(coupling[0], ('y', 'x', 'core'), pairs)  28.6 us
    pallas_call x4, Pallas kernels, product(): pl.pallas_call(functools.partial(product_kernel, call), out_shape=jax.Sha...  27.4 us
    ppermute x1, waiting for transfers between devices, per_device(): near = lax.ppermute(own, ('x', 'core'), along_x)  14.4 us
    all_to_all x1, blocking collectives, per_device(): lax.all_to_all(jnp.broadcast_to(sums, (8, cols)), ('x', 'core'), split_ax...  11.2 us
    ppermute x1, waiting for transfers between devices, per_device(): far = lax.ppermute(near, ('x', 'core'), along_x)  10.4 us
    ppermute x1, waiting for transfers between devices, per_device(): near_beside = lax.ppermute(beside, ('x', 'core'), along_x)  9.29 us
    ppermute x3, starting transfers between devices, per_device(): pieces += [lax.ppermute(p, 'core', CORES) for p in (near, near_beside, far)]  8.61 us
    pallas_call x1, Pallas kernels, spread(): pl.pallas_call(spread_kernel, out_shape=[jax.ShapeDtypeStruct(shape, jnp....  8.41 us
  transfers between devices with their start and end apart: 12, of which 7 were waited for; matrix products, arithmetic and copies ran while one was open for 5% of the time, Pallas kernels for 15%

profile of v6, /device:TPU:1, one launch (start us, length us, event | category | flops | bytes accessed | tf_op | source)
XLA Modules:
  0.0 192.9 jit_solution(15325971063182100920)
XLA Ops:
  7.2 0.0 all-gather.3.cloned.1.call-start
  7.2 0.7 all-gather.3.cloned.1.call-update
  7.9 4.6 %collective-permute-start = (f32[768,384]{1,0:T(8,128)}, f32[768,384]{1,0:T(8,128)S(1)}, u32[]{:S(2)}, u32[]{:S(2)}) collective-permute-start(f32[768,384]{1,0:T(8,128)} %bitcast.24), channel_id=1, source_target_pairs={{0,48},{8,64},{16,144},{24,224},{32,32},{40,112},{48,176},{56,240}... | collective-permute-start | bytes 3538952 | tf_op jit(solution)/shard_map/ppermute | solution.py:241
  12.5 28.6 %collective-permute-done.rest_0_ = f32[768,384]{1,0:T(8,128)S(1)} collective-permute-done((f32[768,384]{1,0:T(8,128)}, f32[768,384]{1,0:T(8,128)S(1)}, u32[]{:S(2)}, u32[]{:S(2)}) %collective-permute-start) | collective-permute-done | bytes 1179680 | tf_op jit(solution)/shard_map/ppermute | solution.py:241
  41.1 1.9 collective-permute-start.2
  43.0 1.9 collective-permute-start.1
  44.9 14.4 %collective-permute-done.2.rest_2_ = f32[768,384]{1,0:T(8,128)S(1)} collective-permute-done((f32[768,384]{1,0:T(8,128)S(1)}, f32[768,384]{1,0:T(8,128)S(1)}, u32[]{:S(2)}, u32[]{:S(2)}) %collective-permute-start.2) | collective-permute-done | bytes 1179680 | tf_op jit(solution)/shard_map/ppermute | solution.py:244
  59.3 2.2 %collective-permute-start.4 = (f32[768,384]{1,0:T(8,128)S(1)}, f32[768,384]{1,0:T(8,128)}, u32[]{:S(2)}, u32[]{:S(2)}) collective-permute-start(f32[768,384]{1,0:T(8,128)S(1)} %collective-permute-done.2.rest_2_), channel_id=1, source_target_pairs={{0,16},{8,56},{16,32},{24,8},{32,48},{40,24},{48,0},{56,40},{1,17}... | collective-permute-start | bytes 3538952 | tf_op jit(solution)/shard_map/ppermute | solution.py:246
  61.5 0.0 collective-permute-done.1.rest_1_
  61.5 2.8 %collective-permute-start.3 = (f32[768,384]{1,0:T(8,128)S(1)}, f32[768,384]{1,0:T(8,128)}, u32[]{:S(2)}, u32[]{:S(2)}) collective-permute-start(f32[768,384]{1,0:T(8,128)S(1)} %collective-permute-done.1.rest_1_), channel_id=1, source_target_pairs={{0,16},{8,56},{16,32},{24,8},{32,48},{40,24},{48,0},{56,40},{1,17}... | collective-permute-start | bytes 3538952 | tf_op jit(solution)/shard_map/ppermute | solution.py:245
  64.4 1.9 collective-permute-start.5
  66.3 10.4 %collective-permute-done.4.rest_4_ = f32[768,384]{1,0:T(8,128)} collective-permute-done((f32[768,384]{1,0:T(8,128)S(1)}, f32[768,384]{1,0:T(8,128)}, u32[]{:S(2)}, u32[]{:S(2)}) %collective-permute-start.4) | collective-permute-done | bytes 1179680 | tf_op jit(solution)/shard_map/ppermute | solution.py:246
  76.7 3.3 %collective-permute-start.7 = (f32[768,384]{1,0:T(8,128)}, f32[768,384]{1,0:T(8,128)}, u32[]{:S(2)}, u32[]{:S(2)}) collective-permute-start(f32[768,384]{1,0:T(8,128)} %collective-permute-done.4.rest_4_), channel_id=1, source_target_pairs={{0,8},{8,0},{1,9},{9,1},{2,10},{10,2},{3,11},{11,3},{4,12},{12,4},... | collective-permute-start | bytes 3538952 | tf_op jit(solution)/shard_map/ppermute | solution.py:248
  80.0 9.3 %collective-permute-done.3.rest_3_ = f32[768,384]{1,0:T(8,128)} collective-permute-done((f32[768,384]{1,0:T(8,128)S(1)}, f32[768,384]{1,0:T(8,128)}, u32[]{:S(2)}, u32[]{:S(2)}) %collective-permute-start.3) | collective-permute-done | bytes 1179680 | tf_op jit(solution)/shard_map/ppermute | solution.py:245
  89.3 3.3 %collective-permute-start.6 = (f32[768,384]{1,0:T(8,128)}, f32[768,384]{1,0:T(8,128)}, u32[]{:S(2)}, u32[]{:S(2)}) collective-permute-start(f32[768,384]{1,0:T(8,128)} %collective-permute-done.3.rest_3_), channel_id=1, source_target_pairs={{0,8},{8,0},{1,9},{9,1},{2,10},{10,2},{3,11},{11,3},{4,12},{12,4},... | collective-permute-start | bytes 3538952 | tf_op jit(solution)/shard_map/ppermute | solution.py:248
  92.7 1.0 slice.3
  93.7 1.6 reshape.114.rows_ref
  95.4 0.7 reshape.113
  96.0 0.7 fusion.2
  96.7 0.7 copy.18
  97.4 0.1 pad_add_fusion
  97.5 0.1 copy.17
  97.6 0.8 and_add_fusion
  98.4 0.6 add_and_fusion
  99.0 0.8 concatenate.10.table
  99.8 0.7 multiply_bitcast_fusion.start_row
  100.5 0.0 collective-permute-done.5.rest_5_
  100.5 0.0 collective-permute-done.7.rest_7_
  100.5 0.0 collective-permute-done.6.rest_6_
  100.5 0.0 copy-start.2
  100.5 0.9 copy-done.2
  101.4 8.4 %shard_map.77 = (bf16[8,768,384]{2,1,0:T(8,128)(2,1)S(1)}, bf16[8,768,384]{2,1,0:T(8,128)(2,1)S(1)}) custom-call(s32[8]{0:T(128)S(1)} %multiply_bitcast_fusion.start_row, s32[384,128]{1,0:T(8,128)S(1)} %copy-done.2, f32[768,384]{1,0:T(8,128)S(1)} %collective-permute-done.rest_0_, f32[768,384]{1,0:T(8,128)S(1)} %collective-permute-done.1.rest_1_, ...), custom_call_target="tpu_custom_call" | custom-call | flops 1207959552 | bytes 18874368 | tf_op jit(solution)/shard_map/pallas_call | solution.py:125
  109.9 0.0 copy-start
  109.9 2.2 %copy-done = bf16[8,768,384]{2,1,0:T(8,128)(2,1)} copy-done((bf16[8,768,384]{2,1,0:T(8,128)(2,1)}, bf16[8,768,384]{2,1,0:T(8,128)(2,1)S(1)}, u32[]{:S(2)}) %copy-start) | copy-done | bytes 4718616
  112.0 0.0 copy-start.1
  112.1 2.1 %copy-done.1 = bf16[8,768,384]{2,1,0:T(8,128)(2,1)} copy-done((bf16[8,768,384]{2,1,0:T(8,128)(2,1)}, bf16[8,768,384]{2,1,0:T(8,128)(2,1)S(1)}, u32[]{:S(2)}) %copy-start.1) | copy-done | bytes 4718616
  114.2 7.2 %all-gather.3.cloned.1.call-done = f32[16384,128]{1,0:T(8,128)} async-done(((f32[1024,128]{1,0:T(8,128)}), f32[16384,128]{1,0:T(8,128)}) %all-gather.3.cloned.1.call-update) | async-done | bytes 8388624 | tf_op jit(solution)/shard_map/all_gather | solution.py:238
  121.4 6.9 %shard_map.80 = f32[768,384]{1,0:T(8,128)S(1)} custom-call(s32[4,21]{1,0:T(4,128)S(1)} %concatenate.10.table, f32[16,1024,128]{2,1,0:T(8,128)} %bitcast.17, bf16[8,768,384]{2,1,0:T(8,128)(2,1)} %copy-done, bf16[8,768,384]{2,1,0:T(8,128)(2,1)} %copy-done.1), custom_call_target="tpu_custom_call" | custom-call | flops 2717908992 | bytes 7077888 | tf_op jit(solution)/shard_map/pallas_call | solution.py:208
  128.2 4.5 %collective-permute-start.8 = (f32[768,384]{1,0:T(8,128)S(1)}, f32[768,384]{1,0:T(8,128)S(1)}, u32[]{:S(2)}, u32[]{:S(2)}) collective-permute-start(f32[768,384]{1,0:T(8,128)S(1)} %shard_map.80), channel_id=1, source_target_pairs={{0,64},{8,200},{64,128},{72,8},{128,192},{136,72},{192,0},{200,136... | collective-permute-start | bytes 3538952 | tf_op jit(solution)/shard_map/ppermute | solution.py:274
  132.8 6.9 %shard_map.81 = f32[768,384]{1,0:T(8,128)S(1)} custom-call(s32[4,21]{1,0:T(4,128)S(1)} %concatenate.10.table, f32[16,1024,128]{2,1,0:T(8,128)} %bitcast.18, bf16[8,768,384]{2,1,0:T(8,128)(2,1)} %copy-done, bf16[8,768,384]{2,1,0:T(8,128)(2,1)} %copy-done.1), custom_call_target="tpu_custom_call" | custom-call | flops 2717908992 | bytes 7077888 | tf_op jit(solution)/shard_map/pallas_call | solution.py:208
  139.6 1.9 collective-permute-start.10
  141.6 6.9 %shard_map.79 = f32[768,384]{1,0:T(8,128)S(1)} custom-call(s32[4,21]{1,0:T(4,128)S(1)} %concatenate.10.table, f32[16,1024,128]{2,1,0:T(8,128)} %bitcast.19, bf16[8,768,384]{2,1,0:T(8,128)(2,1)} %copy-done, bf16[8,768,384]{2,1,0:T(8,128)(2,1)} %copy-done.1), custom_call_target="tpu_custom_call" | custom-call | flops 2717908992 | bytes 7077888 | tf_op jit(solution)/shard_map/pallas_call | solution.py:208
  148.4 0.0 collective-permute-done.8
  148.4 0.1 add.110
  148.6 4.9 %collective-permute-start.9 = (f32[768,384]{1,0:T(8,128)S(1)}, f32[768,384]{1,0:T(8,128)S(1)}, u32[]{:S(2)}, u32[]{:S(2)}) collective-permute-start(f32[768,384]{1,0:T(8,128)S(1)} %add.110), channel_id=1, source_target_pairs={{0,64},{8,200},{64,128},{72,8},{128,192},{136,72},{192,0},{200,136... | collective-permute-start | bytes 3538952 | tf_op jit(solution)/shard_map/ppermute | solution.py:278
  153.5 0.8 fusion.1
  154.3 6.9 %shard_map.78 = f32[768,384]{1,0:T(8,128)S(1)} custom-call(s32[4,21]{1,0:T(4,128)S(1)} %concatenate.10.table, f32[16,1024,128]{2,1,0:T(8,128)} %bitcast.20, bf16[8,768,384]{2,1,0:T(8,128)(2,1)} %copy-done, bf16[8,768,384]{2,1,0:T(8,128)(2,1)} %copy-done.1), custom_call_target="tpu_custom_call" | custom-call | flops 2717908992 | bytes 7077888 | tf_op jit(solution)/shard_map/pallas_call | solution.py:208
  161.2 2.5 %collective-permute-done.10 = f32[768,384]{1,0:T(8,128)} collective-permute-done((f32[768,384]{1,0:T(8,128)S(1)}, f32[768,384]{1,0:T(8,128)}, u32[]{:S(2)}, u32[]{:S(2)}) %collective-permute-start.10) | collective-permute-done | bytes 1179680 | tf_op jit(solution)/shard_map/ppermute | solution.py:276
  163.7 7.3 %collective-permute-done.9 = f32[768,384]{1,0:T(8,128)S(1)} collective-permute-done((f32[768,384]{1,0:T(8,128)S(1)}, f32[768,384]{1,0:T(8,128)S(1)}, u32[]{:S(2)}, u32[]{:S(2)}) %collective-permute-start.9) | collective-permute-done | bytes 1179680 | tf_op jit(solution)/shard_map/ppermute | solution.py:278
  171.0 1.5 add_add_fusion
  172.5 0.0 copy-start.4
  172.5 0.7 convolution_negate_fusion
  173.3 0.0 copy-start.3
  173.3 0.5 copy-done.4
  173.8 0.0 copy-start.5
  173.8 0.2 multiply_reduce_fusion
  174.0 0.3 copy-done.3
  174.3 11.2 %all_to_all.6 = f32[8,1,384]{2,1,0:T(1,128)S(1)} all-to-all(f32[8,1,384]{2,1,0:T(1,128)S(1)} %broadcast_in_dim.15), channel_id=1, replica_groups=mesh['zh'=2,'y'=4,'x'=4,'core'=2,'zl'=8] {'x','core'}, dimensions={0} | all-to-all | bytes 24576 | tf_op jit(solution)/shard_map/all_to_all | solution.py:291
  185.5 0.0 copy-done.5
  185.5 0.6 reshape_subtract_fusion
  (3 shorter events, 0.0 us)
Async XLA Ops:
  7.2 114.2 %all-gather.3.cloned.1.call-start = ((), (), s32[]{:S(2)}) async-start(), calls=%async_computation.1 | async-start | bytes 8912896 | tf_op jit(solution)/shard_map/all_gather | solution.py:238
  7.9 33.2 %collective-permute-start = (f32[768,384]{1,0:T(8,128)}, f32[768,384]{1,0:T(8,128)S(1)}, u32[]{:S(2)}, u32[]{:S(2)}) collective-permute-start(f32[768,384]{1,0:T(8,128)} %bitcast.24), channel_id=1, source_target_pairs={{0,48},{8,64},{16,144},{24,224},{32,32},{40,112},{48,176},{56,240}... | collective-permute-start | bytes 3538952 | tf_op jit(solution)/shard_map/ppermute | solution.py:241
  41.1 18.3 %collective-permute-start.2 = (f32[768,384]{1,0:T(8,128)S(1)}, f32[768,384]{1,0:T(8,128)S(1)}, u32[]{:S(2)}, u32[]{:S(2)}) collective-permute-start(f32[768,384]{1,0:T(8,128)S(1)} %collective-permute-done.rest_0_), channel_id=1, source_target_pairs={{0,16},{8,56},{16,32},{24,8},{32,48},{40,24},{48,0},{56,40},{1,17}... | collective-permute-start | bytes 3538952 | tf_op jit(solution)/shard_map/ppermute | solution.py:244
  43.0 18.6 %collective-permute-start.1 = (f32[768,384]{1,0:T(8,128)S(1)}, f32[768,384]{1,0:T(8,128)S(1)}, u32[]{:S(2)}, u32[]{:S(2)}) collective-permute-start(f32[768,384]{1,0:T(8,128)S(1)} %collective-permute-done.rest_0_), channel_id=1, source_target_pairs={{0,8},{8,0},{1,9},{9,1},{2,10},{10,2},{3,11},{11,3},{4,12},{12,4},... | collective-permute-start | bytes 3538952 | tf_op jit(solution)/shard_map/ppermute | solution.py:243
  59.3 17.3 %collective-permute-start.4 = (f32[768,384]{1,0:T(8,128)S(1)}, f32[768,384]{1,0:T(8,128)}, u32[]{:S(2)}, u32[]{:S(2)}) collective-permute-start(f32[768,384]{1,0:T(8,128)S(1)} %collective-permute-done.2.rest_2_), channel_id=1, source_target_pairs={{0,16},{8,56},{16,32},{24,8},{32,48},{40,24},{48,0},{56,40},{1,17}... | collective-permute-start | bytes 3538952 | tf_op jit(solution)/shard_map/ppermute | solution.py:246
  61.5 27.8 %collective-permute-start.3 = (f32[768,384]{1,0:T(8,128)S(1)}, f32[768,384]{1,0:T(8,128)}, u32[]{:S(2)}, u32[]{:S(2)}) collective-permute-start(f32[768,384]{1,0:T(8,128)S(1)} %collective-permute-done.1.rest_1_), channel_id=1, source_target_pairs={{0,16},{8,56},{16,32},{24,8},{32,48},{40,24},{48,0},{56,40},{1,17}... | collective-permute-start | bytes 3538952 | tf_op jit(solution)/shard_map/ppermute | solution.py:245
  64.4 36.1 %collective-permute-start.5 = (f32[768,384]{1,0:T(8,128)S(1)}, f32[768,384]{1,0:T(8,128)}, u32[]{:S(2)}, u32[]{:S(2)}) collective-permute-start(f32[768,384]{1,0:T(8,128)S(1)} %collective-permute-done.2.rest_2_), channel_id=1, source_target_pairs={{0,8},{8,0},{1,9},{9,1},{2,10},{10,2},{3,11},{11,3},{4,12},{12,4},... | collective-permute-start | bytes 3538952 | tf_op jit(solution)/shard_map/ppermute | solution.py:248
  76.7 23.8 %collective-permute-start.7 = (f32[768,384]{1,0:T(8,128)}, f32[768,384]{1,0:T(8,128)}, u32[]{:S(2)}, u32[]{:S(2)}) collective-permute-start(f32[768,384]{1,0:T(8,128)} %collective-permute-done.4.rest_4_), channel_id=1, source_target_pairs={{0,8},{8,0},{1,9},{9,1},{2,10},{10,2},{3,11},{11,3},{4,12},{12,4},... | collective-permute-start | bytes 3538952 | tf_op jit(solution)/shard_map/ppermute | solution.py:248
  89.3 11.2 %collective-permute-start.6 = (f32[768,384]{1,0:T(8,128)}, f32[768,384]{1,0:T(8,128)}, u32[]{:S(2)}, u32[]{:S(2)}) collective-permute-start(f32[768,384]{1,0:T(8,128)} %collective-permute-done.3.rest_3_), channel_id=1, source_target_pairs={{0,8},{8,0},{1,9},{9,1},{2,10},{10,2},{3,11},{11,3},{4,12},{12,4},... | collective-permute-start | bytes 3538952 | tf_op jit(solution)/shard_map/ppermute | solution.py:248
  100.5 0.9 copy-start.2
  109.9 2.2 %copy-start = (bf16[8,768,384]{2,1,0:T(8,128)(2,1)}, bf16[8,768,384]{2,1,0:T(8,128)(2,1)S(1)}, u32[]{:S(2)}) copy-start(bf16[8,768,384]{2,1,0:T(8,128)(2,1)S(1)} %get-tuple-element.4.high_hbm) | copy-start | bytes 14155780
  112.0 2.1 %copy-start.1 = (bf16[8,768,384]{2,1,0:T(8,128)(2,1)}, bf16[8,768,384]{2,1,0:T(8,128)(2,1)S(1)}, u32[]{:S(2)}) copy-start(bf16[8,768,384]{2,1,0:T(8,128)(2,1)S(1)} %get-tuple-element.5.low_hbm) | copy-start | bytes 14155780
  128.2 20.2 %collective-permute-start.8 = (f32[768,384]{1,0:T(8,128)S(1)}, f32[768,384]{1,0:T(8,128)S(1)}, u32[]{:S(2)}, u32[]{:S(2)}) collective-permute-start(f32[768,384]{1,0:T(8,128)S(1)} %shard_map.80), channel_id=1, source_target_pairs={{0,64},{8,200},{64,128},{72,8},{128,192},{136,72},{192,0},{200,136... | collective-permute-start | bytes 3538952 | tf_op jit(solution)/shard_map/ppermute | solution.py:274
  139.6 24.1 %collective-permute-start.10 = (f32[768,384]{1,0:T(8,128)S(1)}, f32[768,384]{1,0:T(8,128)}, u32[]{:S(2)}, u32[]{:S(2)}) collective-permute-start(f32[768,384]{1,0:T(8,128)S(1)} %shard_map.81), channel_id=1, source_target_pairs={{0,192},{8,72},{64,0},{72,136},{128,64},{136,200},{192,128},{200,8... | collective-permute-start | bytes 3538952 | tf_op jit(solution)/shard_map/ppermute | solution.py:276
  148.6 22.4 %collective-permute-start.9 = (f32[768,384]{1,0:T(8,128)S(1)}, f32[768,384]{1,0:T(8,128)S(1)}, u32[]{:S(2)}, u32[]{:S(2)}) collective-permute-start(f32[768,384]{1,0:T(8,128)S(1)} %add.110), channel_id=1, source_target_pairs={{0,64},{8,200},{64,128},{72,8},{128,192},{136,72},{192,0},{200,136... | collective-permute-start | bytes 3538952 | tf_op jit(solution)/shard_map/ppermute | solution.py:278
  172.5 1.3 copy-start.4
  173.3 1.0 copy-start.3
  173.8 11.7 %copy-start.5 = (f32[1,384]{1,0:T(1,128)S(1)}, f32[1,384]{1,0:T(1,128)}, u32[]{:S(2)}) copy-start(f32[1,384]{1,0:T(1,128)} %param.9) | copy-start | bytes 4612
Sparse Core Ops, SparseCore 0:
  10.1 111.2 all-gather.2

commit v7 on v6

--- a/solution.py
+++ b/solution.py
@@ -69,8 +69,8 @@
 
 
 def spread_kernel(start_row, rows_ref, *rest):
-    pieces = rest[:8]
-    high_hbm, low_hbm, z_f, z_h, z_l, in_sem, out_sem = rest[8:]
+    pieces = rest[:-7]
+    high_hbm, low_hbm, z_f, z_h, z_l, in_sem, out_sem = rest[-7:]
     slots, rows = z_f.shape[:2]
 
     def fetch(i):
@@ -140,7 +140,7 @@
         ],
         compiler_params=pltpu.CompilerParams(vmem_limit_bytes=VMEM_BYTES),
         cost_estimate=pl.CostEstimate(
-            flops=8 * 4 * rows * BLOCK * cols, bytes_accessed=64 * rows * cols, transcendentals=0
+            flops=10 * 4 * rows * BLOCK * cols, bytes_accessed=80 * rows * cols, transcendentals=0
         ),
     )(start_row, root_row, *pieces)
 
@@ -224,6 +224,53 @@
     )(table, root, high, low)
 
 
+def weigh_kernel(piece, first, second, high_hbm, low_hbm, total, sums, high, low, sem):
+    rows, cols = total.shape
+    copies = [
+        pltpu.make_async_copy(high_hbm.at[piece], high, sem.at[0]),
+        pltpu.make_async_copy(low_hbm.at[piece], low, sem.at[1]),
+    ]
+    for copy in copies:
+        copy.start()
+    for copy in copies:
+        copy.wait()
+
+    def one(i, found):
+        at = pl.ds(pl.multiple_of(i * 64, 64), 64)
+        value = first[at, :] + second[at, :]
+        total[at, :] = value
+        factor = high[at, :].astype(jnp.float32) + low[at, :].astype(jnp.float32)
+        return found + jnp.sum((factor * value).reshape(8, 8, cols), axis=0)
+
+    found = lax.fori_loop(0, rows // 64, one, jnp.zeros((8, cols), jnp.float32))
+    sums[...] = jnp.sum(found, axis=0, keepdims=True)
+
+
+def weigh(piece, first, second, high, low):
+    rows, cols = first.shape
+    any_spec = pl.BlockSpec(memory_space=pl.ANY)
+    vmem = pl.BlockSpec(memory_space=pltpu.VMEM)
+    high, low = [pltpu.with_memory_space_constraint(v, pltpu.HBM) for v in (high, low)]
+    return pl.pallas_call(
+        functools.partial(weigh_kernel, piece),
+        out_shape=[
+            jax.ShapeDtypeStruct((rows, cols), jnp.float32),
+            jax.ShapeDtypeStruct((1, cols), jnp.float32),
+        ],
+        in_specs=[vmem, vmem, any_spec, any_spec],
+        out_specs=[vmem, vmem],
+        scratch_shapes=[
+            pltpu.VMEM((rows, cols), jnp.bfloat16),
+            pltpu.VMEM((rows, cols), jnp.bfloat16),
+            pltpu.SemaphoreType.DMA((2,)),
+        ],
+        compiler_params=pltpu.CompilerParams(vmem_limit_bytes=VMEM_BYTES),
+        cost_estimate=pl.CostEstimate(
+            flops=4 * rows * cols, bytes_accessed=16 * rows * cols, transcendentals=0
+        ),
+    )(first, second, high, low)
+
+
 def per_device(root_inverse, root_row, coupling, pivot_variance):
     zh = lax.axis_index("zh")
     y = lax.axis_index("y")
@@ -249,7 +296,10 @@
 
     halves, found = piece_plan(holds)
     spots = lax.dynamic_slice(halves, (device, 0), (1, 8))[0]
-    start_row = ((zh * 4 + (spots & 3)) * ranges + y + 4 * (spots >> 2)) * per_range
+    pieces += [coupling[0], lax.ppermute(coupling[0], ("y", "core"), opposite(4, -1))]
+    child = zh * 4 + jnp.concatenate([spots & 3, jnp.stack([y, (y + 1 - 2 * core) & 3])])
+    ranged = jnp.concatenate([y + 4 * (spots >> 2), jnp.stack([own_range, own_range])])
+    start_row = (child * ranges + ranged) * per_range
     high, low = spread(start_row, root_row.reshape(-1, BLOCK), pieces)
 
     block = (root_row[:, ::BLOCK] >> 7).reshape(-1, ranges, per_range)
@@ -275,9 +325,23 @@
     first = product(1, table, root, high, low)
     back = lax.ppermute(first, ("y", "core"), opposite(4, -1))
     second = product(2, table, root, high, low)
-    forth = lax.ppermute(second + passed, ("y", "core"), opposite(4))
+    last, last_sums = weigh(9, second, passed, high, low)
+    table, last, last_sums = lax.optimization_barrier((table, last, last_sums))
+    last_sums = lax.ppermute(last_sums, ("y", "core"), opposite(4))
     home = product(3, table, root, high, low)
-    summed = home + forth + back
+    last, home, last_sums = lax.optimization_barrier((last, home, last_sums))
+    forth = lax.ppermute(last, ("y", "core"), opposite(4))
+    kept, sums = weigh(8, home, back, high, low)
+    sums = lax.all_to_all(
+        jnp.broadcast_to(sums + last_sums, (8, cols)),
+        ("x", "core"),
+        split_axis=0,
+        concat_axis=0,
+        tiled=True,
+    )
+    marginal = pivot_variance + jnp.sum(sums, axis=0, keepdims=True)
+    kept, marginal = lax.optimization_barrier((kept, marginal))
+    summed = kept + forth
 
     own_place = lax.dynamic_slice(root_row, (zh * 4 + y, own_range * rows), (1, rows))[0]
     own_place = jnp.where(own_place >= 0, own_place & (BLOCK - 1), -1).reshape(per_range, BLOCK)
@@ -286,12 +350,7 @@
         "iuo,ion->iun", hot, summed.reshape(per_range, BLOCK, cols), precision=lax.Precision.HIGHEST
     )
 
-    result = result.reshape(1, rows, cols)
-    sums = jnp.sum(coupling * result, axis=1)
-    sums = lax.all_to_all(
-        jnp.broadcast_to(sums, (8, cols)), ("x", "core"), split_axis=0, concat_axis=0, tiled=True
-    )
-    return result, pivot_variance - jnp.sum(sums, axis=0, keepdims=True)
+    return result.reshape(1, rows, cols), marginal
 
 
 def solution(mesh):

time: 194 us -> 190 us (0.979)
  waiting for transfers between devices: 80.3 us -> 61.6 us
  starting transfers between devices: 33.5 us -> 51.5 us
  blocking collectives: 11.2 us -> 0 us
  Pallas kernels: 35.8 us -> 41.1 us
    all_to_all x1 -> x0, blocking collectives: 11.2 us -> none  [per_device(): lax.all_to_all(jnp.broadcast_to(sums, (8, cols)), ('x', 'core'), split_ax...]
    ppermute x1, waiting for transfers between devices: 10.4 us -> 1.74 us  [per_device(): far = lax.ppermute(near, ('x', 'core'), along_x)]
    all_to_all x0 -> x1, starting transfers between devices: none -> 7.58 us  [per_device(): lax.all_to_all(jnp.broadcast_to(sums + last_sums, (8, cols)), ('x', 'core...]
    ppermute x1 -> x3, waiting for transfers between devices: 7.27 us -> 0.01 us  [the longest x1 0.01 us: per_device(): last_sums = lax.ppermute(last_sums, ('y', 'core'), opposite(4))]
    ppermute x3, starting transfers between devices: 8.61 us -> 15.3 us  [per_device(): pieces += [lax.ppermute(p, 'core', CORES) for p in (near, near_beside, far)]]
    all_gather x1, waiting for transfers between devices: 7.2 us -> 3.03 us  [per_device(): root = lax.all_gather(root_inverse, ('zh', 'zl'), axis=0, tiled=False)]
    all_to_all x0 -> x1, waiting for transfers between devices: none -> 3.81 us  [per_device(): lax.all_to_all(jnp.broadcast_to(sums + last_sums, (8, cols)), ('x', 'core...]
    ppermute x1 -> x3, starting transfers between devices: 4.9 us -> 8.64 us  [the longest x1 4.8 us: per_device(): last_sums = lax.ppermute(last_sums, ('y', 'core'), opposite(4))]
  transfers between devices with their start and end apart: 12 -> 15, of which waited for: 7 -> 6; matrix products, arithmetic and copies ran while one was open for 5% -> 6% of each run, Pallas kernels for 15% -> 18%
where the time goes in v7:
time: 190 us; the launch traced here: 189 us
  waiting for transfers between devices  61.6 us (32%)
  starting transfers between devices  51.5 us (27%)
  Pallas kernels  41.1 us (22%)
  between operations  14.3 us (8%)
  local copies, waits for them, and re-layouts  13.4 us (7%)
  other arithmetic  5.13 us (3%)
    ppermute x1, waiting for transfers between devices, per_device(): own = lax.ppermute(coupling[0], ('y', 'x', 'core'), pairs)  28.6 us
    pallas_call x4, Pallas kernels, product(): pl.pallas_call(functools.partial(product_kernel, call), out_shape=jax.Sha...  27.4 us
    ppermute x3, starting transfers between devices, per_device(): pieces += [lax.ppermute(p, 'core', CORES) for p in (near, near_beside, far)]  15.3 us
    ppermute x1, waiting for transfers between devices, per_device(): near = lax.ppermute(own, ('x', 'core'), along_x)  14.4 us
    pallas_call x1, Pallas kernels, spread(): pl.pallas_call(spread_kernel, out_shape=[jax.ShapeDtypeStruct(shape, jnp....  10.4 us
    ppermute x1, waiting for transfers between devices, per_device(): near_beside = lax.ppermute(beside, ('x', 'core'), along_x)  9.29 us
    all_to_all x1, starting transfers between devices, per_device(): lax.all_to_all(jnp.broadcast_to(sums + last_sums, (8, cols)), ('x', 'core...  7.58 us
    unnamed x8, local copies, waits for them, and re-layouts  7.21 us
  transfers between devices with their start and end apart: 15, of which 6 were waited for; matrix products, arithmetic and copies ran while one was open for 6% of the time, Pallas kernels for 18%

profile of v7, /device:TPU:1, one launch (start us, length us, event | category | flops | bytes accessed | tf_op | source)
XLA Modules:
  0.0 188.7 jit_solution(6286027018336424102)
XLA Ops:
  7.2 0.0 all-gather.3.cloned.1.call-start
  7.2 0.7 all-gather.3.cloned.1.call-update
  7.9 4.6 %collective-permute-start = (f32[768,384]{1,0:T(8,128)}, f32[768,384]{1,0:T(8,128)S(1)}, u32[]{:S(2)}, u32[]{:S(2)}) collective-permute-start(f32[768,384]{1,0:T(8,128)} %bitcast.20), channel_id=1, source_target_pairs={{0,48},{8,64},{16,144},{24,224},{32,32},{40,112},{48,176},{56,240}... | collective-permute-start | bytes 3538952 | tf_op jit(solution)/shard_map/ppermute | solution.py:288
  12.5 28.6 %collective-permute-done.rest_0_ = f32[768,384]{1,0:T(8,128)S(1)} collective-permute-done((f32[768,384]{1,0:T(8,128)}, f32[768,384]{1,0:T(8,128)S(1)}, u32[]{:S(2)}, u32[]{:S(2)}) %collective-permute-start) | collective-permute-done | bytes 1179680 | tf_op jit(solution)/shard_map/ppermute | solution.py:288
  41.1 1.9 %collective-permute-start.2 = (f32[768,384]{1,0:T(8,128)S(1)}, f32[768,384]{1,0:T(8,128)S(1)}, u32[]{:S(2)}, u32[]{:S(2)}) collective-permute-start(f32[768,384]{1,0:T(8,128)S(1)} %collective-permute-done.rest_0_), channel_id=1, source_target_pairs={{0,16},{8,56},{16,32},{24,8},{32,48},{40,24},{48,0},{56,40},{1,17}... | collective-permute-start | bytes 3538952 | tf_op jit(solution)/shard_map/ppermute | solution.py:291
  43.0 1.9 %collective-permute-start.1 = (f32[768,384]{1,0:T(8,128)S(1)}, f32[768,384]{1,0:T(8,128)S(1)}, u32[]{:S(2)}, u32[]{:S(2)}) collective-permute-start(f32[768,384]{1,0:T(8,128)S(1)} %collective-permute-done.rest_0_), channel_id=1, source_target_pairs={{0,8},{8,0},{1,9},{9,1},{2,10},{10,2},{3,11},{11,3},{4,12},{12,4},... | collective-permute-start | bytes 3538952 | tf_op jit(solution)/shard_map/ppermute | solution.py:290
  44.9 14.4 %collective-permute-done.2.rest_2_ = f32[768,384]{1,0:T(8,128)S(1)} collective-permute-done((f32[768,384]{1,0:T(8,128)S(1)}, f32[768,384]{1,0:T(8,128)S(1)}, u32[]{:S(2)}, u32[]{:S(2)}) %collective-permute-start.2) | collective-permute-done | bytes 1179680 | tf_op jit(solution)/shard_map/ppermute | solution.py:291
  59.3 2.2 %collective-permute-start.4 = (f32[768,384]{1,0:T(8,128)S(1)}, f32[768,384]{1,0:T(8,128)}, u32[]{:S(2)}, u32[]{:S(2)}) collective-permute-start(f32[768,384]{1,0:T(8,128)S(1)} %collective-permute-done.2.rest_2_), channel_id=1, source_target_pairs={{0,16},{8,56},{16,32},{24,8},{32,48},{40,24},{48,0},{56,40},{1,17}... | collective-permute-start | bytes 3538952 | tf_op jit(solution)/shard_map/ppermute | solution.py:293
  61.5 0.0 collective-permute-done.1.rest_1_
  61.5 2.8 %collective-permute-start.3 = (f32[768,384]{1,0:T(8,128)S(1)}, f32[768,384]{1,0:T(8,128)}, u32[]{:S(2)}, u32[]{:S(2)}) collective-permute-start(f32[768,384]{1,0:T(8,128)S(1)} %collective-permute-done.1.rest_1_), channel_id=1, source_target_pairs={{0,16},{8,56},{16,32},{24,8},{32,48},{40,24},{48,0},{56,40},{1,17}... | collective-permute-start | bytes 3538952 | tf_op jit(solution)/shard_map/ppermute | solution.py:292
  64.4 1.9 %collective-permute-start.8 = (f32[768,384]{1,0:T(8,128)}, f32[768,384]{1,0:T(8,128)}, u32[]{:S(2)}, u32[]{:S(2)}) collective-permute-start(f32[768,384]{1,0:T(8,128)} %bitcast.21), channel_id=1, source_target_pairs={{0,192},{8,72},{64,0},{72,136},{128,64},{136,200},{192,128},{200,8... | collective-permute-start | bytes 3538952 | tf_op jit(solution)/shard_map/ppermute | solution.py:299
  66.3 8.6 %collective-permute-start.5 = (f32[768,384]{1,0:T(8,128)S(1)}, f32[768,384]{1,0:T(8,128)}, u32[]{:S(2)}, u32[]{:S(2)}) collective-permute-start(f32[768,384]{1,0:T(8,128)S(1)} %collective-permute-done.2.rest_2_), channel_id=1, source_target_pairs={{0,8},{8,0},{1,9},{9,1},{2,10},{10,2},{3,11},{11,3},{4,12},{12,4},... | collective-permute-start | bytes 3538952 | tf_op jit(solution)/shard_map/ppermute | solution.py:295
  74.9 1.7 collective-permute-done.4.rest_4_
  76.7 3.3 %collective-permute-start.7 = (f32[768,384]{1,0:T(8,128)}, f32[768,384]{1,0:T(8,128)}, u32[]{:S(2)}, u32[]{:S(2)}) collective-permute-start(f32[768,384]{1,0:T(8,128)} %collective-permute-done.4.rest_4_), channel_id=1, source_target_pairs={{0,8},{8,0},{1,9},{9,1},{2,10},{10,2},{3,11},{11,3},{4,12},{12,4},... | collective-permute-start | bytes 3538952 | tf_op jit(solution)/shard_map/ppermute | solution.py:295
  80.0 9.3 %collective-permute-done.3.rest_3_ = f32[768,384]{1,0:T(8,128)} collective-permute-done((f32[768,384]{1,0:T(8,128)S(1)}, f32[768,384]{1,0:T(8,128)}, u32[]{:S(2)}, u32[]{:S(2)}) %collective-permute-start.3) | collective-permute-done | bytes 1179680 | tf_op jit(solution)/shard_map/ppermute | solution.py:292
  89.3 3.3 %collective-permute-start.6 = (f32[768,384]{1,0:T(8,128)}, f32[768,384]{1,0:T(8,128)}, u32[]{:S(2)}, u32[]{:S(2)}) collective-permute-start(f32[768,384]{1,0:T(8,128)} %collective-permute-done.3.rest_3_), channel_id=1, source_target_pairs={{0,8},{8,0},{1,9},{9,1},{2,10},{10,2},{3,11},{11,3},{4,12},{12,4},... | collective-permute-start | bytes 3538952 | tf_op jit(solution)/shard_map/ppermute | solution.py:295
  92.7 1.6 reshape.109.rows_ref
  94.3 1.0 slice.3
  95.4 0.7 reshape.108
  96.1 0.7 fusion.2
  96.8 0.7 copy.18
  97.4 0.1 pad_add_fusion
  97.5 0.1 copy.17
  97.6 0.8 and_add_fusion
  98.5 0.6 add_and_fusion
  99.1 0.8 concatenate.16.table
  99.8 0.7 and_bitcast_fusion
  100.5 0.1 fusion.5.start_row
  100.6 0.0 collective-permute-done.8.rest_9_
  100.6 0.0 collective-permute-done.5.rest_5_
  100.6 0.0 collective-permute-done.7.rest_7_
  100.6 0.0 collective-permute-done.6.rest_6_
  100.6 0.0 copy-start.2
  100.6 1.3 copy-done.2
  101.9 0.0 copy-start.3
  101.9 0.9 copy-done.3
  102.8 10.4 %shard_map.77 = (bf16[10,768,384]{2,1,0:T(8,128)(2,1)S(1)}, bf16[10,768,384]{2,1,0:T(8,128)(2,1)S(1)}) custom-call(s32[10]{0:T(128)S(1)} %fusion.5.start_row, s32[384,128]{1,0:T(8,128)S(1)} %copy-done.3, f32[768,384]{1,0:T(8,128)S(1)} %collective-permute-done.rest_0_, f32[768,384]{1,0:T(8,128)S(1)} %collective-permute-done.1.rest_1_, ...), custom_call_target="tpu_custom_call" | custom-call | flops 1509949440 | bytes 23592960 | tf_op jit(solution)/shard_map/pallas_call | solution.py:125
  113.3 0.0 copy-start
  113.3 2.6 %copy-done = bf16[10,768,384]{2,1,0:T(8,128)(2,1)} copy-done((bf16[10,768,384]{2,1,0:T(8,128)(2,1)}, bf16[10,768,384]{2,1,0:T(8,128)(2,1)S(1)}, u32[]{:S(2)}) %copy-start) | copy-done | bytes 5898264
  115.9 0.0 copy-start.1
  115.9 2.5 %copy-done.1 = bf16[10,768,384]{2,1,0:T(8,128)(2,1)} copy-done((bf16[10,768,384]{2,1,0:T(8,128)(2,1)}, bf16[10,768,384]{2,1,0:T(8,128)(2,1)S(1)}, u32[]{:S(2)}) %copy-start.1) | copy-done | bytes 5898264
  118.3 3.0 %all-gather.3.cloned.1.call-done = f32[16384,128]{1,0:T(8,128)} async-done(((f32[1024,128]{1,0:T(8,128)}), f32[16384,128]{1,0:T(8,128)}) %all-gather.3.cloned.1.call-update) | async-done | bytes 8388624 | tf_op jit(solution)/shard_map/all_gather | solution.py:285
  121.4 6.9 %shard_map.79 = f32[768,384]{1,0:T(8,128)S(1)} custom-call(s32[4,21]{1,0:T(4,128)S(1)} %concatenate.16.table, f32[16,1024,128]{2,1,0:T(8,128)} %bitcast.23, bf16[10,768,384]{2,1,0:T(8,128)(2,1)} %copy-done, bf16[10,768,384]{2,1,0:T(8,128)(2,1)} %copy-done.1), custom_call_target="tpu_custom_call" | custom-call | flops 2717908992 | bytes 7077888 | tf_op jit(solution)/shard_map/pallas_call | solution.py:208
  128.2 4.5 %collective-permute-start.9 = (f32[768,384]{1,0:T(8,128)S(1)}, f32[768,384]{1,0:T(8,128)S(1)}, u32[]{:S(2)}, u32[]{:S(2)}) collective-permute-start(f32[768,384]{1,0:T(8,128)S(1)} %shard_map.79), channel_id=1, source_target_pairs={{0,64},{8,200},{64,128},{72,8},{128,192},{136,72},{192,0},{200,136... | collective-permute-start | bytes 3538952 | tf_op jit(solution)/shard_map/ppermute | solution.py:324
  132.8 6.9 %shard_map.82 = f32[768,384]{1,0:T(8,128)S(1)} custom-call(s32[4,21]{1,0:T(4,128)S(1)} %concatenate.16.table, f32[16,1024,128]{2,1,0:T(8,128)} %bitcast.24, bf16[10,768,384]{2,1,0:T(8,128)(2,1)} %copy-done, bf16[10,768,384]{2,1,0:T(8,128)(2,1)} %copy-done.1), custom_call_target="tpu_custom_call" | custom-call | flops 2717908992 | bytes 7077888 | tf_op jit(solution)/shard_map/pallas_call | solution.py:208
  139.6 1.9 %collective-permute-start.11 = (f32[768,384]{1,0:T(8,128)S(1)}, f32[768,384]{1,0:T(8,128)S(1)}, u32[]{:S(2)}, u32[]{:S(2)}) collective-permute-start(f32[768,384]{1,0:T(8,128)S(1)} %shard_map.82), channel_id=1, source_target_pairs={{0,192},{8,72},{64,0},{72,136},{128,64},{136,200},{192,128},{200,8... | collective-permute-start | bytes 3538952 | tf_op jit(solution)/shard_map/ppermute | solution.py:326
  141.6 6.9 %shard_map.78.first = f32[768,384]{1,0:T(8,128)S(1)} custom-call(s32[4,21]{1,0:T(4,128)S(1)} %concatenate.16.table, f32[16,1024,128]{2,1,0:T(8,128)} %bitcast.25, bf16[10,768,384]{2,1,0:T(8,128)(2,1)} %copy-done, bf16[10,768,384]{2,1,0:T(8,128)(2,1)} %copy-done.1), custom_call_target="tpu_custom_call" | custom-call | flops 2717908992 | bytes 7077888 | tf_op jit(solution)/shard_map/pallas_call | solution.py:208
  148.4 0.0 collective-permute-done.9.second
  148.4 1.6 shard_map.80
  150.1 4.8 %collective-permute-start.10 = (f32[1,384]{1,0:T(1,128)S(1)}, f32[1,384]{1,0:T(1,128)S(1)}, u32[]{:S(2)}, u32[]{:S(2)}) collective-permute-start(f32[1,384]{1,0:T(1,128)S(1)} %get-tuple-element.22), channel_id=1, source_target_pairs={{0,64},{8,200},{64,128},{72,8},{128,192},{136,72},{192,0},{200,136... | collective-permute-start | bytes 4616 | tf_op jit(solution)/shard_map/ppermute | solution.py:330
  154.9 6.9 %shard_map.81.first = f32[768,384]{1,0:T(8,128)S(1)} custom-call(s32[4,21]{1,0:T(4,128)S(1)} %concatenate.16.table, f32[16,1024,128]{2,1,0:T(8,128)} %bitcast.26, bf16[10,768,384]{2,1,0:T(8,128)(2,1)} %copy-done, bf16[10,768,384]{2,1,0:T(8,128)(2,1)} %copy-done.1), custom_call_target="tpu_custom_call" | custom-call | flops 2717908992 | bytes 7077888 | tf_op jit(solution)/shard_map/pallas_call | solution.py:208
  161.7 0.0 collective-permute-done.10
  161.7 1.9 %collective-permute-start.12 = (f32[768,384]{1,0:T(8,128)S(1)}, f32[768,384]{1,0:T(8,128)S(1)}, u32[]{:S(2)}, u32[]{:S(2)}) collective-permute-start(f32[768,384]{1,0:T(8,128)S(1)} %get-tuple-element.28), channel_id=1, source_target_pairs={{0,64},{8,200},{64,128},{72,8},{128,192},{136,72},{192,0},{200,136... | collective-permute-start | bytes 3538952 | tf_op jit(solution)/shard_map/ppermute | solution.py:333
  163.7 0.0 collective-permute-done.11.second
  163.7 1.6 shard_map.83
  165.3 0.6 broadcast_in_dim.15
  165.9 7.6 %all-to-all-start = ((f32[8,1,384]{2,1,0:T(1,128)}), f32[8,1,384]{2,1,0:T(1,128)S(1)}, u32[]{:S(2)}, u32[]{:S(2)}) async-start(f32[8,1,384]{2,1,0:T(1,128)} %broadcast_in_dim.15), calls=%async_computation | async-start | bytes 24576 | tf_op jit(solution)/shard_map/all_to_all | solution.py:335
  173.5 0.8 fusion.1
  174.3 3.8 %all-to-all-done = f32[8,1,384]{2,1,0:T(1,128)S(1)} async-done(((f32[8,1,384]{2,1,0:T(1,128)}), f32[8,1,384]{2,1,0:T(1,128)S(1)}, u32[]{:S(2)}, u32[]{:S(2)}) %all-to-all-start) | async-done | bytes 12320 | tf_op jit(solution)/shard_map/all_to_all | solution.py:335
  178.1 0.6 reduce_sum.9
  178.7 1.3 reshape_add_fusion
  180.0 0.0 collective-permute-done.12
  180.0 0.1 add.122
  180.1 1.8 convolution_negate_fusion
  (2 shorter events, 0.0 us)
Async XLA Ops:
  7.2 114.2 %all-gather.3.cloned.1.call-start = ((), (), s32[]{:S(2)}) async-start(), calls=%async_computation.1 | async-start | bytes 8912896 | tf_op jit(solution)/shard_map/all_gather | solution.py:285
  7.9 33.2 %collective-permute-start = (f32[768,384]{1,0:T(8,128)}, f32[768,384]{1,0:T(8,128)S(1)}, u32[]{:S(2)}, u32[]{:S(2)}) collective-permute-start(f32[768,384]{1,0:T(8,128)} %bitcast.20), channel_id=1, source_target_pairs={{0,48},{8,64},{16,144},{24,224},{32,32},{40,112},{48,176},{56,240}... | collective-permute-start | bytes 3538952 | tf_op jit(solution)/shard_map/ppermute | solution.py:288
  41.1 18.3 %collective-permute-start.2 = (f32[768,384]{1,0:T(8,128)S(1)}, f32[768,384]{1,0:T(8,128)S(1)}, u32[]{:S(2)}, u32[]{:S(2)}) collective-permute-start(f32[768,384]{1,0:T(8,128)S(1)} %collective-permute-done.rest_0_), channel_id=1, source_target_pairs={{0,16},{8,56},{16,32},{24,8},{32,48},{40,24},{48,0},{56,40},{1,17}... | collective-permute-start | bytes 3538952 | tf_op jit(solution)/shard_map/ppermute | solution.py:291
  43.0 18.6 %collective-permute-start.1 = (f32[768,384]{1,0:T(8,128)S(1)}, f32[768,384]{1,0:T(8,128)S(1)}, u32[]{:S(2)}, u32[]{:S(2)}) collective-permute-start(f32[768,384]{1,0:T(8,128)S(1)} %collective-permute-done.rest_0_), channel_id=1, source_target_pairs={{0,8},{8,0},{1,9},{9,1},{2,10},{10,2},{3,11},{11,3},{4,12},{12,4},... | collective-permute-start | bytes 3538952 | tf_op jit(solution)/shard_map/ppermute | solution.py:290
  59.3 17.3 %collective-permute-start.4 = (f32[768,384]{1,0:T(8,128)S(1)}, f32[768,384]{1,0:T(8,128)}, u32[]{:S(2)}, u32[]{:S(2)}) collective-permute-start(f32[768,384]{1,0:T(8,128)S(1)} %collective-permute-done.2.rest_2_), channel_id=1, source_target_pairs={{0,16},{8,56},{16,32},{24,8},{32,48},{40,24},{48,0},{56,40},{1,17}... | collective-permute-start | bytes 3538952 | tf_op jit(solution)/shard_map/ppermute | solution.py:293
  61.5 27.8 %collective-permute-start.3 = (f32[768,384]{1,0:T(8,128)S(1)}, f32[768,384]{1,0:T(8,128)}, u32[]{:S(2)}, u32[]{:S(2)}) collective-permute-start(f32[768,384]{1,0:T(8,128)S(1)} %collective-permute-done.1.rest_1_), channel_id=1, source_target_pairs={{0,16},{8,56},{16,32},{24,8},{32,48},{40,24},{48,0},{56,40},{1,17}... | collective-permute-start | bytes 3538952 | tf_op jit(solution)/shard_map/ppermute | solution.py:292
  64.4 36.2 %collective-permute-start.8 = (f32[768,384]{1,0:T(8,128)}, f32[768,384]{1,0:T(8,128)}, u32[]{:S(2)}, u32[]{:S(2)}) collective-permute-start(f32[768,384]{1,0:T(8,128)} %bitcast.21), channel_id=1, source_target_pairs={{0,192},{8,72},{64,0},{72,136},{128,64},{136,200},{192,128},{200,8... | collective-permute-start | bytes 3538952 | tf_op jit(solution)/shard_map/ppermute | solution.py:299
  66.3 34.3 %collective-permute-start.5 = (f32[768,384]{1,0:T(8,128)S(1)}, f32[768,384]{1,0:T(8,128)}, u32[]{:S(2)}, u32[]{:S(2)}) collective-permute-start(f32[768,384]{1,0:T(8,128)S(1)} %collective-permute-done.2.rest_2_), channel_id=1, source_target_pairs={{0,8},{8,0},{1,9},{9,1},{2,10},{10,2},{3,11},{11,3},{4,12},{12,4},... | collective-permute-start | bytes 3538952 | tf_op jit(solution)/shard_map/ppermute | solution.py:295
  76.7 24.0 %collective-permute-start.7 = (f32[768,384]{1,0:T(8,128)}, f32[768,384]{1,0:T(8,128)}, u32[]{:S(2)}, u32[]{:S(2)}) collective-permute-start(f32[768,384]{1,0:T(8,128)} %collective-permute-done.4.rest_4_), channel_id=1, source_target_pairs={{0,8},{8,0},{1,9},{9,1},{2,10},{10,2},{3,11},{11,3},{4,12},{12,4},... | collective-permute-start | bytes 3538952 | tf_op jit(solution)/shard_map/ppermute | solution.py:295
  89.3 11.3 %collective-permute-start.6 = (f32[768,384]{1,0:T(8,128)}, f32[768,384]{1,0:T(8,128)}, u32[]{:S(2)}, u32[]{:S(2)}) collective-permute-start(f32[768,384]{1,0:T(8,128)} %collective-permute-done.3.rest_3_), channel_id=1, source_target_pairs={{0,8},{8,0},{1,9},{9,1},{2,10},{10,2},{3,11},{11,3},{4,12},{12,4},... | collective-permute-start | bytes 3538952 | tf_op jit(solution)/shard_map/ppermute | solution.py:295
  100.6 1.3 copy-start.2
  101.9 0.9 copy-start.3
  113.3 2.6 %copy-start = (bf16[10,768,384]{2,1,0:T(8,128)(2,1)}, bf16[10,768,384]{2,1,0:T(8,128)(2,1)S(1)}, u32[]{:S(2)}) copy-start(bf16[10,768,384]{2,1,0:T(8,128)(2,1)S(1)} %get-tuple-element.16.high_hbm) | copy-start | bytes 17694724
  115.9 2.5 %copy-start.1 = (bf16[10,768,384]{2,1,0:T(8,128)(2,1)}, bf16[10,768,384]{2,1,0:T(8,128)(2,1)S(1)}, u32[]{:S(2)}) copy-start(bf16[10,768,384]{2,1,0:T(8,128)(2,1)S(1)} %get-tuple-element.17.low_hbm) | copy-start | bytes 17694724
  128.2 20.2 %collective-permute-start.9 = (f32[768,384]{1,0:T(8,128)S(1)}, f32[768,384]{1,0:T(8,128)S(1)}, u32[]{:S(2)}, u32[]{:S(2)}) collective-permute-start(f32[768,384]{1,0:T(8,128)S(1)} %shard_map.79), channel_id=1, source_target_pairs={{0,64},{8,200},{64,128},{72,8},{128,192},{136,72},{192,0},{200,136... | collective-permute-start | bytes 3538952 | tf_op jit(solution)/shard_map/ppermute | solution.py:324
  139.6 24.0 %collective-permute-start.11 = (f32[768,384]{1,0:T(8,128)S(1)}, f32[768,384]{1,0:T(8,128)S(1)}, u32[]{:S(2)}, u32[]{:S(2)}) collective-permute-start(f32[768,384]{1,0:T(8,128)S(1)} %shard_map.82), channel_id=1, source_target_pairs={{0,192},{8,72},{64,0},{72,136},{128,64},{136,200},{192,128},{200,8... | collective-permute-start | bytes 3538952 | tf_op jit(solution)/shard_map/ppermute | solution.py:326
  150.1 11.7 %collective-permute-start.10 = (f32[1,384]{1,0:T(1,128)S(1)}, f32[1,384]{1,0:T(1,128)S(1)}, u32[]{:S(2)}, u32[]{:S(2)}) collective-permute-start(f32[1,384]{1,0:T(1,128)S(1)} %get-tuple-element.22), channel_id=1, source_target_pairs={{0,64},{8,200},{64,128},{72,8},{128,192},{136,72},{192,0},{200,136... | collective-permute-start | bytes 4616 | tf_op jit(solution)/shard_map/ppermute | solution.py:330
  161.7 18.3 %collective-permute-start.12 = (f32[768,384]{1,0:T(8,128)S(1)}, f32[768,384]{1,0:T(8,128)S(1)}, u32[]{:S(2)}, u32[]{:S(2)}) collective-permute-start(f32[768,384]{1,0:T(8,128)S(1)} %get-tuple-element.28), channel_id=1, source_target_pairs={{0,64},{8,200},{64,128},{72,8},{128,192},{136,72},{192,0},{200,136... | collective-permute-start | bytes 3538952 | tf_op jit(solution)/shard_map/ppermute | solution.py:333
  165.9 12.2 %all-to-all-start = ((f32[8,1,384]{2,1,0:T(1,128)}), f32[8,1,384]{2,1,0:T(1,128)S(1)}, u32[]{:S(2)}, u32[]{:S(2)}) async-start(f32[8,1,384]{2,1,0:T(1,128)} %broadcast_in_dim.15), calls=%async_computation | async-start | bytes 24576 | tf_op jit(solution)/shard_map/all_to_all | solution.py:335
Sparse Core Ops, SparseCore 0:
  10.1 111.2 all-gather.2

commit v8 on v7

--- a/solution.py
+++ b/solution.py
@@ -124,13 +124,13 @@
     held = (SLOTS, rows, cols)
     return pl.pallas_call(
         spread_kernel,
-        out_shape=[jax.ShapeDtypeStruct(shape, jnp.bfloat16)] * 2,
+        out_shape=[pltpu.HBM(shape, jnp.bfloat16)] * 2,
         in_specs=[
             pl.BlockSpec(memory_space=pltpu.SMEM),
             pl.BlockSpec(memory_space=pltpu.VMEM),
         ]
         + [any_spec] * len(pieces),
-        out_specs=[any_spec] * 2,
+        out_specs=[pl.BlockSpec(memory_space=pltpu.HBM)] * 2,
         scratch_shapes=[
             pltpu.VMEM(held, jnp.float32),
             pltpu.VMEM(held, jnp.bfloat16),
@@ -145,81 +145,93 @@
     )(start_row, root_row, *pieces)
 
 
-def product_kernel(call, table, root_hbm, high_hbm, low_hbm, out, a_f, z_h, z_l, a_sem, z_sem):
-    rows = out.shape[0]
+def product_kernel(calls, table, root_hbm, high_hbm, low_hbm, *rest):
+    outs = rest[: len(calls)]
+    a_f, z_h, z_l, a_sem, z_sem = rest[len(calls) :]
+    rows = outs[0].shape[0]
     per_range = rows // BLOCK
     per_part = PART // BLOCK
     parts = rows // PART
-    c = table[call, 3 * per_range + 2]
-
-    def factor_copies(source, target, first):
+    children = [table[call, 3 * per_range + 2] for call in calls]
+
+    def factor_copies(i, source, target, first):
         return [
             pltpu.make_async_copy(
-                source.at[table[c, 3 * per_range + side]],
-                target.at[pl.ds(side * rows, rows)],
-                z_sem.at[first + side],
+                source.at[table[children[i], 3 * per_range + side]],
+                target.at[i, pl.ds(side * rows, rows)],
+                z_sem.at[i, first + side],
             )
             for side in range(2)
         ]
 
-    def start_root(part):
+    def start_root(i, part):
         for m in range(per_part):
-            mb = pl.multiple_of(table[c, part * per_part + m] * BLOCK, BLOCK)
+            mb = pl.multiple_of(table[children[i], part * per_part + m] * BLOCK, BLOCK)
             pltpu.make_async_copy(
                 root_hbm.at[:, pl.ds(mb, BLOCK)],
-                a_f.at[part, :, pl.ds(m * BLOCK, BLOCK)],
-                a_sem.at[part],
+                a_f.at[i, part, :, pl.ds(m * BLOCK, BLOCK)],
+                a_sem.at[i, part],
             ).start()
 
-    highs_in = factor_copies(high_hbm, z_h, 0)
-    lows_in = factor_copies(low_hbm, z_l, 2)
-    start_root(0)
-    for copy in highs_in + lows_in:
-        copy.start()
-    start_root(1)
-    for part in range(parts):
-        pltpu.make_async_copy(a_f.at[part], a_f.at[part], a_sem.at[part]).wait()
-        if part == 0:
-            for copy in highs_in:
-                copy.wait()
-        if part + 2 < parts:
-            start_root(part + 2)
-        highs, lows = [], []
-        for k in range(2 * per_range):
-            value = a_f[part, table[c, per_range + k]]
-            high = value.astype(jnp.bfloat16)
-            highs.append(high)
-            lows.append((value - high.astype(jnp.float32)).astype(jnp.bfloat16))
-        high = jnp.concatenate(highs, axis=1)
-        low = jnp.concatenate(lows, axis=1)
-        value = jnp.dot(high, z_h[...], preferred_element_type=jnp.float32)
-        value = value + jnp.dot(low, z_h[...], preferred_element_type=jnp.float32)
-        if part == 0:
-            for copy in lows_in:
-                copy.wait()
-        value = value + jnp.dot(high, z_l[...], preferred_element_type=jnp.float32)
-        out[part * PART : (part + 1) * PART, :] = value
-
-
-def product(call, table, root, high, low):
+    highs_in = [factor_copies(i, high_hbm, z_h, 0) for i in range(len(calls))]
+    lows_in = [factor_copies(i, low_hbm, z_l, 2) for i in range(len(calls))]
+
+    def begin(i):
+        start_root(i, 0)
+        for copy in highs_in[i] + lows_in[i]:
+            copy.start()
+        start_root(i, 1)
+
+    begin(0)
+    for i, out in enumerate(outs):
+        for part in range(parts):
+            pltpu.make_async_copy(a_f.at[i, part], a_f.at[i, part], a_sem.at[i, part]).wait()
+            if part == 0:
+                for copy in highs_in[i]:
+                    copy.wait()
+            if part + 2 < parts:
+                start_root(i, part + 2)
+            elif part + 2 == parts and i + 1 < len(calls):
+                begin(i + 1)
+            highs, lows = [], []
+            for k in range(2 * per_range):
+                value = a_f[i, part, table[children[i], per_range + k]]
+                high = value.astype(jnp.bfloat16)
+                highs.append(high)
+                lows.append((value - high.astype(jnp.float32)).astype(jnp.bfloat16))
+            high = jnp.concatenate(highs, axis=1)
+            low = jnp.concatenate(lows, axis=1)
+            value = jnp.dot(high, z_h[i], preferred_element_type=jnp.float32)
+            value = value + jnp.dot(low, z_h[i], preferred_element_type=jnp.float32)
+            if part == 0:
+                for copy in lows_in[i]:
+                    copy.wait()
+            value = value + jnp.dot(high, z_l[i], preferred_element_type=jnp.float32)
+            out[part * PART : (part + 1) * PART, :] = value
+
+
+def product(calls, table, root, high, low):
     rows, cols = high.shape[1:]
+    n = len(calls)
     any_spec = pl.BlockSpec(memory_space=pl.ANY)
     root, high, low = [pltpu.with_memory_space_constraint(v, pltpu.HBM) for v in (root, high, low)]
     return pl.pallas_call(
-        functools.partial(product_kernel, call),
-        out_shape=jax.ShapeDtypeStruct((rows, cols), jnp.float32),
+        functools.partial(product_kernel, calls),
+        out_shape=[jax.ShapeDtypeStruct((rows, cols), jnp.float32)] * n,
         in_specs=[pl.BlockSpec(memory_space=pltpu.SMEM)] + [any_spec] * 3,
-        out_specs=pl.BlockSpec(memory_space=pltpu.VMEM),
+        out_specs=[pl.BlockSpec(memory_space=pltpu.VMEM)] * n,
         scratch_shapes=[
-            pltpu.VMEM((rows // PART, root.shape[0], PART, BLOCK), jnp.float32),
-            pltpu.VMEM((2 * rows, cols), jnp.bfloat16),
-            pltpu.VMEM((2 * rows, cols), jnp.bfloat16),
-            pltpu.SemaphoreType.DMA((rows // PART,)),
-            pltpu.SemaphoreType.DMA((4,)),
-        ],
-        compiler_params=pltpu.CompilerParams(vmem_limit_bytes=VMEM_BYTES),
+            pltpu.VMEM((n, rows // PART, root.shape[0], PART, BLOCK), jnp.float32),
+            pltpu.VMEM((n, 2 * rows, cols), jnp.bfloat16),
+            pltpu.VMEM((n, 2 * rows, cols), jnp.bfloat16),
+            pltpu.SemaphoreType.DMA((n, rows // PART)),
+            pltpu.SemaphoreType.DMA((n, 4)),
+        ],
+        compiler_params=pltpu.CompilerParams(vmem_limit_bytes=(12 + 14 * n) * 1024 * 1024),
         cost_estimate=pl.CostEstimate(
-            flops=3 * 2 * rows * 2 * rows * cols, bytes_accessed=12 * rows * rows, transcendentals=0
+            flops=n * 3 * 2 * rows * 2 * rows * cols,
+            bytes_accessed=n * 12 * rows * rows,
+            transcendentals=0,
         ),
     )(table, root, high, low)
 
@@ -285,23 +297,11 @@
     root = lax.all_gather(root_inverse, ("zh", "zl"), axis=0, tiled=False)
 
     pairs, holds = spread_plan()
-    own = lax.ppermute(coupling[0], ("y", "x", "core"), pairs)
-    along_x = opposite(4)
-    beside = lax.ppermute(own, "core", CORES)
-    near = lax.ppermute(own, ("x", "core"), along_x)
-    near_beside = lax.ppermute(beside, ("x", "core"), along_x)
-    far = lax.ppermute(near, ("x", "core"), along_x)
-    pieces = [own, beside, near, near_beside, far]
-    pieces += [lax.ppermute(p, "core", CORES) for p in (near, near_beside, far)]
-
     halves, found = piece_plan(holds)
     spots = lax.dynamic_slice(halves, (device, 0), (1, 8))[0]
-    pieces += [coupling[0], lax.ppermute(coupling[0], ("y", "core"), opposite(4, -1))]
     child = zh * 4 + jnp.concatenate([spots & 3, jnp.stack([y, (y + 1 - 2 * core) & 3])])
     ranged = jnp.concatenate([y + 4 * (spots >> 2), jnp.stack([own_range, own_range])])
     start_row = (child * ranges + ranged) * per_range
-    high, low = spread(start_row, root_row.reshape(-1, BLOCK), pieces)
-
     block = (root_row[:, ::BLOCK] >> 7).reshape(-1, ranges, per_range)
 
     def blocks_of(r):
@@ -318,18 +318,28 @@
         ],
         axis=1,
     ).astype(jnp.int32)
+    own = lax.ppermute(coupling[0], ("y", "x", "core"), pairs)
+    rows_of = root_row.reshape(-1, BLOCK)
+    own, table, start_row, rows_of = lax.optimization_barrier((own, table, start_row, rows_of))
+    along_x = opposite(4)
+    beside = lax.ppermute(own, "core", CORES)
+    near = lax.ppermute(own, ("x", "core"), along_x)
+    near_beside = lax.ppermute(beside, ("x", "core"), along_x)
+    far = lax.ppermute(near, ("x", "core"), along_x)
+    pieces = [own, beside, near, near_beside, far]
+    pieces += [lax.ppermute(p, "core", CORES) for p in (near, near_beside, far)]
+    pieces += [coupling[0], lax.ppermute(coupling[0], ("y", "core"), opposite(4, -1))]
+    high, low = spread(start_row, rows_of, pieces)
 
     root = root.reshape(-1, *root_inverse.shape)
-    far = product(0, table, root, high, low)
+    (far,) = product((0,), table, root, high, low)
     passed = lax.ppermute(far, ("y", "core"), opposite(4))
-    first = product(1, table, root, high, low)
+    (first,) = product((1,), table, root, high, low)
     back = lax.ppermute(first, ("y", "core"), opposite(4, -1))
-    second = product(2, table, root, high, low)
+    second, home = product((2, 3), table, root, high, low)
     last, last_sums = weigh(9, second, passed, high, low)
-    table, last, last_sums = lax.optimization_barrier((table, last, last_sums))
     last_sums = lax.ppermute(last_sums, ("y", "core"), opposite(4))
-    home = product(3, table, root, high, low)
-    last, home, last_sums = lax.optimization_barrier((last, home, last_sums))
+    last, last_sums = lax.optimization_barrier((last, last_sums))
     forth = lax.ppermute(last, ("y", "core"), opposite(4))
     kept, sums = weigh(8, home, back, high, low)
     sums = lax.all_to_all(

time: 190 us -> 190 us (level); the launches traced: 189 us -> 186 us
  waiting for transfers between devices: 61.6 us -> 71.4 us
  local copies, waits for them, and re-layouts: 13.4 us -> 4.94 us
  Pallas kernels: 41.1 us -> 38.6 us
    all_gather x1, waiting for transfers between devices: 3.03 us -> 17.2 us  [per_device(): root = lax.all_gather(root_inverse, ('zh', 'zl'), axis=0, tiled=False)]
    ppermute x1, waiting for transfers between devices: 9.29 us -> 1.97 us  [per_device(): near_beside = lax.ppermute(beside, ('x', 'core'), along_x)]
    ppermute x1, waiting for transfers between devices: 1.74 us -> 8.28 us  [per_device(): far = lax.ppermute(near, ('x', 'core'), along_x)]
    unnamed x8 -> x2, local copies, waits for them, and re-layouts: 7.21 us -> 1.27 us
    ppermute x1, waiting for transfers between devices: 28.6 us -> 24.6 us  [per_device(): own = lax.ppermute(coupling[0], ('y', 'x', 'core'), pairs)]
    all_to_all x1, starting transfers between devices: 7.58 us -> 4.37 us  [per_device(): lax.all_to_all(jnp.broadcast_to(sums + last_sums, (8, cols)), ('x', 'core...]
    ppermute x1, starting transfers between devices: 1.92 us -> 4.81 us  [per_device(): forth = lax.ppermute(last, ('y', 'core'), opposite(4))]
    ppermute x1, waiting for transfers between devices: 14.4 us -> 11.7 us  [per_device(): near = lax.ppermute(own, ('x', 'core'), along_x)]
  transfers between devices with their start and end apart: 15 -> 15, of which waited for: 6 -> 8; matrix products, arithmetic and copies ran while one was open for 6% -> 4% of each run, Pallas kernels for 18% -> 17%
where the time goes in v8:
time: 190 us; the launch traced here: 186 us
  waiting for transfers between devices  71.4 us (38%)
  starting transfers between devices  51.7 us (27%)
  Pallas kernels  38.6 us (20%)
  between operations  14.3 us (8%)
  local copies, waits for them, and re-layouts  4.94 us (3%)
  other arithmetic  3.7 us (2%)
    pallas_call x3, Pallas kernels, product(): pl.pallas_call(functools.partial(product_kernel, calls), out_shape=[jax.S...  25 us
    ppermute x1, waiting for transfers between devices, per_device(): own = lax.ppermute(coupling[0], ('y', 'x', 'core'), pairs)  24.6 us
    all_gather x1, waiting for transfers between devices, per_device(): root = lax.all_gather(root_inverse, ('zh', 'zl'), axis=0, tiled=False)  17.2 us
    ppermute x3, starting transfers between devices, per_device(): pieces += [lax.ppermute(p, 'core', CORES) for p in (near, near_beside, far)]  13 us
    ppermute x1, waiting for transfers between devices, per_device(): near = lax.ppermute(own, ('x', 'core'), along_x)  11.7 us
    pallas_call x1, Pallas kernels, spread(): pl.pallas_call(spread_kernel, out_shape=[pltpu.HBM(shape, jnp.bfloat16)]...  10.5 us
    ppermute x1, waiting for transfers between devices, per_device(): far = lax.ppermute(near, ('x', 'core'), along_x)  8.28 us
    ppermute x1, starting transfers between devices, per_device(): forth = lax.ppermute(last, ('y', 'core'), opposite(4))  4.81 us
  transfers between devices with their start and end apart: 15, of which 8 were waited for; matrix products, arithmetic and copies ran while one was open for 4% of the time, Pallas kernels for 17%

profile of v8, /device:TPU:1, one launch (start us, length us, event | category | flops | bytes accessed | tf_op | source)
XLA Modules:
  0.0 186.4 jit_solution(2729079364085023052)
XLA Ops:
  7.2 0.0 all-gather.3.cloned.1.call-start
  7.2 0.7 all-gather.3.cloned.1.call-update
  7.9 4.6 %collective-permute-start = (f32[768,384]{1,0:T(8,128)}, f32[768,384]{1,0:T(8,128)S(1)}, u32[]{:S(2)}, u32[]{:S(2)}) collective-permute-start(f32[768,384]{1,0:T(8,128)} %bitcast.20), channel_id=1, source_target_pairs={{0,48},{8,64},{16,144},{24,224},{32,32},{40,112},{48,176},{56,240}... | collective-permute-start | bytes 3538952 | tf_op jit(solution)/shard_map/ppermute | solution.py:321
  12.5 1.0 slice.3
  13.6 1.0 reshape.109.rows_ref
  14.5 0.1 reshape.108
  14.6 0.7 fusion.2
  15.3 0.1 copy.18
  15.4 0.1 pad_add_fusion
  15.5 0.1 copy.17
  15.6 0.1 concatenate.16.table
  15.7 0.7 and_bitcast_fusion
  16.4 0.1 fusion.5.start_row
  16.5 24.6 %collective-permute-done.rest_0_ = f32[768,384]{1,0:T(8,128)S(1)} collective-permute-done((f32[768,384]{1,0:T(8,128)}, f32[768,384]{1,0:T(8,128)S(1)}, u32[]{:S(2)}, u32[]{:S(2)}) %collective-permute-start) | collective-permute-done | bytes 1179680 | tf_op jit(solution)/shard_map/ppermute | solution.py:321
  41.1 1.9 %collective-permute-start.1 = (f32[768,384]{1,0:T(8,128)S(1)}, f32[768,384]{1,0:T(8,128)S(1)}, u32[]{:S(2)}, u32[]{:S(2)}) collective-permute-start(f32[768,384]{1,0:T(8,128)S(1)} %collective-permute-done.rest_0_), channel_id=1, source_target_pairs={{0,8},{8,0},{1,9},{9,1},{2,10},{10,2},{3,11},{11,3},{4,12},{12,4},... | collective-permute-start | bytes 3538952 | tf_op jit(solution)/shard_map/ppermute | solution.py:325
  43.0 3.2 %collective-permute-start.2 = (f32[768,384]{1,0:T(8,128)S(1)}, f32[768,384]{1,0:T(8,128)S(1)}, u32[]{:S(2)}, u32[]{:S(2)}) collective-permute-start(f32[768,384]{1,0:T(8,128)S(1)} %collective-permute-done.rest_0_), channel_id=1, source_target_pairs={{0,16},{8,56},{16,32},{24,8},{32,48},{40,24},{48,0},{56,40},{1,17}... | collective-permute-start | bytes 3538952 | tf_op jit(solution)/shard_map/ppermute | solution.py:326
  46.2 0.0 collective-permute-done.1.rest_1_
  46.2 2.4 %collective-permute-start.3 = (f32[768,384]{1,0:T(8,128)S(1)}, f32[768,384]{1,0:T(8,128)S(1)}, u32[]{:S(2)}, u32[]{:S(2)}) collective-permute-start(f32[768,384]{1,0:T(8,128)S(1)} %collective-permute-done.1.rest_1_), channel_id=1, source_target_pairs={{0,16},{8,56},{16,32},{24,8},{32,48},{40,24},{48,0},{56,40},{1,17}... | collective-permute-start | bytes 3538952 | tf_op jit(solution)/shard_map/ppermute | solution.py:327
  48.6 11.7 %collective-permute-done.2.rest_2_ = f32[768,384]{1,0:T(8,128)S(1)} collective-permute-done((f32[768,384]{1,0:T(8,128)S(1)}, f32[768,384]{1,0:T(8,128)S(1)}, u32[]{:S(2)}, u32[]{:S(2)}) %collective-permute-start.2) | collective-permute-done | bytes 1179680 | tf_op jit(solution)/shard_map/ppermute | solution.py:326
  60.3 4.4 %collective-permute-start.4 = (f32[768,384]{1,0:T(8,128)S(1)}, f32[768,384]{1,0:T(8,128)S(1)}, u32[]{:S(2)}, u32[]{:S(2)}) collective-permute-start(f32[768,384]{1,0:T(8,128)S(1)} %collective-permute-done.2.rest_2_), channel_id=1, source_target_pairs={{0,16},{8,56},{16,32},{24,8},{32,48},{40,24},{48,0},{56,40},{1,17}... | collective-permute-start | bytes 3538952 | tf_op jit(solution)/shard_map/ppermute | solution.py:328
  64.7 1.9 %collective-permute-start.8 = (f32[768,384]{1,0:T(8,128)}, f32[768,384]{1,0:T(8,128)S(1)}, u32[]{:S(2)}, u32[]{:S(2)}) collective-permute-start(f32[768,384]{1,0:T(8,128)} %bitcast.21), channel_id=1, source_target_pairs={{0,192},{8,72},{64,0},{72,136},{128,64},{136,200},{192,128},{200,8... | collective-permute-start | bytes 3538952 | tf_op jit(solution)/shard_map/ppermute | solution.py:331
  66.7 4.3 %collective-permute-start.5 = (f32[768,384]{1,0:T(8,128)S(1)}, f32[768,384]{1,0:T(8,128)S(1)}, u32[]{:S(2)}, u32[]{:S(2)}) collective-permute-start(f32[768,384]{1,0:T(8,128)S(1)} %collective-permute-done.2.rest_2_), channel_id=1, source_target_pairs={{0,8},{8,0},{1,9},{9,1},{2,10},{10,2},{3,11},{11,3},{4,12},{12,4},... | collective-permute-start | bytes 3538952 | tf_op jit(solution)/shard_map/ppermute | solution.py:330
  71.0 2.0 %collective-permute-done.3.rest_3_ = f32[768,384]{1,0:T(8,128)S(1)} collective-permute-done((f32[768,384]{1,0:T(8,128)S(1)}, f32[768,384]{1,0:T(8,128)S(1)}, u32[]{:S(2)}, u32[]{:S(2)}) %collective-permute-start.3) | collective-permute-done | bytes 1179680 | tf_op jit(solution)/shard_map/ppermute | solution.py:327
  73.0 4.4 %collective-permute-start.6 = (f32[768,384]{1,0:T(8,128)S(1)}, f32[768,384]{1,0:T(8,128)S(1)}, u32[]{:S(2)}, u32[]{:S(2)}) collective-permute-start(f32[768,384]{1,0:T(8,128)S(1)} %collective-permute-done.3.rest_3_), channel_id=1, source_target_pairs={{0,8},{8,0},{1,9},{9,1},{2,10},{10,2},{3,11},{11,3},{4,12},{12,4},... | collective-permute-start | bytes 3538952 | tf_op jit(solution)/shard_map/ppermute | solution.py:330
  77.3 8.3 %collective-permute-done.4.rest_4_ = f32[768,384]{1,0:T(8,128)S(1)} collective-permute-done((f32[768,384]{1,0:T(8,128)S(1)}, f32[768,384]{1,0:T(8,128)S(1)}, u32[]{:S(2)}, u32[]{:S(2)}) %collective-permute-start.4) | collective-permute-done | bytes 1179680 | tf_op jit(solution)/shard_map/ppermute | solution.py:328
  85.6 4.4 %collective-permute-start.7 = (f32[768,384]{1,0:T(8,128)S(1)}, f32[768,384]{1,0:T(8,128)S(1)}, u32[]{:S(2)}, u32[]{:S(2)}) collective-permute-start(f32[768,384]{1,0:T(8,128)S(1)} %collective-permute-done.4.rest_4_), channel_id=1, source_target_pairs={{0,8},{8,0},{1,9},{9,1},{2,10},{10,2},{3,11},{11,3},{4,12},{12,4},... | collective-permute-start | bytes 3538952 | tf_op jit(solution)/shard_map/ppermute | solution.py:330
  90.0 0.0 collective-permute-done.8.rest_9_
  90.0 0.0 collective-permute-done.5.rest_5_
  90.0 0.0 collective-permute-done.6.rest_6_
  90.0 2.4 %collective-permute-done.7.rest_7_ = f32[768,384]{1,0:T(8,128)S(1)} collective-permute-done((f32[768,384]{1,0:T(8,128)S(1)}, f32[768,384]{1,0:T(8,128)S(1)}, u32[]{:S(2)}, u32[]{:S(2)}) %collective-permute-start.7) | collective-permute-done | bytes 1179680 | tf_op jit(solution)/shard_map/ppermute | solution.py:330
  92.4 0.0 copy-start
  92.4 1.3 copy-done
  93.7 10.5 %shard_map.77 = (bf16[10,768,384]{2,1,0:T(8,128)(2,1)}, bf16[10,768,384]{2,1,0:T(8,128)(2,1)}) custom-call(s32[10]{0:T(128)S(1)} %fusion.5.start_row, s32[384,128]{1,0:T(8,128)S(1)} %reshape.109.rows_ref, f32[768,384]{1,0:T(8,128)S(1)} %collective-permute-done.rest_0_, f32[768,384]{1,0:T(8,128)S(1)} %collective-permute-done.1.rest_1_, ...), custom_call_target="tpu_custom_call" | custom-call | flops 1509949440 | bytes 23592960 | tf_op jit(solution)/shard_map/pallas_call | solution.py:125
  104.2 17.2 %all-gather.3.cloned.1.call-done = f32[16384,128]{1,0:T(8,128)} async-done(((f32[1024,128]{1,0:T(8,128)}), f32[16384,128]{1,0:T(8,128)}) %all-gather.3.cloned.1.call-update) | async-done | bytes 8388624 | tf_op jit(solution)/shard_map/all_gather | solution.py:297
  121.4 6.9 %shard_map.81 = f32[768,384]{1,0:T(8,128)S(1)} custom-call(s32[4,21]{1,0:T(4,128)S(1)} %concatenate.16.table, f32[16,1024,128]{2,1,0:T(8,128)} %bitcast.23, bf16[10,768,384]{2,1,0:T(8,128)(2,1)} %get-tuple-element.22.high_hbm, bf16[10,768,384]{2,1,0:T(8,128)(2,1)} %get-tuple-element.23.low_hbm), custom_call_target="tpu_custom_call" | custom-call | flops 2717908992 | bytes 7077888 | tf_op jit(solution)/shard_map/pallas_call | solution.py:218
  128.2 4.5 %collective-permute-start.10 = (f32[768,384]{1,0:T(8,128)S(1)}, f32[768,384]{1,0:T(8,128)S(1)}, u32[]{:S(2)}, u32[]{:S(2)}) collective-permute-start(f32[768,384]{1,0:T(8,128)S(1)} %shard_map.81), channel_id=1, source_target_pairs={{0,64},{8,200},{64,128},{72,8},{128,192},{136,72},{192,0},{200,136... | collective-permute-start | bytes 3538952 | tf_op jit(solution)/shard_map/ppermute | solution.py:336
  132.8 6.9 %shard_map.79 = f32[768,384]{1,0:T(8,128)S(1)} custom-call(s32[4,21]{1,0:T(4,128)S(1)} %concatenate.16.table, f32[16,1024,128]{2,1,0:T(8,128)} %bitcast.24, bf16[10,768,384]{2,1,0:T(8,128)(2,1)} %get-tuple-element.22.high_hbm, bf16[10,768,384]{2,1,0:T(8,128)(2,1)} %get-tuple-element.23.low_hbm), custom_call_target="tpu_custom_call" | custom-call | flops 2717908992 | bytes 7077888 | tf_op jit(solution)/shard_map/pallas_call | solution.py:218
  139.7 1.9 %collective-permute-start.9 = (f32[768,384]{1,0:T(8,128)S(1)}, f32[768,384]{1,0:T(8,128)S(1)}, u32[]{:S(2)}, u32[]{:S(2)}) collective-permute-start(f32[768,384]{1,0:T(8,128)S(1)} %shard_map.79), channel_id=1, source_target_pairs={{0,192},{8,72},{64,0},{72,136},{128,64},{136,200},{192,128},{200,8... | collective-permute-start | bytes 3538952 | tf_op jit(solution)/shard_map/ppermute | solution.py:338
  141.6 11.3 %shard_map.78 = (f32[768,384]{1,0:T(8,128)S(1)}, f32[768,384]{1,0:T(8,128)S(1)}) custom-call(s32[4,21]{1,0:T(4,128)S(1)} %concatenate.16.table, f32[16,1024,128]{2,1,0:T(8,128)} %bitcast.25, bf16[10,768,384]{2,1,0:T(8,128)(2,1)} %get-tuple-element.22.high_hbm, bf16[10,768,384]{2,1,0:T(8,128)(2,1)} %get-tuple-element.23.low_hbm), custom_call_target="tpu_custom_call" | custom-call | flops 5435817984 | bytes 14155776 | tf_op jit(solution)/shard_map/pallas_call | solution.py:218
  152.8 0.0 collective-permute-done.10.second
  152.9 1.6 shard_map.82
  154.4 4.6 %collective-permute-start.11 = (f32[1,384]{1,0:T(1,128)S(1)}, f32[1,384]{1,0:T(1,128)S(1)}, u32[]{:S(2)}, u32[]{:S(2)}) collective-permute-start(f32[1,384]{1,0:T(1,128)S(1)} %get-tuple-element.29), channel_id=1, source_target_pairs={{0,64},{8,200},{64,128},{72,8},{128,192},{136,72},{192,0},{200,136... | collective-permute-start | bytes 4616 | tf_op jit(solution)/shard_map/ppermute | solution.py:341
  159.0 0.7 collective-permute-done.11
  159.7 4.8 %collective-permute-start.12 = (f32[768,384]{1,0:T(8,128)S(1)}, f32[768,384]{1,0:T(8,128)S(1)}, u32[]{:S(2)}, u32[]{:S(2)}) collective-permute-start(f32[768,384]{1,0:T(8,128)S(1)} %get-tuple-element.32), channel_id=1, source_target_pairs={{0,64},{8,200},{64,128},{72,8},{128,192},{136,72},{192,0},{200,136... | collective-permute-start | bytes 3538952 | tf_op jit(solution)/shard_map/ppermute | solution.py:343
  164.5 0.0 collective-permute-done.9.second
  164.6 1.6 shard_map.80
  166.2 0.6 broadcast_in_dim.15
  166.8 4.4 %all-to-all-start = ((f32[8,1,384]{2,1,0:T(1,128)}), f32[8,1,384]{2,1,0:T(1,128)S(1)}, u32[]{:S(2)}, u32[]{:S(2)}) async-start(f32[8,1,384]{2,1,0:T(1,128)} %broadcast_in_dim.15), calls=%async_computation | async-start | bytes 24576 | tf_op jit(solution)/shard_map/all_to_all | solution.py:345
  171.2 0.8 fusion.1
  172.0 3.8 %all-to-all-done = f32[8,1,384]{2,1,0:T(1,128)S(1)} async-done(((f32[8,1,384]{2,1,0:T(1,128)}), f32[8,1,384]{2,1,0:T(1,128)S(1)}, u32[]{:S(2)}, u32[]{:S(2)}) %all-to-all-start) | async-done | bytes 12320 | tf_op jit(solution)/shard_map/all_to_all | solution.py:345
  175.8 0.6 reduce_sum.9
  176.4 1.3 reshape_add_fusion
  177.7 0.0 collective-permute-done.12
  177.7 0.1 add.122
  177.8 1.8 convolution_negate_fusion
  (4 shorter events, 0.0 us)
Async XLA Ops:
  7.2 114.2 %all-gather.3.cloned.1.call-start = ((), (), s32[]{:S(2)}) async-start(), calls=%async_computation.1 | async-start | bytes 8912896 | tf_op jit(solution)/shard_map/all_gather | solution.py:297
  7.9 33.2 %collective-permute-start = (f32[768,384]{1,0:T(8,128)}, f32[768,384]{1,0:T(8,128)S(1)}, u32[]{:S(2)}, u32[]{:S(2)}) collective-permute-start(f32[768,384]{1,0:T(8,128)} %bitcast.20), channel_id=1, source_target_pairs={{0,48},{8,64},{16,144},{24,224},{32,32},{40,112},{48,176},{56,240}... | collective-permute-start | bytes 3538952 | tf_op jit(solution)/shard_map/ppermute | solution.py:321
  41.1 5.1 %collective-permute-start.1 = (f32[768,384]{1,0:T(8,128)S(1)}, f32[768,384]{1,0:T(8,128)S(1)}, u32[]{:S(2)}, u32[]{:S(2)}) collective-permute-start(f32[768,384]{1,0:T(8,128)S(1)} %collective-permute-done.rest_0_), channel_id=1, source_target_pairs={{0,8},{8,0},{1,9},{9,1},{2,10},{10,2},{3,11},{11,3},{4,12},{12,4},... | collective-permute-start | bytes 3538952 | tf_op jit(solution)/shard_map/ppermute | solution.py:325
  43.0 17.3 %collective-permute-start.2 = (f32[768,384]{1,0:T(8,128)S(1)}, f32[768,384]{1,0:T(8,128)S(1)}, u32[]{:S(2)}, u32[]{:S(2)}) collective-permute-start(f32[768,384]{1,0:T(8,128)S(1)} %collective-permute-done.rest_0_), channel_id=1, source_target_pairs={{0,16},{8,56},{16,32},{24,8},{32,48},{40,24},{48,0},{56,40},{1,17}... | collective-permute-start | bytes 3538952 | tf_op jit(solution)/shard_map/ppermute | solution.py:326
  46.2 26.8 %collective-permute-start.3 = (f32[768,384]{1,0:T(8,128)S(1)}, f32[768,384]{1,0:T(8,128)S(1)}, u32[]{:S(2)}, u32[]{:S(2)}) collective-permute-start(f32[768,384]{1,0:T(8,128)S(1)} %collective-permute-done.1.rest_1_), channel_id=1, source_target_pairs={{0,16},{8,56},{16,32},{24,8},{32,48},{40,24},{48,0},{56,40},{1,17}... | collective-permute-start | bytes 3538952 | tf_op jit(solution)/shard_map/ppermute | solution.py:327
  60.3 25.3 %collective-permute-start.4 = (f32[768,384]{1,0:T(8,128)S(1)}, f32[768,384]{1,0:T(8,128)S(1)}, u32[]{:S(2)}, u32[]{:S(2)}) collective-permute-start(f32[768,384]{1,0:T(8,128)S(1)} %collective-permute-done.2.rest_2_), channel_id=1, source_target_pairs={{0,16},{8,56},{16,32},{24,8},{32,48},{40,24},{48,0},{56,40},{1,17}... | collective-permute-start | bytes 3538952 | tf_op jit(solution)/shard_map/ppermute | solution.py:328
  64.7 25.2 %collective-permute-start.8 = (f32[768,384]{1,0:T(8,128)}, f32[768,384]{1,0:T(8,128)S(1)}, u32[]{:S(2)}, u32[]{:S(2)}) collective-permute-start(f32[768,384]{1,0:T(8,128)} %bitcast.21), channel_id=1, source_target_pairs={{0,192},{8,72},{64,0},{72,136},{128,64},{136,200},{192,128},{200,8... | collective-permute-start | bytes 3538952 | tf_op jit(solution)/shard_map/ppermute | solution.py:331
  66.7 23.3 %collective-permute-start.5 = (f32[768,384]{1,0:T(8,128)S(1)}, f32[768,384]{1,0:T(8,128)S(1)}, u32[]{:S(2)}, u32[]{:S(2)}) collective-permute-start(f32[768,384]{1,0:T(8,128)S(1)} %collective-permute-done.2.rest_2_), channel_id=1, source_target_pairs={{0,8},{8,0},{1,9},{9,1},{2,10},{10,2},{3,11},{11,3},{4,12},{12,4},... | collective-permute-start | bytes 3538952 | tf_op jit(solution)/shard_map/ppermute | solution.py:330
  73.0 17.0 %collective-permute-start.6 = (f32[768,384]{1,0:T(8,128)S(1)}, f32[768,384]{1,0:T(8,128)S(1)}, u32[]{:S(2)}, u32[]{:S(2)}) collective-permute-start(f32[768,384]{1,0:T(8,128)S(1)} %collective-permute-done.3.rest_3_), channel_id=1, source_target_pairs={{0,8},{8,0},{1,9},{9,1},{2,10},{10,2},{3,11},{11,3},{4,12},{12,4},... | collective-permute-start | bytes 3538952 | tf_op jit(solution)/shard_map/ppermute | solution.py:330
  85.6 6.8 %collective-permute-start.7 = (f32[768,384]{1,0:T(8,128)S(1)}, f32[768,384]{1,0:T(8,128)S(1)}, u32[]{:S(2)}, u32[]{:S(2)}) collective-permute-start(f32[768,384]{1,0:T(8,128)S(1)} %collective-permute-done.4.rest_4_), channel_id=1, source_target_pairs={{0,8},{8,0},{1,9},{9,1},{2,10},{10,2},{3,11},{11,3},{4,12},{12,4},... | collective-permute-start | bytes 3538952 | tf_op jit(solution)/shard_map/ppermute | solution.py:330
  92.4 1.3 copy-start
  128.2 24.6 %collective-permute-start.10 = (f32[768,384]{1,0:T(8,128)S(1)}, f32[768,384]{1,0:T(8,128)S(1)}, u32[]{:S(2)}, u32[]{:S(2)}) collective-permute-start(f32[768,384]{1,0:T(8,128)S(1)} %shard_map.81), channel_id=1, source_target_pairs={{0,64},{8,200},{64,128},{72,8},{128,192},{136,72},{192,0},{200,136... | collective-permute-start | bytes 3538952 | tf_op jit(solution)/shard_map/ppermute | solution.py:336
  139.7 24.9 %collective-permute-start.9 = (f32[768,384]{1,0:T(8,128)S(1)}, f32[768,384]{1,0:T(8,128)S(1)}, u32[]{:S(2)}, u32[]{:S(2)}) collective-permute-start(f32[768,384]{1,0:T(8,128)S(1)} %shard_map.79), channel_id=1, source_target_pairs={{0,192},{8,72},{64,0},{72,136},{128,64},{136,200},{192,128},{200,8... | collective-permute-start | bytes 3538952 | tf_op jit(solution)/shard_map/ppermute | solution.py:338
  154.4 5.3 %collective-permute-start.11 = (f32[1,384]{1,0:T(1,128)S(1)}, f32[1,384]{1,0:T(1,128)S(1)}, u32[]{:S(2)}, u32[]{:S(2)}) collective-permute-start(f32[1,384]{1,0:T(1,128)S(1)} %get-tuple-element.29), channel_id=1, source_target_pairs={{0,64},{8,200},{64,128},{72,8},{128,192},{136,72},{192,0},{200,136... | collective-permute-start | bytes 4616 | tf_op jit(solution)/shard_map/ppermute | solution.py:341
  159.7 17.9 %collective-permute-start.12 = (f32[768,384]{1,0:T(8,128)S(1)}, f32[768,384]{1,0:T(8,128)S(1)}, u32[]{:S(2)}, u32[]{:S(2)}) collective-permute-start(f32[768,384]{1,0:T(8,128)S(1)} %get-tuple-element.32), channel_id=1, source_target_pairs={{0,64},{8,200},{64,128},{72,8},{128,192},{136,72},{192,0},{200,136... | collective-permute-start | bytes 3538952 | tf_op jit(solution)/shard_map/ppermute | solution.py:343
  166.8 9.0 %all-to-all-start = ((f32[8,1,384]{2,1,0:T(1,128)}), f32[8,1,384]{2,1,0:T(1,128)S(1)}, u32[]{:S(2)}, u32[]{:S(2)}) async-start(f32[8,1,384]{2,1,0:T(1,128)} %broadcast_in_dim.15), calls=%async_computation | async-start | bytes 24576 | tf_op jit(solution)/shard_map/all_to_all | solution.py:345
Sparse Core Ops, SparseCore 0:
  10.1 111.2 all-gather.2

commit v9 on v8

--- a/solution.py
+++ b/solution.py
@@ -332,11 +332,11 @@
     high, low = spread(start_row, rows_of, pieces)
 
     root = root.reshape(-1, *root_inverse.shape)
-    (far,) = product((0,), table, root, high, low)
+    far, first = product((0, 1), table, root, high, low)
     passed = lax.ppermute(far, ("y", "core"), opposite(4))
-    (first,) = product((1,), table, root, high, low)
+    second, home = product((2, 3), table, root, high, low)
+    first, second = lax.optimization_barrier((first, second))
     back = lax.ppermute(first, ("y", "core"), opposite(4, -1))
-    second, home = product((2, 3), table, root, high, low)
     last, last_sums = weigh(9, second, passed, high, low)
     last_sums = lax.ppermute(last_sums, ("y", "core"), opposite(4))
     last, last_sums = lax.optimization_barrier((last, last_sums))

time: 190 us -> 193 us (1.016); the launches traced: 186 us -> 192 us
  starting transfers between devices: 51.7 us -> 55.6 us
  waiting for transfers between devices: 71.4 us -> 75.3 us
  Pallas kernels: 38.6 us -> 36.2 us
    ppermute x1, waiting for transfers between devices: 0.01 us -> 3.97 us  [per_device(): back = lax.ppermute(first, ('y', 'core'), opposite(4, -1))]
    all_to_all x1, starting transfers between devices: 4.37 us -> 7.63 us  [per_device(): lax.all_to_all(jnp.broadcast_to(sums + last_sums, (8, cols)), ('x', 'core...]
    pallas_call x3 -> x2, Pallas kernels: 25 us -> 22.5 us  [product(): pl.pallas_call(functools.partial(product_kernel, calls), out_shape=[jax.S...]
  transfers between devices with their start and end apart: 15 -> 15, of which waited for: 8 -> 9; matrix products, arithmetic and copies ran while one was open for 4% -> 4% of each run, Pallas kernels for 17% -> 13%
where the time goes in v9:
time: 193 us; the launch traced here: 192 us
  waiting for transfers between devices  75.3 us (39%)
  starting transfers between devices  55.6 us (29%)
  Pallas kernels  36.2 us (19%)
  between operations  14.3 us (7%)
  local copies, waits for them, and re-layouts  4.94 us (3%)
  other arithmetic  3.7 us (2%)
    ppermute x1, waiting for transfers between devices, per_device(): own = lax.ppermute(coupling[0], ('y', 'x', 'core'), pairs)  24.6 us
    pallas_call x2, Pallas kernels, product(): pl.pallas_call(functools.partial(product_kernel, calls), out_shape=[jax.S...  22.5 us
    all_gather x1, waiting for transfers between devices, per_device(): root = lax.all_gather(root_inverse, ('zh', 'zl'), axis=0, tiled=False)  17.2 us
    ppermute x3, starting transfers between devices, per_device(): pieces += [lax.ppermute(p, 'core', CORES) for p in (near, near_beside, far)]  13 us
    ppermute x1, waiting for transfers between devices, per_device(): near = lax.ppermute(own, ('x', 'core'), along_x)  11.7 us
    pallas_call x1, Pallas kernels, spread(): pl.pallas_call(spread_kernel, out_shape=[pltpu.HBM(shape, jnp.bfloat16)]...  10.5 us
    ppermute x1, waiting for transfers between devices, per_device(): far = lax.ppermute(near, ('x', 'core'), along_x)  8.28 us
    all_to_all x1, starting transfers between devices, per_device(): lax.all_to_all(jnp.broadcast_to(sums + last_sums, (8, cols)), ('x', 'core...  7.63 us
  transfers between devices with their start and end apart: 15, of which 9 were waited for; matrix products, arithmetic and copies ran while one was open for 4% of the time, Pallas kernels for 13%

profile of v9, /device:TPU:1, one launch (start us, length us, event | category | flops | bytes accessed | tf_op | source)
XLA Modules:
  0.0 191.7 jit_solution(6962239837756242726)
XLA Ops:
  7.2 0.0 all-gather.3.cloned.1.call-start
  7.2 0.7 all-gather.3.cloned.1.call-update
  7.9 4.6 %collective-permute-start = (f32[768,384]{1,0:T(8,128)}, f32[768,384]{1,0:T(8,128)S(1)}, u32[]{:S(2)}, u32[]{:S(2)}) collective-permute-start(f32[768,384]{1,0:T(8,128)} %bitcast.20), channel_id=1, source_target_pairs={{0,48},{8,64},{16,144},{24,224},{32,32},{40,112},{48,176},{56,240}... | collective-permute-start | bytes 3538952 | tf_op jit(solution)/shard_map/ppermute | solution.py:321
  12.5 1.0 slice.3
  13.6 1.0 reshape.109.rows_ref
  14.5 0.1 reshape.108
  14.6 0.7 fusion.2
  15.3 0.1 copy.18
  15.4 0.1 pad_add_fusion
  15.5 0.1 copy.17
  15.6 0.1 concatenate.16.table
  15.7 0.7 and_bitcast_fusion
  16.4 0.1 fusion.5.start_row
  16.5 24.6 %collective-permute-done.rest_0_ = f32[768,384]{1,0:T(8,128)S(1)} collective-permute-done((f32[768,384]{1,0:T(8,128)}, f32[768,384]{1,0:T(8,128)S(1)}, u32[]{:S(2)}, u32[]{:S(2)}) %collective-permute-start) | collective-permute-done | bytes 1179680 | tf_op jit(solution)/shard_map/ppermute | solution.py:321
  41.1 1.9 collective-permute-start.1
  43.0 3.2 %collective-permute-start.2 = (f32[768,384]{1,0:T(8,128)S(1)}, f32[768,384]{1,0:T(8,128)S(1)}, u32[]{:S(2)}, u32[]{:S(2)}) collective-permute-start(f32[768,384]{1,0:T(8,128)S(1)} %collective-permute-done.rest_0_), channel_id=1, source_target_pairs={{0,16},{8,56},{16,32},{24,8},{32,48},{40,24},{48,0},{56,40},{1,17}... | collective-permute-start | bytes 3538952 | tf_op jit(solution)/shard_map/ppermute | solution.py:326
  46.2 0.0 collective-permute-done.1.rest_1_
  46.2 2.4 %collective-permute-start.3 = (f32[768,384]{1,0:T(8,128)S(1)}, f32[768,384]{1,0:T(8,128)S(1)}, u32[]{:S(2)}, u32[]{:S(2)}) collective-permute-start(f32[768,384]{1,0:T(8,128)S(1)} %collective-permute-done.1.rest_1_), channel_id=1, source_target_pairs={{0,16},{8,56},{16,32},{24,8},{32,48},{40,24},{48,0},{56,40},{1,17}... | collective-permute-start | bytes 3538952 | tf_op jit(solution)/shard_map/ppermute | solution.py:327
  48.6 11.7 %collective-permute-done.2.rest_2_ = f32[768,384]{1,0:T(8,128)S(1)} collective-permute-done((f32[768,384]{1,0:T(8,128)S(1)}, f32[768,384]{1,0:T(8,128)S(1)}, u32[]{:S(2)}, u32[]{:S(2)}) %collective-permute-start.2) | collective-permute-done | bytes 1179680 | tf_op jit(solution)/shard_map/ppermute | solution.py:326
  60.3 4.4 %collective-permute-start.4 = (f32[768,384]{1,0:T(8,128)S(1)}, f32[768,384]{1,0:T(8,128)S(1)}, u32[]{:S(2)}, u32[]{:S(2)}) collective-permute-start(f32[768,384]{1,0:T(8,128)S(1)} %collective-permute-done.2.rest_2_), channel_id=1, source_target_pairs={{0,16},{8,56},{16,32},{24,8},{32,48},{40,24},{48,0},{56,40},{1,17}... | collective-permute-start | bytes 3538952 | tf_op jit(solution)/shard_map/ppermute | solution.py:328
  64.7 1.9 %collective-permute-start.8 = (f32[768,384]{1,0:T(8,128)}, f32[768,384]{1,0:T(8,128)S(1)}, u32[]{:S(2)}, u32[]{:S(2)}) collective-permute-start(f32[768,384]{1,0:T(8,128)} %bitcast.21), channel_id=1, source_target_pairs={{0,192},{8,72},{64,0},{72,136},{128,64},{136,200},{192,128},{200,8... | collective-permute-start | bytes 3538952 | tf_op jit(solution)/shard_map/ppermute | solution.py:331
  66.7 4.3 %collective-permute-start.5 = (f32[768,384]{1,0:T(8,128)S(1)}, f32[768,384]{1,0:T(8,128)S(1)}, u32[]{:S(2)}, u32[]{:S(2)}) collective-permute-start(f32[768,384]{1,0:T(8,128)S(1)} %collective-permute-done.2.rest_2_), channel_id=1, source_target_pairs={{0,8},{8,0},{1,9},{9,1},{2,10},{10,2},{3,11},{11,3},{4,12},{12,4},... | collective-permute-start | bytes 3538952 | tf_op jit(solution)/shard_map/ppermute | solution.py:330
  71.0 2.0 %collective-permute-done.3.rest_3_ = f32[768,384]{1,0:T(8,128)S(1)} collective-permute-done((f32[768,384]{1,0:T(8,128)S(1)}, f32[768,384]{1,0:T(8,128)S(1)}, u32[]{:S(2)}, u32[]{:S(2)}) %collective-permute-start.3) | collective-permute-done | bytes 1179680 | tf_op jit(solution)/shard_map/ppermute | solution.py:327
  73.0 4.4 %collective-permute-start.6 = (f32[768,384]{1,0:T(8,128)S(1)}, f32[768,384]{1,0:T(8,128)S(1)}, u32[]{:S(2)}, u32[]{:S(2)}) collective-permute-start(f32[768,384]{1,0:T(8,128)S(1)} %collective-permute-done.3.rest_3_), channel_id=1, source_target_pairs={{0,8},{8,0},{1,9},{9,1},{2,10},{10,2},{3,11},{11,3},{4,12},{12,4},... | collective-permute-start | bytes 3538952 | tf_op jit(solution)/shard_map/ppermute | solution.py:330
  77.3 8.3 %collective-permute-done.4.rest_4_ = f32[768,384]{1,0:T(8,128)S(1)} collective-permute-done((f32[768,384]{1,0:T(8,128)S(1)}, f32[768,384]{1,0:T(8,128)S(1)}, u32[]{:S(2)}, u32[]{:S(2)}) %collective-permute-start.4) | collective-permute-done | bytes 1179680 | tf_op jit(solution)/shard_map/ppermute | solution.py:328
  85.6 4.4 %collective-permute-start.7 = (f32[768,384]{1,0:T(8,128)S(1)}, f32[768,384]{1,0:T(8,128)S(1)}, u32[]{:S(2)}, u32[]{:S(2)}) collective-permute-start(f32[768,384]{1,0:T(8,128)S(1)} %collective-permute-done.4.rest_4_), channel_id=1, source_target_pairs={{0,8},{8,0},{1,9},{9,1},{2,10},{10,2},{3,11},{11,3},{4,12},{12,4},... | collective-permute-start | bytes 3538952 | tf_op jit(solution)/shard_map/ppermute | solution.py:330
  90.0 0.0 collective-permute-done.8.rest_9_
  90.0 0.0 collective-permute-done.5.rest_5_
  90.0 0.0 collective-permute-done.6.rest_6_
  90.0 2.4 %collective-permute-done.7.rest_7_ = f32[768,384]{1,0:T(8,128)S(1)} collective-permute-done((f32[768,384]{1,0:T(8,128)S(1)}, f32[768,384]{1,0:T(8,128)S(1)}, u32[]{:S(2)}, u32[]{:S(2)}) %collective-permute-start.7) | collective-permute-done | bytes 1179680 | tf_op jit(solution)/shard_map/ppermute | solution.py:330
  92.4 0.0 copy-start
  92.4 1.3 copy-done
  93.7 10.5 %shard_map.77 = (bf16[10,768,384]{2,1,0:T(8,128)(2,1)}, bf16[10,768,384]{2,1,0:T(8,128)(2,1)}) custom-call(s32[10]{0:T(128)S(1)} %fusion.5.start_row, s32[384,128]{1,0:T(8,128)S(1)} %reshape.109.rows_ref, f32[768,384]{1,0:T(8,128)S(1)} %collective-permute-done.rest_0_, f32[768,384]{1,0:T(8,128)S(1)} %collective-permute-done.1.rest_1_, ...), custom_call_target="tpu_custom_call" | custom-call | flops 1509949440 | bytes 23592960 | tf_op jit(solution)/shard_map/pallas_call | solution.py:125
  104.2 17.2 %all-gather.3.cloned.1.call-done = f32[16384,128]{1,0:T(8,128)} async-done(((f32[1024,128]{1,0:T(8,128)}), f32[16384,128]{1,0:T(8,128)}) %all-gather.3.cloned.1.call-update) | async-done | bytes 8388624 | tf_op jit(solution)/shard_map/all_gather | solution.py:297
  121.4 11.3 %shard_map.79 = (f32[768,384]{1,0:T(8,128)S(1)}, f32[768,384]{1,0:T(8,128)S(1)}) custom-call(s32[4,21]{1,0:T(4,128)S(1)} %concatenate.16.table, f32[16,1024,128]{2,1,0:T(8,128)} %bitcast.23, bf16[10,768,384]{2,1,0:T(8,128)(2,1)} %get-tuple-element.26.high_hbm, bf16[10,768,384]{2,1,0:T(8,128)(2,1)} %get-tuple-element.27.low_hbm), custom_call_target="tpu_custom_call" | custom-call | flops 5435817984 | bytes 14155776 | tf_op jit(solution)/shard_map/pallas_call | solution.py:218
  132.6 4.5 %collective-permute-start.10 = (f32[768,384]{1,0:T(8,128)S(1)}, f32[768,384]{1,0:T(8,128)S(1)}, u32[]{:S(2)}, u32[]{:S(2)}) collective-permute-start(f32[768,384]{1,0:T(8,128)S(1)} %get-tuple-element.35), channel_id=1, source_target_pairs={{0,64},{8,200},{64,128},{72,8},{128,192},{136,72},{192,0},{200,136... | collective-permute-start | bytes 3538952 | tf_op jit(solution)/shard_map/ppermute | solution.py:336
  137.2 11.3 %shard_map.78 = (f32[768,384]{1,0:T(8,128)S(1)}, f32[768,384]{1,0:T(8,128)S(1)}) custom-call(s32[4,21]{1,0:T(4,128)S(1)} %concatenate.16.table, f32[16,1024,128]{2,1,0:T(8,128)} %bitcast.24, bf16[10,768,384]{2,1,0:T(8,128)(2,1)} %get-tuple-element.26.high_hbm, bf16[10,768,384]{2,1,0:T(8,128)(2,1)} %get-tuple-element.27.low_hbm), custom_call_target="tpu_custom_call" | custom-call | flops 5435817984 | bytes 14155776 | tf_op jit(solution)/shard_map/pallas_call | solution.py:218
  148.4 1.9 %collective-permute-start.9 = (f32[768,384]{1,0:T(8,128)S(1)}, f32[768,384]{1,0:T(8,128)S(1)}, u32[]{:S(2)}, u32[]{:S(2)}) collective-permute-start(f32[768,384]{1,0:T(8,128)S(1)} %get-tuple-element.31), channel_id=1, source_target_pairs={{0,192},{8,72},{64,0},{72,136},{128,64},{136,200},{192,128},{200,8... | collective-permute-start | bytes 3538952 | tf_op jit(solution)/shard_map/ppermute | solution.py:339
  150.4 0.0 collective-permute-done.10.second
  150.4 1.6 shard_map.81
  152.0 4.8 %collective-permute-start.11 = (f32[1,384]{1,0:T(1,128)S(1)}, f32[1,384]{1,0:T(1,128)S(1)}, u32[]{:S(2)}, u32[]{:S(2)}) collective-permute-start(f32[1,384]{1,0:T(1,128)S(1)} %get-tuple-element.37), channel_id=1, source_target_pairs={{0,64},{8,200},{64,128},{72,8},{128,192},{136,72},{192,0},{200,136... | collective-permute-start | bytes 4616 | tf_op jit(solution)/shard_map/ppermute | solution.py:341
  156.8 0.7 collective-permute-done.11
  157.5 5.2 %collective-permute-start.12 = (f32[768,384]{1,0:T(8,128)S(1)}, f32[768,384]{1,0:T(8,128)S(1)}, u32[]{:S(2)}, u32[]{:S(2)}) collective-permute-start(f32[768,384]{1,0:T(8,128)S(1)} %get-tuple-element.40), channel_id=1, source_target_pairs={{0,64},{8,200},{64,128},{72,8},{128,192},{136,72},{192,0},{200,136... | collective-permute-start | bytes 3538952 | tf_op jit(solution)/shard_map/ppermute | solution.py:343
  162.7 4.0 %collective-permute-done.9.second = f32[768,384]{1,0:T(8,128)S(1)} collective-permute-done((f32[768,384]{1,0:T(8,128)S(1)}, f32[768,384]{1,0:T(8,128)S(1)}, u32[]{:S(2)}, u32[]{:S(2)}) %collective-permute-start.9) | collective-permute-done | bytes 1179680 | tf_op jit(solution)/shard_map/ppermute | solution.py:339
  166.6 1.6 shard_map.80
  168.2 0.6 broadcast_in_dim.15
  168.8 7.6 %all-to-all-start = ((f32[8,1,384]{2,1,0:T(1,128)}), f32[8,1,384]{2,1,0:T(1,128)S(1)}, u32[]{:S(2)}, u32[]{:S(2)}) async-start(f32[8,1,384]{2,1,0:T(1,128)} %broadcast_in_dim.15), calls=%async_computation | async-start | bytes 24576 | tf_op jit(solution)/shard_map/all_to_all | solution.py:345
  176.5 0.8 fusion.1
  177.3 3.8 %all-to-all-done = f32[8,1,384]{2,1,0:T(1,128)S(1)} async-done(((f32[8,1,384]{2,1,0:T(1,128)}), f32[8,1,384]{2,1,0:T(1,128)S(1)}, u32[]{:S(2)}, u32[]{:S(2)}) %all-to-all-start) | async-done | bytes 12320 | tf_op jit(solution)/shard_map/all_to_all | solution.py:345
  181.1 0.6 reduce_sum.9
  181.7 1.3 reshape_add_fusion
  183.0 0.0 collective-permute-done.12
  183.0 0.1 add.122
  183.1 1.8 convolution_negate_fusion
  (4 shorter events, 0.0 us)
Async XLA Ops:
  7.2 114.2 %all-gather.3.cloned.1.call-start = ((), (), s32[]{:S(2)}) async-start(), calls=%async_computation.1 | async-start | bytes 8912896 | tf_op jit(solution)/shard_map/all_gather | solution.py:297
  7.9 33.2 %collective-permute-start = (f32[768,384]{1,0:T(8,128)}, f32[768,384]{1,0:T(8,128)S(1)}, u32[]{:S(2)}, u32[]{:S(2)}) collective-permute-start(f32[768,384]{1,0:T(8,128)} %bitcast.20), channel_id=1, source_target_pairs={{0,48},{8,64},{16,144},{24,224},{32,32},{40,112},{48,176},{56,240}... | collective-permute-start | bytes 3538952 | tf_op jit(solution)/shard_map/ppermute | solution.py:321
  41.1 5.1 %collective-permute-start.1 = (f32[768,384]{1,0:T(8,128)S(1)}, f32[768,384]{1,0:T(8,128)S(1)}, u32[]{:S(2)}, u32[]{:S(2)}) collective-permute-start(f32[768,384]{1,0:T(8,128)S(1)} %collective-permute-done.rest_0_), channel_id=1, source_target_pairs={{0,8},{8,0},{1,9},{9,1},{2,10},{10,2},{3,11},{11,3},{4,12},{12,4},... | collective-permute-start | bytes 3538952 | tf_op jit(solution)/shard_map/ppermute | solution.py:325
  43.0 17.3 %collective-permute-start.2 = (f32[768,384]{1,0:T(8,128)S(1)}, f32[768,384]{1,0:T(8,128)S(1)}, u32[]{:S(2)}, u32[]{:S(2)}) collective-permute-start(f32[768,384]{1,0:T(8,128)S(1)} %collective-permute-done.rest_0_), channel_id=1, source_target_pairs={{0,16},{8,56},{16,32},{24,8},{32,48},{40,24},{48,0},{56,40},{1,17}... | collective-permute-start | bytes 3538952 | tf_op jit(solution)/shard_map/ppermute | solution.py:326
  46.2 26.8 %collective-permute-start.3 = (f32[768,384]{1,0:T(8,128)S(1)}, f32[768,384]{1,0:T(8,128)S(1)}, u32[]{:S(2)}, u32[]{:S(2)}) collective-permute-start(f32[768,384]{1,0:T(8,128)S(1)} %collective-permute-done.1.rest_1_), channel_id=1, source_target_pairs={{0,16},{8,56},{16,32},{24,8},{32,48},{40,24},{48,0},{56,40},{1,17}... | collective-permute-start | bytes 3538952 | tf_op jit(solution)/shard_map/ppermute | solution.py:327
  60.3 25.3 %collective-permute-start.4 = (f32[768,384]{1,0:T(8,128)S(1)}, f32[768,384]{1,0:T(8,128)S(1)}, u32[]{:S(2)}, u32[]{:S(2)}) collective-permute-start(f32[768,384]{1,0:T(8,128)S(1)} %collective-permute-done.2.rest_2_), channel_id=1, source_target_pairs={{0,16},{8,56},{16,32},{24,8},{32,48},{40,24},{48,0},{56,40},{1,17}... | collective-permute-start | bytes 3538952 | tf_op jit(solution)/shard_map/ppermute | solution.py:328
  64.7 25.2 %collective-permute-start.8 = (f32[768,384]{1,0:T(8,128)}, f32[768,384]{1,0:T(8,128)S(1)}, u32[]{:S(2)}, u32[]{:S(2)}) collective-permute-start(f32[768,384]{1,0:T(8,128)} %bitcast.21), channel_id=1, source_target_pairs={{0,192},{8,72},{64,0},{72,136},{128,64},{136,200},{192,128},{200,8... | collective-permute-start | bytes 3538952 | tf_op jit(solution)/shard_map/ppermute | solution.py:331
  66.7 23.3 %collective-permute-start.5 = (f32[768,384]{1,0:T(8,128)S(1)}, f32[768,384]{1,0:T(8,128)S(1)}, u32[]{:S(2)}, u32[]{:S(2)}) collective-permute-start(f32[768,384]{1,0:T(8,128)S(1)} %collective-permute-done.2.rest_2_), channel_id=1, source_target_pairs={{0,8},{8,0},{1,9},{9,1},{2,10},{10,2},{3,11},{11,3},{4,12},{12,4},... | collective-permute-start | bytes 3538952 | tf_op jit(solution)/shard_map/ppermute | solution.py:330
  73.0 17.0 %collective-permute-start.6 = (f32[768,384]{1,0:T(8,128)S(1)}, f32[768,384]{1,0:T(8,128)S(1)}, u32[]{:S(2)}, u32[]{:S(2)}) collective-permute-start(f32[768,384]{1,0:T(8,128)S(1)} %collective-permute-done.3.rest_3_), channel_id=1, source_target_pairs={{0,8},{8,0},{1,9},{9,1},{2,10},{10,2},{3,11},{11,3},{4,12},{12,4},... | collective-permute-start | bytes 3538952 | tf_op jit(solution)/shard_map/ppermute | solution.py:330
  85.6 6.8 %collective-permute-start.7 = (f32[768,384]{1,0:T(8,128)S(1)}, f32[768,384]{1,0:T(8,128)S(1)}, u32[]{:S(2)}, u32[]{:S(2)}) collective-permute-start(f32[768,384]{1,0:T(8,128)S(1)} %collective-permute-done.4.rest_4_), channel_id=1, source_target_pairs={{0,8},{8,0},{1,9},{9,1},{2,10},{10,2},{3,11},{11,3},{4,12},{12,4},... | collective-permute-start | bytes 3538952 | tf_op jit(solution)/shard_map/ppermute | solution.py:330
  92.4 1.3 copy-start
  132.6 17.7 %collective-permute-start.10 = (f32[768,384]{1,0:T(8,128)S(1)}, f32[768,384]{1,0:T(8,128)S(1)}, u32[]{:S(2)}, u32[]{:S(2)}) collective-permute-start(f32[768,384]{1,0:T(8,128)S(1)} %get-tuple-element.35), channel_id=1, source_target_pairs={{0,64},{8,200},{64,128},{72,8},{128,192},{136,72},{192,0},{200,136... | collective-permute-start | bytes 3538952 | tf_op jit(solution)/shard_map/ppermute | solution.py:336
  148.4 18.2 %collective-permute-start.9 = (f32[768,384]{1,0:T(8,128)S(1)}, f32[768,384]{1,0:T(8,128)S(1)}, u32[]{:S(2)}, u32[]{:S(2)}) collective-permute-start(f32[768,384]{1,0:T(8,128)S(1)} %get-tuple-element.31), channel_id=1, source_target_pairs={{0,192},{8,72},{64,0},{72,136},{128,64},{136,200},{192,128},{200,8... | collective-permute-start | bytes 3538952 | tf_op jit(solution)/shard_map/ppermute | solution.py:339
  152.0 5.5 %collective-permute-start.11 = (f32[1,384]{1,0:T(1,128)S(1)}, f32[1,384]{1,0:T(1,128)S(1)}, u32[]{:S(2)}, u32[]{:S(2)}) collective-permute-start(f32[1,384]{1,0:T(1,128)S(1)} %get-tuple-element.37), channel_id=1, source_target_pairs={{0,64},{8,200},{64,128},{72,8},{128,192},{136,72},{192,0},{200,136... | collective-permute-start | bytes 4616 | tf_op jit(solution)/shard_map/ppermute | solution.py:341
  157.5 25.5 %collective-permute-start.12 = (f32[768,384]{1,0:T(8,128)S(1)}, f32[768,384]{1,0:T(8,128)S(1)}, u32[]{:S(2)}, u32[]{:S(2)}) collective-permute-start(f32[768,384]{1,0:T(8,128)S(1)} %get-tuple-element.40), channel_id=1, source_target_pairs={{0,64},{8,200},{64,128},{72,8},{128,192},{136,72},{192,0},{200,136... | collective-permute-start | bytes 3538952 | tf_op jit(solution)/shard_map/ppermute | solution.py:343
  168.8 12.3 %all-to-all-start = ((f32[8,1,384]{2,1,0:T(1,128)}), f32[8,1,384]{2,1,0:T(1,128)S(1)}, u32[]{:S(2)}, u32[]{:S(2)}) async-start(f32[8,1,384]{2,1,0:T(1,128)} %broadcast_in_dim.15), calls=%async_computation | async-start | bytes 24576 | tf_op jit(solution)/shard_map/all_to_all | solution.py:345
Sparse Core Ops, SparseCore 0:
  10.1 111.2 all-gather.2

commit v10 on v9

--- a/solution.py
+++ b/solution.py
@@ -145,21 +145,32 @@
     )(start_row, root_row, *pieces)
 
 
-def product_kernel(calls, table, root_hbm, high_hbm, low_hbm, *rest):
-    outs = rest[: len(calls)]
-    a_f, z_h, z_l, a_sem, z_sem = rest[len(calls) :]
+def product_kernel(calls, ahead, given, table, root_hbm, high_hbm, low_hbm, *rest):
+    fetched = len(calls) - given
+    slots, rest = ([rest[:3]], rest[3:]) if given else ([], rest)
+    outs, rest = rest[: len(calls)], rest[len(calls) :]
+    if ahead is not None:
+        next_slot, rest = rest[:3], rest[3:]
+    if fetched:
+        slots = slots + [[ref.at[i] for ref in rest[:3]] for i in range(fetched)]
+        rest = rest[3:]
+    a_sem, z_sem = rest
     rows = outs[0].shape[0]
     per_range = rows // BLOCK
     per_part = PART // BLOCK
     parts = rows // PART
-    children = [table[call, 3 * per_range + 2] for call in calls]
-
-    def factor_copies(i, source, target, first):
+    wanted = list(calls)
+    if ahead is not None:
+        slots = slots + [next_slot]
+        wanted.append(ahead)
+    children = [table[call, 3 * per_range + 2] for call in wanted]
+
+    def factor_copies(i, source, which):
         return [
             pltpu.make_async_copy(
                 source.at[table[children[i], 3 * per_range + side]],
-                target.at[i, pl.ds(side * rows, rows)],
-                z_sem.at[i, first + side],
+                slots[i][which].at[pl.ds(side * rows, rows)],
+                z_sem.at[i, 2 * (which - 1) + side],
             )
             for side in range(2)
         ]
@@ -169,71 +180,94 @@
             mb = pl.multiple_of(table[children[i], part * per_part + m] * BLOCK, BLOCK)
             pltpu.make_async_copy(
                 root_hbm.at[:, pl.ds(mb, BLOCK)],
-                a_f.at[i, part, :, pl.ds(m * BLOCK, BLOCK)],
+                slots[i][0].at[part, :, pl.ds(m * BLOCK, BLOCK)],
                 a_sem.at[i, part],
             ).start()
 
-    highs_in = [factor_copies(i, high_hbm, z_h, 0) for i in range(len(calls))]
-    lows_in = [factor_copies(i, low_hbm, z_l, 2) for i in range(len(calls))]
+    def wait_root(i, part):
+        whole = slots[i][0].at[part]
+        pltpu.make_async_copy(whole, whole, a_sem.at[i, part]).wait()
 
     def begin(i):
         start_root(i, 0)
-        for copy in highs_in[i] + lows_in[i]:
+        for copy in factor_copies(i, high_hbm, 1) + factor_copies(i, low_hbm, 2):
             copy.start()
-        start_root(i, 1)
-
-    begin(0)
+        for part in range(1, parts):
+            start_root(i, part)
+
+    begin(0 if not given else 1)
     for i, out in enumerate(outs):
+        here = i >= given
         for part in range(parts):
-            pltpu.make_async_copy(a_f.at[i, part], a_f.at[i, part], a_sem.at[i, part]).wait()
-            if part == 0:
-                for copy in highs_in[i]:
+            if here:
+                wait_root(i, part)
+            if here and part == 0:
+                for copy in factor_copies(i, high_hbm, 1):
                     copy.wait()
-            if part + 2 < parts:
-                start_root(i, part + 2)
-            elif part + 2 == parts and i + 1 < len(calls):
-                begin(i + 1)
+            if part == 1 and (i + 1 if here else i + 2) < len(wanted):
+                begin(i + 1 if here else i + 2)
             highs, lows = [], []
             for k in range(2 * per_range):
-                value = a_f[i, part, table[children[i], per_range + k]]
+                value = slots[i][0][part, table[children[i], per_range + k]]
                 high = value.astype(jnp.bfloat16)
                 highs.append(high)
                 lows.append((value - high.astype(jnp.float32)).astype(jnp.bfloat16))
             high = jnp.concatenate(highs, axis=1)
             low = jnp.concatenate(lows, axis=1)
-            value = jnp.dot(high, z_h[i], preferred_element_type=jnp.float32)
-            value = value + jnp.dot(low, z_h[i], preferred_element_type=jnp.float32)
-            if part == 0:
-                for copy in lows_in[i]:
+            value = jnp.dot(high, slots[i][1][...], preferred_element_type=jnp.float32)
+            value = value + jnp.dot(low, slots[i][1][...], preferred_element_type=jnp.float32)
+            if here and part == 0:
+                for copy in factor_copies(i, low_hbm, 2):
                     copy.wait()
-            value = value + jnp.dot(high, z_l[i], preferred_element_type=jnp.float32)
+            value = value + jnp.dot(high, slots[i][2][...], preferred_element_type=jnp.float32)
             out[part * PART : (part + 1) * PART, :] = value
-
-
-def product(calls, table, root, high, low):
+    if ahead is not None:
+        i = len(wanted) - 1
+        for part in range(parts):
+            wait_root(i, part)
+        for copy in factor_copies(i, high_hbm, 1) + factor_copies(i, low_hbm, 2):
+            copy.wait()
+
+
+def product(calls, ahead, given, table, root, high, low):
     rows, cols = high.shape[1:]
     n = len(calls)
+    total = n + (ahead is not None)
+    fetched = n - (given is not None)
     any_spec = pl.BlockSpec(memory_space=pl.ANY)
-    root, high, low = [pltpu.with_memory_space_constraint(v, pltpu.HBM) for v in (root, high, low)]
-    return pl.pallas_call(
-        functools.partial(product_kernel, calls),
-        out_shape=[jax.ShapeDtypeStruct((rows, cols), jnp.float32)] * n,
-        in_specs=[pl.BlockSpec(memory_space=pltpu.SMEM)] + [any_spec] * 3,
-        out_specs=[pl.BlockSpec(memory_space=pltpu.VMEM)] * n,
-        scratch_shapes=[
-            pltpu.VMEM((n, rows // PART, root.shape[0], PART, BLOCK), jnp.float32),
-            pltpu.VMEM((n, 2 * rows, cols), jnp.bfloat16),
-            pltpu.VMEM((n, 2 * rows, cols), jnp.bfloat16),
-            pltpu.SemaphoreType.DMA((n, rows // PART)),
-            pltpu.SemaphoreType.DMA((n, 4)),
+    vmem = pl.BlockSpec(memory_space=pltpu.VMEM)
+    slot = [
+        ((rows // PART, root.shape[0], PART, BLOCK), jnp.float32),
+        ((2 * rows, cols), jnp.bfloat16),
+        ((2 * rows, cols), jnp.bfloat16),
+    ]
+    args = [pltpu.with_memory_space_constraint(v, pltpu.HBM) for v in (root, high, low)]
+    if given is not None:
+        args += [pltpu.with_memory_space_constraint(v, pltpu.VMEM) for v in given]
+    out_shape = [jax.ShapeDtypeStruct((rows, cols), jnp.float32)] * n
+    if ahead is not None:
+        out_shape += [pltpu.VMEM(shape, dtype) for shape, dtype in slot]
+    scratch = [pltpu.VMEM((fetched, *shape), dtype) for shape, dtype in slot if fetched]
+    found = pl.pallas_call(
+        functools.partial(product_kernel, calls, ahead, int(given is not None)),
+        out_shape=out_shape,
+        in_specs=[pl.BlockSpec(memory_space=pltpu.SMEM)]
+        + [any_spec] * 3
+        + [vmem] * (len(args) - 3),
+        out_specs=[vmem] * len(out_shape),
+        scratch_shapes=scratch
+        + [
+            pltpu.SemaphoreType.DMA((total, rows // PART)),
+            pltpu.SemaphoreType.DMA((total, 4)),
         ],
-        compiler_params=pltpu.CompilerParams(vmem_limit_bytes=(12 + 14 * n) * 1024 * 1024),
+        compiler_params=pltpu.CompilerParams(vmem_limit_bytes=28 * 1024 * 1024),
         cost_estimate=pl.CostEstimate(
             flops=n * 3 * 2 * rows * 2 * rows * cols,
             bytes_accessed=n * 12 * rows * rows,
             transcendentals=0,
         ),
-    )(table, root, high, low)
+    )(table, *args)
+    return found[:n], found[n:]
 
 
 def weigh_kernel(piece, first, second, high_hbm, low_hbm, total, sums, high, low, sem):
@@ -332,11 +366,11 @@
     high, low = spread(start_row, rows_of, pieces)
 
     root = root.reshape(-1, *root_inverse.shape)
-    far, first = product((0, 1), table, root, high, low)
+    (far,), given = product((0,), 1, None, table, root, high, low)
     passed = lax.ppermute(far, ("y", "core"), opposite(4))
-    second, home = product((2, 3), table, root, high, low)
-    first, second = lax.optimization_barrier((first, second))
+    (first,), given = product((1,), 2, given, table, root, high, low)
     back = lax.ppermute(first, ("y", "core"), opposite(4, -1))
+    (second, home), _ = product((2, 3), None, given, table, root, high, low)
     last, last_sums = weigh(9, second, passed, high, low)
     last_sums = lax.ppermute(last_sums, ("y", "core"), opposite(4))
     last, last_sums = lax.optimization_barrier((last, last_sums))

time: 193 us -> 191 us (0.990)
  Pallas kernels: 36.2 us -> 40.1 us
  starting transfers between devices: 55.6 us -> 51.7 us
  waiting for transfers between devices: 75.3 us -> 71.4 us
    ppermute x1, waiting for transfers between devices: 3.97 us -> 0.01 us  [per_device(): back = lax.ppermute(first, ('y', 'core'), opposite(4, -1))]
    pallas_call x2 -> x3, Pallas kernels: 22.5 us -> 26.4 us  [product(): pl.pallas_call(functools.partial(product_kernel, calls, ahead, int(given...]
    all_to_all x1, starting transfers between devices: 7.63 us -> 4.37 us  [per_device(): lax.all_to_all(jnp.broadcast_to(sums + last_sums, (8, cols)), ('x', 'core...]
  transfers between devices with their start and end apart: 15 -> 15, of which waited for: 9 -> 8; matrix products, arithmetic and copies ran while one was open for 4% -> 4% of each run, Pallas kernels for 13% -> 17%
where the time goes in v10:
time: 191 us; the launch traced here: 188 us
  waiting for transfers between devices  71.4 us (37%)
  starting transfers between devices  51.7 us (27%)
  Pallas kernels  40.1 us (21%)
  between operations  14.3 us (7%)
  local copies, waits for them, and re-layouts  4.94 us (3%)
  other arithmetic  3.7 us (2%)
    pallas_call x3, Pallas kernels, product(): pl.pallas_call(functools.partial(product_kernel, calls, ahead, int(given...  26.4 us
    ppermute x1, waiting for transfers between devices, per_device(): own = lax.ppermute(coupling[0], ('y', 'x', 'core'), pairs)  24.6 us
    all_gather x1, waiting for transfers between devices, per_device(): root = lax.all_gather(root_inverse, ('zh', 'zl'), axis=0, tiled=False)  17.2 us
    ppermute x3, starting transfers between devices, per_device(): pieces += [lax.ppermute(p, 'core', CORES) for p in (near, near_beside, far)]  13 us
    ppermute x1, waiting for transfers between devices, per_device(): near = lax.ppermute(own, ('x', 'core'), along_x)  11.7 us
    pallas_call x1, Pallas kernels, spread(): pl.pallas_call(spread_kernel, out_shape=[pltpu.HBM(shape, jnp.bfloat16)]...  10.5 us
    ppermute x1, waiting for transfers between devices, per_device(): far = lax.ppermute(near, ('x', 'core'), along_x)  8.28 us
    ppermute x1, starting transfers between devices, per_device(): forth = lax.ppermute(last, ('y', 'core'), opposite(4))  4.81 us
  transfers between devices with their start and end apart: 15, of which 8 were waited for; matrix products, arithmetic and copies ran while one was open for 4% of the time, Pallas kernels for 17%

profile of v10, /device:TPU:1, one launch (start us, length us, event | category | flops | bytes accessed | tf_op | source)
XLA Modules:
  0.0 187.9 jit_solution(5450768891668013507)
XLA Ops:
  7.2 0.0 all-gather.3.cloned.1.call-start
  7.2 0.7 all-gather.3.cloned.1.call-update
  7.9 4.6 %collective-permute-start = (f32[768,384]{1,0:T(8,128)}, f32[768,384]{1,0:T(8,128)S(1)}, u32[]{:S(2)}, u32[]{:S(2)}) collective-permute-start(f32[768,384]{1,0:T(8,128)} %bitcast.20), channel_id=1, source_target_pairs={{0,48},{8,64},{16,144},{24,224},{32,32},{40,112},{48,176},{56,240}... | collective-permute-start | bytes 3538952 | tf_op jit(solution)/shard_map/ppermute | solution.py:355
  12.5 1.0 slice.3
  13.6 1.0 reshape.109.rows_ref
  14.5 0.1 reshape.108
  14.6 0.7 fusion.2
  15.3 0.1 copy.18
  15.4 0.1 pad_add_fusion
  15.5 0.1 copy.17
  15.6 0.1 concatenate.16.table
  15.7 0.7 and_bitcast_fusion
  16.4 0.1 fusion.5.start_row
  16.5 24.6 %collective-permute-done.rest_0_ = f32[768,384]{1,0:T(8,128)S(1)} collective-permute-done((f32[768,384]{1,0:T(8,128)}, f32[768,384]{1,0:T(8,128)S(1)}, u32[]{:S(2)}, u32[]{:S(2)}) %collective-permute-start) | collective-permute-done | bytes 1179680 | tf_op jit(solution)/shard_map/ppermute | solution.py:355
  41.1 1.9 %collective-permute-start.1 = (f32[768,384]{1,0:T(8,128)S(1)}, f32[768,384]{1,0:T(8,128)S(1)}, u32[]{:S(2)}, u32[]{:S(2)}) collective-permute-start(f32[768,384]{1,0:T(8,128)S(1)} %collective-permute-done.rest_0_), channel_id=1, source_target_pairs={{0,8},{8,0},{1,9},{9,1},{2,10},{10,2},{3,11},{11,3},{4,12},{12,4},... | collective-permute-start | bytes 3538952 | tf_op jit(solution)/shard_map/ppermute | solution.py:359
  43.0 3.2 %collective-permute-start.2 = (f32[768,384]{1,0:T(8,128)S(1)}, f32[768,384]{1,0:T(8,128)S(1)}, u32[]{:S(2)}, u32[]{:S(2)}) collective-permute-start(f32[768,384]{1,0:T(8,128)S(1)} %collective-permute-done.rest_0_), channel_id=1, source_target_pairs={{0,16},{8,56},{16,32},{24,8},{32,48},{40,24},{48,0},{56,40},{1,17}... | collective-permute-start | bytes 3538952 | tf_op jit(solution)/shard_map/ppermute | solution.py:360
  46.2 0.0 collective-permute-done.1.rest_1_
  46.2 2.4 %collective-permute-start.3 = (f32[768,384]{1,0:T(8,128)S(1)}, f32[768,384]{1,0:T(8,128)S(1)}, u32[]{:S(2)}, u32[]{:S(2)}) collective-permute-start(f32[768,384]{1,0:T(8,128)S(1)} %collective-permute-done.1.rest_1_), channel_id=1, source_target_pairs={{0,16},{8,56},{16,32},{24,8},{32,48},{40,24},{48,0},{56,40},{1,17}... | collective-permute-start | bytes 3538952 | tf_op jit(solution)/shard_map/ppermute | solution.py:361
  48.6 11.7 %collective-permute-done.2.rest_2_ = f32[768,384]{1,0:T(8,128)S(1)} collective-permute-done((f32[768,384]{1,0:T(8,128)S(1)}, f32[768,384]{1,0:T(8,128)S(1)}, u32[]{:S(2)}, u32[]{:S(2)}) %collective-permute-start.2) | collective-permute-done | bytes 1179680 | tf_op jit(solution)/shard_map/ppermute | solution.py:360
  60.3 4.4 %collective-permute-start.4 = (f32[768,384]{1,0:T(8,128)S(1)}, f32[768,384]{1,0:T(8,128)S(1)}, u32[]{:S(2)}, u32[]{:S(2)}) collective-permute-start(f32[768,384]{1,0:T(8,128)S(1)} %collective-permute-done.2.rest_2_), channel_id=1, source_target_pairs={{0,16},{8,56},{16,32},{24,8},{32,48},{40,24},{48,0},{56,40},{1,17}... | collective-permute-start | bytes 3538952 | tf_op jit(solution)/shard_map/ppermute | solution.py:362
  64.7 1.9 %collective-permute-start.8 = (f32[768,384]{1,0:T(8,128)}, f32[768,384]{1,0:T(8,128)S(1)}, u32[]{:S(2)}, u32[]{:S(2)}) collective-permute-start(f32[768,384]{1,0:T(8,128)} %bitcast.21), channel_id=1, source_target_pairs={{0,192},{8,72},{64,0},{72,136},{128,64},{136,200},{192,128},{200,8... | collective-permute-start | bytes 3538952 | tf_op jit(solution)/shard_map/ppermute | solution.py:365
  66.7 4.3 %collective-permute-start.5 = (f32[768,384]{1,0:T(8,128)S(1)}, f32[768,384]{1,0:T(8,128)S(1)}, u32[]{:S(2)}, u32[]{:S(2)}) collective-permute-start(f32[768,384]{1,0:T(8,128)S(1)} %collective-permute-done.2.rest_2_), channel_id=1, source_target_pairs={{0,8},{8,0},{1,9},{9,1},{2,10},{10,2},{3,11},{11,3},{4,12},{12,4},... | collective-permute-start | bytes 3538952 | tf_op jit(solution)/shard_map/ppermute | solution.py:364
  71.0 2.0 %collective-permute-done.3.rest_3_ = f32[768,384]{1,0:T(8,128)S(1)} collective-permute-done((f32[768,384]{1,0:T(8,128)S(1)}, f32[768,384]{1,0:T(8,128)S(1)}, u32[]{:S(2)}, u32[]{:S(2)}) %collective-permute-start.3) | collective-permute-done | bytes 1179680 | tf_op jit(solution)/shard_map/ppermute | solution.py:361
  73.0 4.4 %collective-permute-start.6 = (f32[768,384]{1,0:T(8,128)S(1)}, f32[768,384]{1,0:T(8,128)S(1)}, u32[]{:S(2)}, u32[]{:S(2)}) collective-permute-start(f32[768,384]{1,0:T(8,128)S(1)} %collective-permute-done.3.rest_3_), channel_id=1, source_target_pairs={{0,8},{8,0},{1,9},{9,1},{2,10},{10,2},{3,11},{11,3},{4,12},{12,4},... | collective-permute-start | bytes 3538952 | tf_op jit(solution)/shard_map/ppermute | solution.py:364
  77.3 8.3 %collective-permute-done.4.rest_4_ = f32[768,384]{1,0:T(8,128)S(1)} collective-permute-done((f32[768,384]{1,0:T(8,128)S(1)}, f32[768,384]{1,0:T(8,128)S(1)}, u32[]{:S(2)}, u32[]{:S(2)}) %collective-permute-start.4) | collective-permute-done | bytes 1179680 | tf_op jit(solution)/shard_map/ppermute | solution.py:362
  85.6 4.4 %collective-permute-start.7 = (f32[768,384]{1,0:T(8,128)S(1)}, f32[768,384]{1,0:T(8,128)S(1)}, u32[]{:S(2)}, u32[]{:S(2)}) collective-permute-start(f32[768,384]{1,0:T(8,128)S(1)} %collective-permute-done.4.rest_4_), channel_id=1, source_target_pairs={{0,8},{8,0},{1,9},{9,1},{2,10},{10,2},{3,11},{11,3},{4,12},{12,4},... | collective-permute-start | bytes 3538952 | tf_op jit(solution)/shard_map/ppermute | solution.py:364
  90.0 0.0 collective-permute-done.8.rest_9_
  90.0 0.0 collective-permute-done.5.rest_5_
  90.0 0.0 collective-permute-done.6.rest_6_
  90.0 2.4 %collective-permute-done.7.rest_7_ = f32[768,384]{1,0:T(8,128)S(1)} collective-permute-done((f32[768,384]{1,0:T(8,128)S(1)}, f32[768,384]{1,0:T(8,128)S(1)}, u32[]{:S(2)}, u32[]{:S(2)}) %collective-permute-start.7) | collective-permute-done | bytes 1179680 | tf_op jit(solution)/shard_map/ppermute | solution.py:364
  92.4 0.0 copy-start
  92.4 1.3 copy-done
  93.7 10.5 %shard_map.77 = (bf16[10,768,384]{2,1,0:T(8,128)(2,1)}, bf16[10,768,384]{2,1,0:T(8,128)(2,1)}) custom-call(s32[10]{0:T(128)S(1)} %fusion.5.start_row, s32[384,128]{1,0:T(8,128)S(1)} %reshape.109.rows_ref, f32[768,384]{1,0:T(8,128)S(1)} %collective-permute-done.rest_0_, f32[768,384]{1,0:T(8,128)S(1)} %collective-permute-done.1.rest_1_, ...), custom_call_target="tpu_custom_call" | custom-call | flops 1509949440 | bytes 23592960 | tf_op jit(solution)/shard_map/pallas_call | solution.py:125
  104.2 17.2 %all-gather.3.cloned.1.call-done = f32[16384,128]{1,0:T(8,128)} async-done(((f32[1024,128]{1,0:T(8,128)}), f32[16384,128]{1,0:T(8,128)}) %all-gather.3.cloned.1.call-update) | async-done | bytes 8388624 | tf_op jit(solution)/shard_map/all_gather | solution.py:331
  121.4 8.3 %shard_map.78 = (f32[768,384]{1,0:T(8,128)S(1)}, f32[3,16,256,128]{3,2,1,0:T(8,128)S(1)}, bf16[1536,384]{1,0:T(8,128)(2,1)S(1)}, bf16[1536,384]{1,0:T(8,128)(2,1)S(1)}) custom-call(s32[4,21]{1,0:T(4,128)S(1)} %concatenate.16.table, f32[16,1024,128]{2,1,0:T(8,128)} %bitcast.23, bf16[10,768,384]{2,1,0:T(8,128)(2,1)} %get-tuple-element.30.high_hbm, ...), custom_call_target="tpu_custom_call" | custom-call | flops 2717908992 | bytes 7077888 | tf_op jit(solution)/shard_map/pallas_call | solution.py:251
  129.7 4.6 %collective-permute-start.10 = (f32[768,384]{1,0:T(8,128)S(1)}, f32[768,384]{1,0:T(8,128)S(1)}, u32[]{:S(2)}, u32[]{:S(2)}) collective-permute-start(f32[768,384]{1,0:T(8,128)S(1)} %get-tuple-element.43), channel_id=1, source_target_pairs={{0,64},{8,200},{64,128},{72,8},{128,192},{136,72},{192,0},{200,136... | collective-permute-start | bytes 3538952 | tf_op jit(solution)/shard_map/ppermute | solution.py:370
  134.3 7.3 %shard_map.79 = (f32[768,384]{1,0:T(8,128)S(1)}, f32[3,16,256,128]{3,2,1,0:T(8,128)S(1)}, bf16[1536,384]{1,0:T(8,128)(2,1)S(1)}, bf16[1536,384]{1,0:T(8,128)(2,1)S(1)}) custom-call(s32[4,21]{1,0:T(4,128)S(1)} %concatenate.16.table, f32[16,1024,128]{2,1,0:T(8,128)} %bitcast.24, bf16[10,768,384]{2,1,0:T(8,128)(2,1)} %get-tuple-element.30.high_hbm, ...), custom_call_target="tpu_custom_call" | custom-call | flops 2717908992 | bytes 7077888 | tf_op jit(solution)/shard_map/pallas_call | solution.py:251
  141.5 1.9 %collective-permute-start.9 = (f32[768,384]{1,0:T(8,128)S(1)}, f32[768,384]{1,0:T(8,128)S(1)}, u32[]{:S(2)}, u32[]{:S(2)}) collective-permute-start(f32[768,384]{1,0:T(8,128)S(1)} %get-tuple-element.39), channel_id=1, source_target_pairs={{0,192},{8,72},{64,0},{72,136},{128,64},{136,200},{192,128},{200,8... | collective-permute-start | bytes 3538952 | tf_op jit(solution)/shard_map/ppermute | solution.py:372
  143.5 10.8 %shard_map.80 = (f32[768,384]{1,0:T(8,128)S(1)}, f32[768,384]{1,0:T(8,128)S(1)}) custom-call(s32[4,21]{1,0:T(4,128)S(1)} %concatenate.16.table, f32[16,1024,128]{2,1,0:T(8,128)} %bitcast.25, bf16[10,768,384]{2,1,0:T(8,128)(2,1)} %get-tuple-element.30.high_hbm, bf16[10,768,384]{2,1,0:T(8,128)(2,1)} %get-tuple-element.31.low_hbm, ...), custom_call_target="tpu_custom_call" | custom-call | flops 5435817984 | bytes 14155776 | tf_op jit(solution)/shard_map/pallas_call | solution.py:251
  154.3 0.0 collective-permute-done.10.second
  154.3 1.6 shard_map.82
  155.9 4.6 %collective-permute-start.11 = (f32[1,384]{1,0:T(1,128)S(1)}, f32[1,384]{1,0:T(1,128)S(1)}, u32[]{:S(2)}, u32[]{:S(2)}) collective-permute-start(f32[1,384]{1,0:T(1,128)S(1)} %get-tuple-element.45), channel_id=1, source_target_pairs={{0,64},{8,200},{64,128},{72,8},{128,192},{136,72},{192,0},{200,136... | collective-permute-start | bytes 4616 | tf_op jit(solution)/shard_map/ppermute | solution.py:375
  160.5 0.7 collective-permute-done.11
  161.2 4.8 %collective-permute-start.12 = (f32[768,384]{1,0:T(8,128)S(1)}, f32[768,384]{1,0:T(8,128)S(1)}, u32[]{:S(2)}, u32[]{:S(2)}) collective-permute-start(f32[768,384]{1,0:T(8,128)S(1)} %get-tuple-element.48), channel_id=1, source_target_pairs={{0,64},{8,200},{64,128},{72,8},{128,192},{136,72},{192,0},{200,136... | collective-permute-start | bytes 3538952 | tf_op jit(solution)/shard_map/ppermute | solution.py:377
  166.0 0.0 collective-permute-done.9.second
  166.0 1.6 shard_map.81
  167.7 0.6 broadcast_in_dim.15
  168.3 4.4 %all-to-all-start = ((f32[8,1,384]{2,1,0:T(1,128)}), f32[8,1,384]{2,1,0:T(1,128)S(1)}, u32[]{:S(2)}, u32[]{:S(2)}) async-start(f32[8,1,384]{2,1,0:T(1,128)} %broadcast_in_dim.15), calls=%async_computation | async-start | bytes 24576 | tf_op jit(solution)/shard_map/all_to_all | solution.py:379
  172.6 0.8 fusion.1
  173.5 3.8 %all-to-all-done = f32[8,1,384]{2,1,0:T(1,128)S(1)} async-done(((f32[8,1,384]{2,1,0:T(1,128)}), f32[8,1,384]{2,1,0:T(1,128)S(1)}, u32[]{:S(2)}, u32[]{:S(2)}) %all-to-all-start) | async-done | bytes 12320 | tf_op jit(solution)/shard_map/all_to_all | solution.py:379
  177.3 0.6 reduce_sum.9
  177.9 1.3 reshape_add_fusion
  179.1 0.0 collective-permute-done.12
  179.2 0.1 add.122
  179.3 1.8 convolution_negate_fusion
  (4 shorter events, 0.0 us)
Async XLA Ops:
  7.2 114.2 %all-gather.3.cloned.1.call-start = ((), (), s32[]{:S(2)}) async-start(), calls=%async_computation.1 | async-start | bytes 8912896 | tf_op jit(solution)/shard_map/all_gather | solution.py:331
  7.9 33.2 %collective-permute-start = (f32[768,384]{1,0:T(8,128)}, f32[768,384]{1,0:T(8,128)S(1)}, u32[]{:S(2)}, u32[]{:S(2)}) collective-permute-start(f32[768,384]{1,0:T(8,128)} %bitcast.20), channel_id=1, source_target_pairs={{0,48},{8,64},{16,144},{24,224},{32,32},{40,112},{48,176},{56,240}... | collective-permute-start | bytes 3538952 | tf_op jit(solution)/shard_map/ppermute | solution.py:355
  41.1 5.1 %collective-permute-start.1 = (f32[768,384]{1,0:T(8,128)S(1)}, f32[768,384]{1,0:T(8,128)S(1)}, u32[]{:S(2)}, u32[]{:S(2)}) collective-permute-start(f32[768,384]{1,0:T(8,128)S(1)} %collective-permute-done.rest_0_), channel_id=1, source_target_pairs={{0,8},{8,0},{1,9},{9,1},{2,10},{10,2},{3,11},{11,3},{4,12},{12,4},... | collective-permute-start | bytes 3538952 | tf_op jit(solution)/shard_map/ppermute | solution.py:359
  43.0 17.3 %collective-permute-start.2 = (f32[768,384]{1,0:T(8,128)S(1)}, f32[768,384]{1,0:T(8,128)S(1)}, u32[]{:S(2)}, u32[]{:S(2)}) collective-permute-start(f32[768,384]{1,0:T(8,128)S(1)} %collective-permute-done.rest_0_), channel_id=1, source_target_pairs={{0,16},{8,56},{16,32},{24,8},{32,48},{40,24},{48,0},{56,40},{1,17}... | collective-permute-start | bytes 3538952 | tf_op jit(solution)/shard_map/ppermute | solution.py:360
  46.2 26.8 %collective-permute-start.3 = (f32[768,384]{1,0:T(8,128)S(1)}, f32[768,384]{1,0:T(8,128)S(1)}, u32[]{:S(2)}, u32[]{:S(2)}) collective-permute-start(f32[768,384]{1,0:T(8,128)S(1)} %collective-permute-done.1.rest_1_), channel_id=1, source_target_pairs={{0,16},{8,56},{16,32},{24,8},{32,48},{40,24},{48,0},{56,40},{1,17}... | collective-permute-start | bytes 3538952 | tf_op jit(solution)/shard_map/ppermute | solution.py:361
  60.3 25.3 %collective-permute-start.4 = (f32[768,384]{1,0:T(8,128)S(1)}, f32[768,384]{1,0:T(8,128)S(1)}, u32[]{:S(2)}, u32[]{:S(2)}) collective-permute-start(f32[768,384]{1,0:T(8,128)S(1)} %collective-permute-done.2.rest_2_), channel_id=1, source_target_pairs={{0,16},{8,56},{16,32},{24,8},{32,48},{40,24},{48,0},{56,40},{1,17}... | collective-permute-start | bytes 3538952 | tf_op jit(solution)/shard_map/ppermute | solution.py:362
  64.7 25.2 %collective-permute-start.8 = (f32[768,384]{1,0:T(8,128)}, f32[768,384]{1,0:T(8,128)S(1)}, u32[]{:S(2)}, u32[]{:S(2)}) collective-permute-start(f32[768,384]{1,0:T(8,128)} %bitcast.21), channel_id=1, source_target_pairs={{0,192},{8,72},{64,0},{72,136},{128,64},{136,200},{192,128},{200,8... | collective-permute-start | bytes 3538952 | tf_op jit(solution)/shard_map/ppermute | solution.py:365
  66.7 23.3 %collective-permute-start.5 = (f32[768,384]{1,0:T(8,128)S(1)}, f32[768,384]{1,0:T(8,128)S(1)}, u32[]{:S(2)}, u32[]{:S(2)}) collective-permute-start(f32[768,384]{1,0:T(8,128)S(1)} %collective-permute-done.2.rest_2_), channel_id=1, source_target_pairs={{0,8},{8,0},{1,9},{9,1},{2,10},{10,2},{3,11},{11,3},{4,12},{12,4},... | collective-permute-start | bytes 3538952 | tf_op jit(solution)/shard_map/ppermute | solution.py:364
  73.0 17.0 %collective-permute-start.6 = (f32[768,384]{1,0:T(8,128)S(1)}, f32[768,384]{1,0:T(8,128)S(1)}, u32[]{:S(2)}, u32[]{:S(2)}) collective-permute-start(f32[768,384]{1,0:T(8,128)S(1)} %collective-permute-done.3.rest_3_), channel_id=1, source_target_pairs={{0,8},{8,0},{1,9},{9,1},{2,10},{10,2},{3,11},{11,3},{4,12},{12,4},... | collective-permute-start | bytes 3538952 | tf_op jit(solution)/shard_map/ppermute | solution.py:364
  85.6 6.8 %collective-permute-start.7 = (f32[768,384]{1,0:T(8,128)S(1)}, f32[768,384]{1,0:T(8,128)S(1)}, u32[]{:S(2)}, u32[]{:S(2)}) collective-permute-start(f32[768,384]{1,0:T(8,128)S(1)} %collective-permute-done.4.rest_4_), channel_id=1, source_target_pairs={{0,8},{8,0},{1,9},{9,1},{2,10},{10,2},{3,11},{11,3},{4,12},{12,4},... | collective-permute-start | bytes 3538952 | tf_op jit(solution)/shard_map/ppermute | solution.py:364
  92.4 1.3 copy-start
  129.7 24.6 %collective-permute-start.10 = (f32[768,384]{1,0:T(8,128)S(1)}, f32[768,384]{1,0:T(8,128)S(1)}, u32[]{:S(2)}, u32[]{:S(2)}) collective-permute-start(f32[768,384]{1,0:T(8,128)S(1)} %get-tuple-element.43), channel_id=1, source_target_pairs={{0,64},{8,200},{64,128},{72,8},{128,192},{136,72},{192,0},{200,136... | collective-permute-start | bytes 3538952 | tf_op jit(solution)/shard_map/ppermute | solution.py:370
  141.5 24.5 %collective-permute-start.9 = (f32[768,384]{1,0:T(8,128)S(1)}, f32[768,384]{1,0:T(8,128)S(1)}, u32[]{:S(2)}, u32[]{:S(2)}) collective-permute-start(f32[768,384]{1,0:T(8,128)S(1)} %get-tuple-element.39), channel_id=1, source_target_pairs={{0,192},{8,72},{64,0},{72,136},{128,64},{136,200},{192,128},{200,8... | collective-permute-start | bytes 3538952 | tf_op jit(solution)/shard_map/ppermute | solution.py:372
  155.9 5.3 %collective-permute-start.11 = (f32[1,384]{1,0:T(1,128)S(1)}, f32[1,384]{1,0:T(1,128)S(1)}, u32[]{:S(2)}, u32[]{:S(2)}) collective-permute-start(f32[1,384]{1,0:T(1,128)S(1)} %get-tuple-element.45), channel_id=1, source_target_pairs={{0,64},{8,200},{64,128},{72,8},{128,192},{136,72},{192,0},{200,136... | collective-permute-start | bytes 4616 | tf_op jit(solution)/shard_map/ppermute | solution.py:375
  161.2 17.9 %collective-permute-start.12 = (f32[768,384]{1,0:T(8,128)S(1)}, f32[768,384]{1,0:T(8,128)S(1)}, u32[]{:S(2)}, u32[]{:S(2)}) collective-permute-start(f32[768,384]{1,0:T(8,128)S(1)} %get-tuple-element.48), channel_id=1, source_target_pairs={{0,64},{8,200},{64,128},{72,8},{128,192},{136,72},{192,0},{200,136... | collective-permute-start | bytes 3538952 | tf_op jit(solution)/shard_map/ppermute | solution.py:377
  168.3 9.0 %all-to-all-start = ((f32[8,1,384]{2,1,0:T(1,128)}), f32[8,1,384]{2,1,0:T(1,128)S(1)}, u32[]{:S(2)}, u32[]{:S(2)}) async-start(f32[8,1,384]{2,1,0:T(1,128)} %broadcast_in_dim.15), calls=%async_computation | async-start | bytes 24576 | tf_op jit(solution)/shard_map/all_to_all | solution.py:379
Sparse Core Ops, SparseCore 0:
  10.1 111.2 all-gather.2

commit v11 on v8

--- a/solution.py
+++ b/solution.py
@@ -334,13 +334,13 @@
     root = root.reshape(-1, *root_inverse.shape)
     (far,) = product((0,), table, root, high, low)
     passed = lax.ppermute(far, ("y", "core"), opposite(4))
-    (first,) = product((1,), table, root, high, low)
+    second, first = product((2, 1), table, root, high, low)
     back = lax.ppermute(first, ("y", "core"), opposite(4, -1))
-    second, home = product((2, 3), table, root, high, low)
     last, last_sums = weigh(9, second, passed, high, low)
     last_sums = lax.ppermute(last_sums, ("y", "core"), opposite(4))
-    last, last_sums = lax.optimization_barrier((last, last_sums))
+    table, last, last_sums = lax.optimization_barrier((table, last, last_sums))
     forth = lax.ppermute(last, ("y", "core"), opposite(4))
+    (home,) = product((3,), table, root, high, low)
     kept, sums = weigh(8, home, back, high, low)
     sums = lax.all_to_all(
         jnp.broadcast_to(sums + last_sums, (8, cols)),

time: 190 us -> 188 us (0.989); the launches traced: 186 us -> 187 us
  transfers between devices with their start and end apart: 15 -> 15, of which waited for: 8 -> 8; matrix products, arithmetic and copies ran while one was open for 4% -> 3% of each run, Pallas kernels for 17% -> 17%
where the time goes in v11:
time: 188 us; the launch traced here: 187 us
  waiting for transfers between devices  71.4 us (38%)
  starting transfers between devices  52.6 us (28%)
  Pallas kernels  38.7 us (21%)
  between operations  14.3 us (8%)
  local copies, waits for them, and re-layouts  4.94 us (3%)
  other arithmetic  3.7 us (2%)
    pallas_call x3, Pallas kernels, product(): pl.pallas_call(functools.partial(product_kernel, calls), out_shape=[jax.S...  25 us
    ppermute x1, waiting for transfers between devices, per_device(): own = lax.ppermute(coupling[0], ('y', 'x', 'core'), pairs)  24.6 us
    all_gather x1, waiting for transfers between devices, per_device(): root = lax.all_gather(root_inverse, ('zh', 'zl'), axis=0, tiled=False)  17.2 us
    ppermute x3, starting transfers between devices, per_device(): pieces += [lax.ppermute(p, 'core', CORES) for p in (near, near_beside, far)]  13 us
    ppermute x1, waiting for transfers between devices, per_device(): near = lax.ppermute(own, ('x', 'core'), along_x)  11.7 us
    pallas_call x1, Pallas kernels, spread(): pl.pallas_call(spread_kernel, out_shape=[pltpu.HBM(shape, jnp.bfloat16)]...  10.5 us
    ppermute x1, waiting for transfers between devices, per_device(): far = lax.ppermute(near, ('x', 'core'), along_x)  8.28 us
    ppermute x1, starting transfers between devices, per_device(): forth = lax.ppermute(last, ('y', 'core'), opposite(4))  5.4 us
  transfers between devices with their start and end apart: 15, of which 8 were waited for; matrix products, arithmetic and copies ran while one was open for 3% of the time, Pallas kernels for 17%

profile of v11, /device:TPU:1, one launch (start us, length us, event | category | flops | bytes accessed | tf_op | source)
XLA Modules:
  0.0 187.4 jit_solution(17585538312564529984)
XLA Ops:
  7.2 0.0 all-gather.3.cloned.1.call-start
  7.2 0.7 all-gather.3.cloned.1.call-update
  7.9 4.6 %collective-permute-start = (f32[768,384]{1,0:T(8,128)}, f32[768,384]{1,0:T(8,128)S(1)}, u32[]{:S(2)}, u32[]{:S(2)}) collective-permute-start(f32[768,384]{1,0:T(8,128)} %bitcast.20), channel_id=1, source_target_pairs={{0,48},{8,64},{16,144},{24,224},{32,32},{40,112},{48,176},{56,240}... | collective-permute-start | bytes 3538952 | tf_op jit(solution)/shard_map/ppermute | solution.py:321
  12.5 1.0 slice.3
  13.6 1.0 reshape.109.rows_ref
  14.5 0.1 reshape.108
  14.6 0.7 fusion.2
  15.3 0.1 copy.18
  15.4 0.1 pad_add_fusion
  15.5 0.1 copy.17
  15.6 0.1 concatenate.16.table
  15.7 0.7 and_bitcast_fusion
  16.4 0.1 fusion.5.start_row
  16.5 24.6 %collective-permute-done.rest_0_ = f32[768,384]{1,0:T(8,128)S(1)} collective-permute-done((f32[768,384]{1,0:T(8,128)}, f32[768,384]{1,0:T(8,128)S(1)}, u32[]{:S(2)}, u32[]{:S(2)}) %collective-permute-start) | collective-permute-done | bytes 1179680 | tf_op jit(solution)/shard_map/ppermute | solution.py:321
  41.1 1.9 %collective-permute-start.1 = (f32[768,384]{1,0:T(8,128)S(1)}, f32[768,384]{1,0:T(8,128)S(1)}, u32[]{:S(2)}, u32[]{:S(2)}) collective-permute-start(f32[768,384]{1,0:T(8,128)S(1)} %collective-permute-done.rest_0_), channel_id=1, source_target_pairs={{0,8},{8,0},{1,9},{9,1},{2,10},{10,2},{3,11},{11,3},{4,12},{12,4},... | collective-permute-start | bytes 3538952 | tf_op jit(solution)/shard_map/ppermute | solution.py:325
  43.0 3.2 %collective-permute-start.2 = (f32[768,384]{1,0:T(8,128)S(1)}, f32[768,384]{1,0:T(8,128)S(1)}, u32[]{:S(2)}, u32[]{:S(2)}) collective-permute-start(f32[768,384]{1,0:T(8,128)S(1)} %collective-permute-done.rest_0_), channel_id=1, source_target_pairs={{0,16},{8,56},{16,32},{24,8},{32,48},{40,24},{48,0},{56,40},{1,17}... | collective-permute-start | bytes 3538952 | tf_op jit(solution)/shard_map/ppermute | solution.py:326
  46.2 0.0 collective-permute-done.1.rest_1_
  46.2 2.4 %collective-permute-start.3 = (f32[768,384]{1,0:T(8,128)S(1)}, f32[768,384]{1,0:T(8,128)S(1)}, u32[]{:S(2)}, u32[]{:S(2)}) collective-permute-start(f32[768,384]{1,0:T(8,128)S(1)} %collective-permute-done.1.rest_1_), channel_id=1, source_target_pairs={{0,16},{8,56},{16,32},{24,8},{32,48},{40,24},{48,0},{56,40},{1,17}... | collective-permute-start | bytes 3538952 | tf_op jit(solution)/shard_map/ppermute | solution.py:327
  48.6 11.7 %collective-permute-done.2.rest_2_ = f32[768,384]{1,0:T(8,128)S(1)} collective-permute-done((f32[768,384]{1,0:T(8,128)S(1)}, f32[768,384]{1,0:T(8,128)S(1)}, u32[]{:S(2)}, u32[]{:S(2)}) %collective-permute-start.2) | collective-permute-done | bytes 1179680 | tf_op jit(solution)/shard_map/ppermute | solution.py:326
  60.3 4.4 %collective-permute-start.4 = (f32[768,384]{1,0:T(8,128)S(1)}, f32[768,384]{1,0:T(8,128)S(1)}, u32[]{:S(2)}, u32[]{:S(2)}) collective-permute-start(f32[768,384]{1,0:T(8,128)S(1)} %collective-permute-done.2.rest_2_), channel_id=1, source_target_pairs={{0,16},{8,56},{16,32},{24,8},{32,48},{40,24},{48,0},{56,40},{1,17}... | collective-permute-start | bytes 3538952 | tf_op jit(solution)/shard_map/ppermute | solution.py:328
  64.7 1.9 %collective-permute-start.8 = (f32[768,384]{1,0:T(8,128)}, f32[768,384]{1,0:T(8,128)S(1)}, u32[]{:S(2)}, u32[]{:S(2)}) collective-permute-start(f32[768,384]{1,0:T(8,128)} %bitcast.21), channel_id=1, source_target_pairs={{0,192},{8,72},{64,0},{72,136},{128,64},{136,200},{192,128},{200,8... | collective-permute-start | bytes 3538952 | tf_op jit(solution)/shard_map/ppermute | solution.py:331
  66.7 4.3 %collective-permute-start.5 = (f32[768,384]{1,0:T(8,128)S(1)}, f32[768,384]{1,0:T(8,128)S(1)}, u32[]{:S(2)}, u32[]{:S(2)}) collective-permute-start(f32[768,384]{1,0:T(8,128)S(1)} %collective-permute-done.2.rest_2_), channel_id=1, source_target_pairs={{0,8},{8,0},{1,9},{9,1},{2,10},{10,2},{3,11},{11,3},{4,12},{12,4},... | collective-permute-start | bytes 3538952 | tf_op jit(solution)/shard_map/ppermute | solution.py:330
  71.0 2.0 %collective-permute-done.3.rest_3_ = f32[768,384]{1,0:T(8,128)S(1)} collective-permute-done((f32[768,384]{1,0:T(8,128)S(1)}, f32[768,384]{1,0:T(8,128)S(1)}, u32[]{:S(2)}, u32[]{:S(2)}) %collective-permute-start.3) | collective-permute-done | bytes 1179680 | tf_op jit(solution)/shard_map/ppermute | solution.py:327
  73.0 4.4 %collective-permute-start.6 = (f32[768,384]{1,0:T(8,128)S(1)}, f32[768,384]{1,0:T(8,128)S(1)}, u32[]{:S(2)}, u32[]{:S(2)}) collective-permute-start(f32[768,384]{1,0:T(8,128)S(1)} %collective-permute-done.3.rest_3_), channel_id=1, source_target_pairs={{0,8},{8,0},{1,9},{9,1},{2,10},{10,2},{3,11},{11,3},{4,12},{12,4},... | collective-permute-start | bytes 3538952 | tf_op jit(solution)/shard_map/ppermute | solution.py:330
  77.3 8.3 %collective-permute-done.4.rest_4_ = f32[768,384]{1,0:T(8,128)S(1)} collective-permute-done((f32[768,384]{1,0:T(8,128)S(1)}, f32[768,384]{1,0:T(8,128)S(1)}, u32[]{:S(2)}, u32[]{:S(2)}) %collective-permute-start.4) | collective-permute-done | bytes 1179680 | tf_op jit(solution)/shard_map/ppermute | solution.py:328
  85.6 4.4 %collective-permute-start.7 = (f32[768,384]{1,0:T(8,128)S(1)}, f32[768,384]{1,0:T(8,128)S(1)}, u32[]{:S(2)}, u32[]{:S(2)}) collective-permute-start(f32[768,384]{1,0:T(8,128)S(1)} %collective-permute-done.4.rest_4_), channel_id=1, source_target_pairs={{0,8},{8,0},{1,9},{9,1},{2,10},{10,2},{3,11},{11,3},{4,12},{12,4},... | collective-permute-start | bytes 3538952 | tf_op jit(solution)/shard_map/ppermute | solution.py:330
  90.0 0.0 collective-permute-done.8.rest_9_
  90.0 0.0 collective-permute-done.5.rest_5_
  90.0 0.0 collective-permute-done.6.rest_6_
  90.0 2.4 %collective-permute-done.7.rest_7_ = f32[768,384]{1,0:T(8,128)S(1)} collective-permute-done((f32[768,384]{1,0:T(8,128)S(1)}, f32[768,384]{1,0:T(8,128)S(1)}, u32[]{:S(2)}, u32[]{:S(2)}) %collective-permute-start.7) | collective-permute-done | bytes 1179680 | tf_op jit(solution)/shard_map/ppermute | solution.py:330
  92.4 0.0 copy-start
  92.4 1.3 copy-done
  93.7 10.5 %shard_map.77 = (bf16[10,768,384]{2,1,0:T(8,128)(2,1)}, bf16[10,768,384]{2,1,0:T(8,128)(2,1)}) custom-call(s32[10]{0:T(128)S(1)} %fusion.5.start_row, s32[384,128]{1,0:T(8,128)S(1)} %reshape.109.rows_ref, f32[768,384]{1,0:T(8,128)S(1)} %collective-permute-done.rest_0_, f32[768,384]{1,0:T(8,128)S(1)} %collective-permute-done.1.rest_1_, ...), custom_call_target="tpu_custom_call" | custom-call | flops 1509949440 | bytes 23592960 | tf_op jit(solution)/shard_map/pallas_call | solution.py:125
  104.2 17.2 %all-gather.3.cloned.1.call-done = f32[16384,128]{1,0:T(8,128)} async-done(((f32[1024,128]{1,0:T(8,128)}), f32[16384,128]{1,0:T(8,128)}) %all-gather.3.cloned.1.call-update) | async-done | bytes 8388624 | tf_op jit(solution)/shard_map/all_gather | solution.py:297
  121.4 6.9 %shard_map.79 = f32[768,384]{1,0:T(8,128)S(1)} custom-call(s32[4,21]{1,0:T(4,128)S(1)} %concatenate.16.table, f32[16,1024,128]{2,1,0:T(8,128)} %bitcast.23, bf16[10,768,384]{2,1,0:T(8,128)(2,1)} %get-tuple-element.23.high_hbm, bf16[10,768,384]{2,1,0:T(8,128)(2,1)} %get-tuple-element.24.low_hbm), custom_call_target="tpu_custom_call" | custom-call | flops 2717908992 | bytes 7077888 | tf_op jit(solution)/shard_map/pallas_call | solution.py:218
  128.2 4.5 %collective-permute-start.9 = (f32[768,384]{1,0:T(8,128)S(1)}, f32[768,384]{1,0:T(8,128)S(1)}, u32[]{:S(2)}, u32[]{:S(2)}) collective-permute-start(f32[768,384]{1,0:T(8,128)S(1)} %shard_map.79), channel_id=1, source_target_pairs={{0,64},{8,200},{64,128},{72,8},{128,192},{136,72},{192,0},{200,136... | collective-permute-start | bytes 3538952 | tf_op jit(solution)/shard_map/ppermute | solution.py:336
  132.8 11.2 %shard_map.78 = (f32[768,384]{1,0:T(8,128)S(1)}, f32[768,384]{1,0:T(8,128)S(1)}) custom-call(s32[4,21]{1,0:T(4,128)S(1)} %concatenate.16.table, f32[16,1024,128]{2,1,0:T(8,128)} %bitcast.24, bf16[10,768,384]{2,1,0:T(8,128)(2,1)} %get-tuple-element.23.high_hbm, bf16[10,768,384]{2,1,0:T(8,128)(2,1)} %get-tuple-element.24.low_hbm), custom_call_target="tpu_custom_call" | custom-call | flops 5435817984 | bytes 14155776 | tf_op jit(solution)/shard_map/pallas_call | solution.py:218
  144.0 1.9 %collective-permute-start.11 = (f32[768,384]{1,0:T(8,128)S(1)}, f32[768,384]{1,0:T(8,128)S(1)}, u32[]{:S(2)}, u32[]{:S(2)}) collective-permute-start(f32[768,384]{1,0:T(8,128)S(1)} %get-tuple-element.29), channel_id=1, source_target_pairs={{0,192},{8,72},{64,0},{72,136},{128,64},{136,200},{192,128},{200,8... | collective-permute-start | bytes 3538952 | tf_op jit(solution)/shard_map/ppermute | solution.py:338
  146.0 0.0 collective-permute-done.9.second
  146.0 1.6 shard_map.80
  147.6 4.8 %collective-permute-start.10 = (f32[1,384]{1,0:T(1,128)S(1)}, f32[1,384]{1,0:T(1,128)S(1)}, u32[]{:S(2)}, u32[]{:S(2)}) collective-permute-start(f32[1,384]{1,0:T(1,128)S(1)} %get-tuple-element.27), channel_id=1, source_target_pairs={{0,64},{8,200},{64,128},{72,8},{128,192},{136,72},{192,0},{200,136... | collective-permute-start | bytes 4616 | tf_op jit(solution)/shard_map/ppermute | solution.py:340
  152.4 0.7 collective-permute-done.10
  153.1 5.4 %collective-permute-start.12 = (f32[768,384]{1,0:T(8,128)S(1)}, f32[768,384]{1,0:T(8,128)}, u32[]{:S(2)}, u32[]{:S(2)}) collective-permute-start(f32[768,384]{1,0:T(8,128)S(1)} %get-tuple-element.34), channel_id=1, source_target_pairs={{0,64},{8,200},{64,128},{72,8},{128,192},{136,72},{192,0},{200,136... | collective-permute-start | bytes 3538952 | tf_op jit(solution)/shard_map/ppermute | solution.py:342
  158.5 6.9 %shard_map.81.first = f32[768,384]{1,0:T(8,128)S(1)} custom-call(s32[4,21]{1,0:T(4,128)S(1)} %concatenate.16.table, f32[16,1024,128]{2,1,0:T(8,128)} %bitcast.25, bf16[10,768,384]{2,1,0:T(8,128)(2,1)} %get-tuple-element.23.high_hbm, bf16[10,768,384]{2,1,0:T(8,128)(2,1)} %get-tuple-element.24.low_hbm), custom_call_target="tpu_custom_call" | custom-call | flops 2717908992 | bytes 7077888 | tf_op jit(solution)/shard_map/pallas_call | solution.py:218
  165.4 0.0 copy-start.1
  165.4 0.0 collective-permute-done.11.second
  165.4 1.6 shard_map.82
  167.1 0.6 broadcast_in_dim.15
  167.7 4.5 %all-to-all-start = ((f32[8,1,384]{2,1,0:T(1,128)}), f32[8,1,384]{2,1,0:T(1,128)S(1)}, u32[]{:S(2)}, u32[]{:S(2)}) async-start(f32[8,1,384]{2,1,0:T(1,128)} %broadcast_in_dim.15), calls=%async_computation | async-start | bytes 24576 | tf_op jit(solution)/shard_map/all_to_all | solution.py:345
  172.1 0.8 fusion.1
  173.0 3.8 %all-to-all-done = f32[8,1,384]{2,1,0:T(1,128)S(1)} async-done(((f32[8,1,384]{2,1,0:T(1,128)}), f32[8,1,384]{2,1,0:T(1,128)S(1)}, u32[]{:S(2)}, u32[]{:S(2)}) %all-to-all-start) | async-done | bytes 12320 | tf_op jit(solution)/shard_map/all_to_all | solution.py:345
  176.8 0.0 copy-done.1
  176.8 0.6 reshape_add_fusion
  177.4 0.0 collective-permute-done.12
  177.4 1.4 add.122
  178.8 1.8 convolution_negate_fusion
  (5 shorter events, 0.1 us)
Async XLA Ops:
  7.2 114.2 %all-gather.3.cloned.1.call-start = ((), (), s32[]{:S(2)}) async-start(), calls=%async_computation.1 | async-start | bytes 8912896 | tf_op jit(solution)/shard_map/all_gather | solution.py:297
  7.9 33.2 %collective-permute-start = (f32[768,384]{1,0:T(8,128)}, f32[768,384]{1,0:T(8,128)S(1)}, u32[]{:S(2)}, u32[]{:S(2)}) collective-permute-start(f32[768,384]{1,0:T(8,128)} %bitcast.20), channel_id=1, source_target_pairs={{0,48},{8,64},{16,144},{24,224},{32,32},{40,112},{48,176},{56,240}... | collective-permute-start | bytes 3538952 | tf_op jit(solution)/shard_map/ppermute | solution.py:321
  41.1 5.1 %collective-permute-start.1 = (f32[768,384]{1,0:T(8,128)S(1)}, f32[768,384]{1,0:T(8,128)S(1)}, u32[]{:S(2)}, u32[]{:S(2)}) collective-permute-start(f32[768,384]{1,0:T(8,128)S(1)} %collective-permute-done.rest_0_), channel_id=1, source_target_pairs={{0,8},{8,0},{1,9},{9,1},{2,10},{10,2},{3,11},{11,3},{4,12},{12,4},... | collective-permute-start | bytes 3538952 | tf_op jit(solution)/shard_map/ppermute | solution.py:325
  43.0 17.3 %collective-permute-start.2 = (f32[768,384]{1,0:T(8,128)S(1)}, f32[768,384]{1,0:T(8,128)S(1)}, u32[]{:S(2)}, u32[]{:S(2)}) collective-permute-start(f32[768,384]{1,0:T(8,128)S(1)} %collective-permute-done.rest_0_), channel_id=1, source_target_pairs={{0,16},{8,56},{16,32},{24,8},{32,48},{40,24},{48,0},{56,40},{1,17}... | collective-permute-start | bytes 3538952 | tf_op jit(solution)/shard_map/ppermute | solution.py:326
  46.2 26.8 %collective-permute-start.3 = (f32[768,384]{1,0:T(8,128)S(1)}, f32[768,384]{1,0:T(8,128)S(1)}, u32[]{:S(2)}, u32[]{:S(2)}) collective-permute-start(f32[768,384]{1,0:T(8,128)S(1)} %collective-permute-done.1.rest_1_), channel_id=1, source_target_pairs={{0,16},{8,56},{16,32},{24,8},{32,48},{40,24},{48,0},{56,40},{1,17}... | collective-permute-start | bytes 3538952 | tf_op jit(solution)/shard_map/ppermute | solution.py:327
  60.3 25.3 %collective-permute-start.4 = (f32[768,384]{1,0:T(8,128)S(1)}, f32[768,384]{1,0:T(8,128)S(1)}, u32[]{:S(2)}, u32[]{:S(2)}) collective-permute-start(f32[768,384]{1,0:T(8,128)S(1)} %collective-permute-done.2.rest_2_), channel_id=1, source_target_pairs={{0,16},{8,56},{16,32},{24,8},{32,48},{40,24},{48,0},{56,40},{1,17}... | collective-permute-start | bytes 3538952 | tf_op jit(solution)/shard_map/ppermute | solution.py:328
  64.7 25.2 %collective-permute-start.8 = (f32[768,384]{1,0:T(8,128)}, f32[768,384]{1,0:T(8,128)S(1)}, u32[]{:S(2)}, u32[]{:S(2)}) collective-permute-start(f32[768,384]{1,0:T(8,128)} %bitcast.21), channel_id=1, source_target_pairs={{0,192},{8,72},{64,0},{72,136},{128,64},{136,200},{192,128},{200,8... | collective-permute-start | bytes 3538952 | tf_op jit(solution)/shard_map/ppermute | solution.py:331
  66.7 23.3 %collective-permute-start.5 = (f32[768,384]{1,0:T(8,128)S(1)}, f32[768,384]{1,0:T(8,128)S(1)}, u32[]{:S(2)}, u32[]{:S(2)}) collective-permute-start(f32[768,384]{1,0:T(8,128)S(1)} %collective-permute-done.2.rest_2_), channel_id=1, source_target_pairs={{0,8},{8,0},{1,9},{9,1},{2,10},{10,2},{3,11},{11,3},{4,12},{12,4},... | collective-permute-start | bytes 3538952 | tf_op jit(solution)/shard_map/ppermute | solution.py:330
  73.0 17.0 %collective-permute-start.6 = (f32[768,384]{1,0:T(8,128)S(1)}, f32[768,384]{1,0:T(8,128)S(1)}, u32[]{:S(2)}, u32[]{:S(2)}) collective-permute-start(f32[768,384]{1,0:T(8,128)S(1)} %collective-permute-done.3.rest_3_), channel_id=1, source_target_pairs={{0,8},{8,0},{1,9},{9,1},{2,10},{10,2},{3,11},{11,3},{4,12},{12,4},... | collective-permute-start | bytes 3538952 | tf_op jit(solution)/shard_map/ppermute | solution.py:330
  85.6 6.8 %collective-permute-start.7 = (f32[768,384]{1,0:T(8,128)S(1)}, f32[768,384]{1,0:T(8,128)S(1)}, u32[]{:S(2)}, u32[]{:S(2)}) collective-permute-start(f32[768,384]{1,0:T(8,128)S(1)} %collective-permute-done.4.rest_4_), channel_id=1, source_target_pairs={{0,8},{8,0},{1,9},{9,1},{2,10},{10,2},{3,11},{11,3},{4,12},{12,4},... | collective-permute-start | bytes 3538952 | tf_op jit(solution)/shard_map/ppermute | solution.py:330
  92.4 1.3 copy-start
  128.2 17.7 %collective-permute-start.9 = (f32[768,384]{1,0:T(8,128)S(1)}, f32[768,384]{1,0:T(8,128)S(1)}, u32[]{:S(2)}, u32[]{:S(2)}) collective-permute-start(f32[768,384]{1,0:T(8,128)S(1)} %shard_map.79), channel_id=1, source_target_pairs={{0,64},{8,200},{64,128},{72,8},{128,192},{136,72},{192,0},{200,136... | collective-permute-start | bytes 3538952 | tf_op jit(solution)/shard_map/ppermute | solution.py:336
  144.0 21.3 %collective-permute-start.11 = (f32[768,384]{1,0:T(8,128)S(1)}, f32[768,384]{1,0:T(8,128)S(1)}, u32[]{:S(2)}, u32[]{:S(2)}) collective-permute-start(f32[768,384]{1,0:T(8,128)S(1)} %get-tuple-element.29), channel_id=1, source_target_pairs={{0,192},{8,72},{64,0},{72,136},{128,64},{136,200},{192,128},{200,8... | collective-permute-start | bytes 3538952 | tf_op jit(solution)/shard_map/ppermute | solution.py:338
  147.6 5.5 %collective-permute-start.10 = (f32[1,384]{1,0:T(1,128)S(1)}, f32[1,384]{1,0:T(1,128)S(1)}, u32[]{:S(2)}, u32[]{:S(2)}) collective-permute-start(f32[1,384]{1,0:T(1,128)S(1)} %get-tuple-element.27), channel_id=1, source_target_pairs={{0,64},{8,200},{64,128},{72,8},{128,192},{136,72},{192,0},{200,136... | collective-permute-start | bytes 4616 | tf_op jit(solution)/shard_map/ppermute | solution.py:340
  153.1 24.3 %collective-permute-start.12 = (f32[768,384]{1,0:T(8,128)S(1)}, f32[768,384]{1,0:T(8,128)}, u32[]{:S(2)}, u32[]{:S(2)}) collective-permute-start(f32[768,384]{1,0:T(8,128)S(1)} %get-tuple-element.34), channel_id=1, source_target_pairs={{0,64},{8,200},{64,128},{72,8},{128,192},{136,72},{192,0},{200,136... | collective-permute-start | bytes 3538952 | tf_op jit(solution)/shard_map/ppermute | solution.py:342
  165.4 11.4 %copy-start.1 = (f32[1,384]{1,0:T(1,128)S(1)}, f32[1,384]{1,0:T(1,128)}, u32[]{:S(2)}) copy-start(f32[1,384]{1,0:T(1,128)} %param.9) | copy-start | bytes 4612
  167.7 9.1 %all-to-all-start = ((f32[8,1,384]{2,1,0:T(1,128)}), f32[8,1,384]{2,1,0:T(1,128)S(1)}, u32[]{:S(2)}, u32[]{:S(2)}) async-start(f32[8,1,384]{2,1,0:T(1,128)} %broadcast_in_dim.15), calls=%async_computation | async-start | bytes 24576 | tf_op jit(solution)/shard_map/all_to_all | solution.py:345
Sparse Core Ops, SparseCore 0:
  10.1 111.2 all-gather.2

commit v12 on v11

--- a/solution.py
+++ b/solution.py
@@ -337,20 +337,16 @@
     second, first = product((2, 1), table, root, high, low)
     back = lax.ppermute(first, ("y", "core"), opposite(4, -1))
     last, last_sums = weigh(9, second, passed, high, low)
+    table, last, last_sums = lax.optimization_barrier((table, last, last_sums))
     last_sums = lax.ppermute(last_sums, ("y", "core"), opposite(4))
-    table, last, last_sums = lax.optimization_barrier((table, last, last_sums))
+    (home,) = product((3,), table, root, high, low)
+    last, home, last_sums = lax.optimization_barrier((last, home, last_sums))
     forth = lax.ppermute(last, ("y", "core"), opposite(4))
-    (home,) = product((3,), table, root, high, low)
     kept, sums = weigh(8, home, back, high, low)
-    sums = lax.all_to_all(
-        jnp.broadcast_to(sums + last_sums, (8, cols)),
-        ("x", "core"),
-        split_axis=0,
-        concat_axis=0,
-        tiled=True,
-    )
+    sums = jnp.broadcast_to(sums + last_sums, (8, cols))
+    kept, sums = lax.optimization_barrier((kept, sums))
+    sums = lax.all_to_all(sums, ("x", "core"), split_axis=0, concat_axis=0, tiled=True)
     marginal = pivot_variance + jnp.sum(sums, axis=0, keepdims=True)
-    kept, marginal = lax.optimization_barrier((kept, marginal))
     summed = kept + forth
 
     own_place = lax.dynamic_slice(root_row, (zh * 4 + y, own_range * rows), (1, rows))[0]

time: 188 us -> 188 us (level)
  starting transfers between devices: 52.6 us -> 49.6 us
  waiting for transfers between devices: 71.4 us -> 73.9 us
    ppermute x1, starting transfers between devices: 5.4 us -> 1.93 us  [per_device(): forth = lax.ppermute(last, ('y', 'core'), opposite(4))]
    ppermute x1, waiting for transfers between devices: 0.01 us -> 2.36 us  [per_device(): forth = lax.ppermute(last, ('y', 'core'), opposite(4))]
  transfers between devices with their start and end apart: 15 -> 15, of which waited for: 8 -> 9; matrix products, arithmetic and copies ran while one was open for 3% -> 3% of each run, Pallas kernels for 17% -> 17%
where the time goes in v12:
time: 188 us; the launch traced here: 187 us
  waiting for transfers between devices  73.9 us (39%)
  starting transfers between devices  49.6 us (26%)
  Pallas kernels  38.7 us (21%)
  between operations  14.3 us (8%)
  local copies, waits for them, and re-layouts  4.95 us (3%)
  other arithmetic  3.7 us (2%)
    pallas_call x3, Pallas kernels, product(): pl.pallas_call(functools.partial(product_kernel, calls), out_shape=[jax.S...  25 us
    ppermute x1, waiting for transfers between devices, per_device(): own = lax.ppermute(coupling[0], ('y', 'x', 'core'), pairs)  24.6 us
    all_gather x1, waiting for transfers between devices, per_device(): root = lax.all_gather(root_inverse, ('zh', 'zl'), axis=0, tiled=False)  17.2 us
    ppermute x3, starting transfers between devices, per_device(): pieces += [lax.ppermute(p, 'core', CORES) for p in (near, near_beside, far)]  13 us
    ppermute x1, waiting for transfers between devices, per_device(): near = lax.ppermute(own, ('x', 'core'), along_x)  11.7 us
    pallas_call x1, Pallas kernels, spread(): pl.pallas_call(spread_kernel, out_shape=[pltpu.HBM(shape, jnp.bfloat16)]...  10.5 us
    ppermute x1, waiting for transfers between devices, per_device(): far = lax.ppermute(near, ('x', 'core'), along_x)  8.28 us
    ppermute x1, starting transfers between devices, per_device(): last_sums = lax.ppermute(last_sums, ('y', 'core'), opposite(4))  4.99 us
  transfers between devices with their start and end apart: 15, of which 9 were waited for; matrix products, arithmetic and copies ran while one was open for 3% of the time, Pallas kernels for 17%

profile of v12, /device:TPU:1, one launch (start us, length us, event | category | flops | bytes accessed | tf_op | source)
XLA Modules:
  0.0 186.9 jit_solution(17345500570208167284)
XLA Ops:
  7.2 0.0 all-gather.3.cloned.1.call-start
  7.2 0.7 all-gather.3.cloned.1.call-update
  7.9 4.6 %collective-permute-start = (f32[768,384]{1,0:T(8,128)}, f32[768,384]{1,0:T(8,128)S(1)}, u32[]{:S(2)}, u32[]{:S(2)}) collective-permute-start(f32[768,384]{1,0:T(8,128)} %bitcast.20), channel_id=1, source_target_pairs={{0,48},{8,64},{16,144},{24,224},{32,32},{40,112},{48,176},{56,240}... | collective-permute-start | bytes 3538952 | tf_op jit(solution)/shard_map/ppermute | solution.py:321
  12.5 1.0 slice.3
  13.6 1.0 reshape.105.rows_ref
  14.5 0.1 reshape.104
  14.6 0.7 fusion.2
  15.3 0.1 copy.14
  15.4 0.1 pad_add_fusion
  15.5 0.1 copy.13
  15.6 0.1 concatenate.16.table
  15.7 0.7 and_bitcast_fusion
  16.4 0.1 fusion.5.start_row
  16.5 24.6 %collective-permute-done.rest_0_ = f32[768,384]{1,0:T(8,128)S(1)} collective-permute-done((f32[768,384]{1,0:T(8,128)}, f32[768,384]{1,0:T(8,128)S(1)}, u32[]{:S(2)}, u32[]{:S(2)}) %collective-permute-start) | collective-permute-done | bytes 1179680 | tf_op jit(solution)/shard_map/ppermute | solution.py:321
  41.1 1.9 %collective-permute-start.1 = (f32[768,384]{1,0:T(8,128)S(1)}, f32[768,384]{1,0:T(8,128)S(1)}, u32[]{:S(2)}, u32[]{:S(2)}) collective-permute-start(f32[768,384]{1,0:T(8,128)S(1)} %collective-permute-done.rest_0_), channel_id=1, source_target_pairs={{0,8},{8,0},{1,9},{9,1},{2,10},{10,2},{3,11},{11,3},{4,12},{12,4},... | collective-permute-start | bytes 3538952 | tf_op jit(solution)/shard_map/ppermute | solution.py:325
  43.0 3.2 %collective-permute-start.2 = (f32[768,384]{1,0:T(8,128)S(1)}, f32[768,384]{1,0:T(8,128)S(1)}, u32[]{:S(2)}, u32[]{:S(2)}) collective-permute-start(f32[768,384]{1,0:T(8,128)S(1)} %collective-permute-done.rest_0_), channel_id=1, source_target_pairs={{0,16},{8,56},{16,32},{24,8},{32,48},{40,24},{48,0},{56,40},{1,17}... | collective-permute-start | bytes 3538952 | tf_op jit(solution)/shard_map/ppermute | solution.py:326
  46.2 0.0 collective-permute-done.1.rest_1_
  46.2 2.4 %collective-permute-start.3 = (f32[768,384]{1,0:T(8,128)S(1)}, f32[768,384]{1,0:T(8,128)S(1)}, u32[]{:S(2)}, u32[]{:S(2)}) collective-permute-start(f32[768,384]{1,0:T(8,128)S(1)} %collective-permute-done.1.rest_1_), channel_id=1, source_target_pairs={{0,16},{8,56},{16,32},{24,8},{32,48},{40,24},{48,0},{56,40},{1,17}... | collective-permute-start | bytes 3538952 | tf_op jit(solution)/shard_map/ppermute | solution.py:327
  48.6 11.7 %collective-permute-done.2.rest_2_ = f32[768,384]{1,0:T(8,128)S(1)} collective-permute-done((f32[768,384]{1,0:T(8,128)S(1)}, f32[768,384]{1,0:T(8,128)S(1)}, u32[]{:S(2)}, u32[]{:S(2)}) %collective-permute-start.2) | collective-permute-done | bytes 1179680 | tf_op jit(solution)/shard_map/ppermute | solution.py:326
  60.3 4.4 %collective-permute-start.4 = (f32[768,384]{1,0:T(8,128)S(1)}, f32[768,384]{1,0:T(8,128)S(1)}, u32[]{:S(2)}, u32[]{:S(2)}) collective-permute-start(f32[768,384]{1,0:T(8,128)S(1)} %collective-permute-done.2.rest_2_), channel_id=1, source_target_pairs={{0,16},{8,56},{16,32},{24,8},{32,48},{40,24},{48,0},{56,40},{1,17}... | collective-permute-start | bytes 3538952 | tf_op jit(solution)/shard_map/ppermute | solution.py:328
  64.7 1.9 %collective-permute-start.8 = (f32[768,384]{1,0:T(8,128)}, f32[768,384]{1,0:T(8,128)S(1)}, u32[]{:S(2)}, u32[]{:S(2)}) collective-permute-start(f32[768,384]{1,0:T(8,128)} %bitcast.21), channel_id=1, source_target_pairs={{0,192},{8,72},{64,0},{72,136},{128,64},{136,200},{192,128},{200,8... | collective-permute-start | bytes 3538952 | tf_op jit(solution)/shard_map/ppermute | solution.py:331
  66.7 4.3 %collective-permute-start.5 = (f32[768,384]{1,0:T(8,128)S(1)}, f32[768,384]{1,0:T(8,128)S(1)}, u32[]{:S(2)}, u32[]{:S(2)}) collective-permute-start(f32[768,384]{1,0:T(8,128)S(1)} %collective-permute-done.2.rest_2_), channel_id=1, source_target_pairs={{0,8},{8,0},{1,9},{9,1},{2,10},{10,2},{3,11},{11,3},{4,12},{12,4},... | collective-permute-start | bytes 3538952 | tf_op jit(solution)/shard_map/ppermute | solution.py:330
  71.0 2.0 %collective-permute-done.3.rest_3_ = f32[768,384]{1,0:T(8,128)S(1)} collective-permute-done((f32[768,384]{1,0:T(8,128)S(1)}, f32[768,384]{1,0:T(8,128)S(1)}, u32[]{:S(2)}, u32[]{:S(2)}) %collective-permute-start.3) | collective-permute-done | bytes 1179680 | tf_op jit(solution)/shard_map/ppermute | solution.py:327
  73.0 4.4 %collective-permute-start.6 = (f32[768,384]{1,0:T(8,128)S(1)}, f32[768,384]{1,0:T(8,128)S(1)}, u32[]{:S(2)}, u32[]{:S(2)}) collective-permute-start(f32[768,384]{1,0:T(8,128)S(1)} %collective-permute-done.3.rest_3_), channel_id=1, source_target_pairs={{0,8},{8,0},{1,9},{9,1},{2,10},{10,2},{3,11},{11,3},{4,12},{12,4},... | collective-permute-start | bytes 3538952 | tf_op jit(solution)/shard_map/ppermute | solution.py:330
  77.3 8.3 %collective-permute-done.4.rest_4_ = f32[768,384]{1,0:T(8,128)S(1)} collective-permute-done((f32[768,384]{1,0:T(8,128)S(1)}, f32[768,384]{1,0:T(8,128)S(1)}, u32[]{:S(2)}, u32[]{:S(2)}) %collective-permute-start.4) | collective-permute-done | bytes 1179680 | tf_op jit(solution)/shard_map/ppermute | solution.py:328
  85.6 4.4 %collective-permute-start.7 = (f32[768,384]{1,0:T(8,128)S(1)}, f32[768,384]{1,0:T(8,128)S(1)}, u32[]{:S(2)}, u32[]{:S(2)}) collective-permute-start(f32[768,384]{1,0:T(8,128)S(1)} %collective-permute-done.4.rest_4_), channel_id=1, source_target_pairs={{0,8},{8,0},{1,9},{9,1},{2,10},{10,2},{3,11},{11,3},{4,12},{12,4},... | collective-permute-start | bytes 3538952 | tf_op jit(solution)/shard_map/ppermute | solution.py:330
  90.0 0.0 collective-permute-done.8.rest_9_
  90.0 0.0 collective-permute-done.5.rest_5_
  90.0 0.0 collective-permute-done.6.rest_6_
  90.0 2.4 %collective-permute-done.7.rest_7_ = f32[768,384]{1,0:T(8,128)S(1)} collective-permute-done((f32[768,384]{1,0:T(8,128)S(1)}, f32[768,384]{1,0:T(8,128)S(1)}, u32[]{:S(2)}, u32[]{:S(2)}) %collective-permute-start.7) | collective-permute-done | bytes 1179680 | tf_op jit(solution)/shard_map/ppermute | solution.py:330
  92.4 0.0 copy-start
  92.4 1.3 copy-done
  93.7 10.5 %shard_map.77 = (bf16[10,768,384]{2,1,0:T(8,128)(2,1)}, bf16[10,768,384]{2,1,0:T(8,128)(2,1)}) custom-call(s32[10]{0:T(128)S(1)} %fusion.5.start_row, s32[384,128]{1,0:T(8,128)S(1)} %reshape.105.rows_ref, f32[768,384]{1,0:T(8,128)S(1)} %collective-permute-done.rest_0_, f32[768,384]{1,0:T(8,128)S(1)} %collective-permute-done.1.rest_1_, ...), custom_call_target="tpu_custom_call" | custom-call | flops 1509949440 | bytes 23592960 | tf_op jit(solution)/shard_map/pallas_call | solution.py:125
  104.2 17.2 %all-gather.3.cloned.1.call-done = f32[16384,128]{1,0:T(8,128)} async-done(((f32[1024,128]{1,0:T(8,128)}), f32[16384,128]{1,0:T(8,128)}) %all-gather.3.cloned.1.call-update) | async-done | bytes 8388624 | tf_op jit(solution)/shard_map/all_gather | solution.py:297
  121.4 6.9 %shard_map.79 = f32[768,384]{1,0:T(8,128)S(1)} custom-call(s32[4,21]{1,0:T(4,128)S(1)} %concatenate.16.table, f32[16,1024,128]{2,1,0:T(8,128)} %bitcast.23, bf16[10,768,384]{2,1,0:T(8,128)(2,1)} %get-tuple-element.26.high_hbm, bf16[10,768,384]{2,1,0:T(8,128)(2,1)} %get-tuple-element.27.low_hbm), custom_call_target="tpu_custom_call" | custom-call | flops 2717908992 | bytes 7077888 | tf_op jit(solution)/shard_map/pallas_call | solution.py:218
  128.2 4.5 %collective-permute-start.9 = (f32[768,384]{1,0:T(8,128)S(1)}, f32[768,384]{1,0:T(8,128)S(1)}, u32[]{:S(2)}, u32[]{:S(2)}) collective-permute-start(f32[768,384]{1,0:T(8,128)S(1)} %shard_map.79), channel_id=1, source_target_pairs={{0,64},{8,200},{64,128},{72,8},{128,192},{136,72},{192,0},{200,136... | collective-permute-start | bytes 3538952 | tf_op jit(solution)/shard_map/ppermute | solution.py:336
  132.8 11.2 %shard_map.78 = (f32[768,384]{1,0:T(8,128)S(1)}, f32[768,384]{1,0:T(8,128)S(1)}) custom-call(s32[4,21]{1,0:T(4,128)S(1)} %concatenate.16.table, f32[16,1024,128]{2,1,0:T(8,128)} %bitcast.24, bf16[10,768,384]{2,1,0:T(8,128)(2,1)} %get-tuple-element.26.high_hbm, bf16[10,768,384]{2,1,0:T(8,128)(2,1)} %get-tuple-element.27.low_hbm), custom_call_target="tpu_custom_call" | custom-call | flops 5435817984 | bytes 14155776 | tf_op jit(solution)/shard_map/pallas_call | solution.py:218
  144.0 1.9 %collective-permute-start.11 = (f32[768,384]{1,0:T(8,128)S(1)}, f32[768,384]{1,0:T(8,128)S(1)}, u32[]{:S(2)}, u32[]{:S(2)}) collective-permute-start(f32[768,384]{1,0:T(8,128)S(1)} %get-tuple-element.35), channel_id=1, source_target_pairs={{0,192},{8,72},{64,0},{72,136},{128,64},{136,200},{192,128},{200,8... | collective-permute-start | bytes 3538952 | tf_op jit(solution)/shard_map/ppermute | solution.py:338
  146.0 0.0 collective-permute-done.9.second
  146.0 1.6 shard_map.80
  147.6 5.0 %collective-permute-start.10 = (f32[1,384]{1,0:T(1,128)S(1)}, f32[1,384]{1,0:T(1,128)S(1)}, u32[]{:S(2)}, u32[]{:S(2)}) collective-permute-start(f32[1,384]{1,0:T(1,128)S(1)} %get-tuple-element.33), channel_id=1, source_target_pairs={{0,64},{8,200},{64,128},{72,8},{128,192},{136,72},{192,0},{200,136... | collective-permute-start | bytes 4616 | tf_op jit(solution)/shard_map/ppermute | solution.py:341
  152.6 6.9 %shard_map.81.first = f32[768,384]{1,0:T(8,128)S(1)} custom-call(s32[4,21]{1,0:T(4,128)S(1)} %concatenate.16.table, f32[16,1024,128]{2,1,0:T(8,128)} %bitcast.25, bf16[10,768,384]{2,1,0:T(8,128)(2,1)} %get-tuple-element.26.high_hbm, bf16[10,768,384]{2,1,0:T(8,128)(2,1)} %get-tuple-element.27.low_hbm), custom_call_target="tpu_custom_call" | custom-call | flops 2717908992 | bytes 7077888 | tf_op jit(solution)/shard_map/pallas_call | solution.py:218
  159.5 0.0 copy-start.1
  159.5 0.0 collective-permute-done.10
  159.5 1.9 %collective-permute-start.12 = (f32[768,384]{1,0:T(8,128)S(1)}, f32[768,384]{1,0:T(8,128)}, u32[]{:S(2)}, u32[]{:S(2)}) collective-permute-start(f32[768,384]{1,0:T(8,128)S(1)} %get-tuple-element.40), channel_id=1, source_target_pairs={{0,64},{8,200},{64,128},{72,8},{128,192},{136,72},{192,0},{200,136... | collective-permute-start | bytes 3538952 | tf_op jit(solution)/shard_map/ppermute | solution.py:344
  161.4 0.8 collective-permute-done.11.second
  162.2 1.6 shard_map.82
  163.9 0.6 all_to_all.6
  164.5 4.7 %all-to-all-start = ((f32[8,1,384]{2,1,0:T(1,128)}), f32[8,1,384]{2,1,0:T(1,128)S(1)}, u32[]{:S(2)}, u32[]{:S(2)}) async-start(f32[8,1,384]{2,1,0:T(1,128)} %all_to_all.6), calls=%async_computation | async-start | bytes 24576 | tf_op jit(solution)/shard_map/all_to_all | solution.py:348
  169.2 0.8 fusion.1
  170.0 3.9 %all-to-all-done = f32[8,1,384]{2,1,0:T(1,128)S(1)} async-done(((f32[8,1,384]{2,1,0:T(1,128)}), f32[8,1,384]{2,1,0:T(1,128)S(1)}, u32[]{:S(2)}, u32[]{:S(2)}) %all-to-all-start) | async-done | bytes 12320 | tf_op jit(solution)/shard_map/all_to_all | solution.py:348
  173.9 0.0 copy-done.1
  173.9 0.6 reshape_add_fusion
  174.5 2.4 %collective-permute-done.12 = f32[768,384]{1,0:T(8,128)} collective-permute-done((f32[768,384]{1,0:T(8,128)S(1)}, f32[768,384]{1,0:T(8,128)}, u32[]{:S(2)}, u32[]{:S(2)}) %collective-permute-start.12) | collective-permute-done | bytes 1179680 | tf_op jit(solution)/shard_map/ppermute | solution.py:344
  176.8 1.4 add.118
  178.2 1.8 convolution_negate_fusion
  (6 shorter events, 0.1 us)
Async XLA Ops:
  7.2 114.2 %all-gather.3.cloned.1.call-start = ((), (), s32[]{:S(2)}) async-start(), calls=%async_computation.1 | async-start | bytes 8912896 | tf_op jit(solution)/shard_map/all_gather | solution.py:297
  7.9 33.2 %collective-permute-start = (f32[768,384]{1,0:T(8,128)}, f32[768,384]{1,0:T(8,128)S(1)}, u32[]{:S(2)}, u32[]{:S(2)}) collective-permute-start(f32[768,384]{1,0:T(8,128)} %bitcast.20), channel_id=1, source_target_pairs={{0,48},{8,64},{16,144},{24,224},{32,32},{40,112},{48,176},{56,240}... | collective-permute-start | bytes 3538952 | tf_op jit(solution)/shard_map/ppermute | solution.py:321
  41.1 5.1 %collective-permute-start.1 = (f32[768,384]{1,0:T(8,128)S(1)}, f32[768,384]{1,0:T(8,128)S(1)}, u32[]{:S(2)}, u32[]{:S(2)}) collective-permute-start(f32[768,384]{1,0:T(8,128)S(1)} %collective-permute-done.rest_0_), channel_id=1, source_target_pairs={{0,8},{8,0},{1,9},{9,1},{2,10},{10,2},{3,11},{11,3},{4,12},{12,4},... | collective-permute-start | bytes 3538952 | tf_op jit(solution)/shard_map/ppermute | solution.py:325
  43.0 17.3 %collective-permute-start.2 = (f32[768,384]{1,0:T(8,128)S(1)}, f32[768,384]{1,0:T(8,128)S(1)}, u32[]{:S(2)}, u32[]{:S(2)}) collective-permute-start(f32[768,384]{1,0:T(8,128)S(1)} %collective-permute-done.rest_0_), channel_id=1, source_target_pairs={{0,16},{8,56},{16,32},{24,8},{32,48},{40,24},{48,0},{56,40},{1,17}... | collective-permute-start | bytes 3538952 | tf_op jit(solution)/shard_map/ppermute | solution.py:326
  46.2 26.8 %collective-permute-start.3 = (f32[768,384]{1,0:T(8,128)S(1)}, f32[768,384]{1,0:T(8,128)S(1)}, u32[]{:S(2)}, u32[]{:S(2)}) collective-permute-start(f32[768,384]{1,0:T(8,128)S(1)} %collective-permute-done.1.rest_1_), channel_id=1, source_target_pairs={{0,16},{8,56},{16,32},{24,8},{32,48},{40,24},{48,0},{56,40},{1,17}... | collective-permute-start | bytes 3538952 | tf_op jit(solution)/shard_map/ppermute | solution.py:327
  60.3 25.3 %collective-permute-start.4 = (f32[768,384]{1,0:T(8,128)S(1)}, f32[768,384]{1,0:T(8,128)S(1)}, u32[]{:S(2)}, u32[]{:S(2)}) collective-permute-start(f32[768,384]{1,0:T(8,128)S(1)} %collective-permute-done.2.rest_2_), channel_id=1, source_target_pairs={{0,16},{8,56},{16,32},{24,8},{32,48},{40,24},{48,0},{56,40},{1,17}... | collective-permute-start | bytes 3538952 | tf_op jit(solution)/shard_map/ppermute | solution.py:328
  64.7 25.2 %collective-permute-start.8 = (f32[768,384]{1,0:T(8,128)}, f32[768,384]{1,0:T(8,128)S(1)}, u32[]{:S(2)}, u32[]{:S(2)}) collective-permute-start(f32[768,384]{1,0:T(8,128)} %bitcast.21), channel_id=1, source_target_pairs={{0,192},{8,72},{64,0},{72,136},{128,64},{136,200},{192,128},{200,8... | collective-permute-start | bytes 3538952 | tf_op jit(solution)/shard_map/ppermute | solution.py:331
  66.7 23.3 %collective-permute-start.5 = (f32[768,384]{1,0:T(8,128)S(1)}, f32[768,384]{1,0:T(8,128)S(1)}, u32[]{:S(2)}, u32[]{:S(2)}) collective-permute-start(f32[768,384]{1,0:T(8,128)S(1)} %collective-permute-done.2.rest_2_), channel_id=1, source_target_pairs={{0,8},{8,0},{1,9},{9,1},{2,10},{10,2},{3,11},{11,3},{4,12},{12,4},... | collective-permute-start | bytes 3538952 | tf_op jit(solution)/shard_map/ppermute | solution.py:330
  73.0 17.0 %collective-permute-start.6 = (f32[768,384]{1,0:T(8,128)S(1)}, f32[768,384]{1,0:T(8,128)S(1)}, u32[]{:S(2)}, u32[]{:S(2)}) collective-permute-start(f32[768,384]{1,0:T(8,128)S(1)} %collective-permute-done.3.rest_3_), channel_id=1, source_target_pairs={{0,8},{8,0},{1,9},{9,1},{2,10},{10,2},{3,11},{11,3},{4,12},{12,4},... | collective-permute-start | bytes 3538952 | tf_op jit(solution)/shard_map/ppermute | solution.py:330
  85.6 6.8 %collective-permute-start.7 = (f32[768,384]{1,0:T(8,128)S(1)}, f32[768,384]{1,0:T(8,128)S(1)}, u32[]{:S(2)}, u32[]{:S(2)}) collective-permute-start(f32[768,384]{1,0:T(8,128)S(1)} %collective-permute-done.4.rest_4_), channel_id=1, source_target_pairs={{0,8},{8,0},{1,9},{9,1},{2,10},{10,2},{3,11},{11,3},{4,12},{12,4},... | collective-permute-start | bytes 3538952 | tf_op jit(solution)/shard_map/ppermute | solution.py:330
  92.4 1.3 copy-start
  128.2 17.7 %collective-permute-start.9 = (f32[768,384]{1,0:T(8,128)S(1)}, f32[768,384]{1,0:T(8,128)S(1)}, u32[]{:S(2)}, u32[]{:S(2)}) collective-permute-start(f32[768,384]{1,0:T(8,128)S(1)} %shard_map.79), channel_id=1, source_target_pairs={{0,64},{8,200},{64,128},{72,8},{128,192},{136,72},{192,0},{200,136... | collective-permute-start | bytes 3538952 | tf_op jit(solution)/shard_map/ppermute | solution.py:336
  144.0 18.2 %collective-permute-start.11 = (f32[768,384]{1,0:T(8,128)S(1)}, f32[768,384]{1,0:T(8,128)S(1)}, u32[]{:S(2)}, u32[]{:S(2)}) collective-permute-start(f32[768,384]{1,0:T(8,128)S(1)} %get-tuple-element.35), channel_id=1, source_target_pairs={{0,192},{8,72},{64,0},{72,136},{128,64},{136,200},{192,128},{200,8... | collective-permute-start | bytes 3538952 | tf_op jit(solution)/shard_map/ppermute | solution.py:338
  147.6 11.9 %collective-permute-start.10 = (f32[1,384]{1,0:T(1,128)S(1)}, f32[1,384]{1,0:T(1,128)S(1)}, u32[]{:S(2)}, u32[]{:S(2)}) collective-permute-start(f32[1,384]{1,0:T(1,128)S(1)} %get-tuple-element.33), channel_id=1, source_target_pairs={{0,64},{8,200},{64,128},{72,8},{128,192},{136,72},{192,0},{200,136... | collective-permute-start | bytes 4616 | tf_op jit(solution)/shard_map/ppermute | solution.py:341
  159.5 14.4 %copy-start.1 = (f32[1,384]{1,0:T(1,128)S(1)}, f32[1,384]{1,0:T(1,128)}, u32[]{:S(2)}) copy-start(f32[1,384]{1,0:T(1,128)} %param.9) | copy-start | bytes 4612
  159.5 17.3 %collective-permute-start.12 = (f32[768,384]{1,0:T(8,128)S(1)}, f32[768,384]{1,0:T(8,128)}, u32[]{:S(2)}, u32[]{:S(2)}) collective-permute-start(f32[768,384]{1,0:T(8,128)S(1)} %get-tuple-element.40), channel_id=1, source_target_pairs={{0,64},{8,200},{64,128},{72,8},{128,192},{136,72},{192,0},{200,136... | collective-permute-start | bytes 3538952 | tf_op jit(solution)/shard_map/ppermute | solution.py:344
  164.5 9.4 %all-to-all-start = ((f32[8,1,384]{2,1,0:T(1,128)}), f32[8,1,384]{2,1,0:T(1,128)S(1)}, u32[]{:S(2)}, u32[]{:S(2)}) async-start(f32[8,1,384]{2,1,0:T(1,128)} %all_to_all.6), calls=%async_computation | async-start | bytes 24576 | tf_op jit(solution)/shard_map/all_to_all | solution.py:348
Sparse Core Ops, SparseCore 0:
  10.1 111.2 all-gather.2

commit v13 on v12

--- a/solution.py
+++ b/solution.py
@@ -337,16 +337,14 @@
     second, first = product((2, 1), table, root, high, low)
     back = lax.ppermute(first, ("y", "core"), opposite(4, -1))
     last, last_sums = weigh(9, second, passed, high, low)
+    last_sums = lax.ppermute(last_sums, ("y", "core"), opposite(4))
     table, last, last_sums = lax.optimization_barrier((table, last, last_sums))
-    last_sums = lax.ppermute(last_sums, ("y", "core"), opposite(4))
+    forth = lax.ppermute(last, ("y", "core"), opposite(4))
     (home,) = product((3,), table, root, high, low)
-    last, home, last_sums = lax.optimization_barrier((last, home, last_sums))
-    forth = lax.ppermute(last, ("y", "core"), opposite(4))
     kept, sums = weigh(8, home, back, high, low)
     sums = jnp.broadcast_to(sums + last_sums, (8, cols))
     kept, sums = lax.optimization_barrier((kept, sums))
     sums = lax.all_to_all(sums, ("x", "core"), split_axis=0, concat_axis=0, tiled=True)
-    marginal = pivot_variance + jnp.sum(sums, axis=0, keepdims=True)
     summed = kept + forth
 
     own_place = lax.dynamic_slice(root_row, (zh * 4 + y, own_range * rows), (1, rows))[0]
@@ -355,7 +353,8 @@
     result = -jnp.einsum(
         "iuo,ion->iun", hot, summed.reshape(per_range, BLOCK, cols), precision=lax.Precision.HIGHEST
     )
-
+    result, sums = lax.optimization_barrier((result, sums))
+    marginal = pivot_variance + jnp.sum(sums, axis=0, keepdims=True)
     return result.reshape(1, rows, cols), marginal
 
 

time: 188 us -> 188 us (level)
  starting transfers between devices: 49.6 us -> 52.6 us
  waiting for transfers between devices: 73.9 us -> 71.4 us
    ppermute x1, starting transfers between devices: 1.93 us -> 5.4 us  [per_device(): forth = lax.ppermute(last, ('y', 'core'), opposite(4))]
    ppermute x1, waiting for transfers between devices: 2.36 us -> 0.01 us  [per_device(): forth = lax.ppermute(last, ('y', 'core'), opposite(4))]
  transfers between devices with their start and end apart: 15 -> 15, of which waited for: 9 -> 8; matrix products, arithmetic and copies ran while one was open for 3% -> 3% of each run, Pallas kernels for 17% -> 17%
where the time goes in v13:
time: 188 us; the launch traced here: 187 us
  waiting for transfers between devices  71.4 us (38%)
  starting transfers between devices  52.6 us (28%)
  Pallas kernels  38.7 us (21%)
  between operations  14.3 us (8%)
  local copies, waits for them, and re-layouts  4.95 us (3%)
  other arithmetic  3.69 us (2%)
    pallas_call x3, Pallas kernels, product(): pl.pallas_call(functools.partial(product_kernel, calls), out_shape=[jax.S...  25 us
    ppermute x1, waiting for transfers between devices, per_device(): own = lax.ppermute(coupling[0], ('y', 'x', 'core'), pairs)  24.6 us
    all_gather x1, waiting for transfers between devices, per_device(): root = lax.all_gather(root_inverse, ('zh', 'zl'), axis=0, tiled=False)  17.2 us
    ppermute x3, starting transfers between devices, per_device(): pieces += [lax.ppermute(p, 'core', CORES) for p in (near, near_beside, far)]  13 us
    ppermute x1, waiting for transfers between devices, per_device(): near = lax.ppermute(own, ('x', 'core'), along_x)  11.7 us
    pallas_call x1, Pallas kernels, spread(): pl.pallas_call(spread_kernel, out_shape=[pltpu.HBM(shape, jnp.bfloat16)]...  10.5 us
    ppermute x1, waiting for transfers between devices, per_device(): far = lax.ppermute(near, ('x', 'core'), along_x)  8.28 us
    ppermute x1, starting transfers between devices, per_device(): forth = lax.ppermute(last, ('y', 'core'), opposite(4))  5.4 us
  transfers between devices with their start and end apart: 15, of which 8 were waited for; matrix products, arithmetic and copies ran while one was open for 3% of the time, Pallas kernels for 17%

profile of v13, /device:TPU:1, one launch (start us, length us, event | category | flops | bytes accessed | tf_op | source)
XLA Modules:
  0.0 187.4 jit_solution(11790131649099232132)
XLA Ops:
  7.2 0.0 all-gather.3.cloned.1.call-start
  7.2 0.7 all-gather.3.cloned.1.call-update
  7.9 4.6 %collective-permute-start = (f32[768,384]{1,0:T(8,128)}, f32[768,384]{1,0:T(8,128)S(1)}, u32[]{:S(2)}, u32[]{:S(2)}) collective-permute-start(f32[768,384]{1,0:T(8,128)} %bitcast.23), channel_id=1, source_target_pairs={{0,48},{8,64},{16,144},{24,224},{32,32},{40,112},{48,176},{56,240}... | collective-permute-start | bytes 3538952 | tf_op jit(solution)/shard_map/ppermute | solution.py:321
  12.5 1.0 slice.3
  13.6 1.0 reshape.105.rows_ref
  14.5 0.1 reshape.104
  14.6 0.7 fusion.2
  15.3 0.1 copy.14
  15.4 0.1 pad_add_fusion
  15.5 0.1 copy.13
  15.6 0.1 concatenate.16.table
  15.7 0.7 and_bitcast_fusion
  16.4 0.1 fusion.5.start_row
  16.5 24.6 %collective-permute-done.rest_0_ = f32[768,384]{1,0:T(8,128)S(1)} collective-permute-done((f32[768,384]{1,0:T(8,128)}, f32[768,384]{1,0:T(8,128)S(1)}, u32[]{:S(2)}, u32[]{:S(2)}) %collective-permute-start) | collective-permute-done | bytes 1179680 | tf_op jit(solution)/shard_map/ppermute | solution.py:321
  41.1 1.9 %collective-permute-start.1 = (f32[768,384]{1,0:T(8,128)S(1)}, f32[768,384]{1,0:T(8,128)S(1)}, u32[]{:S(2)}, u32[]{:S(2)}) collective-permute-start(f32[768,384]{1,0:T(8,128)S(1)} %collective-permute-done.rest_0_), channel_id=1, source_target_pairs={{0,8},{8,0},{1,9},{9,1},{2,10},{10,2},{3,11},{11,3},{4,12},{12,4},... | collective-permute-start | bytes 3538952 | tf_op jit(solution)/shard_map/ppermute | solution.py:325
  43.0 3.2 %collective-permute-start.2 = (f32[768,384]{1,0:T(8,128)S(1)}, f32[768,384]{1,0:T(8,128)S(1)}, u32[]{:S(2)}, u32[]{:S(2)}) collective-permute-start(f32[768,384]{1,0:T(8,128)S(1)} %collective-permute-done.rest_0_), channel_id=1, source_target_pairs={{0,16},{8,56},{16,32},{24,8},{32,48},{40,24},{48,0},{56,40},{1,17}... | collective-permute-start | bytes 3538952 | tf_op jit(solution)/shard_map/ppermute | solution.py:326
  46.2 0.0 collective-permute-done.1.rest_1_
  46.2 2.4 %collective-permute-start.3 = (f32[768,384]{1,0:T(8,128)S(1)}, f32[768,384]{1,0:T(8,128)S(1)}, u32[]{:S(2)}, u32[]{:S(2)}) collective-permute-start(f32[768,384]{1,0:T(8,128)S(1)} %collective-permute-done.1.rest_1_), channel_id=1, source_target_pairs={{0,16},{8,56},{16,32},{24,8},{32,48},{40,24},{48,0},{56,40},{1,17}... | collective-permute-start | bytes 3538952 | tf_op jit(solution)/shard_map/ppermute | solution.py:327
  48.6 11.7 %collective-permute-done.2.rest_2_ = f32[768,384]{1,0:T(8,128)S(1)} collective-permute-done((f32[768,384]{1,0:T(8,128)S(1)}, f32[768,384]{1,0:T(8,128)S(1)}, u32[]{:S(2)}, u32[]{:S(2)}) %collective-permute-start.2) | collective-permute-done | bytes 1179680 | tf_op jit(solution)/shard_map/ppermute | solution.py:326
  60.3 4.4 %collective-permute-start.4 = (f32[768,384]{1,0:T(8,128)S(1)}, f32[768,384]{1,0:T(8,128)S(1)}, u32[]{:S(2)}, u32[]{:S(2)}) collective-permute-start(f32[768,384]{1,0:T(8,128)S(1)} %collective-permute-done.2.rest_2_), channel_id=1, source_target_pairs={{0,16},{8,56},{16,32},{24,8},{32,48},{40,24},{48,0},{56,40},{1,17}... | collective-permute-start | bytes 3538952 | tf_op jit(solution)/shard_map/ppermute | solution.py:328
  64.7 1.9 %collective-permute-start.8 = (f32[768,384]{1,0:T(8,128)}, f32[768,384]{1,0:T(8,128)S(1)}, u32[]{:S(2)}, u32[]{:S(2)}) collective-permute-start(f32[768,384]{1,0:T(8,128)} %bitcast.24), channel_id=1, source_target_pairs={{0,192},{8,72},{64,0},{72,136},{128,64},{136,200},{192,128},{200,8... | collective-permute-start | bytes 3538952 | tf_op jit(solution)/shard_map/ppermute | solution.py:331
  66.7 4.3 %collective-permute-start.5 = (f32[768,384]{1,0:T(8,128)S(1)}, f32[768,384]{1,0:T(8,128)S(1)}, u32[]{:S(2)}, u32[]{:S(2)}) collective-permute-start(f32[768,384]{1,0:T(8,128)S(1)} %collective-permute-done.2.rest_2_), channel_id=1, source_target_pairs={{0,8},{8,0},{1,9},{9,1},{2,10},{10,2},{3,11},{11,3},{4,12},{12,4},... | collective-permute-start | bytes 3538952 | tf_op jit(solution)/shard_map/ppermute | solution.py:330
  71.0 2.0 %collective-permute-done.3.rest_3_ = f32[768,384]{1,0:T(8,128)S(1)} collective-permute-done((f32[768,384]{1,0:T(8,128)S(1)}, f32[768,384]{1,0:T(8,128)S(1)}, u32[]{:S(2)}, u32[]{:S(2)}) %collective-permute-start.3) | collective-permute-done | bytes 1179680 | tf_op jit(solution)/shard_map/ppermute | solution.py:327
  73.0 4.4 %collective-permute-start.6 = (f32[768,384]{1,0:T(8,128)S(1)}, f32[768,384]{1,0:T(8,128)S(1)}, u32[]{:S(2)}, u32[]{:S(2)}) collective-permute-start(f32[768,384]{1,0:T(8,128)S(1)} %collective-permute-done.3.rest_3_), channel_id=1, source_target_pairs={{0,8},{8,0},{1,9},{9,1},{2,10},{10,2},{3,11},{11,3},{4,12},{12,4},... | collective-permute-start | bytes 3538952 | tf_op jit(solution)/shard_map/ppermute | solution.py:330
  77.3 8.3 %collective-permute-done.4.rest_4_ = f32[768,384]{1,0:T(8,128)S(1)} collective-permute-done((f32[768,384]{1,0:T(8,128)S(1)}, f32[768,384]{1,0:T(8,128)S(1)}, u32[]{:S(2)}, u32[]{:S(2)}) %collective-permute-start.4) | collective-permute-done | bytes 1179680 | tf_op jit(solution)/shard_map/ppermute | solution.py:328
  85.6 4.4 %collective-permute-start.7 = (f32[768,384]{1,0:T(8,128)S(1)}, f32[768,384]{1,0:T(8,128)S(1)}, u32[]{:S(2)}, u32[]{:S(2)}) collective-permute-start(f32[768,384]{1,0:T(8,128)S(1)} %collective-permute-done.4.rest_4_), channel_id=1, source_target_pairs={{0,8},{8,0},{1,9},{9,1},{2,10},{10,2},{3,11},{11,3},{4,12},{12,4},... | collective-permute-start | bytes 3538952 | tf_op jit(solution)/shard_map/ppermute | solution.py:330
  90.0 0.0 collective-permute-done.8.rest_9_
  90.0 0.0 collective-permute-done.5.rest_5_
  90.0 0.0 collective-permute-done.6.rest_6_
  90.0 2.4 %collective-permute-done.7.rest_7_ = f32[768,384]{1,0:T(8,128)S(1)} collective-permute-done((f32[768,384]{1,0:T(8,128)S(1)}, f32[768,384]{1,0:T(8,128)S(1)}, u32[]{:S(2)}, u32[]{:S(2)}) %collective-permute-start.7) | collective-permute-done | bytes 1179680 | tf_op jit(solution)/shard_map/ppermute | solution.py:330
  92.4 0.0 copy-start
  92.4 1.3 copy-done
  93.7 10.5 %shard_map.77 = (bf16[10,768,384]{2,1,0:T(8,128)(2,1)}, bf16[10,768,384]{2,1,0:T(8,128)(2,1)}) custom-call(s32[10]{0:T(128)S(1)} %fusion.5.start_row, s32[384,128]{1,0:T(8,128)S(1)} %reshape.105.rows_ref, f32[768,384]{1,0:T(8,128)S(1)} %collective-permute-done.rest_0_, f32[768,384]{1,0:T(8,128)S(1)} %collective-permute-done.1.rest_1_, ...), custom_call_target="tpu_custom_call" | custom-call | flops 1509949440 | bytes 23592960 | tf_op jit(solution)/shard_map/pallas_call | solution.py:125
  104.2 17.2 %all-gather.3.cloned.1.call-done = f32[16384,128]{1,0:T(8,128)} async-done(((f32[1024,128]{1,0:T(8,128)}), f32[16384,128]{1,0:T(8,128)}) %all-gather.3.cloned.1.call-update) | async-done | bytes 8388624 | tf_op jit(solution)/shard_map/all_gather | solution.py:297
  121.4 6.9 %shard_map.79 = f32[768,384]{1,0:T(8,128)S(1)} custom-call(s32[4,21]{1,0:T(4,128)S(1)} %concatenate.16.table, f32[16,1024,128]{2,1,0:T(8,128)} %bitcast.26, bf16[10,768,384]{2,1,0:T(8,128)(2,1)} %get-tuple-element.25.high_hbm, bf16[10,768,384]{2,1,0:T(8,128)(2,1)} %get-tuple-element.26.low_hbm), custom_call_target="tpu_custom_call" | custom-call | flops 2717908992 | bytes 7077888 | tf_op jit(solution)/shard_map/pallas_call | solution.py:218
  128.2 4.5 %collective-permute-start.9 = (f32[768,384]{1,0:T(8,128)S(1)}, f32[768,384]{1,0:T(8,128)S(1)}, u32[]{:S(2)}, u32[]{:S(2)}) collective-permute-start(f32[768,384]{1,0:T(8,128)S(1)} %shard_map.79), channel_id=1, source_target_pairs={{0,64},{8,200},{64,128},{72,8},{128,192},{136,72},{192,0},{200,136... | collective-permute-start | bytes 3538952 | tf_op jit(solution)/shard_map/ppermute | solution.py:336
  132.8 11.2 %shard_map.78 = (f32[768,384]{1,0:T(8,128)S(1)}, f32[768,384]{1,0:T(8,128)S(1)}) custom-call(s32[4,21]{1,0:T(4,128)S(1)} %concatenate.16.table, f32[16,1024,128]{2,1,0:T(8,128)} %bitcast.27, bf16[10,768,384]{2,1,0:T(8,128)(2,1)} %get-tuple-element.25.high_hbm, bf16[10,768,384]{2,1,0:T(8,128)(2,1)} %get-tuple-element.26.low_hbm), custom_call_target="tpu_custom_call" | custom-call | flops 5435817984 | bytes 14155776 | tf_op jit(solution)/shard_map/pallas_call | solution.py:218
  144.0 1.9 %collective-permute-start.11 = (f32[768,384]{1,0:T(8,128)S(1)}, f32[768,384]{1,0:T(8,128)S(1)}, u32[]{:S(2)}, u32[]{:S(2)}) collective-permute-start(f32[768,384]{1,0:T(8,128)S(1)} %get-tuple-element.31), channel_id=1, source_target_pairs={{0,192},{8,72},{64,0},{72,136},{128,64},{136,200},{192,128},{200,8... | collective-permute-start | bytes 3538952 | tf_op jit(solution)/shard_map/ppermute | solution.py:338
  146.0 0.0 collective-permute-done.9.second
  146.0 1.6 shard_map.80
  147.6 4.8 %collective-permute-start.10 = (f32[1,384]{1,0:T(1,128)S(1)}, f32[1,384]{1,0:T(1,128)S(1)}, u32[]{:S(2)}, u32[]{:S(2)}) collective-permute-start(f32[1,384]{1,0:T(1,128)S(1)} %get-tuple-element.29), channel_id=1, source_target_pairs={{0,64},{8,200},{64,128},{72,8},{128,192},{136,72},{192,0},{200,136... | collective-permute-start | bytes 4616 | tf_op jit(solution)/shard_map/ppermute | solution.py:340
  152.4 0.7 collective-permute-done.10
  153.1 5.4 %collective-permute-start.12 = (f32[768,384]{1,0:T(8,128)S(1)}, f32[768,384]{1,0:T(8,128)}, u32[]{:S(2)}, u32[]{:S(2)}) collective-permute-start(f32[768,384]{1,0:T(8,128)S(1)} %get-tuple-element.36), channel_id=1, source_target_pairs={{0,64},{8,200},{64,128},{72,8},{128,192},{136,72},{192,0},{200,136... | collective-permute-start | bytes 3538952 | tf_op jit(solution)/shard_map/ppermute | solution.py:342
  158.5 6.9 %shard_map.81.first = f32[768,384]{1,0:T(8,128)S(1)} custom-call(s32[4,21]{1,0:T(4,128)S(1)} %concatenate.16.table, f32[16,1024,128]{2,1,0:T(8,128)} %bitcast.28, bf16[10,768,384]{2,1,0:T(8,128)(2,1)} %get-tuple-element.25.high_hbm, bf16[10,768,384]{2,1,0:T(8,128)(2,1)} %get-tuple-element.26.low_hbm), custom_call_target="tpu_custom_call" | custom-call | flops 2717908992 | bytes 7077888 | tf_op jit(solution)/shard_map/pallas_call | solution.py:218
  165.4 0.0 collective-permute-done.11.second
  165.4 1.6 shard_map.82
  167.0 0.6 all_to_all.8
  167.7 4.5 %all-to-all-start = ((f32[8,1,384]{2,1,0:T(1,128)}), f32[8,1,384]{2,1,0:T(1,128)S(1)}, u32[]{:S(2)}, u32[]{:S(2)}) async-start(f32[8,1,384]{2,1,0:T(1,128)} %all_to_all.8), calls=%async_computation | async-start | bytes 24576 | tf_op jit(solution)/shard_map/all_to_all | solution.py:347
  172.1 0.8 fusion.1
  173.0 3.8 %all-to-all-done = f32[8,1,384]{2,1,0:T(1,128)S(1)} async-done(((f32[8,1,384]{2,1,0:T(1,128)}), f32[8,1,384]{2,1,0:T(1,128)S(1)}, u32[]{:S(2)}, u32[]{:S(2)}) %all-to-all-start) | async-done | bytes 12320 | tf_op jit(solution)/shard_map/all_to_all | solution.py:347
  176.8 0.0 collective-permute-done.12
  176.8 1.4 add.118
  178.2 0.0 copy-start.1
  178.2 1.8 convolution_negate_fusion
  180.0 0.0 copy-done.1
  180.0 0.6 reshape_add_fusion
  (7 shorter events, 0.1 us)
Async XLA Ops:
  7.2 114.2 %all-gather.3.cloned.1.call-start = ((), (), s32[]{:S(2)}) async-start(), calls=%async_computation.1 | async-start | bytes 8912896 | tf_op jit(solution)/shard_map/all_gather | solution.py:297
  7.9 33.2 %collective-permute-start = (f32[768,384]{1,0:T(8,128)}, f32[768,384]{1,0:T(8,128)S(1)}, u32[]{:S(2)}, u32[]{:S(2)}) collective-permute-start(f32[768,384]{1,0:T(8,128)} %bitcast.23), channel_id=1, source_target_pairs={{0,48},{8,64},{16,144},{24,224},{32,32},{40,112},{48,176},{56,240}... | collective-permute-start | bytes 3538952 | tf_op jit(solution)/shard_map/ppermute | solution.py:321
  41.1 5.1 %collective-permute-start.1 = (f32[768,384]{1,0:T(8,128)S(1)}, f32[768,384]{1,0:T(8,128)S(1)}, u32[]{:S(2)}, u32[]{:S(2)}) collective-permute-start(f32[768,384]{1,0:T(8,128)S(1)} %collective-permute-done.rest_0_), channel_id=1, source_target_pairs={{0,8},{8,0},{1,9},{9,1},{2,10},{10,2},{3,11},{11,3},{4,12},{12,4},... | collective-permute-start | bytes 3538952 | tf_op jit(solution)/shard_map/ppermute | solution.py:325
  43.0 17.3 %collective-permute-start.2 = (f32[768,384]{1,0:T(8,128)S(1)}, f32[768,384]{1,0:T(8,128)S(1)}, u32[]{:S(2)}, u32[]{:S(2)}) collective-permute-start(f32[768,384]{1,0:T(8,128)S(1)} %collective-permute-done.rest_0_), channel_id=1, source_target_pairs={{0,16},{8,56},{16,32},{24,8},{32,48},{40,24},{48,0},{56,40},{1,17}... | collective-permute-start | bytes 3538952 | tf_op jit(solution)/shard_map/ppermute | solution.py:326
  46.2 26.8 %collective-permute-start.3 = (f32[768,384]{1,0:T(8,128)S(1)}, f32[768,384]{1,0:T(8,128)S(1)}, u32[]{:S(2)}, u32[]{:S(2)}) collective-permute-start(f32[768,384]{1,0:T(8,128)S(1)} %collective-permute-done.1.rest_1_), channel_id=1, source_target_pairs={{0,16},{8,56},{16,32},{24,8},{32,48},{40,24},{48,0},{56,40},{1,17}... | collective-permute-start | bytes 3538952 | tf_op jit(solution)/shard_map/ppermute | solution.py:327
  60.3 25.3 %collective-permute-start.4 = (f32[768,384]{1,0:T(8,128)S(1)}, f32[768,384]{1,0:T(8,128)S(1)}, u32[]{:S(2)}, u32[]{:S(2)}) collective-permute-start(f32[768,384]{1,0:T(8,128)S(1)} %collective-permute-done.2.rest_2_), channel_id=1, source_target_pairs={{0,16},{8,56},{16,32},{24,8},{32,48},{40,24},{48,0},{56,40},{1,17}... | collective-permute-start | bytes 3538952 | tf_op jit(solution)/shard_map/ppermute | solution.py:328
  64.7 25.2 %collective-permute-start.8 = (f32[768,384]{1,0:T(8,128)}, f32[768,384]{1,0:T(8,128)S(1)}, u32[]{:S(2)}, u32[]{:S(2)}) collective-permute-start(f32[768,384]{1,0:T(8,128)} %bitcast.24), channel_id=1, source_target_pairs={{0,192},{8,72},{64,0},{72,136},{128,64},{136,200},{192,128},{200,8... | collective-permute-start | bytes 3538952 | tf_op jit(solution)/shard_map/ppermute | solution.py:331
  66.7 23.3 %collective-permute-start.5 = (f32[768,384]{1,0:T(8,128)S(1)}, f32[768,384]{1,0:T(8,128)S(1)}, u32[]{:S(2)}, u32[]{:S(2)}) collective-permute-start(f32[768,384]{1,0:T(8,128)S(1)} %collective-permute-done.2.rest_2_), channel_id=1, source_target_pairs={{0,8},{8,0},{1,9},{9,1},{2,10},{10,2},{3,11},{11,3},{4,12},{12,4},... | collective-permute-start | bytes 3538952 | tf_op jit(solution)/shard_map/ppermute | solution.py:330
  73.0 17.0 %collective-permute-start.6 = (f32[768,384]{1,0:T(8,128)S(1)}, f32[768,384]{1,0:T(8,128)S(1)}, u32[]{:S(2)}, u32[]{:S(2)}) collective-permute-start(f32[768,384]{1,0:T(8,128)S(1)} %collective-permute-done.3.rest_3_), channel_id=1, source_target_pairs={{0,8},{8,0},{1,9},{9,1},{2,10},{10,2},{3,11},{11,3},{4,12},{12,4},... | collective-permute-start | bytes 3538952 | tf_op jit(solution)/shard_map/ppermute | solution.py:330
  85.6 6.8 %collective-permute-start.7 = (f32[768,384]{1,0:T(8,128)S(1)}, f32[768,384]{1,0:T(8,128)S(1)}, u32[]{:S(2)}, u32[]{:S(2)}) collective-permute-start(f32[768,384]{1,0:T(8,128)S(1)} %collective-permute-done.4.rest_4_), channel_id=1, source_target_pairs={{0,8},{8,0},{1,9},{9,1},{2,10},{10,2},{3,11},{11,3},{4,12},{12,4},... | collective-permute-start | bytes 3538952 | tf_op jit(solution)/shard_map/ppermute | solution.py:330
  92.4 1.3 copy-start
  128.2 17.7 %collective-permute-start.9 = (f32[768,384]{1,0:T(8,128)S(1)}, f32[768,384]{1,0:T(8,128)S(1)}, u32[]{:S(2)}, u32[]{:S(2)}) collective-permute-start(f32[768,384]{1,0:T(8,128)S(1)} %shard_map.79), channel_id=1, source_target_pairs={{0,64},{8,200},{64,128},{72,8},{128,192},{136,72},{192,0},{200,136... | collective-permute-start | bytes 3538952 | tf_op jit(solution)/shard_map/ppermute | solution.py:336
  144.0 21.3 %collective-permute-start.11 = (f32[768,384]{1,0:T(8,128)S(1)}, f32[768,384]{1,0:T(8,128)S(1)}, u32[]{:S(2)}, u32[]{:S(2)}) collective-permute-start(f32[768,384]{1,0:T(8,128)S(1)} %get-tuple-element.31), channel_id=1, source_target_pairs={{0,192},{8,72},{64,0},{72,136},{128,64},{136,200},{192,128},{200,8... | collective-permute-start | bytes 3538952 | tf_op jit(solution)/shard_map/ppermute | solution.py:338
  147.6 5.5 %collective-permute-start.10 = (f32[1,384]{1,0:T(1,128)S(1)}, f32[1,384]{1,0:T(1,128)S(1)}, u32[]{:S(2)}, u32[]{:S(2)}) collective-permute-start(f32[1,384]{1,0:T(1,128)S(1)} %get-tuple-element.29), channel_id=1, source_target_pairs={{0,64},{8,200},{64,128},{72,8},{128,192},{136,72},{192,0},{200,136... | collective-permute-start | bytes 4616 | tf_op jit(solution)/shard_map/ppermute | solution.py:340
  153.1 23.7 %collective-permute-start.12 = (f32[768,384]{1,0:T(8,128)S(1)}, f32[768,384]{1,0:T(8,128)}, u32[]{:S(2)}, u32[]{:S(2)}) collective-permute-start(f32[768,384]{1,0:T(8,128)S(1)} %get-tuple-element.36), channel_id=1, source_target_pairs={{0,64},{8,200},{64,128},{72,8},{128,192},{136,72},{192,0},{200,136... | collective-permute-start | bytes 3538952 | tf_op jit(solution)/shard_map/ppermute | solution.py:342
  167.7 9.1 %all-to-all-start = ((f32[8,1,384]{2,1,0:T(1,128)}), f32[8,1,384]{2,1,0:T(1,128)S(1)}, u32[]{:S(2)}, u32[]{:S(2)}) async-start(f32[8,1,384]{2,1,0:T(1,128)} %all_to_all.8), calls=%async_computation | async-start | bytes 24576 | tf_op jit(solution)/shard_map/all_to_all | solution.py:347
  178.2 1.8 copy-start.1
Sparse Core Ops, SparseCore 0:
  10.1 111.2 all-gather.2

commit v14 on v13

--- a/solution.py
+++ b/solution.py
@@ -283,6 +283,33 @@
     )(first, second, high, low)
 
 
+def select_kernel(place_ref, first, second, out):
+    row = lax.broadcasted_iota(jnp.int32, (BLOCK, BLOCK), 0)
+    for i in range(out.shape[0] // BLOCK):
+        here = pl.ds(i * BLOCK, BLOCK)
+        value = -(first[here, :] + second[here, :])
+        high = value.astype(jnp.bfloat16)
+        low = (value - high.astype(jnp.float32)).astype(jnp.bfloat16)
+        hot = (place_ref[i : i + 1, :] == row).astype(jnp.float32).T.astype(jnp.bfloat16)
+        found = jnp.dot(hot, low, preferred_element_type=jnp.float32)
+        out[here, :] = found + jnp.dot(hot, high, preferred_element_type=jnp.float32)
+
+
+def select(place, first, second):
+    rows, cols = first.shape
+    vmem = pl.BlockSpec(memory_space=pltpu.VMEM)
+    return pl.pallas_call(
+        select_kernel,
+        out_shape=jax.ShapeDtypeStruct((rows, cols), jnp.float32),
+        in_specs=[vmem] * 3,
+        out_specs=vmem,
+        compiler_params=pltpu.CompilerParams(vmem_limit_bytes=VMEM_BYTES),
+        cost_estimate=pl.CostEstimate(
+            flops=4 * rows * BLOCK * cols, bytes_accessed=12 * rows * cols, transcendentals=0
+        ),
+    )(place, first, second)
+
+
 def per_device(root_inverse, root_row, coupling, pivot_variance):
     zh = lax.axis_index("zh")
     y = lax.axis_index("y")
@@ -345,14 +372,10 @@
     sums = jnp.broadcast_to(sums + last_sums, (8, cols))
     kept, sums = lax.optimization_barrier((kept, sums))
     sums = lax.all_to_all(sums, ("x", "core"), split_axis=0, concat_axis=0, tiled=True)
-    summed = kept + forth
-
     own_place = lax.dynamic_slice(root_row, (zh * 4 + y, own_range * rows), (1, rows))[0]
     own_place = jnp.where(own_place >= 0, own_place & (BLOCK - 1), -1).reshape(per_range, BLOCK)
-    hot = (own_place[:, :, None] == jnp.arange(BLOCK, dtype=jnp.int32)).astype(jnp.float32)
-    result = -jnp.einsum(
-        "iuo,ion->iun", hot, summed.reshape(per_range, BLOCK, cols), precision=lax.Precision.HIGHEST
-    )
+    result = select(own_place, kept, forth)
+
     result, sums = lax.optimization_barrier((result, sums))
     marginal = pivot_variance + jnp.sum(sums, axis=0, keepdims=True)
     return result.reshape(1, rows, cols), marginal

time: 188 us -> 187 us (level)
  no operation moved by 1% of the time
where the time goes in v14:
time: 187 us; the launch traced here: 186 us
  waiting for transfers between devices  71.4 us (38%)
  starting transfers between devices  52.6 us (28%)
  Pallas kernels  40.2 us (21%)
  between operations  14.3 us (8%)
  local copies, waits for them, and re-layouts  5.55 us (3%)
  other arithmetic  2.3 us (1%)
    pallas_call x3, Pallas kernels, product(): pl.pallas_call(functools.partial(product_kernel, calls), out_shape=[jax.S...  25 us
    ppermute x1, waiting for transfers between devices, per_device(): own = lax.ppermute(coupling[0], ('y', 'x', 'core'), pairs)  24.6 us
    all_gather x1, waiting for transfers between devices, per_device(): root = lax.all_gather(root_inverse, ('zh', 'zl'), axis=0, tiled=False)  17.2 us
    ppermute x3, starting transfers between devices, per_device(): pieces += [lax.ppermute(p, 'core', CORES) for p in (near, near_beside, far)]  13 us
    ppermute x1, waiting for transfers between devices, per_device(): near = lax.ppermute(own, ('x', 'core'), along_x)  11.7 us
    pallas_call x1, Pallas kernels, spread(): pl.pallas_call(spread_kernel, out_shape=[pltpu.HBM(shape, jnp.bfloat16)]...  10.5 us
    ppermute x1, waiting for transfers between devices, per_device(): far = lax.ppermute(near, ('x', 'core'), along_x)  8.28 us
    ppermute x1, starting transfers between devices, per_device(): forth = lax.ppermute(last, ('y', 'core'), opposite(4))  5.4 us
  transfers between devices with their start and end apart: 15, of which 8 were waited for; matrix products, arithmetic and copies ran while one was open for 3% of the time, Pallas kernels for 17%

profile of v14, /device:TPU:1, one launch (start us, length us, event | category | flops | bytes accessed | tf_op | source)
XLA Modules:
  0.0 186.4 jit_solution(10395743394383363181)
XLA Ops:
  7.2 0.0 all-gather.3.cloned.1.call-start
  7.2 0.7 all-gather.3.cloned.1.call-update
  7.9 4.6 %collective-permute-start = (f32[768,384]{1,0:T(8,128)}, f32[768,384]{1,0:T(8,128)S(1)}, u32[]{:S(2)}, u32[]{:S(2)}) collective-permute-start(f32[768,384]{1,0:T(8,128)} %bitcast.21), channel_id=1, source_target_pairs={{0,48},{8,64},{16,144},{24,224},{32,32},{40,112},{48,176},{56,240}... | collective-permute-start | bytes 3538952 | tf_op jit(solution)/shard_map/ppermute | solution.py:348
  12.5 1.0 slice.3
  13.6 1.0 reshape.94.rows_ref
  14.5 0.1 reshape.93
  14.6 0.7 fusion.1
  15.3 0.1 copy.14
  15.4 0.1 pad_add_fusion
  15.5 0.1 copy.13
  15.6 0.1 concatenate.16.table
  15.7 0.7 and_bitcast_fusion
  16.4 0.1 fusion.4.start_row
  16.5 24.6 %collective-permute-done.rest_0_ = f32[768,384]{1,0:T(8,128)S(1)} collective-permute-done((f32[768,384]{1,0:T(8,128)}, f32[768,384]{1,0:T(8,128)S(1)}, u32[]{:S(2)}, u32[]{:S(2)}) %collective-permute-start) | collective-permute-done | bytes 1179680 | tf_op jit(solution)/shard_map/ppermute | solution.py:348
  41.1 1.9 %collective-permute-start.1 = (f32[768,384]{1,0:T(8,128)S(1)}, f32[768,384]{1,0:T(8,128)S(1)}, u32[]{:S(2)}, u32[]{:S(2)}) collective-permute-start(f32[768,384]{1,0:T(8,128)S(1)} %collective-permute-done.rest_0_), channel_id=1, source_target_pairs={{0,8},{8,0},{1,9},{9,1},{2,10},{10,2},{3,11},{11,3},{4,12},{12,4},... | collective-permute-start | bytes 3538952 | tf_op jit(solution)/shard_map/ppermute | solution.py:352
  43.0 3.2 %collective-permute-start.2 = (f32[768,384]{1,0:T(8,128)S(1)}, f32[768,384]{1,0:T(8,128)S(1)}, u32[]{:S(2)}, u32[]{:S(2)}) collective-permute-start(f32[768,384]{1,0:T(8,128)S(1)} %collective-permute-done.rest_0_), channel_id=1, source_target_pairs={{0,16},{8,56},{16,32},{24,8},{32,48},{40,24},{48,0},{56,40},{1,17}... | collective-permute-start | bytes 3538952 | tf_op jit(solution)/shard_map/ppermute | solution.py:353
  46.2 0.0 collective-permute-done.1.rest_1_
  46.2 2.4 %collective-permute-start.3 = (f32[768,384]{1,0:T(8,128)S(1)}, f32[768,384]{1,0:T(8,128)S(1)}, u32[]{:S(2)}, u32[]{:S(2)}) collective-permute-start(f32[768,384]{1,0:T(8,128)S(1)} %collective-permute-done.1.rest_1_), channel_id=1, source_target_pairs={{0,16},{8,56},{16,32},{24,8},{32,48},{40,24},{48,0},{56,40},{1,17}... | collective-permute-start | bytes 3538952 | tf_op jit(solution)/shard_map/ppermute | solution.py:354
  48.6 11.7 %collective-permute-done.2.rest_2_ = f32[768,384]{1,0:T(8,128)S(1)} collective-permute-done((f32[768,384]{1,0:T(8,128)S(1)}, f32[768,384]{1,0:T(8,128)S(1)}, u32[]{:S(2)}, u32[]{:S(2)}) %collective-permute-start.2) | collective-permute-done | bytes 1179680 | tf_op jit(solution)/shard_map/ppermute | solution.py:353
  60.3 4.4 %collective-permute-start.4 = (f32[768,384]{1,0:T(8,128)S(1)}, f32[768,384]{1,0:T(8,128)S(1)}, u32[]{:S(2)}, u32[]{:S(2)}) collective-permute-start(f32[768,384]{1,0:T(8,128)S(1)} %collective-permute-done.2.rest_2_), channel_id=1, source_target_pairs={{0,16},{8,56},{16,32},{24,8},{32,48},{40,24},{48,0},{56,40},{1,17}... | collective-permute-start | bytes 3538952 | tf_op jit(solution)/shard_map/ppermute | solution.py:355
  64.7 1.9 %collective-permute-start.8 = (f32[768,384]{1,0:T(8,128)}, f32[768,384]{1,0:T(8,128)S(1)}, u32[]{:S(2)}, u32[]{:S(2)}) collective-permute-start(f32[768,384]{1,0:T(8,128)} %bitcast.22), channel_id=1, source_target_pairs={{0,192},{8,72},{64,0},{72,136},{128,64},{136,200},{192,128},{200,8... | collective-permute-start | bytes 3538952 | tf_op jit(solution)/shard_map/ppermute | solution.py:358
  66.7 4.3 %collective-permute-start.5 = (f32[768,384]{1,0:T(8,128)S(1)}, f32[768,384]{1,0:T(8,128)S(1)}, u32[]{:S(2)}, u32[]{:S(2)}) collective-permute-start(f32[768,384]{1,0:T(8,128)S(1)} %collective-permute-done.2.rest_2_), channel_id=1, source_target_pairs={{0,8},{8,0},{1,9},{9,1},{2,10},{10,2},{3,11},{11,3},{4,12},{12,4},... | collective-permute-start | bytes 3538952 | tf_op jit(solution)/shard_map/ppermute | solution.py:357
  71.0 2.0 %collective-permute-done.3.rest_3_ = f32[768,384]{1,0:T(8,128)S(1)} collective-permute-done((f32[768,384]{1,0:T(8,128)S(1)}, f32[768,384]{1,0:T(8,128)S(1)}, u32[]{:S(2)}, u32[]{:S(2)}) %collective-permute-start.3) | collective-permute-done | bytes 1179680 | tf_op jit(solution)/shard_map/ppermute | solution.py:354
  73.0 4.4 %collective-permute-start.6 = (f32[768,384]{1,0:T(8,128)S(1)}, f32[768,384]{1,0:T(8,128)S(1)}, u32[]{:S(2)}, u32[]{:S(2)}) collective-permute-start(f32[768,384]{1,0:T(8,128)S(1)} %collective-permute-done.3.rest_3_), channel_id=1, source_target_pairs={{0,8},{8,0},{1,9},{9,1},{2,10},{10,2},{3,11},{11,3},{4,12},{12,4},... | collective-permute-start | bytes 3538952 | tf_op jit(solution)/shard_map/ppermute | solution.py:357
  77.3 8.3 %collective-permute-done.4.rest_4_ = f32[768,384]{1,0:T(8,128)S(1)} collective-permute-done((f32[768,384]{1,0:T(8,128)S(1)}, f32[768,384]{1,0:T(8,128)S(1)}, u32[]{:S(2)}, u32[]{:S(2)}) %collective-permute-start.4) | collective-permute-done | bytes 1179680 | tf_op jit(solution)/shard_map/ppermute | solution.py:355
  85.6 4.4 %collective-permute-start.7 = (f32[768,384]{1,0:T(8,128)S(1)}, f32[768,384]{1,0:T(8,128)S(1)}, u32[]{:S(2)}, u32[]{:S(2)}) collective-permute-start(f32[768,384]{1,0:T(8,128)S(1)} %collective-permute-done.4.rest_4_), channel_id=1, source_target_pairs={{0,8},{8,0},{1,9},{9,1},{2,10},{10,2},{3,11},{11,3},{4,12},{12,4},... | collective-permute-start | bytes 3538952 | tf_op jit(solution)/shard_map/ppermute | solution.py:357
  90.0 0.0 collective-permute-done.8.rest_9_
  90.0 0.0 collective-permute-done.5.rest_5_
  90.0 0.0 collective-permute-done.6.rest_6_
  90.0 2.4 %collective-permute-done.7.rest_7_ = f32[768,384]{1,0:T(8,128)S(1)} collective-permute-done((f32[768,384]{1,0:T(8,128)S(1)}, f32[768,384]{1,0:T(8,128)S(1)}, u32[]{:S(2)}, u32[]{:S(2)}) %collective-permute-start.7) | collective-permute-done | bytes 1179680 | tf_op jit(solution)/shard_map/ppermute | solution.py:357
  92.4 0.0 copy-start
  92.4 1.3 copy-done
  93.7 10.5 %shard_map.77 = (bf16[10,768,384]{2,1,0:T(8,128)(2,1)}, bf16[10,768,384]{2,1,0:T(8,128)(2,1)}) custom-call(s32[10]{0:T(128)S(1)} %fusion.4.start_row, s32[384,128]{1,0:T(8,128)S(1)} %reshape.94.rows_ref, f32[768,384]{1,0:T(8,128)S(1)} %collective-permute-done.rest_0_, f32[768,384]{1,0:T(8,128)S(1)} %collective-permute-done.1.rest_1_, ...), custom_call_target="tpu_custom_call" | custom-call | flops 1509949440 | bytes 23592960 | tf_op jit(solution)/shard_map/pallas_call | solution.py:125
  104.2 17.2 %all-gather.3.cloned.1.call-done = f32[16384,128]{1,0:T(8,128)} async-done(((f32[1024,128]{1,0:T(8,128)}), f32[16384,128]{1,0:T(8,128)}) %all-gather.3.cloned.1.call-update) | async-done | bytes 8388624 | tf_op jit(solution)/shard_map/all_gather | solution.py:324
  121.4 6.9 %shard_map.79 = f32[768,384]{1,0:T(8,128)S(1)} custom-call(s32[4,21]{1,0:T(4,128)S(1)} %concatenate.16.table, f32[16,1024,128]{2,1,0:T(8,128)} %bitcast.25, bf16[10,768,384]{2,1,0:T(8,128)(2,1)} %get-tuple-element.25.high_hbm, bf16[10,768,384]{2,1,0:T(8,128)(2,1)} %get-tuple-element.26.low_hbm), custom_call_target="tpu_custom_call" | custom-call | flops 2717908992 | bytes 7077888 | tf_op jit(solution)/shard_map/pallas_call | solution.py:218
  128.2 4.5 %collective-permute-start.9 = (f32[768,384]{1,0:T(8,128)S(1)}, f32[768,384]{1,0:T(8,128)S(1)}, u32[]{:S(2)}, u32[]{:S(2)}) collective-permute-start(f32[768,384]{1,0:T(8,128)S(1)} %shard_map.79), channel_id=1, source_target_pairs={{0,64},{8,200},{64,128},{72,8},{128,192},{136,72},{192,0},{200,136... | collective-permute-start | bytes 3538952 | tf_op jit(solution)/shard_map/ppermute | solution.py:363
  132.8 11.2 %shard_map.78 = (f32[768,384]{1,0:T(8,128)S(1)}, f32[768,384]{1,0:T(8,128)S(1)}) custom-call(s32[4,21]{1,0:T(4,128)S(1)} %concatenate.16.table, f32[16,1024,128]{2,1,0:T(8,128)} %bitcast.26, bf16[10,768,384]{2,1,0:T(8,128)(2,1)} %get-tuple-element.25.high_hbm, bf16[10,768,384]{2,1,0:T(8,128)(2,1)} %get-tuple-element.26.low_hbm), custom_call_target="tpu_custom_call" | custom-call | flops 5435817984 | bytes 14155776 | tf_op jit(solution)/shard_map/pallas_call | solution.py:218
  144.0 1.9 %collective-permute-start.11 = (f32[768,384]{1,0:T(8,128)S(1)}, f32[768,384]{1,0:T(8,128)S(1)}, u32[]{:S(2)}, u32[]{:S(2)}) collective-permute-start(f32[768,384]{1,0:T(8,128)S(1)} %get-tuple-element.31), channel_id=1, source_target_pairs={{0,192},{8,72},{64,0},{72,136},{128,64},{136,200},{192,128},{200,8... | collective-permute-start | bytes 3538952 | tf_op jit(solution)/shard_map/ppermute | solution.py:365
  146.0 0.0 collective-permute-done.9.second
  146.0 1.6 shard_map.80
  147.6 4.8 %collective-permute-start.10 = (f32[1,384]{1,0:T(1,128)S(1)}, f32[1,384]{1,0:T(1,128)S(1)}, u32[]{:S(2)}, u32[]{:S(2)}) collective-permute-start(f32[1,384]{1,0:T(1,128)S(1)} %get-tuple-element.29), channel_id=1, source_target_pairs={{0,64},{8,200},{64,128},{72,8},{128,192},{136,72},{192,0},{200,136... | collective-permute-start | bytes 4616 | tf_op jit(solution)/shard_map/ppermute | solution.py:367
  152.4 0.7 collective-permute-done.10
  153.1 5.4 %collective-permute-start.12 = (f32[768,384]{1,0:T(8,128)S(1)}, f32[768,384]{1,0:T(8,128)S(1)}, u32[]{:S(2)}, u32[]{:S(2)}) collective-permute-start(f32[768,384]{1,0:T(8,128)S(1)} %get-tuple-element.36), channel_id=1, source_target_pairs={{0,64},{8,200},{64,128},{72,8},{128,192},{136,72},{192,0},{200,136... | collective-permute-start | bytes 3538952 | tf_op jit(solution)/shard_map/ppermute | solution.py:369
  158.5 6.9 %shard_map.81.first = f32[768,384]{1,0:T(8,128)S(1)} custom-call(s32[4,21]{1,0:T(4,128)S(1)} %concatenate.16.table, f32[16,1024,128]{2,1,0:T(8,128)} %bitcast.27, bf16[10,768,384]{2,1,0:T(8,128)(2,1)} %get-tuple-element.25.high_hbm, bf16[10,768,384]{2,1,0:T(8,128)(2,1)} %get-tuple-element.26.low_hbm), custom_call_target="tpu_custom_call" | custom-call | flops 2717908992 | bytes 7077888 | tf_op jit(solution)/shard_map/pallas_call | solution.py:218
  165.4 0.0 collective-permute-done.11.second
  165.4 1.6 shard_map.82
  167.0 0.6 all_to_all.8
  167.7 4.5 %all-to-all-start = ((f32[8,1,384]{2,1,0:T(1,128)}), f32[8,1,384]{2,1,0:T(1,128)S(1)}, u32[]{:S(2)}, u32[]{:S(2)}) async-start(f32[8,1,384]{2,1,0:T(1,128)} %all_to_all.8), calls=%async_computation | async-start | bytes 24576 | tf_op jit(solution)/shard_map/all_to_all | solution.py:374
  172.1 0.8 fusion
  173.0 3.8 %all-to-all-done = f32[8,1,384]{2,1,0:T(1,128)S(1)} async-done(((f32[8,1,384]{2,1,0:T(1,128)}), f32[8,1,384]{2,1,0:T(1,128)S(1)}, u32[]{:S(2)}, u32[]{:S(2)}) %all-to-all-start) | async-done | bytes 12320 | tf_op jit(solution)/shard_map/all_to_all | solution.py:374
  176.8 0.6 copy.17
  177.4 0.0 collective-permute-done.12.second
  177.4 0.0 copy-start.1
  177.4 0.0 copy-start.2
  177.4 1.5 shard_map.83
  178.9 0.0 copy-done.1
  178.9 0.0 copy-done.2
  179.0 0.6 reshape_add_fusion
  (6 shorter events, 0.1 us)
Async XLA Ops:
  7.2 114.2 %all-gather.3.cloned.1.call-start = ((), (), s32[]{:S(2)}) async-start(), calls=%async_computation.1 | async-start | bytes 8912896 | tf_op jit(solution)/shard_map/all_gather | solution.py:324
  7.9 33.2 %collective-permute-start = (f32[768,384]{1,0:T(8,128)}, f32[768,384]{1,0:T(8,128)S(1)}, u32[]{:S(2)}, u32[]{:S(2)}) collective-permute-start(f32[768,384]{1,0:T(8,128)} %bitcast.21), channel_id=1, source_target_pairs={{0,48},{8,64},{16,144},{24,224},{32,32},{40,112},{48,176},{56,240}... | collective-permute-start | bytes 3538952 | tf_op jit(solution)/shard_map/ppermute | solution.py:348
  41.1 5.1 %collective-permute-start.1 = (f32[768,384]{1,0:T(8,128)S(1)}, f32[768,384]{1,0:T(8,128)S(1)}, u32[]{:S(2)}, u32[]{:S(2)}) collective-permute-start(f32[768,384]{1,0:T(8,128)S(1)} %collective-permute-done.rest_0_), channel_id=1, source_target_pairs={{0,8},{8,0},{1,9},{9,1},{2,10},{10,2},{3,11},{11,3},{4,12},{12,4},... | collective-permute-start | bytes 3538952 | tf_op jit(solution)/shard_map/ppermute | solution.py:352
  43.0 17.3 %collective-permute-start.2 = (f32[768,384]{1,0:T(8,128)S(1)}, f32[768,384]{1,0:T(8,128)S(1)}, u32[]{:S(2)}, u32[]{:S(2)}) collective-permute-start(f32[768,384]{1,0:T(8,128)S(1)} %collective-permute-done.rest_0_), channel_id=1, source_target_pairs={{0,16},{8,56},{16,32},{24,8},{32,48},{40,24},{48,0},{56,40},{1,17}... | collective-permute-start | bytes 3538952 | tf_op jit(solution)/shard_map/ppermute | solution.py:353
  46.2 26.8 %collective-permute-start.3 = (f32[768,384]{1,0:T(8,128)S(1)}, f32[768,384]{1,0:T(8,128)S(1)}, u32[]{:S(2)}, u32[]{:S(2)}) collective-permute-start(f32[768,384]{1,0:T(8,128)S(1)} %collective-permute-done.1.rest_1_), channel_id=1, source_target_pairs={{0,16},{8,56},{16,32},{24,8},{32,48},{40,24},{48,0},{56,40},{1,17}... | collective-permute-start | bytes 3538952 | tf_op jit(solution)/shard_map/ppermute | solution.py:354
  60.3 25.3 %collective-permute-start.4 = (f32[768,384]{1,0:T(8,128)S(1)}, f32[768,384]{1,0:T(8,128)S(1)}, u32[]{:S(2)}, u32[]{:S(2)}) collective-permute-start(f32[768,384]{1,0:T(8,128)S(1)} %collective-permute-done.2.rest_2_), channel_id=1, source_target_pairs={{0,16},{8,56},{16,32},{24,8},{32,48},{40,24},{48,0},{56,40},{1,17}... | collective-permute-start | bytes 3538952 | tf_op jit(solution)/shard_map/ppermute | solution.py:355
  64.7 25.2 %collective-permute-start.8 = (f32[768,384]{1,0:T(8,128)}, f32[768,384]{1,0:T(8,128)S(1)}, u32[]{:S(2)}, u32[]{:S(2)}) collective-permute-start(f32[768,384]{1,0:T(8,128)} %bitcast.22), channel_id=1, source_target_pairs={{0,192},{8,72},{64,0},{72,136},{128,64},{136,200},{192,128},{200,8... | collective-permute-start | bytes 3538952 | tf_op jit(solution)/shard_map/ppermute | solution.py:358
  66.7 23.3 %collective-permute-start.5 = (f32[768,384]{1,0:T(8,128)S(1)}, f32[768,384]{1,0:T(8,128)S(1)}, u32[]{:S(2)}, u32[]{:S(2)}) collective-permute-start(f32[768,384]{1,0:T(8,128)S(1)} %collective-permute-done.2.rest_2_), channel_id=1, source_target_pairs={{0,8},{8,0},{1,9},{9,1},{2,10},{10,2},{3,11},{11,3},{4,12},{12,4},... | collective-permute-start | bytes 3538952 | tf_op jit(solution)/shard_map/ppermute | solution.py:357
  73.0 17.0 %collective-permute-start.6 = (f32[768,384]{1,0:T(8,128)S(1)}, f32[768,384]{1,0:T(8,128)S(1)}, u32[]{:S(2)}, u32[]{:S(2)}) collective-permute-start(f32[768,384]{1,0:T(8,128)S(1)} %collective-permute-done.3.rest_3_), channel_id=1, source_target_pairs={{0,8},{8,0},{1,9},{9,1},{2,10},{10,2},{3,11},{11,3},{4,12},{12,4},... | collective-permute-start | bytes 3538952 | tf_op jit(solution)/shard_map/ppermute | solution.py:357
  85.6 6.8 %collective-permute-start.7 = (f32[768,384]{1,0:T(8,128)S(1)}, f32[768,384]{1,0:T(8,128)S(1)}, u32[]{:S(2)}, u32[]{:S(2)}) collective-permute-start(f32[768,384]{1,0:T(8,128)S(1)} %collective-permute-done.4.rest_4_), channel_id=1, source_target_pairs={{0,8},{8,0},{1,9},{9,1},{2,10},{10,2},{3,11},{11,3},{4,12},{12,4},... | collective-permute-start | bytes 3538952 | tf_op jit(solution)/shard_map/ppermute | solution.py:357
  92.4 1.3 copy-start
  128.2 17.7 %collective-permute-start.9 = (f32[768,384]{1,0:T(8,128)S(1)}, f32[768,384]{1,0:T(8,128)S(1)}, u32[]{:S(2)}, u32[]{:S(2)}) collective-permute-start(f32[768,384]{1,0:T(8,128)S(1)} %shard_map.79), channel_id=1, source_target_pairs={{0,64},{8,200},{64,128},{72,8},{128,192},{136,72},{192,0},{200,136... | collective-permute-start | bytes 3538952 | tf_op jit(solution)/shard_map/ppermute | solution.py:363
  144.0 21.3 %collective-permute-start.11 = (f32[768,384]{1,0:T(8,128)S(1)}, f32[768,384]{1,0:T(8,128)S(1)}, u32[]{:S(2)}, u32[]{:S(2)}) collective-permute-start(f32[768,384]{1,0:T(8,128)S(1)} %get-tuple-element.31), channel_id=1, source_target_pairs={{0,192},{8,72},{64,0},{72,136},{128,64},{136,200},{192,128},{200,8... | collective-permute-start | bytes 3538952 | tf_op jit(solution)/shard_map/ppermute | solution.py:365
  147.6 5.5 %collective-permute-start.10 = (f32[1,384]{1,0:T(1,128)S(1)}, f32[1,384]{1,0:T(1,128)S(1)}, u32[]{:S(2)}, u32[]{:S(2)}) collective-permute-start(f32[1,384]{1,0:T(1,128)S(1)} %get-tuple-element.29), channel_id=1, source_target_pairs={{0,64},{8,200},{64,128},{72,8},{128,192},{136,72},{192,0},{200,136... | collective-permute-start | bytes 4616 | tf_op jit(solution)/shard_map/ppermute | solution.py:367
  153.1 24.3 %collective-permute-start.12 = (f32[768,384]{1,0:T(8,128)S(1)}, f32[768,384]{1,0:T(8,128)S(1)}, u32[]{:S(2)}, u32[]{:S(2)}) collective-permute-start(f32[768,384]{1,0:T(8,128)S(1)} %get-tuple-element.36), channel_id=1, source_target_pairs={{0,64},{8,200},{64,128},{72,8},{128,192},{136,72},{192,0},{200,136... | collective-permute-start | bytes 3538952 | tf_op jit(solution)/shard_map/ppermute | solution.py:369
  167.7 9.1 %all-to-all-start = ((f32[8,1,384]{2,1,0:T(1,128)}), f32[8,1,384]{2,1,0:T(1,128)S(1)}, u32[]{:S(2)}, u32[]{:S(2)}) async-start(f32[8,1,384]{2,1,0:T(1,128)} %all_to_all.8), calls=%async_computation | async-start | bytes 24576 | tf_op jit(solution)/shard_map/all_to_all | solution.py:374
  177.4 1.6 copy-start.1
  177.4 1.6 copy-start.2
Sparse Core Ops, SparseCore 0:
  10.1 111.2 all-gather.2
